TPU v7x, 32 devices: a whole 2x2x4 slice. The times are simulated.
32 devices in a mesh: dp: 8 (over z, y), mp: 4 (over x, core).
Axes of the slice: x: 2, y: 2, z: 4, core: 2. Of those that a mesh axis runs over, the one named last changes fastest.
Arguments:
- tokens: bfloat16 [4096, 2048], P('dp'), may hold values from -6 to 6
- gain_first: float32 [2048], replicated, may hold values from 0.25 to 1.75
- w_qkv: bfloat16 [2048, 3, 2048], P(None, None, 'mp'), may hold values from -0.125 to 0.125
- w_out: bfloat16 [2048, 2048], P('mp'), may hold values from -0.5 to 0.5
- gain_second: float32 [2048], replicated, may hold values from 0.25 to 1.75
- router: float32 [2048, 4], replicated, may hold values from -0.09375 to 0.09375
- w_up: bfloat16 [4, 2048, 2048], P(None, None, 'mp'), may hold values from -0.125 to 0.125
- w_down: bfloat16 [4, 2048, 2048], P(None, 'mp'), may hold values from -0.0625 to 0.0625
- slot: int32 [4096], P('dp'), may hold values from 0 to 639, as said below
- cotangent: bfloat16 [4096, 2048], P('dp'), may hold values from -6 to 6
Outputs:
- output: bfloat16 [4096, 2048], P('dp')
- grad_tokens: bfloat16 [4096, 2048], P('dp')
- grad_gain_first: float32 [2048], replicated
- grad_qkv: float32 [2048, 3, 2048], P(None, None, 'mp')
- grad_out: float32 [2048, 2048], P('mp')
- grad_gain_second: float32 [2048], replicated
- grad_router: float32 [2048, 4], replicated
- grad_up: float32 [4, 2048, 2048], P(None, None, 'mp')
- grad_down: float32 [4, 2048, 2048], P(None, 'mp')
Inputs may be any that keep to these rules, and one draw needn't show every extreme that they name: Within the 512 tokens of one index of dp all slots differ; a token with slot s goes to index floor(s / 80) of dp, row s mod 80 of that index's block from the sender. One index of dp, drawn from the seed, receives exactly 80 tokens from every index.
All inputs are finite; a program needn't handle non-finite values.
Results may differ from a plain program's by a relative error of at most 0.022.
Values may be sent and summed in bfloat16 or wider, within the bound.
No kernel may reach another device: no remote copies, remote signals or barrier semaphores. Data moves between devices by JAX's collectives and lax.ppermute only.
A program may use at most 192 MiB of HBM per device.

v0:
```python
from functools import partial

import jax
import jax.numpy as jnp
from jax import lax
from jax.sharding import PartitionSpec as P

HEAD = 128


HIGHEST = lax.Precision.HIGHEST
EPSILON = 1e-05


def normalize(values, gain):
    return values * lax.rsqrt(jnp.mean(values * values, -1, keepdims=True) + EPSILON) * gain


def rotary_table(length, head_size):
    position = jnp.arange(length, dtype=jnp.float32)
    inverse = 10000.0 ** (-jnp.arange(0, head_size, 2, dtype=jnp.float32) / head_size)
    angles = position[:, None] * inverse[None, :]
    angles = jnp.concatenate([angles, angles], -1)
    return (jnp.cos(angles), jnp.sin(angles))


def rotate(values, cos_table, sin_table):
    middle = values.shape[-1] // 2
    turned = jnp.concatenate([-values[..., middle:], values[..., :middle]], -1)
    return values * cos_table[:, None, :] + turned * sin_table[:, None, :]


def rotate_pair(first, second, cos_table, sin_table):
    return (rotate(first, cos_table, sin_table), rotate(second, cos_table, sin_table))


def masked_scores(query_rows, key_rows, scale):
    length = query_rows.shape[0]
    scores = (
        jnp.einsum("qhe,khe->hqk", query_rows, key_rows, preferred_element_type=jnp.float32) * scale
    )
    causal = jnp.arange(length)[:, None] >= jnp.arange(length)[None, :]
    return jnp.where(causal[None], scores, -1000000000.0)


def nested_quarters(sent_rows, grad_rows, row_buckets, w_up, w_down, row_bounds):
    length, model = sent_rows.shape
    partial_rows = jnp.zeros((length, model), jnp.float32)
    partial_grad = jnp.zeros((length, model), jnp.float32)
    up_terms = []
    down_terms = []
    for level in range(len(row_bounds)):
        rows = row_bounds[level]
        inputs = sent_rows[:rows]
        upstream = grad_rows[:rows]
        keep = (row_buckets[:rows] >= level).astype(jnp.float32)[:, None]
        pre = jnp.dot(inputs, w_up[level], preferred_element_type=jnp.float32)
        active = jax.nn.relu(pre) * keep
        act = jnp.square(active).astype(jnp.bfloat16)
        partial_rows = partial_rows.at[:rows].add(
            jnp.dot(act, w_down[level], preferred_element_type=jnp.float32)
        )
        grad_act = jnp.dot(upstream, w_down[level].T, preferred_element_type=jnp.float32)
        grad_pre = (grad_act * 2.0 * active).astype(jnp.bfloat16)
        down_terms.append(jnp.dot(act.T, upstream, preferred_element_type=jnp.float32))
        up_terms.append(jnp.dot(inputs.T, grad_pre, preferred_element_type=jnp.float32))
        partial_grad = partial_grad.at[:rows].add(
            jnp.dot(grad_pre, w_up[level].T, preferred_element_type=jnp.float32)
        )
    return (partial_rows, partial_grad, jnp.stack(up_terms), jnp.stack(down_terms))


def on_device(tokens, gain_first, w_qkv, w_out, gain_second, router, w_up, w_down, slot, cotangent):
    length = tokens.shape[0]
    local_heads = w_qkv.shape[2] // HEAD
    buckets = w_up.shape[0]
    devices_dp = lax.axis_size("dp")
    groups = devices_dp // buckets
    capacity = length * 5 // (4 * devices_dp)
    bucket_ids = slot // capacity // groups
    scale = HEAD ** (-0.5)
    source = tokens.astype(jnp.float32)
    normed_first, first_back = jax.vjp(normalize, source, gain_first)
    normed_low = normed_first.astype(jnp.bfloat16)
    cos_table, sin_table = rotary_table(length, HEAD)
    projected = jnp.einsum("td,dch->cth", normed_low, w_qkv, preferred_element_type=jnp.float32)
    split_heads = projected.reshape(3, length, local_heads, HEAD)
    (query_turned, key_turned), rope_back = jax.vjp(
        partial(rotate_pair, cos_table=cos_table, sin_table=sin_table),
        split_heads[0],
        split_heads[1],
    )
    query_low = query_turned.astype(jnp.bfloat16)
    key_low = key_turned.astype(jnp.bfloat16)
    value_low = split_heads[2].astype(jnp.bfloat16)
    scores = masked_scores(query_low, key_low, scale)
    top_score = jnp.max(scores, -1, keepdims=True)
    log_total = top_score + jnp.log(jnp.sum(jnp.exp(scores - top_score), -1, keepdims=True))
    weights_low = jnp.exp(scores - log_total).astype(jnp.bfloat16)
    mixed = jnp.einsum("hqk,khe->qhe", weights_low, value_low, preferred_element_type=jnp.float32)
    mixed = mixed.reshape(length, local_heads * HEAD).astype(jnp.bfloat16)
    attn = lax.psum(jnp.dot(mixed, w_out, preferred_element_type=jnp.float32), "mp")
    resid = source + attn
    normed_second, second_back = jax.vjp(normalize, resid, gain_second)
    logits = jnp.dot(normed_second, router, precision=HIGHEST)
    prob = jax.nn.softmax(logits, axis=-1)
    onehot = (bucket_ids[:, None] == jnp.arange(buckets)[None, :]).astype(jnp.float32)
    gate = buckets * jnp.sum(prob * onehot, -1)
    sent = normed_second.astype(jnp.bfloat16)
    grad_output = cotangent.astype(jnp.float32)
    grad_ffn = (gate[:, None] * grad_output).astype(jnp.bfloat16)
    positions = jnp.arange(length, dtype=jnp.int32)
    order = jnp.argsort((buckets - 1 - bucket_ids) * length + positions)
    inverse = jnp.zeros_like(order).at[order].set(positions)
    row_bounds = [min(length, (buckets - level) * groups * capacity) for level in range(buckets)]
    partial_rows, partial_grad, grad_up, grad_down = nested_quarters(
        sent[order], grad_ffn[order], bucket_ids[order], w_up, w_down, row_bounds
    )
    summed_rows = lax.psum(partial_rows, "mp").astype(jnp.bfloat16)
    ffn_rows = summed_rows[inverse].astype(jnp.float32)
    summed_grad = lax.psum(partial_grad, "mp").astype(jnp.bfloat16)
    grad_sent = summed_grad[inverse].astype(jnp.float32)
    output = (resid + gate[:, None] * ffn_rows).astype(jnp.bfloat16)
    grad_gate = jnp.sum(grad_output * ffn_rows, -1)
    grad_prob = buckets * grad_gate[:, None] * onehot
    grad_logits = prob * (grad_prob - jnp.sum(grad_prob * prob, -1, keepdims=True))
    grad_router = jnp.dot(normed_second.T, grad_logits, precision=HIGHEST)
    grad_second = grad_sent + jnp.dot(grad_logits, router.T, precision=HIGHEST)
    grad_resid, grad_gain_second = second_back(grad_second)
    grad_resid = grad_resid + grad_output
    grad_attn = grad_resid.astype(jnp.bfloat16)
    grad_wout = jnp.einsum("th,td->hd", mixed, grad_attn, preferred_element_type=jnp.float32)
    grad_mixed = jnp.einsum("td,hd->th", grad_attn, w_out, preferred_element_type=jnp.float32)
    grad_mixed = grad_mixed.reshape(length, local_heads, HEAD).astype(jnp.bfloat16)
    scores_again = masked_scores(query_low, key_low, scale)
    probs_again = jnp.exp(scores_again - log_total)
    grad_probs = jnp.einsum(
        "qhe,khe->hqk", grad_mixed, value_low, preferred_element_type=jnp.float32
    )
    grad_scores = probs_again * (grad_probs - jnp.sum(grad_probs * probs_again, -1, keepdims=True))
    grad_scores_low = grad_scores.astype(jnp.bfloat16)
    grad_query = (
        jnp.einsum("hqk,khe->qhe", grad_scores_low, key_low, preferred_element_type=jnp.float32)
        * scale
    )
    grad_key = (
        jnp.einsum("hqk,qhe->khe", grad_scores_low, query_low, preferred_element_type=jnp.float32)
        * scale
    )
    grad_value = jnp.einsum(
        "hqk,qhe->khe", weights_low, grad_mixed, preferred_element_type=jnp.float32
    )
    grad_query_raw, grad_key_raw = rope_back((grad_query, grad_key))
    grad_projected = jnp.stack([grad_query_raw, grad_key_raw, grad_value]).reshape(
        3, length, local_heads * HEAD
    )
    grad_projected = grad_projected.astype(jnp.bfloat16)
    grad_wqkv = jnp.einsum(
        "td,cth->dch", normed_low, grad_projected, preferred_element_type=jnp.float32
    )
    partial_first = jnp.einsum(
        "cth,dch->td", grad_projected, w_qkv, preferred_element_type=jnp.float32
    )
    grad_first = lax.psum(partial_first.astype(jnp.bfloat16), "mp").astype(jnp.float32)
    grad_source, grad_gain_first = first_back(grad_first)
    grad_tokens = (grad_source + grad_resid).astype(jnp.bfloat16)
    summed = (
        lax.psum(grad_gain_first.astype(jnp.bfloat16), "dp").astype(jnp.float32),
        lax.psum(grad_wqkv.astype(jnp.bfloat16), "dp").astype(jnp.float32),
        lax.psum(grad_wout.astype(jnp.bfloat16), "dp").astype(jnp.float32),
        lax.psum(grad_gain_second.astype(jnp.bfloat16), "dp").astype(jnp.float32),
        lax.psum(grad_router.astype(jnp.bfloat16), "dp").astype(jnp.float32),
        lax.psum(grad_up.astype(jnp.bfloat16), "dp").astype(jnp.float32),
        lax.psum(grad_down.astype(jnp.bfloat16), "dp").astype(jnp.float32),
    )
    return (
        output,
        grad_tokens,
        summed[0],
        summed[1],
        summed[2],
        summed[3],
        summed[4],
        summed[5],
        summed[6],
    )


def solution(mesh):
    placed = (
        P("dp", None),
        P(),
        P(None, None, "mp"),
        P("mp", None),
        P(),
        P(),
        P(None, None, "mp"),
        P(None, "mp", None),
        P("dp"),
        P("dp", None),
    )
    return jax.shard_map(
        on_device,
        mesh=mesh,
        in_specs=placed,
        out_specs=(
            P("dp", None),
            P("dp", None),
            P(),
            P(None, None, "mp"),
            P("mp", None),
            P(),
            P(),
            P(None, None, "mp"),
            P(None, "mp", None),
        ),
        check_vma=False,
    )
```

profile of v0, /device:TPU:0, one launch (start us, length us, event | category | flops | bytes accessed | tf_op | source)
XLA Modules:
  0.0 1276.4 jit_solution(15622935353198770677)
XLA Ops:
  9.6 6.4 convolution_bitcast_fusion
  36.6 78.2 %all-reduce.12.cloned.1.call-done = f32[512,2048]{1,0:T(8,128)} async-done(((f32[512,2048]{1,0:T(8,128)}), f32[512,2048]{1,0:T(8,128)}) %all-reduce.12.cloned.1.call-update) | async-done | bytes 4194320 | tf_op jit(solution)/shard_map/psum | solution.py:102
  124.9 7.5 gather_fusion
  148.4 5.3 constant_dynamic-update-slice_fusion.3
  157.6 76.4 %all-reduce.17 = bf16[512,2048]{1,0:T(8,128)(2,1)} all-reduce(f32[512,2048]{1,0:T(8,128)} %fusion.25), channel_id=1, replica_groups=mesh['dp'=8,'mp'=4] {'mp'}, use_global_device_ids=true, to_apply=%region_9.10 | all-reduce | flops 1048576 | bytes 6291456 | tf_op jit(solution)/shard_map/psum | solution.py:119
  234.0 7.1 gather_fusion.2
  245.9 7.2 gather_fusion.3
  283.5 5.3 constant_dynamic-update-slice_fusion.1
  293.4 77.5 %all-reduce.18 = bf16[512,2048]{1,0:T(8,128)(2,1)} all-reduce(f32[512,2048]{1,0:T(8,128)} %fusion.24), channel_id=1, replica_groups=mesh['dp'=8,'mp'=4] {'mp'}, use_global_device_ids=true, to_apply=%region_11.12 | all-reduce | flops 1048576 | bytes 6291456 | tf_op jit(solution)/shard_map/psum | solution.py:121
  370.9 7.1 gather_fusion.4
  378.0 6.9 multiply_reduce_fusion
  399.9 4.7 multiply_convert_fusion
  409.0 8.1 bitcast_convert_fusion
  417.2 8.2 convolution_convert_fusion
  425.4 7.4 pad_maximum_fusion.1
  439.7 4.9 fusion.26
  444.5 32.7 %all-reduce.14.cloned.1.call-done = bf16[512,2048]{1,0:T(8,128)(2,1)} async-done(((bf16[512,2048]{1,0:T(8,128)(2,1)}), bf16[512,2048]{1,0:T(8,128)(2,1)}) %all-reduce.14.cloned.1.call-update) | async-done | bytes 2097168 | tf_op jit(solution)/shard_map/psum | solution.py:164
  481.2 38.9 %all-reduce.4 = (bf16[2048]{0:T(1024)(128)(2,1)S(1)}, bf16[2048]{0:T(1024)(128)(2,1)S(1)}, bf16[2048,4]{0,1:T(4,128)(2,1)S(1)}) all-reduce(bf16[2048]{0:T(1024)(128)(2,1)S(1)} %get-tuple-element.125, bf16[2048]{0:T(1024)(128)(2,1)S(1)} %get-tuple-element.123, bf16[2048,4]{0,1:T(4,128)(2,1)S(1)} %fusion.26), channel_id=1, replica_groups=mesh['dp'=8,'mp'=4] {'dp'}, use_global_device_ids=true, to_apply=%region_19.20 | all-reduce | flops 12288 | bytes 49152 | tf_op jit(solution)/shard_map/psum | solution.py:168
  521.9 6.0 fusion.9
  527.9 707.3 %all-reduce.16.cloned.1.call-done = (bf16[2048,3,512]{2,0,1:T(8,128)(2,1)}, bf16[512,2048]{1,0:T(8,128)(2,1)}, bf16[4,2048,512]{2,1,0:T(8,128)(2,1)}, bf16[4,512,2048]{2,1,0:T(8,128)(2,1)}) async-done(((bf16[2048,3,512]{2,0,1:T(8,128)(2,1)}, bf16[512,2048]{1,0:T(8,128)(2,1)}, bf16[4,2048,512]{2,1,0:T(8,128)(2,1)}, bf16[4,512,2048]{2,1,0:T(8,128)(2,1)}), (bf16[2048,3,512]{2,0,1:T(8,128)(2,1)}, ...) | async-done | bytes 25165840 | tf_op jit(solution)/shard_map/psum | solution.py:169
  1235.2 4.3 convert_element_type.194
  1239.5 6.6 convert_element_type.192
  1246.0 11.9 convert_element_type.199
  1258.0 11.7 convert_element_type.200
  (181 shorter events, 124.2 us)
Async XLA Ops:
  7.2 16.0 %copy-start = (bf16[512,2048]{1,0:T(8,128)(2,1)S(1)}, bf16[512,2048]{1,0:T(8,128)(2,1)}, u32[]{:S(2)}) copy-start(bf16[512,2048]{1,0:T(8,128)(2,1)} %param.33) | copy-start | bytes 6291460
  7.2 107.7 %all-reduce.12.cloned.1.call-start = ((), (), s32[]{:S(2)}) async-start(), calls=%async_computation | async-start | bytes 8388608 | tf_op jit(solution)/shard_map/psum | solution.py:102
  9.5 6.5 copy-start.39
  26.5 450.8 %all-reduce.14.cloned.1.call-start = ((), (), s32[]{:S(2)}) async-start(), calls=%async_computation.1 | async-start | bytes 4194304 | tf_op jit(solution)/shard_map/psum | solution.py:164
  36.6 81.8 %copy-start.36 = (f32[2048]{0:T(1024)S(1)}, f32[2048]{0:T(1024)}, u32[]{:S(2)}) copy-start(f32[2048]{0:T(1024)} %param.34) | copy-start | bytes 24580
  134.8 21.2 %copy-start.22 = (f32[160,512]{1,0:T(8,128)}, f32[160,512]{1,0:T(8,128)S(1)}, u32[]{:S(2)}) copy-start(f32[160,512]{1,0:T(8,128)S(1)} %fusion.143) | copy-start | bytes 983044
  134.8 10.3 slice-start.2
  137.8 15.8 %copy-start.14 = (f32[320,512]{1,0:T(8,128)}, f32[320,512]{1,0:T(8,128)S(1)}, u32[]{:S(2)}) copy-start(f32[320,512]{1,0:T(8,128)S(1)} %fusion.122) | copy-start | bytes 1966084
  137.8 7.3 slice-start.3
  140.9 7.5 copy-start.26
  255.8 35.6 %copy-start.28 = (bf16[160,512]{1,0:T(8,128)(2,1)}, bf16[160,512]{1,0:T(8,128)(2,1)S(1)}, u32[]{:S(2)}) copy-start(bf16[160,512]{1,0:T(8,128)(2,1)S(1)} %fusion.146) | copy-start | bytes 491524
  259.0 29.8 %copy-start.34 = (bf16[320,512]{1,0:T(8,128)(2,1)}, bf16[320,512]{1,0:T(8,128)(2,1)S(1)}, u32[]{:S(2)}) copy-start(bf16[320,512]{1,0:T(8,128)(2,1)S(1)} %fusion.131) | copy-start | bytes 983044
  270.2 7.4 slice-start
  377.9 7.0 copy-start.2
  377.9 7.0 copy-start.5
  377.9 7.0 copy-start.7
  409.0 8.1 copy-start.30
  409.0 8.1 copy-start.31
  409.0 8.1 copy-start.38
  425.4 7.4 copy-start.29
  425.4 8.2 copy-start.35
  425.4 809.8 %all-reduce.16.cloned.1.call-start = ((), (), s32[]{:S(2)}) async-start(), calls=%async_computation.2 | async-start | bytes 50331648 | tf_op jit(solution)/shard_map/psum | solution.py:169
  425.4 7.4 copy-start.13
  439.7 82.2 %copy-start.40 = (f32[512]{0:T(512)S(1)}, f32[512]{0:T(512)}, u32[]{:S(2)}) copy-start(f32[512]{0:T(512)} %copy-done.39) | copy-start | bytes 6148
  (25 other events, 73.4 us)
Sparse Core Ops, SparseCore 0:
  26.6 88.2 all-reduce.11
  425.5 51.6 all-reduce.13
  483.3 751.8 all-reduce.15
where the time goes:
time: 1280 us
  waiting for transfers between devices  818 us (64%)
  blocking collectives  193 us (15%)
  matrix products  121 us (9%)
  other arithmetic  86.1 us (7%)
  local copies, waits for them, and re-layouts  43.3 us (3%)
  between operations  14.7 us (1%)
    psum x1, waiting for transfers between devices, on_device(): lax.psum(grad_wqkv.astype(jnp.bfloat16), 'dp').astype(jnp.float32)  707 us
    psum x1, waiting for transfers between devices, on_device(): lax.psum(jnp.dot(mixed, w_out, preferred_element_type=jnp.float32), 'mp')  78.2 us
    psum x1, blocking collectives, on_device(): summed_grad = lax.psum(partial_grad, 'mp').astype(jnp.bfloat16)  77.5 us
    psum x1, blocking collectives, on_device(): summed_rows = lax.psum(partial_rows, 'mp').astype(jnp.bfloat16)  76.4 us
    psum x1, blocking collectives, on_device(): lax.psum(grad_gain_first.astype(jnp.bfloat16), 'dp').astype(jnp.float32)  38.9 us
    psum x1, waiting for transfers between devices, on_device(): lax.psum(partial_first.astype(jnp.bfloat16), 'mp').astype(jnp.float32)  32.7 us
  transfers between devices with their start and end apart: 3, of which 3 were waited for; matrix products, arithmetic and copies ran while one was open for 3% of the time, Pallas kernels for 0%

commit v1 on v0

v1 whole, which is shorter than its diff:
```python
from functools import partial

import jax
import jax.numpy as jnp
from jax import lax
from jax.experimental import pallas as pl
from jax.experimental.pallas import tpu as pltpu
from jax.sharding import PartitionSpec as P

HEAD = 128
HIGHEST = lax.Precision.HIGHEST
EPSILON = 1e-05
F32 = jnp.float32
BF16 = jnp.bfloat16
VMEM_LIMIT = 56 * 1024 * 1024
NN = (((1,), (0,)), ((), ()))
NT = (((1,), (1,)), ((), ()))


def dot(a, b, dims=NN):
    return lax.dot_general(a, b, dims, preferred_element_type=F32)


def low(x):
    return lax.reduce_precision(x, 8, 7).astype(BF16)


def params():
    return pltpu.CompilerParams(vmem_limit_bytes=VMEM_LIMIT)


def cost(flops, nbytes, transcendentals=0):
    return pl.CostEstimate(flops=flops, bytes_accessed=nbytes, transcendentals=transcendentals)


def rotary_table(length, head_size):
    position = jnp.arange(length, dtype=F32)
    inverse = 10000.0 ** (-jnp.arange(0, head_size, 2, dtype=F32) / head_size)
    angles = position[:, None] * inverse[None, :]
    angles = jnp.concatenate([angles, angles], -1)
    sign = jnp.where(jnp.arange(head_size) < head_size // 2, -1.0, 1.0)
    return jnp.cos(angles), jnp.sin(angles) * sign


def attend_kernel(x_ref, gain_ref, w_ref, cos_ref, sin_ref, wout_ref,
                  part_ref, normed_ref, qkv_ref, lse_ref, mixed_ref, *, heads, steps):
    g = pl.program_id(0)
    length = x_ref.shape[0]
    half = length // 2
    scale = HEAD ** -0.5

    @pl.when(g == 0)
    def _():
        values = x_ref[...].astype(F32)
        inv = lax.rsqrt(jnp.mean(values * values, -1, keepdims=True) + EPSILON)
        normed_ref[...] = (values * inv * gain_ref[...]).astype(BF16)

    normed = normed_ref[...]
    cos, sin = cos_ref[...], sin_ref[...]
    projected = [dot(normed, w_ref[c]) for c in range(3)]
    for h in range(heads):
        cols = slice(h * HEAD, (h + 1) * HEAD)
        q, k, v = (p[:, cols] for p in projected)
        q = (q * cos + pltpu.roll(q, HEAD // 2, 1) * sin).astype(BF16)
        k = (k * cos + pltpu.roll(k, HEAD // 2, 1) * sin).astype(BF16)
        v = v.astype(BF16)
        qkv_ref[0, :, cols] = q
        qkv_ref[1, :, cols] = k
        qkv_ref[2, :, cols] = v
        for b in range(2):
            rows = slice(b * half, (b + 1) * half)
            keys = (b + 1) * half
            scores = dot(q[rows], k[:keys], NT) * scale
            at = lax.broadcasted_iota(jnp.int32, scores.shape, 0) + b * half
            to = lax.broadcasted_iota(jnp.int32, scores.shape, 1)
            scores = jnp.where(at >= to, scores, -1000000000.0)
            top = jnp.max(scores, -1, keepdims=True)
            weights = jnp.exp(scores - top)
            total = jnp.sum(weights, -1, keepdims=True)
            lse_ref[h, rows, :] = jnp.broadcast_to(top + jnp.log(total), (half, HEAD))
            low = (weights * (1.0 / total)).astype(BF16)
            mixed_ref[rows, pl.ds(pl.multiple_of((g * heads + h) * HEAD, HEAD), HEAD)] = dot(low, v[:keys]).astype(BF16)

    @pl.when(g == steps - 1)
    def _():
        part_ref[...] = dot(mixed_ref[...], wout_ref[...]).astype(BF16)


def attend(tokens, gain, w3, cos, sin, w_out):
    length, model = tokens.shape
    local = w3.shape[2]
    local_heads = local // HEAD
    heads = 2 if local_heads % 2 == 0 else 1
    steps = local_heads // heads
    wide = heads * HEAD
    full = lambda *shape: pl.BlockSpec(shape, lambda g: (0,) * len(shape))
    return pl.pallas_call(
        partial(attend_kernel, heads=heads, steps=steps),
        grid=(steps,),
        in_specs=[
            full(length, model), full(1, model),
            pl.BlockSpec((3, model, wide), lambda g: (0, 0, g)),
            full(length, HEAD), full(length, HEAD), full(local, model),
        ],
        out_specs=[
            full(length, model), full(length, model),
            pl.BlockSpec((3, length, wide), lambda g: (0, 0, g)),
            pl.BlockSpec((heads, length, HEAD), lambda g: (g, 0, 0)),
            full(length, local),
        ],
        out_shape=[
            jax.ShapeDtypeStruct((length, model), BF16),
            jax.ShapeDtypeStruct((length, model), BF16),
            jax.ShapeDtypeStruct((3, length, local), BF16),
            jax.ShapeDtypeStruct((local_heads, length, HEAD), F32),
            jax.ShapeDtypeStruct((length, local), BF16),
        ],
        compiler_params=params(),
        cost_estimate=cost(2 * length * model * local * 4 + 4 * length * length * local,
                           2 * (2 * length * model + 4 * model * local), length * length * local_heads),
        name="attend",
    )(tokens, gain, w3, cos, sin, w_out)


def attend_back_kernel(ga_ref, normed_t_ref, qkv_ref, lse_ref, mixed_t_ref, wout_ref, w_ref, cos_ref, sin_ref,
                       *rest, heads, steps, deps):
    gqkv_ref, gout_ref, first_ref, acc_ref, gp_ref = rest[deps:]
    g = pl.program_id(0)
    length = ga_ref.shape[0]
    model = ga_ref.shape[1]
    half = length // 2
    scale = HEAD ** -0.5
    cos, sin = cos_ref[...], sin_ref[...]
    ga = ga_ref[...]
    gmixed = dot(ga, wout_ref[...], NT).astype(BF16)
    for h in range(heads):
        cols = slice(h * HEAD, (h + 1) * HEAD)
        q, k, v = (qkv_ref[c, :, cols] for c in range(3))
        gm = gmixed[:, cols]
        gq, gk, gv = [], [None, None], [None, None]
        for b in range(2):
            rows = slice(b * half, (b + 1) * half)
            keys = (b + 1) * half
            scores = dot(q[rows], k[:keys], NT) * scale
            at = lax.broadcasted_iota(jnp.int32, scores.shape, 0) + b * half
            to = lax.broadcasted_iota(jnp.int32, scores.shape, 1)
            probs = jnp.where(at >= to, jnp.exp(scores - lse_ref[h, rows, :1]), 0.0)
            gprobs = dot(gm[rows], v[:keys], NT)
            gscores = probs * (gprobs - jnp.sum(gprobs * probs, -1, keepdims=True))
            gs = gscores.astype(BF16)
            low = probs.astype(BF16)
            gq.append(dot(gs, k[:keys]) * scale)
            gs_t, low_t = gs.T, low.T
            for j in range(b + 1):
                part = slice(j * half, (j + 1) * half)
                a = dot(gs_t[part], q[rows]) * scale
                c = dot(low_t[part], gm[rows])
                gk[j] = a if gk[j] is None else gk[j] + a
                gv[j] = c if gv[j] is None else gv[j] + c
        gq = jnp.concatenate(gq, 0)
        gk = jnp.concatenate(gk, 0)
        gv = jnp.concatenate(gv, 0)
        gp_ref[0, :, cols] = (gq * cos - pltpu.roll(gq, HEAD // 2, 1) * sin).astype(BF16)
        gp_ref[1, :, cols] = (gk * cos - pltpu.roll(gk, HEAD // 2, 1) * sin).astype(BF16)
        gp_ref[2, :, cols] = gv.astype(BF16)

    gout_ref[...] = dot(mixed_t_ref[...], ga).astype(BF16)
    for c in range(3):
        gqkv_ref[c] = dot(normed_t_ref[...], gp_ref[c]).astype(BF16)
    total = dot(gp_ref[0], w_ref[0], NT)
    for c in (1, 2):
        total = total + dot(gp_ref[c], w_ref[c], NT)

    @pl.when(g > 0)
    def _():
        acc_ref[...] += total

    @pl.when(g == 0)
    def _():
        acc_ref[...] = total

    @pl.when(g == steps - 1)
    def _():
        first_ref[...] = acc_ref[...].astype(BF16)


def attend_back(ga, normed_t, qkv, lse, mixed_t, w_out, w3, cos, sin, deps=()):
    length, model = ga.shape
    local = w3.shape[2]
    local_heads = local // HEAD
    heads = 2 if local_heads % 2 == 0 else 1
    steps = local_heads // heads
    wide = heads * HEAD
    full = lambda *shape: pl.BlockSpec(shape, lambda g: (0,) * len(shape))
    return pl.pallas_call(
        partial(attend_back_kernel, heads=heads, steps=steps, deps=len(deps)),
        grid=(steps,),
        in_specs=[
            full(length, model), full(model, length),
            pl.BlockSpec((3, length, wide), lambda g: (0, 0, g)),
            pl.BlockSpec((heads, length, HEAD), lambda g: (g, 0, 0)),
            pl.BlockSpec((wide, length), lambda g: (g, 0)),
            pl.BlockSpec((wide, model), lambda g: (g, 0)),
            pl.BlockSpec((3, model, wide), lambda g: (0, 0, g)),
            full(length, HEAD), full(length, HEAD),
        ] + [pl.BlockSpec(memory_space=pl.ANY)] * len(deps),
        out_specs=[
            pl.BlockSpec((3, model, wide), lambda g: (0, 0, g)),
            pl.BlockSpec((wide, model), lambda g: (g, 0)),
            full(length, model),
        ],
        out_shape=[
            jax.ShapeDtypeStruct((3, model, local), BF16),
            jax.ShapeDtypeStruct((local, model), BF16),
            jax.ShapeDtypeStruct((length, model), BF16),
        ],
        scratch_shapes=[pltpu.VMEM((length, model), F32), pltpu.VMEM((3, length, wide), BF16)],
        compiler_params=params(),
        cost_estimate=cost(2 * length * model * local * 8 + 10 * length * length * local,
                           2 * (4 * length * model + 8 * model * local), length * length * local_heads),
        name="attend_back",
    )(ga, normed_t, qkv, lse, mixed_t, w_out, w3, cos, sin, *deps)


def own_grad_kernel(sent_ref, cot_ref, bucket_ref, gate_ref, unsort_ref, up_ref, down_ref, *rest, row_bounds, deps):
    gsent_ref, act_ref, acc_ref = rest[deps:]
    level = pl.program_id(0)
    for q, rows in enumerate(row_bounds):
        @pl.when(level == q)
        def _(q=q, rows=rows):
            keep = bucket_ref[:rows, :1] >= q
            pre = dot(sent_ref[:rows], up_ref[0])
            active = jnp.where(keep, jnp.maximum(pre, 0.0), 0.0)
            act_ref[0, :rows] = (active * active).astype(BF16)
            gact = dot(cot_ref[:rows], down_ref[0], NT)
            gpre = (gact * (2.0 * gate_ref[:rows, :1]) * active).astype(BF16)
            s = dot(gpre, up_ref[0], NT)
            if q == 0:
                acc_ref[...] = s
            else:
                acc_ref[:rows] += s
            if q == len(row_bounds) - 1:
                gsent_ref[...] = dot(unsort_ref[...], acc_ref[...].astype(BF16)).astype(BF16)


def own_grad(sent, cot, bucket, gate, unsort, w_up, w_down, row_bounds, deps=()):
    length, model = sent.shape
    levels, _, hidden = w_up.shape
    full = lambda *shape: pl.BlockSpec(shape, lambda q: (0,) * len(shape))
    return pl.pallas_call(
        partial(own_grad_kernel, row_bounds=tuple(row_bounds), deps=len(deps)),
        grid=(levels,),
        in_specs=[
            full(length, model), full(length, model), full(length, 128), full(length, 128), full(length, length),
            pl.BlockSpec((1, model, hidden), lambda q: (q, 0, 0)),
            pl.BlockSpec((1, hidden, model), lambda q: (q, 0, 0)),
        ] + [pl.BlockSpec(memory_space=pl.ANY)] * len(deps),
        out_specs=[full(length, model), pl.BlockSpec((1, length, hidden), lambda q: (q, 0, 0))],
        out_shape=[jax.ShapeDtypeStruct((length, model), BF16), jax.ShapeDtypeStruct((levels, length, hidden), BF16)],
        scratch_shapes=[pltpu.VMEM((length, model), F32)],
        compiler_params=params(),
        cost_estimate=cost(6 * sum(row_bounds) * model * hidden, 4 * levels * model * hidden + 6 * length * model),
        name="own_grad",
    )(sent, cot, bucket, gate, unsort, w_up, w_down, *deps)


def own_forward_kernel(act_ref, cot_ref, unsort_ref, down_ref, *rest, row_bounds, deps):
    ffn_ref, ggate_ref, acc_ref = rest[deps:]
    level = pl.program_id(0)
    for q, rows in enumerate(row_bounds):
        @pl.when(level == q)
        def _(q=q, rows=rows):
            f = dot(act_ref[0, :rows], down_ref[0])
            if q == 0:
                acc_ref[...] = f
            else:
                acc_ref[:rows] += f
            if q == len(row_bounds) - 1:
                total = acc_ref[...]
                ggate = jnp.sum(total * cot_ref[...].astype(F32), -1, keepdims=True)
                ggate_ref[...] = jnp.broadcast_to(ggate, ggate_ref.shape)
                ffn_ref[...] = dot(unsort_ref[...], total.astype(BF16)).astype(BF16)


def own_forward(act, cot, unsort, w_down, row_bounds, deps=()):
    length, model = cot.shape
    levels, hidden, _ = w_down.shape
    full = lambda *shape: pl.BlockSpec(shape, lambda q: (0,) * len(shape))
    return pl.pallas_call(
        partial(own_forward_kernel, row_bounds=tuple(row_bounds), deps=len(deps)),
        grid=(levels,),
        in_specs=[
            pl.BlockSpec((1, length, hidden), lambda q: (q, 0, 0)),
            full(length, model), full(length, length),
            pl.BlockSpec((1, hidden, model), lambda q: (q, 0, 0)),
        ] + [pl.BlockSpec(memory_space=pl.ANY)] * len(deps),
        out_specs=[full(length, model), full(length, 128)],
        out_shape=[jax.ShapeDtypeStruct((length, model), BF16), jax.ShapeDtypeStruct((length, 128), F32)],
        scratch_shapes=[pltpu.VMEM((length, model), F32)],
        compiler_params=params(),
        cost_estimate=cost(2 * sum(row_bounds) * model * hidden, 2 * levels * model * hidden + 6 * length * model),
        name="own_forward",
    )(act, cot, unsort, w_down, *deps)


AUX = 16


def block_copies(s_refs, c_refs, s_buf, aux_buf, c_buf, sems, k, slot):
    core = lax.rem(lax.axis_index("mp"), 2)
    part, rows = s_buf.shape[1] // 2, c_buf.shape[1] // 2
    at = lambda c, size: pl.ds(pl.multiple_of(c * size, size), size)
    mine, other = core, 1 - core
    ends = [
        (s_refs[2 * k].at[pl.ds(0, part)], s_buf.at[slot, at(mine, part)]),
        (s_refs[2 * k].at[pl.ds(part, AUX)], aux_buf.at[slot]),
        (s_refs[2 * k + 1].at[pl.ds(0, part)], s_buf.at[slot, at(other, part)]),
        (c_refs[2 * k], c_buf.at[slot, at(mine, rows)]),
        (c_refs[2 * k + 1], c_buf.at[slot, at(other, rows)]),
    ]
    return [pltpu.make_async_copy(src, dst, sems.at[slot, i]) for i, (src, dst) in enumerate(ends)]


def fetch_block(s_refs, c_refs, s_buf, aux_buf, c_buf, sems):
    b = pl.program_id(0)
    count = len(s_refs) // 2
    copies = partial(block_copies, s_refs, c_refs, s_buf, aux_buf, c_buf, sems)
    for k in range(count):
        @pl.when(b == (k if k == 0 else k - 1))
        def _(k=k):
            for c in copies(k, k % 2):
                c.start()
    for k in range(count):
        @pl.when(b == k)
        def _(k=k):
            for c in copies(k, k % 2):
                c.wait()
    return lax.rem(b, 2)


def weight_first_kernel(*refs, level, rows, count, deps):
    s_refs, c_refs = refs[:2 * count], refs[2 * count:4 * count]
    up_t_ref, down_ref = refs[4 * count:4 * count + 2]
    act_ref, gpre_ref, s_buf, aux_buf, c_buf, sems = refs[4 * count + 2 + deps:]
    slot = fetch_block(s_refs, c_refs, s_buf, aux_buf, c_buf, sems)
    aux = aux_buf[slot, :, :rows].astype(F32)
    gate = aux[0:1] + aux[1:2] + aux[2:3]
    keep = aux[3:4] >= level
    pre = dot(up_t_ref[0], s_buf[slot, :, :rows])
    active = jnp.where(keep, jnp.maximum(pre, 0.0), 0.0)
    act_ref[0] = (active * active * gate).astype(BF16)
    gact = dot(down_ref[0], c_buf[slot, :rows], NT)
    gpre_ref[0] = (gact * (2.0 * gate) * active).astype(BF16)


def weight_second_kernel(*refs, rows, count, deps):
    s_refs, c_refs = refs[:2 * count], refs[2 * count:4 * count]
    act_ref, gpre_ref = refs[4 * count:4 * count + 2]
    gup_ref, gdown_ref, s_buf, aux_buf, c_buf, sems = refs[4 * count + 2 + deps:]
    b = pl.program_id(0)
    slot = fetch_block(s_refs, c_refs, s_buf, aux_buf, c_buf, sems)
    u = dot(s_buf[slot, :, :rows], gpre_ref[0], NT)
    d = dot(act_ref[0], c_buf[slot, :rows])

    @pl.when(b == 0)
    def _():
        gup_ref[0] = u
        gdown_ref[0] = d

    @pl.when(b > 0)
    def _():
        gup_ref[0] += u
        gdown_ref[0] += d


def block_scratch(length, model):
    return [
        pltpu.VMEM((2, model, length), BF16), pltpu.VMEM((2, AUX, length), BF16),
        pltpu.VMEM((2, length, model), BF16), pltpu.SemaphoreType.DMA((2, 5)),
    ]


def weight_first(level, rows, sents, cots, up_t, w_down, deps=()):
    count = len(sents) // 2
    levels, hidden, model = up_t.shape
    length = sents[0].shape[1]
    rows = -(-rows // 128) * 128
    anywhere = pl.BlockSpec(memory_space=pl.ANY)
    return pl.pallas_call(
        partial(weight_first_kernel, level=level, rows=rows, count=count, deps=len(deps)),
        grid=(count,),
        in_specs=[anywhere] * (4 * count) + [
            pl.BlockSpec((1, hidden, model), lambda b: (level, 0, 0)),
            pl.BlockSpec((1, hidden, model), lambda b: (level, 0, 0)),
        ] + [anywhere] * len(deps),
        out_specs=[pl.BlockSpec((1, hidden, rows), lambda b: (b, 0, 0))] * 2,
        out_shape=[jax.ShapeDtypeStruct((count, hidden, rows), BF16)] * 2,
        scratch_shapes=block_scratch(length, model),
        compiler_params=params(),
        cost_estimate=cost(4 * count * rows * model * hidden, 4 * count * rows * model),
        name=f"weight_first_{level}",
    )(*sents, *cots, up_t, w_down, *deps)


def weight_second(level, levels, rows, sents, cots, act, gpre, carried, deps=()):
    count = len(sents) // 2
    _, hidden, rows = act.shape
    length, model = sents[0].shape[1], cots[0].shape[1]
    anywhere = pl.BlockSpec(memory_space=pl.ANY)
    first = 4 * count + 2
    return pl.pallas_call(
        partial(weight_second_kernel, rows=rows, count=count, deps=len(carried) + len(deps)),
        grid=(count,),
        in_specs=[anywhere] * (4 * count) + [pl.BlockSpec((1, hidden, rows), lambda b: (b, 0, 0))] * 2
        + [anywhere] * (len(carried) + len(deps)),
        out_specs=[
            pl.BlockSpec((1, model, hidden), lambda b: (level, 0, 0)),
            pl.BlockSpec((1, hidden, model), lambda b: (level, 0, 0)),
        ],
        out_shape=[jax.ShapeDtypeStruct((levels, model, hidden), F32), jax.ShapeDtypeStruct((levels, hidden, model), F32)],
        input_output_aliases={first: 0, first + 1: 1} if carried else {},
        scratch_shapes=block_scratch(length, model),
        compiler_params=params(),
        cost_estimate=cost(4 * count * rows * model * hidden, 4 * count * rows * model + 8 * model * hidden),
        name=f"weight_second_{level}",
    )(*sents, *cots, act, gpre, *carried, *deps)


def ring_order(count):
    nz = 4 if count % 4 == 0 else 1
    ny = count // nz
    if nz == 1 or ny % 2:
        return list(range(count))
    order = [(z, 0) for z in range(nz)]
    for y in range(1, ny):
        line = list(range(1, nz))
        order += [(z, y) for z in (reversed(line) if y % 2 else line)]
    order += [(0, y) for y in range(ny - 1, 0, -1)]
    return [z * ny + y for z, y in order]


class Ring:
    def __init__(self):
        self.log = []
        self.count = lax.axis_size("dp")
        self.order = ring_order(self.count)
        n = self.count
        place = [0] * n
        for p, d in enumerate(self.order):
            place[d] = p
        self.position = jnp.array(place, jnp.int32)[lax.axis_index("dp")]
        self.right = [(self.order[p], self.order[(p + 1) % n]) for p in range(n)]
        self.left = [(self.order[(p + 1) % n], self.order[p]) for p in range(n)]

    def to_right(self, x):
        out = lax.ppermute(x, "dp", self.right)
        self.log.append(out)
        return out

    def to_left(self, x):
        out = lax.ppermute(x, "dp", self.left)
        self.log.append(out)
        return out

    def logged(self, f, *args):
        self.log = []
        out = f(*args)
        pairs = [tuple(self.log[i:i + 2]) for i in range(0, len(self.log), 2)]
        self.log = []
        return out, pairs

    def gather(self, x, axis):
        out = [x]
        r = l = x
        for _ in range(self.count // 2 - 1):
            r, l = self.to_right(r), self.to_left(l)
            out += [r, l]
        cut = x.shape[axis] // 2
        first = self.to_right(lax.slice_in_dim(r, 0, cut, axis=axis))
        second = self.to_left(lax.slice_in_dim(l, cut, 2 * cut, axis=axis))
        out.append(jnp.concatenate([first, second], axis))
        return out

    def offsets(self):
        out = [0]
        for k in range(1, self.count // 2):
            out += [-k, k]
        return out + [self.count // 2]

    def indices(self):
        return [(self.position + k) % self.count for k in self.offsets()]

    def reduce_scatter(self, x, axis):
        n = self.count
        size = x.shape[axis] // n
        cut = size // 2

        def piece(k, start=0, length=size):
            at = ((self.position + k) % n) * size + start
            return lax.dynamic_slice_in_dim(x, at, length, axis=axis)

        def join(a, b):
            return low(a.astype(F32) + b.astype(F32))

        far = n // 2
        r = self.to_right(piece(far, 0, cut))
        l = self.to_left(piece(-far, cut, cut))
        k = far - 1
        r = jnp.concatenate([join(r, piece(k, 0, cut)), piece(k, cut, cut)], axis)
        l = jnp.concatenate([piece(-k, 0, cut), join(l, piece(-k, cut, cut))], axis)
        r, l = self.to_right(r), self.to_left(l)
        for k in range(far - 2, 0, -1):
            r, l = self.to_right(join(r, piece(k))), self.to_left(join(l, piece(-k)))
        return low(r.astype(F32) + l.astype(F32) + piece(0).astype(F32))


def core_swap(x):
    n = lax.axis_size("mp")
    return lax.ppermute(x, "mp", [(i, i ^ 1) for i in range(n)])


def sum_over_x(x):
    n = lax.axis_size("mp") // 2
    index = lax.axis_index("mp")
    parts = [x] + [
        lax.ppermute(x, "mp", [(i, (i + 2 * k) % (2 * n)) for i in range(2 * n)]) for k in range(1, n)
    ]
    if n == 1:
        return x.astype(F32)
    if n == 2:
        return parts[0].astype(F32) + parts[1].astype(F32)
    stacked = jnp.stack(parts)
    total = None
    for j in range(n):
        term = lax.dynamic_index_in_dim(stacked, (index // 2 - j) % n, 0, keepdims=False).astype(F32)
        total = term if total is None else total + term
    return total


def sum_over_all(x):
    x = x + core_swap(x)
    n = lax.axis_size("dp")
    step = 1
    while step < n:
        x = x + lax.ppermute(x, "dp", [(i, i ^ step) for i in range(n)])
        step *= 2
    return x


def on_device(tokens, gain_first, w_qkv, w_out, gain_second, router, w_up, w_down, slot, cotangent):
    length, model = tokens.shape
    buckets = w_up.shape[0]
    devices_dp = lax.axis_size("dp")
    groups = devices_dp // buckets
    capacity = length * 5 // (4 * devices_dp)
    row_bounds = [min(length, (buckets - level) * groups * capacity) for level in range(buckets)]
    ring = Ring()
    core = lax.axis_index("mp") % 2
    half = length // 2

    bucket_ids = slot // capacity // groups
    places = jnp.arange(length, dtype=jnp.int32)
    key = (buckets - 1 - bucket_ids) * length + places
    rank = jnp.sum((key[None, :] < key[:, None]).astype(jnp.int32), 1)
    rank_here = jnp.roll(rank, -core * half)
    sort_rows = places[:, None] == rank[None, :]
    sort_here = places[:, None] == rank_here[None, :]
    sort_low = sort_here.astype(BF16)
    unsort_low = (rank_here[:, None] == places[None, :]).astype(BF16)
    bucket_sorted = jnp.sum(jnp.where(sort_rows, bucket_ids[None, :], 0), 1)

    def part_of(x, c, axis=0):
        size = x.shape[axis] // 2
        return lax.dynamic_slice_in_dim(x, c * size, size, axis=axis)

    def own_rows(x):
        return part_of(x, core)

    def other_rows(x):
        return part_of(x, 1 - core)

    def sum_halves(mine, others):
        return sum_over_x(low(mine.astype(F32) + core_swap(others).astype(F32)))

    def joined(mine, other):
        return jnp.concatenate([jnp.where(core == 0, mine, other), jnp.where(core == 0, other, mine)], 0)

    cot_sorted = dot(sort_rows.astype(BF16), cotangent).astype(BF16)
    cot_halves, cot_steps = ring.logged(ring.gather, own_rows(cot_sorted), 0)

    w3 = jnp.transpose(w_qkv, (1, 0, 2))
    cos, sin = rotary_table(length, HEAD)
    part, normed_low, qkv, lse, mixed = attend(tokens, gain_first[None, :], w3, cos, sin, w_out)
    attn = sum_halves(own_rows(part), other_rows(part))
    normed_t, mixed_t, up_t = normed_low.T, mixed.T, jnp.transpose(w_up, (0, 2, 1))

    resid = own_rows(tokens).astype(F32) + attn
    inv = lax.rsqrt(jnp.mean(resid * resid, -1, keepdims=True) + EPSILON)
    xhat = resid * inv
    normed_second = xhat * gain_second
    logits = jnp.dot(normed_second, router, precision=HIGHEST)
    prob = jax.nn.softmax(logits, axis=-1)
    onehot = (own_rows(bucket_ids)[:, None] == jnp.arange(buckets)[None, :]).astype(F32)
    gate = buckets * jnp.sum(prob * onehot, -1)
    sent_half = normed_second.astype(BF16)
    sent_both = jnp.concatenate([sent_half, core_swap(sent_half)], 0)
    gate_both = jnp.concatenate([gate, core_swap(gate)], 0)
    gate_sorted = jnp.sum(jnp.where(sort_here, gate_both[None, :], 0.0), 1)

    sent_sorted = dot(sort_low, sent_both).astype(BF16)
    sent_sorted_t = lax.dot_general(sent_both, sort_low, (((0,), (1,)), ((), ())), preferred_element_type=F32).astype(BF16)

    gate_1 = low(gate_sorted)
    gate_2 = low(gate_sorted - gate_1.astype(F32))
    gate_3 = low(gate_sorted - gate_1.astype(F32) - gate_2.astype(F32))
    aux = jnp.stack([gate_1, gate_2, gate_3, bucket_sorted.astype(BF16)] + [jnp.zeros_like(gate_1)] * (AUX - 4))
    sent_own = jnp.concatenate([part_of(sent_sorted_t, core), aux], 0)
    sent_halves, sent_steps = ring.logged(ring.gather, sent_own, 1)

    wide = lambda x: jnp.broadcast_to(x[:, None], (length, 128))
    gsent_part, act = own_grad(
        sent_sorted, cot_sorted, wide(bucket_sorted), wide(gate_sorted), unsort_low, w_up, w_down, row_bounds, cot_steps[0])
    grad_sent = sum_halves(gsent_part[:half], gsent_part[half:]).astype(BF16).astype(F32)
    ffn_part, ggate_part = own_forward(act, cot_sorted, unsort_low, w_down, row_bounds, cot_steps[1])
    ffn_rows = sum_halves(ffn_part[:half], ffn_part[half:]).astype(BF16).astype(F32)
    ggate_part = jnp.sum(jnp.where(sort_rows, ggate_part[:, :1], 0.0), 0)
    grad_gate = ggate_part + core_swap(ggate_part)
    grad_gate = sum_over_x(own_rows(grad_gate))

    grad_output = own_rows(cotangent).astype(F32)
    output_half = (resid + gate[:, None] * ffn_rows).astype(BF16)
    grad_prob = buckets * grad_gate[:, None] * onehot
    grad_logits = prob * (grad_prob - jnp.sum(grad_prob * prob, -1, keepdims=True))
    grad_router = jnp.dot(normed_second.T, grad_logits, precision=HIGHEST)
    grad_second = grad_sent + jnp.dot(grad_logits, router.T, precision=HIGHEST)
    grad_gain_second = jnp.sum(grad_second * xhat, 0)
    scaled = grad_second * gain_second
    grad_resid = grad_output + inv * (scaled - xhat * jnp.mean(scaled * xhat, -1, keepdims=True))
    ga_half = low(grad_resid)
    grad_attn = joined(ga_half, core_swap(ga_half))

    gqkv, gout, first_part = attend_back(grad_attn, normed_t, qkv, lse, mixed_t, w_out, w3, cos, sin, cot_steps[2])

    gqkv_chunk, qkv_steps = ring.logged(ring.reduce_scatter, gqkv, 1)
    gout_chunk, out_steps = ring.logged(ring.reduce_scatter, gout, 0)
    gqkv_chunks, qkv_more = ring.logged(ring.gather, gqkv_chunk, 1)
    gout_chunks, out_more = ring.logged(ring.gather, gout_chunk, 0)
    sum_steps = [a + b for a, b in zip(qkv_steps + qkv_more, out_steps + out_more)]
    grad_wout = jnp.zeros(gout.shape, F32)
    grad_wqkv = jnp.zeros(gqkv.shape, F32)
    for at, a, b in zip(ring.indices(), gout_chunks, gqkv_chunks):
        grad_wout = lax.dynamic_update_slice_in_dim(grad_wout, a.astype(F32), at * a.shape[0], 0)
        grad_wqkv = lax.dynamic_update_slice_in_dim(grad_wqkv, b.astype(F32), at * b.shape[1], 1)

    grad_first = sum_halves(own_rows(first_part), other_rows(first_part))
    source = own_rows(tokens).astype(F32)
    inv_first = lax.rsqrt(jnp.mean(source * source, -1, keepdims=True) + EPSILON)
    xhat_first = source * inv_first
    grad_gain_first = jnp.sum(grad_first * xhat_first, 0)
    scaled_first = grad_first * gain_first
    grad_source = inv_first * (scaled_first - xhat_first * jnp.mean(scaled_first * xhat_first, -1, keepdims=True))
    tokens_half = (grad_source + grad_resid).astype(BF16)
    output = joined(output_half, core_swap(output_half))
    grad_tokens = joined(tokens_half, core_swap(tokens_half))
    small = jnp.concatenate([grad_router.T, grad_gain_second[None], grad_gain_first[None]], 0)
    small = sum_over_all(small)

    sents = [sent_own, part_of(sent_sorted_t, 1 - core)]
    cots = [cot_halves[0], other_rows(cot_sorted)]
    for k in range(1, devices_dp):
        sents += [sent_halves[k], core_swap(sent_halves[k])]
        cots += [cot_halves[k], core_swap(cot_halves[k])]
    carried = ()
    for level, rows in enumerate(row_bounds):
        deps = [sum_steps[i] if 0 <= i < len(sum_steps) else () for i in (2 * level - 1, 2 * level)]
        act_all, gpre_all = weight_first(level, rows, sents, cots, up_t, w_down, deps[0])
        carried = weight_second(level, buckets, rows, sents, cots, act_all, gpre_all, carried, deps[1])
    grad_up, grad_down = carried

    return (
        output,
        grad_tokens,
        small[buckets + 1],
        jnp.transpose(grad_wqkv, (1, 0, 2)),
        grad_wout,
        small[buckets],
        small[:buckets].T,
        grad_up,
        grad_down,
    )


def solution(mesh):
    placed = (
        P("dp", None),
        P(),
        P(None, None, "mp"),
        P("mp", None),
        P(),
        P(),
        P(None, None, "mp"),
        P(None, "mp", None),
        P("dp"),
        P("dp", None),
    )
    return jax.shard_map(
        on_device,
        mesh=mesh,
        in_specs=placed,
        out_specs=(
            P("dp", None),
            P("dp", None),
            P(),
            P(None, None, "mp"),
            P("mp", None),
            P(),
            P(),
            P(None, None, "mp"),
            P(None, "mp", None),
        ),
        check_vma=False,
    )
```

time: 1280 us -> 622 us (0.49)
  waiting for transfers between devices: 818 us -> 123 us
  Pallas kernels: 0 us -> 287 us
  blocking collectives: 193 us -> 0 us
  matrix products: 121 us -> 12.6 us
  starting transfers between devices: 0.12 us -> 66 us
  other arithmetic: 86.1 us -> 61.2 us
    psum x3 -> x0, waiting for transfers between devices: 818 us -> none  [the longest x1 707 us: on_device(): lax.psum(grad_wqkv.astype(jnp.bfloat16), 'dp').astype(jnp.float32)]
    pallas_call x0 -> x12, Pallas kernels: none -> 287 us  [the longest x4 125 us: weight_second(): pl.pallas_call(partial(weight_second_kernel, rows=rows, count=count, deps...]
    psum x3 -> x0, blocking collectives: 193 us -> none  [the longest x1 77.5 us: on_device(): summed_grad = lax.psum(partial_grad, 'mp').astype(jnp.bfloat16)]
    ppermute x0 -> x81, waiting for transfers between devices: none -> 123 us  [the longest x24 46.2 us: to_right(): out = lax.ppermute(x, 'dp', self.right)]
    dot_general x36 -> x3, matrix products: 105 us -> 5.17 us  [the longest x2 3.86 us: dot(): return lax.dot_general(a, b, dims, preferred_element_type=F32)]
    ppermute x0 -> x81, starting transfers between devices: none -> 66 us  [the longest x24 34.7 us: to_right(): out = lax.ppermute(x, 'dp', self.right)]
    gather x5 -> x0, local copies, waits for them, and re-layouts: 32.4 us -> none  [the longest x1 7.5 us: on_device(): sent[order]]
    convert_element_type x16, other arithmetic: 51.4 us -> 22.5 us  [the longest x12 17 us: low(): return lax.reduce_precision(x, 8, 7).astype(BF16)]
  transfers between devices with their start and end apart: 3 -> 81, of which waited for: 3 -> 20; matrix products, arithmetic and copies ran while one was open for 3% -> 19% of each run, Pallas kernels for 0% -> 44%
where the time goes in v1:
time: 622 us; the launch traced here: 613 us
  Pallas kernels  287 us (46%)
  waiting for transfers between devices  123 us (20%)
  starting transfers between devices  66 us (11%)
  other arithmetic  61.2 us (10%)
  local copies, waits for them, and re-layouts  53.5 us (9%)
  matrix products  12.6 us (2%)
  between operations  9.64 us (2%)
    pallas_call x4, Pallas kernels, weight_second(): pl.pallas_call(partial(weight_second_kernel, rows=rows, count=count, deps...  125 us
    pallas_call x4, Pallas kernels, weight_first(): pl.pallas_call(partial(weight_first_kernel, level=level, rows=rows, count...  96 us
    ppermute x24, waiting for transfers between devices, to_right(): out = lax.ppermute(x, 'dp', self.right)  46.2 us
    ppermute x24, waiting for transfers between devices, to_left(): out = lax.ppermute(x, 'dp', self.left)  39 us
    ppermute x24, starting transfers between devices, to_right(): out = lax.ppermute(x, 'dp', self.right)  34.7 us
    ppermute x5, waiting for transfers between devices, sum_over_x(): lax.ppermute(x, 'mp', [(i, (i + 2 * k) % (2 * n)) for i in range(2 * n)])  31.8 us
    pallas_call x1, Pallas kernels, attend_back(): pl.pallas_call(partial(attend_back_kernel, heads=heads, steps=steps, deps...  23 us
    ppermute x24, starting transfers between devices, to_left(): out = lax.ppermute(x, 'dp', self.left)  17.4 us
  transfers between devices with their start and end apart: 81, of which 20 were waited for; matrix products, arithmetic and copies ran while one was open for 19% of the time, Pallas kernels for 44%

profile of v1, /device:TPU:0, one launch (start us, length us, event | category | flops | bytes accessed | tf_op | source)
XLA Modules:
  0.0 612.9 jit_solution(4095847427776192980)
XLA Ops:
  2.6 15.7 %attend.1 = (bf16[512,2048]{1,0:T(8,128)(2,1)}, bf16[512,2048]{1,0:T(8,128)(2,1)}, bf16[3,512,512]{2,1,0:T(8,128)(2,1)}, f32[4,512,128]{2,1,0:T(8,128)}, bf16[512,512]{1,0:T(8,128)(2,1)}) custom-call(bf16[512,2048]{1,0:T(8,128)(2,1)} %x_ref.1, f32[1,2048]{1,0:T(1,128)} %bitcast.27, bf16[3,2048,512]{2,1,0:T(8,128)(2,1)} %bitcast.31, ...), custom_call_target="tpu_custom_call" | custom-call | flops 4831838208 | bytes 12582912 | tf_op jit(solution)/shard_map/attend/pallas_call | solution.py:97
  34.6 17.4 %collective-permute-done.1 = bf16[256,2048]{1,0:T(8,128)(2,1)} collective-permute-done((bf16[256,2048]{1,0:T(8,128)(2,1)}, bf16[256,2048]{1,0:T(8,128)(2,1)}, u32[]{:S(2)}, u32[]{:S(2)}) %collective-permute-start.1) | collective-permute-done | bytes 1048608 | tf_op jit(solution)/shard_map/ppermute | solution.py:526
  64.3 17.3 %own_grad.1 = (bf16[512,2048]{1,0:T(8,128)(2,1)}, bf16[4,512,512]{2,1,0:T(8,128)(2,1)}) custom-call(bf16[512,2048]{1,0:T(8,128)(2,1)} %convolution_convert_fusion.2.sent_ref, bf16[512,2048]{1,0:T(8,128)(2,1)} %copy-done.27, s32[512,128]{1,0:T(8,128)} %broadcast_in_dim.63.bucket_ref, f32[512,128]{1,0:T(8,128)} %broadcast_in_dim.66.gate_ref, ...), custom_call_target="tpu_custom_call" | custom-call | flops 9261023232 | bytes 23068672 | tf_op jit(solution)/shard_map/own_grad/pallas_call | solution.py:250
  86.2 10.3 %own_forward.1 = (bf16[512,2048]{1,0:T(8,128)(2,1)}, f32[512,128]{1,0:T(8,128)}) custom-call(bf16[4,512,512]{2,1,0:T(8,128)(2,1)} %get-tuple-element.38.act_ref, bf16[512,2048]{1,0:T(8,128)(2,1)} %copy-done.27, bf16[512,512]{1,0:T(8,128)(2,1)} %fusion.21.unsort_ref, bf16[4,512,2048]{2,1,0:T(8,128)(2,1)} %refs_33_.7, ...), custom_call_target="tpu_custom_call" | custom-call | flops 3087007744 | bytes 14680064 | tf_op jit(solution)/shard_map/own_forward/pallas_call | solution.py:289
  109.0 14.3 %collective-permute-done.14 = f32[256]{0:T(256)S(1)} collective-permute-done((f32[256]{0:T(256)S(1)}, f32[256]{0:T(256)S(1)}, u32[]{:S(2)}, u32[]{:S(2)}) %collective-permute-start.14) | collective-permute-done | bytes 1056 | tf_op jit(solution)/shard_map/ppermute | solution.py:526
  125.1 4.3 multiply_reduce_fusion
  133.3 11.4 %copy.34 = bf16[4,2048,512]{1,2,0:T(8,128)(2,1)} copy(bf16[4,2048,512]{2,1,0:T(8,128)(2,1)} %up_ref.1) | data formatting | bytes 16777216 | tf_op args[6]
  167.1 7.1 %collective-permute-done.79 = bf16[128,2048]{1,0:T(8,128)(2,1)S(1)} collective-permute-done((bf16[128,2048]{1,0:T(8,128)(2,1)S(1)}, bf16[128,2048]{1,0:T(8,128)(2,1)S(1)}, u32[]{:S(2)}, u32[]{:S(2)}) %collective-permute-start.79) | collective-permute-done | bytes 524320 | tf_op jit(solution)/shard_map/ppermute | solution.py:461
  179.6 23.0 %attend_back.1 = (bf16[3,2048,512]{2,1,0:T(8,128)(2,1)}, bf16[512,2048]{1,0:T(8,128)(2,1)}, bf16[512,2048]{1,0:T(8,128)(2,1)}) custom-call(bf16[512,2048]{1,0:T(8,128)(2,1)} %pad_maximum_fusion.2.ga_ref, bf16[2048,512]{1,0:T(8,128)(2,1)} %bitcast.21, bf16[3,512,512]{2,1,0:T(8,128)(2,1)} %get-tuple-element.43.qkv_ref, ...), custom_call_target="tpu_custom_call" | custom-call | flops 9932111872 | bytes 25165824 | tf_op jit(solution)/shard_map/attend_back/pallas_call | solution.py:195
  216.2 19.2 %collective-permute-done.65.refs_10_ = bf16[1040,512]{1,0:T(8,128)(2,1)S(1)} collective-permute-done((bf16[1040,512]{1,0:T(8,128)(2,1)S(1)}, bf16[1040,512]{1,0:T(8,128)(2,1)S(1)}, u32[]{:S(2)}, u32[]{:S(2)}) %collective-permute-start.65) | collective-permute-done | bytes 1064992 | tf_op jit(solution)/shard_map/ppermute | solution.py:456
  243.0 7.0 %collective-permute-done.25.refs_34_ = bf16[3,128,512]{2,1,0:T(8,128)(2,1)S(1)} collective-permute-done((bf16[3,128,512]{2,1,0:T(8,128)(2,1)S(1)}, bf16[3,128,512]{2,1,0:T(8,128)(2,1)S(1)}, u32[]{:S(2)}, u32[]{:S(2)}) %collective-permute-start.25) | collective-permute-done | bytes 393248 | tf_op jit(solution)/shard_map/ppermute | solution.py:456
  262.3 8.6 %collective-permute-done.69 = bf16[1040,256]{1,0:T(8,128)(2,1)S(1)} collective-permute-done((bf16[1040,256]{1,0:T(8,128)(2,1)S(1)}, bf16[1040,256]{1,0:T(8,128)(2,1)S(1)}, u32[]{:S(2)}, u32[]{:S(2)}) %collective-permute-start.69) | collective-permute-done | bytes 532512 | tf_op jit(solution)/shard_map/ppermute | solution.py:456
  290.3 16.8 %collective-permute-done.50.refs_39_ = bf16[64,2048]{1,0:T(8,128)(2,1)S(1)} collective-permute-done((bf16[64,2048]{1,0:T(8,128)(2,1)S(1)}, bf16[64,2048]{1,0:T(8,128)(2,1)S(1)}, u32[]{:S(2)}, u32[]{:S(2)}) %collective-permute-start.50) | collective-permute-done | bytes 262176 | tf_op jit(solution)/shard_map/ppermute | solution.py:461
  310.2 4.5 collective-permute-done.52.refs_37_
  326.0 25.6 %weight_first_0.1 = (bf16[8,512,512]{2,1,0:T(8,128)(2,1)}, bf16[8,512,512]{2,1,0:T(8,128)(2,1)}) custom-call(bf16[1040,512]{1,0:T(8,128)(2,1)} %copy-done.2, bf16[1024,512]{1,0:T(8,128)(2,1)} %get-tuple-element.91.refs_1_, bf16[1040,512]{1,0:T(8,128)(2,1)} %collective-permute-done.57.refs_2_, bf16[1040,512]{1,0:T(8,128)(2,1)} %copy-done.12, ...), custom_call_target="tpu_custom_call" | custom-call | flops 17179869184 | bytes 33554432 | tf_op jit(solution)/shard_map/weight_first_0/pallas_call | solution.py:389
  351.6 25.7 %weight_first_1.1 = (bf16[8,512,512]{2,1,0:T(8,128)(2,1)}, bf16[8,512,512]{2,1,0:T(8,128)(2,1)}) custom-call(bf16[1040,512]{1,0:T(8,128)(2,1)} %copy-done.2, bf16[1024,512]{1,0:T(8,128)(2,1)} %get-tuple-element.91.refs_1_, bf16[1040,512]{1,0:T(8,128)(2,1)} %collective-permute-done.57.refs_2_, bf16[1040,512]{1,0:T(8,128)(2,1)} %copy-done.12, ...), custom_call_target="tpu_custom_call" | custom-call | flops 17179869184 | bytes 33554432 | tf_op jit(solution)/shard_map/weight_first_1/pallas_call | solution.py:389
  377.3 33.5 %weight_second_0.1 = (f32[4,2048,512]{2,1,0:T(8,128)}, f32[4,512,2048]{2,1,0:T(8,128)}) custom-call(bf16[1040,512]{1,0:T(8,128)(2,1)} %copy-done.2, bf16[1024,512]{1,0:T(8,128)(2,1)} %get-tuple-element.91.refs_1_, bf16[1040,512]{1,0:T(8,128)(2,1)} %collective-permute-done.57.refs_2_, bf16[1040,512]{1,0:T(8,128)(2,1)} %copy-done.12, ...), custom_call_target="tpu_custom_call" | custom-call | flops 17179869184 | bytes 41943040 | tf_op jit(solution)/shard_map/weight_second_0/pallas_call | solution.py:411
  429.8 33.6 %weight_second_1.1 = (f32[4,2048,512]{2,1,0:T(8,128)}, f32[4,512,2048]{2,1,0:T(8,128)}) custom-call(bf16[1040,512]{1,0:T(8,128)(2,1)} %copy-done.2, bf16[1024,512]{1,0:T(8,128)(2,1)} %get-tuple-element.91.refs_1_, bf16[1040,512]{1,0:T(8,128)(2,1)} %collective-permute-done.57.refs_2_, ...), custom_call_target="tpu_custom_call", output_to_operand_aliasing={{0}: (34, {}), {1}: (35, {})} | custom-call | flops 17179869184 | bytes 41943040 | tf_op jit(solution)/shard_map/weight_second_1/pallas_call | solution.py:411
  469.1 4.3 fusion.7
  475.2 6.4 %broadcast_in_dim.111 = f32[3,2048,512]{2,1,0:T(8,128)} broadcast(f32[]{:T(128)} %constant.194.clone.1), dimensions={} | broadcast | bytes 12582916 | tf_op jit(solution)/shard_map/broadcast_in_dim | solution.py:650
  486.6 25.3 %weight_first_2.1 = (bf16[8,512,384]{2,1,0:T(8,128)(2,1)}, bf16[8,512,384]{2,1,0:T(8,128)(2,1)}) custom-call(bf16[1040,512]{1,0:T(8,128)(2,1)} %copy-done.2, bf16[1024,512]{1,0:T(8,128)(2,1)} %get-tuple-element.91.refs_1_, bf16[1040,512]{1,0:T(8,128)(2,1)} %collective-permute-done.57.refs_2_, bf16[1040,512]{1,0:T(8,128)(2,1)} %copy-done.12, ...), custom_call_target="tpu_custom_call" | custom-call | flops 12884901888 | bytes 25165824 | tf_op jit(solution)/shard_map/weight_first_2/pallas_call | solution.py:389
  522.8 33.3 %weight_second_2.1 = (f32[4,2048,512]{2,1,0:T(8,128)}, f32[4,512,2048]{2,1,0:T(8,128)}) custom-call(bf16[1040,512]{1,0:T(8,128)(2,1)} %copy-done.2, bf16[1024,512]{1,0:T(8,128)(2,1)} %get-tuple-element.91.refs_1_, bf16[1040,512]{1,0:T(8,128)(2,1)} %collective-permute-done.57.refs_2_, ...), custom_call_target="tpu_custom_call", output_to_operand_aliasing={{0}: (34, {}), {1}: (35, {})} | custom-call | flops 12884901888 | bytes 33554432 | tf_op jit(solution)/shard_map/weight_second_2/pallas_call | solution.py:411
  560.9 19.5 %weight_first_3.1 = (bf16[8,512,256]{2,1,0:T(8,128)(2,1)}, bf16[8,512,256]{2,1,0:T(8,128)(2,1)}) custom-call(bf16[1040,512]{1,0:T(8,128)(2,1)} %copy-done.2, bf16[1024,512]{1,0:T(8,128)(2,1)} %get-tuple-element.91.refs_1_, bf16[1040,512]{1,0:T(8,128)(2,1)} %collective-permute-done.57.refs_2_, bf16[1040,512]{1,0:T(8,128)(2,1)} %copy-done.12, ...), custom_call_target="tpu_custom_call" | custom-call | flops 8589934592 | bytes 16777216 | tf_op jit(solution)/shard_map/weight_first_3/pallas_call | solution.py:389
  582.6 24.5 %weight_second_3.1 = (f32[4,2048,512]{2,1,0:T(8,128)}, f32[4,512,2048]{2,1,0:T(8,128)}) custom-call(bf16[1040,512]{1,0:T(8,128)(2,1)} %copy-done.2, bf16[1024,512]{1,0:T(8,128)(2,1)} %get-tuple-element.91.refs_1_, bf16[1040,512]{1,0:T(8,128)(2,1)} %collective-permute-done.57.refs_2_, ...), custom_call_target="tpu_custom_call", output_to_operand_aliasing={{0}: (34, {}), {1}: (35, {})} | custom-call | flops 8589934592 | bytes 25165824 | tf_op jit(solution)/shard_map/weight_second_3/pallas_call | solution.py:411
  (414 shorter events, 194.7 us)
Async XLA Ops:
  84.0 47.1 %collective-permute-start.16 = (bf16[256,2048]{1,0:T(8,128)(2,1)}, bf16[256,2048]{1,0:T(8,128)(2,1)}, u32[]{:S(2)}, u32[]{:S(2)}) collective-permute-start(bf16[256,2048]{1,0:T(8,128)(2,1)} %collective-permute-done.6.rest_0_.refs_22_), channel_id=1, source_target_pairs={{0,8},{8,16},{16,24},{24,28},{28,20},{20,12},{12,4},{4,0},{1,9},{9... | collective-permute-start | bytes 3145736 | tf_op jit(solution)/shard_map/ppermute | solution.py:456
  85.8 72.8 %collective-permute-start.17 = (bf16[256,2048]{1,0:T(8,128)(2,1)}, bf16[256,2048]{1,0:T(8,128)(2,1)}, u32[]{:S(2)}, u32[]{:S(2)}) collective-permute-start(bf16[256,2048]{1,0:T(8,128)(2,1)} %collective-permute-done.7.rest_1_.refs_24_), channel_id=1, source_target_pairs={{8,0},{16,8},{24,16},{28,24},{20,28},{12,20},{4,12},{0,4},{9,1},{1... | collective-permute-start | bytes 3145736 | tf_op jit(solution)/shard_map/ppermute | solution.py:461
  107.1 67.2 %collective-permute-start.57 = (bf16[1040,512]{1,0:T(8,128)(2,1)S(1)}, bf16[1040,512]{1,0:T(8,128)(2,1)}, u32[]{:S(2)}, u32[]{:S(2)}) collective-permute-start(bf16[1040,512]{1,0:T(8,128)(2,1)S(1)} %concatenate.74.refs_0_), channel_id=1, source_target_pairs={{0,8},{8,16},{16,24},{24,28},{28,20},{20,12},{12,4},{4,0},{1,9},{9... | collective-permute-start | bytes 3194888 | tf_op jit(solution)/shard_map/ppermute | solution.py:456
  123.3 52.7 %collective-permute-start.59 = (bf16[1040,512]{1,0:T(8,128)(2,1)S(1)}, bf16[1040,512]{1,0:T(8,128)(2,1)}, u32[]{:S(2)}, u32[]{:S(2)}) collective-permute-start(bf16[1040,512]{1,0:T(8,128)(2,1)S(1)} %concatenate.74.refs_0_), channel_id=1, source_target_pairs={{8,0},{16,8},{24,16},{28,24},{20,28},{12,20},{4,12},{0,4},{9,1},{1... | collective-permute-start | bytes 3194888 | tf_op jit(solution)/shard_map/ppermute | solution.py:461
  131.0 45.3 %collective-permute-start.15 = (bf16[256,2048]{1,0:T(8,128)(2,1)}, bf16[256,2048]{1,0:T(8,128)(2,1)}, u32[]{:S(2)}, u32[]{:S(2)}) collective-permute-start(bf16[256,2048]{1,0:T(8,128)(2,1)} %reduce-precision_convert_fusion.1), channel_id=1, source_target_pairs={{0,1},{1,0},{2,3},{3,2},{4,5},{5,4},{6,7},{7,6},{8,9},{9,8},{10,11... | collective-permute-start | bytes 3145736 | tf_op jit(solution)/shard_map/ppermute | solution.py:519
  132.9 33.1 %collective-permute-start.78 = (bf16[128,2048]{1,0:T(8,128)(2,1)}, bf16[128,2048]{1,0:T(8,128)(2,1)}, u32[]{:S(2)}, u32[]{:S(2)}) collective-permute-start(bf16[128,2048]{1,0:T(8,128)(2,1)} %slice.73), channel_id=1, source_target_pairs={{0,8},{8,16},{16,24},{24,28},{28,20},{20,12},{12,4},{4,0},{1,9},{9... | collective-permute-start | bytes 1572872 | tf_op jit(solution)/shard_map/ppermute | solution.py:456
  166.0 71.3 %collective-permute-start.72 = (bf16[256,2048]{1,0:T(8,128)(2,1)}, bf16[256,2048]{1,0:T(8,128)(2,1)}, u32[]{:S(2)}, u32[]{:S(2)}) collective-permute-start(bf16[256,2048]{1,0:T(8,128)(2,1)} %collective-permute-done.4.rest_0_.refs_18_), channel_id=1, source_target_pairs={{0,1},{1,0},{2,3},{3,2},{4,5},{5,4},{6,7},{7,6},{8,9},{9,8},{10,11... | collective-permute-start | bytes 3145736 | tf_op jit(solution)/shard_map/ppermute | solution.py:519
  174.3 34.7 %collective-permute-start.61 = (bf16[1040,512]{1,0:T(8,128)(2,1)}, bf16[1040,512]{1,0:T(8,128)(2,1)S(1)}, u32[]{:S(2)}, u32[]{:S(2)}) collective-permute-start(bf16[1040,512]{1,0:T(8,128)(2,1)} %collective-permute-done.57.refs_2_), channel_id=1, source_target_pairs={{0,8},{8,16},{16,24},{24,28},{28,20},{20,12},{12,4},{4,0},{1,9},{9... | collective-permute-start | bytes 3194888 | tf_op jit(solution)/shard_map/ppermute | solution.py:456
  176.0 34.7 %collective-permute-start.63 = (bf16[1040,512]{1,0:T(8,128)(2,1)}, bf16[1040,512]{1,0:T(8,128)(2,1)S(1)}, u32[]{:S(2)}, u32[]{:S(2)}) collective-permute-start(bf16[1040,512]{1,0:T(8,128)(2,1)} %collective-permute-done.59.refs_4_), channel_id=1, source_target_pairs={{8,0},{16,8},{24,16},{28,24},{20,28},{12,20},{4,12},{0,4},{9,1},{1... | collective-permute-start | bytes 3194888 | tf_op jit(solution)/shard_map/ppermute | solution.py:461
  319.8 100.7 %collective-permute-start.19 = (bf16[256,2048]{1,0:T(8,128)(2,1)}, bf16[256,2048]{1,0:T(8,128)(2,1)}, u32[]{:S(2)}, u32[]{:S(2)}) collective-permute-start(bf16[256,2048]{1,0:T(8,128)(2,1)} %reduce-precision_convert_fusion), channel_id=1, source_target_pairs={{0,2},{1,3},{2,0},{3,1},{4,6},{5,7},{6,4},{7,5},{8,10},{9,11},{10,... | collective-permute-start | bytes 3145736 | tf_op jit(solution)/shard_map/ppermute | solution.py:526
  321.3 102.2 %collective-permute-start.27 = (bf16[3,256,512]{2,1,0:T(8,128)(2,1)}, bf16[3,256,512]{2,1,0:T(8,128)(2,1)S(1)}, u32[]{:S(2)}, u32[]{:S(2)}) collective-permute-start(bf16[3,256,512]{2,1,0:T(8,128)(2,1)} %get-tuple-element.81), channel_id=1, source_target_pairs={{0,8},{8,16},{16,24},{24,28},{28,20},{20,12},{12,4},{4,0},{1,9},{9... | collective-permute-start | bytes 2359304 | tf_op jit(solution)/shard_map/ppermute | solution.py:456
  322.9 100.6 %collective-permute-start.31 = (bf16[3,256,512]{2,1,0:T(8,128)(2,1)}, bf16[3,256,512]{2,1,0:T(8,128)(2,1)S(1)}, u32[]{:S(2)}, u32[]{:S(2)}) collective-permute-start(bf16[3,256,512]{2,1,0:T(8,128)(2,1)} %get-tuple-element.82), channel_id=1, source_target_pairs={{8,0},{16,8},{24,16},{28,24},{20,28},{12,20},{4,12},{0,4},{9,1},{1... | collective-permute-start | bytes 2359304 | tf_op jit(solution)/shard_map/ppermute | solution.py:461
  323.4 87.4 %collective-permute-start.53 = (bf16[64,2048]{1,0:T(8,128)(2,1)}, bf16[64,2048]{1,0:T(8,128)(2,1)}, u32[]{:S(2)}, u32[]{:S(2)}) collective-permute-start(bf16[64,2048]{1,0:T(8,128)(2,1)} %collective-permute-done.51.refs_36_), channel_id=1, source_target_pairs={{0,8},{8,16},{16,24},{24,28},{28,20},{20,12},{12,4},{4,0},{1,9},{9... | collective-permute-start | bytes 786440 | tf_op jit(solution)/shard_map/ppermute | solution.py:456
  325.0 88.5 %collective-permute-start.54 = (bf16[64,2048]{1,0:T(8,128)(2,1)}, bf16[64,2048]{1,0:T(8,128)(2,1)}, u32[]{:S(2)}, u32[]{:S(2)}) collective-permute-start(bf16[64,2048]{1,0:T(8,128)(2,1)} %collective-permute-done.52.refs_37_), channel_id=1, source_target_pairs={{8,0},{16,8},{24,16},{28,24},{20,28},{12,20},{4,12},{0,4},{9,1},{1... | collective-permute-start | bytes 786440 | tf_op jit(solution)/shard_map/ppermute | solution.py:461
  418.7 50.4 %collective-permute-start.9 = (bf16[256,2048]{1,0:T(8,128)(2,1)S(1)}, bf16[256,2048]{1,0:T(8,128)(2,1)}, u32[]{:S(2)}, u32[]{:S(2)}) collective-permute-start(bf16[256,2048]{1,0:T(8,128)(2,1)S(1)} %reduce-precision_convert_fusion.3), channel_id=1, source_target_pairs={{0,2},{1,3},{2,0},{3,1},{4,6},{5,7},{6,4},{7,5},{8,10},{9,11},{10,... | collective-permute-start | bytes 3145736 | tf_op jit(solution)/shard_map/ppermute | solution.py:526
  427.1 48.1 %collective-permute-start.28 = (bf16[3,256,512]{2,1,0:T(8,128)(2,1)}, bf16[3,256,512]{2,1,0:T(8,128)(2,1)S(1)}, u32[]{:S(2)}, u32[]{:S(2)}) collective-permute-start(bf16[3,256,512]{2,1,0:T(8,128)(2,1)} %get-tuple-element.79), channel_id=1, source_target_pairs={{0,8},{8,16},{16,24},{24,28},{28,20},{20,12},{12,4},{4,0},{1,9},{9... | collective-permute-start | bytes 2359304 | tf_op jit(solution)/shard_map/ppermute | solution.py:456
  428.3 46.9 %collective-permute-start.32 = (bf16[3,256,512]{2,1,0:T(8,128)(2,1)}, bf16[3,256,512]{2,1,0:T(8,128)(2,1)}, u32[]{:S(2)}, u32[]{:S(2)}) collective-permute-start(bf16[3,256,512]{2,1,0:T(8,128)(2,1)} %get-tuple-element.80), channel_id=1, source_target_pairs={{8,0},{16,8},{24,16},{28,24},{20,28},{12,20},{4,12},{0,4},{9,1},{1... | collective-permute-start | bytes 2359304 | tf_op jit(solution)/shard_map/ppermute | solution.py:461
  429.2 34.2 %collective-permute-start.22 = (f32[6,2048]{1,0:T(8,128)S(1)}, f32[6,2048]{1,0:T(8,128)S(1)}, u32[]{:S(2)}, u32[]{:S(2)}) collective-permute-start(f32[6,2048]{1,0:T(8,128)S(1)} %fusion.50), channel_id=1, source_target_pairs={{0,4},{4,0},{8,12},{12,8},{16,20},{20,16},{24,28},{28,24},{1,5},{5... | collective-permute-start | bytes 147464 | tf_op jit(solution)/shard_map/ppermute | solution.py:545
  473.4 38.4 %collective-permute-start.20 = (bf16[256,2048]{1,0:T(8,128)(2,1)}, bf16[256,2048]{1,0:T(8,128)(2,1)S(1)}, u32[]{:S(2)}, u32[]{:S(2)}) collective-permute-start(bf16[256,2048]{1,0:T(8,128)(2,1)} %get-tuple-element.105), channel_id=1, source_target_pairs={{0,1},{1,0},{2,3},{3,2},{4,5},{5,4},{6,7},{7,6},{8,9},{9,8},{10,11... | collective-permute-start | bytes 3145736 | tf_op jit(solution)/shard_map/ppermute | solution.py:519
  473.4 41.3 %collective-permute-start.10 = (bf16[256,2048]{1,0:T(8,128)(2,1)}, bf16[256,2048]{1,0:T(8,128)(2,1)S(1)}, u32[]{:S(2)}, u32[]{:S(2)}) collective-permute-start(bf16[256,2048]{1,0:T(8,128)(2,1)} %get-tuple-element.106), channel_id=1, source_target_pairs={{0,1},{1,0},{2,3},{3,2},{4,5},{5,4},{6,7},{7,6},{8,9},{9,8},{10,11... | collective-permute-start | bytes 3145736 | tf_op jit(solution)/shard_map/ppermute | solution.py:519
  484.5 33.2 %collective-permute-start.33 = (bf16[3,256,512]{2,1,0:T(8,128)(2,1)S(1)}, bf16[3,256,512]{2,1,0:T(8,128)(2,1)S(1)}, u32[]{:S(2)}, u32[]{:S(2)}) collective-permute-start(bf16[3,256,512]{2,1,0:T(8,128)(2,1)S(1)} %get-tuple-element.72), channel_id=1, source_target_pairs={{0,8},{8,16},{16,24},{24,28},{28,20},{20,12},{12,4},{4,0},{1,9},{9... | collective-permute-start | bytes 2359304 | tf_op jit(solution)/shard_map/ppermute | solution.py:456
  485.4 33.2 %collective-permute-start.34 = (bf16[3,256,512]{2,1,0:T(8,128)(2,1)S(1)}, bf16[3,256,512]{2,1,0:T(8,128)(2,1)S(1)}, u32[]{:S(2)}, u32[]{:S(2)}) collective-permute-start(bf16[3,256,512]{2,1,0:T(8,128)(2,1)S(1)} %get-tuple-element.72), channel_id=1, source_target_pairs={{8,0},{16,8},{24,16},{28,24},{20,28},{12,20},{4,12},{0,4},{9,1},{1... | collective-permute-start | bytes 2359304 | tf_op jit(solution)/shard_map/ppermute | solution.py:461
  517.7 38.3 %collective-permute-start.35 = (bf16[3,256,512]{2,1,0:T(8,128)(2,1)S(1)}, bf16[3,256,512]{2,1,0:T(8,128)(2,1)S(1)}, u32[]{:S(2)}, u32[]{:S(2)}) collective-permute-start(bf16[3,256,512]{2,1,0:T(8,128)(2,1)S(1)} %collective-permute-done.33.refs_36_), channel_id=1, source_target_pairs={{0,8},{8,16},{16,24},{24,28},{28,20},{20,12},{12,4},{4,0},{1,9},{9... | collective-permute-start | bytes 2359304 | tf_op jit(solution)/shard_map/ppermute | solution.py:456
  518.6 38.4 %collective-permute-start.36 = (bf16[3,256,512]{2,1,0:T(8,128)(2,1)S(1)}, bf16[3,256,512]{2,1,0:T(8,128)(2,1)S(1)}, u32[]{:S(2)}, u32[]{:S(2)}) collective-permute-start(bf16[3,256,512]{2,1,0:T(8,128)(2,1)S(1)} %collective-permute-done.34.refs_37_), channel_id=1, source_target_pairs={{8,0},{16,8},{24,16},{28,24},{20,28},{12,20},{4,12},{0,4},{9,1},{1... | collective-permute-start | bytes 2359304 | tf_op jit(solution)/shard_map/ppermute | solution.py:461
  (132 other events, 1987.5 us)

commit v2 on v1

v2 whole, which is shorter than its diff:
```python
from functools import partial

import jax
import jax.numpy as jnp
from jax import lax
from jax.experimental import pallas as pl
from jax.experimental.pallas import tpu as pltpu
from jax.sharding import PartitionSpec as P

HEAD = 128
HIGHEST = lax.Precision.HIGHEST
EPSILON = 1e-05
F32 = jnp.float32
BF16 = jnp.bfloat16
VMEM_LIMIT = 56 * 1024 * 1024
COST = 4
NN = (((1,), (0,)), ((), ()))
NT = (((1,), (1,)), ((), ()))
TN = (((0,), (0,)), ((), ()))


def dot(a, b, dims=NN):
    return lax.dot_general(a, b, dims, preferred_element_type=F32)


def low(x):
    return lax.reduce_precision(x, 8, 7).astype(BF16)


def params():
    return pltpu.CompilerParams(vmem_limit_bytes=VMEM_LIMIT)


def cost(flops, nbytes, transcendentals=0):
    return pl.CostEstimate(flops=flops // COST, bytes_accessed=nbytes // COST, transcendentals=transcendentals // COST)


def rotary_table(length, head_size):
    position = jnp.arange(length, dtype=F32)
    inverse = 10000.0 ** (-jnp.arange(0, head_size, 2, dtype=F32) / head_size)
    angles = position[:, None] * inverse[None, :]
    angles = jnp.concatenate([angles, angles], -1)
    sign = jnp.where(jnp.arange(head_size) < head_size // 2, -1.0, 1.0)
    return jnp.cos(angles), jnp.sin(angles) * sign


def attend_kernel(x_ref, gain_ref, w_ref, cos_ref, sin_ref, wout_ref,
                  mine_ref, other_ref, normed_ref, qkv_ref, lse_ref, mixed_ref, *, heads, steps):
    g = pl.program_id(0)
    length = x_ref.shape[0]
    half = length // 2
    scale = HEAD ** -0.5

    @pl.when(g == 0)
    def _():
        values = x_ref[...].astype(F32)
        inv = lax.rsqrt(jnp.mean(values * values, -1, keepdims=True) + EPSILON)
        normed_ref[...] = (values * inv * gain_ref[...]).astype(BF16)

    normed = normed_ref[...]
    cos, sin = cos_ref[...], sin_ref[...]
    projected = [dot(normed, w_ref[c]) for c in range(3)]
    for h in range(heads):
        cols = slice(h * HEAD, (h + 1) * HEAD)
        q, k, v = (p[:, cols] for p in projected)
        q = (q * cos + pltpu.roll(q, HEAD // 2, 1) * sin).astype(BF16)
        k = (k * cos + pltpu.roll(k, HEAD // 2, 1) * sin).astype(BF16)
        v = v.astype(BF16)
        qkv_ref[0, :, cols] = q
        qkv_ref[1, :, cols] = k
        qkv_ref[2, :, cols] = v
        for b in range(2):
            rows = slice(b * half, (b + 1) * half)
            keys = (b + 1) * half
            scores = dot(q[rows], k[:keys], NT) * scale
            at = lax.broadcasted_iota(jnp.int32, scores.shape, 0) + b * half
            to = lax.broadcasted_iota(jnp.int32, scores.shape, 1)
            scores = jnp.where(at >= to, scores, -1000000000.0)
            top = jnp.max(scores, -1, keepdims=True)
            weights = jnp.exp(scores - top)
            total = jnp.sum(weights, -1, keepdims=True)
            lse_ref[h, rows, :] = jnp.broadcast_to(top + jnp.log(total), (half, HEAD))
            low = (weights * (1.0 / total)).astype(BF16)
            mixed_ref[rows, pl.ds(pl.multiple_of((g * heads + h) * HEAD, HEAD), HEAD)] = dot(low, v[:keys]).astype(BF16)

    @pl.when(g == steps - 1)
    def _():
        core = lax.rem(lax.axis_index("mp"), 2)
        for ref, c in ((other_ref, 1 - core), (mine_ref, core)):
            rows = pl.ds(pl.multiple_of(c * half, half), half)
            ref[...] = dot(mixed_ref[rows, :], wout_ref[...]).astype(BF16)


def attend(tokens, gain, w3, cos, sin, w_out):
    length, model = tokens.shape
    local = w3.shape[2]
    local_heads = local // HEAD
    heads = 2 if local_heads % 2 == 0 else 1
    steps = local_heads // heads
    wide = heads * HEAD
    full = lambda *shape: pl.BlockSpec(shape, lambda g: (0,) * len(shape))
    return pl.pallas_call(
        partial(attend_kernel, heads=heads, steps=steps),
        grid=(steps,),
        in_specs=[
            full(length, model), full(1, model),
            pl.BlockSpec((3, model, wide), lambda g: (0, 0, g)),
            full(length, HEAD), full(length, HEAD), full(local, model),
        ],
        out_specs=[
            full(length // 2, model), full(length // 2, model), full(length, model),
            pl.BlockSpec((3, length, wide), lambda g: (0, 0, g)),
            pl.BlockSpec((heads, length, HEAD), lambda g: (g, 0, 0)),
            full(length, local),
        ],
        out_shape=[
            jax.ShapeDtypeStruct((length // 2, model), BF16),
            jax.ShapeDtypeStruct((length // 2, model), BF16),
            jax.ShapeDtypeStruct((length, model), BF16),
            jax.ShapeDtypeStruct((3, length, local), BF16),
            jax.ShapeDtypeStruct((local_heads, length, HEAD), F32),
            jax.ShapeDtypeStruct((length, local), BF16),
        ],
        compiler_params=params(),
        cost_estimate=cost(2 * length * model * local * 4 + 4 * length * length * local,
                           2 * (2 * length * model + 4 * model * local), length * length * local_heads),
        name="attend",
    )(tokens, gain, w3, cos, sin, w_out)


def attend_back_kernel(ga_ref, normed_ref, qkv_ref, lse_ref, mixed_ref, wout_ref, w_ref, cos_ref, sin_ref,
                       *rest, heads, steps, deps):
    grad_ref, first_ref, acc_ref = rest[deps:]
    g = pl.program_id(0)
    length = ga_ref.shape[0]
    half = length // 2
    scale = HEAD ** -0.5
    cos, sin = cos_ref[...], sin_ref[...]
    ga = ga_ref[...]
    gmixed = dot(ga, wout_ref[...], NT).astype(BF16)
    gproj = [[], [], []]
    for h in range(heads):
        cols = slice(h * HEAD, (h + 1) * HEAD)
        q, k, v = (qkv_ref[c, :, cols] for c in range(3))
        gm = gmixed[:, cols]
        gq, gk, gv = [], [None, None], [None, None]
        for b in range(2):
            rows = slice(b * half, (b + 1) * half)
            keys = (b + 1) * half
            scores = dot(q[rows], k[:keys], NT) * scale
            at = lax.broadcasted_iota(jnp.int32, scores.shape, 0) + b * half
            to = lax.broadcasted_iota(jnp.int32, scores.shape, 1)
            probs = jnp.where(at >= to, jnp.exp(scores - lse_ref[h, rows, :1]), 0.0)
            gprobs = dot(gm[rows], v[:keys], NT)
            gscores = probs * (gprobs - jnp.sum(gprobs * probs, -1, keepdims=True))
            gs = gscores.astype(BF16)
            low_probs = probs.astype(BF16)
            gq.append(dot(gs, k[:keys]) * scale)
            for j in range(b + 1):
                part = slice(j * half, (j + 1) * half)
                a = dot(gs[:, part], q[rows], TN) * scale
                c = dot(low_probs[:, part], gm[rows], TN)
                gk[j] = a if gk[j] is None else gk[j] + a
                gv[j] = c if gv[j] is None else gv[j] + c
        gq = jnp.concatenate(gq, 0)
        gk = jnp.concatenate(gk, 0)
        gv = jnp.concatenate(gv, 0)
        gproj[0].append((gq * cos - pltpu.roll(gq, HEAD // 2, 1) * sin).astype(BF16))
        gproj[1].append((gk * cos - pltpu.roll(gk, HEAD // 2, 1) * sin).astype(BF16))
        gproj[2].append(gv.astype(BF16))
    gproj = [jnp.concatenate(p, 1) for p in gproj]

    @pl.when(g == 0)
    def _():
        acc_ref[...] = jnp.zeros_like(acc_ref)

    grad_ref[3] = dot(ga, mixed_ref[...], TN).astype(BF16)
    for c in range(3):
        grad_ref[c] = dot(normed_ref[...], gproj[c], TN).astype(BF16)
        acc_ref[...] += dot(gproj[c], w_ref[c], NT)

    @pl.when(g == steps - 1)
    def _():
        first_ref[...] = acc_ref[...].astype(BF16)


def attend_back(ga, normed, qkv, lse, mixed, w_out, w3, cos, sin, deps=()):
    length, model = ga.shape
    local = w3.shape[2]
    local_heads = local // HEAD
    heads = 2 if local_heads % 2 == 0 else 1
    steps = local_heads // heads
    wide = heads * HEAD
    full = lambda *shape: pl.BlockSpec(shape, lambda g: (0,) * len(shape))
    return pl.pallas_call(
        partial(attend_back_kernel, heads=heads, steps=steps, deps=len(deps)),
        grid=(steps,),
        in_specs=[
            full(length, model), full(length, model),
            pl.BlockSpec((3, length, wide), lambda g: (0, 0, g)),
            pl.BlockSpec((heads, length, HEAD), lambda g: (g, 0, 0)),
            pl.BlockSpec((length, wide), lambda g: (0, g)),
            pl.BlockSpec((wide, model), lambda g: (g, 0)),
            pl.BlockSpec((3, model, wide), lambda g: (0, 0, g)),
            full(length, HEAD), full(length, HEAD),
        ] + [pl.BlockSpec(memory_space=pl.ANY)] * len(deps),
        out_specs=[pl.BlockSpec((4, model, wide), lambda g: (0, 0, g)), full(length, model)],
        out_shape=[
            jax.ShapeDtypeStruct((4, model, local), BF16),
            jax.ShapeDtypeStruct((length, model), BF16),
        ],
        scratch_shapes=[pltpu.VMEM((length, model), F32)],
        compiler_params=params(),
        cost_estimate=cost(2 * length * model * local * 8 + 10 * length * length * local,
                           2 * (4 * length * model + 8 * model * local), length * length * local_heads),
        name="attend_back",
    )(ga, normed, qkv, lse, mixed, w_out, w3, cos, sin, *deps)


def own_grad_kernel(sent_ref, cot_ref, bucket_ref, gate_ref, unsort_ref, up_ref, down_ref, *rest, row_bounds, deps):
    mine_ref, other_ref, act_ref, acc_ref = rest[deps:]
    level = pl.program_id(0)
    for q, rows in enumerate(row_bounds):
        @pl.when(level == q)
        def _(q=q, rows=rows):
            keep = bucket_ref[:rows, :1] >= q
            pre = dot(sent_ref[:rows], up_ref[0])
            active = jnp.where(keep, jnp.maximum(pre, 0.0), 0.0)
            act_ref[0, :rows] = (active * active).astype(BF16)
            gact = dot(cot_ref[:rows], down_ref[0], NT)
            gpre = (gact * (2.0 * gate_ref[:rows, :1]) * active).astype(BF16)
            s = dot(gpre, up_ref[0], NT)
            if q == 0:
                acc_ref[...] = s
            else:
                acc_ref[:rows] += s
            if q == len(row_bounds) - 1:
                half = mine_ref.shape[0]
                total = acc_ref[...].astype(BF16)
                other_ref[...] = dot(unsort_ref[half:], total).astype(BF16)
                mine_ref[...] = dot(unsort_ref[:half], total).astype(BF16)


def own_grad(sent, cot, bucket, gate, unsort, w_up, w_down, row_bounds, deps=()):
    length, model = sent.shape
    levels, _, hidden = w_up.shape
    full = lambda *shape: pl.BlockSpec(shape, lambda q: (0,) * len(shape))
    return pl.pallas_call(
        partial(own_grad_kernel, row_bounds=tuple(row_bounds), deps=len(deps)),
        grid=(levels,),
        in_specs=[
            full(length, model), full(length, model), full(length, 128), full(length, 128), full(length, length),
            pl.BlockSpec((1, model, hidden), lambda q: (q, 0, 0)),
            pl.BlockSpec((1, hidden, model), lambda q: (q, 0, 0)),
        ] + [pl.BlockSpec(memory_space=pl.ANY)] * len(deps),
        out_specs=[full(length // 2, model)] * 2 + [pl.BlockSpec((1, length, hidden), lambda q: (q, 0, 0))],
        out_shape=[jax.ShapeDtypeStruct((length // 2, model), BF16)] * 2
        + [jax.ShapeDtypeStruct((levels, length, hidden), BF16)],
        scratch_shapes=[pltpu.VMEM((length, model), F32)],
        compiler_params=params(),
        cost_estimate=cost(6 * sum(row_bounds) * model * hidden, 4 * levels * model * hidden + 6 * length * model),
        name="own_grad",
    )(sent, cot, bucket, gate, unsort, w_up, w_down, *deps)


def own_forward_kernel(act_ref, cot_ref, unsort_ref, down_ref, *rest, row_bounds, deps):
    ffn_ref, ggate_ref, acc_ref = rest[deps:]
    level = pl.program_id(0)
    for q, rows in enumerate(row_bounds):
        @pl.when(level == q)
        def _(q=q, rows=rows):
            f = dot(act_ref[0, :rows], down_ref[0])
            if q == 0:
                acc_ref[...] = f
            else:
                acc_ref[:rows] += f
            if q == len(row_bounds) - 1:
                total = acc_ref[...]
                ggate = jnp.sum(total * cot_ref[...].astype(F32), -1, keepdims=True)
                ggate_ref[...] = jnp.broadcast_to(ggate, ggate_ref.shape)
                ffn_ref[...] = dot(unsort_ref[...], total.astype(BF16)).astype(BF16)


def own_forward(act, cot, unsort, w_down, row_bounds, deps=()):
    length, model = cot.shape
    levels, hidden, _ = w_down.shape
    full = lambda *shape: pl.BlockSpec(shape, lambda q: (0,) * len(shape))
    return pl.pallas_call(
        partial(own_forward_kernel, row_bounds=tuple(row_bounds), deps=len(deps)),
        grid=(levels,),
        in_specs=[
            pl.BlockSpec((1, length, hidden), lambda q: (q, 0, 0)),
            full(length, model), full(length, length),
            pl.BlockSpec((1, hidden, model), lambda q: (q, 0, 0)),
        ] + [pl.BlockSpec(memory_space=pl.ANY)] * len(deps),
        out_specs=[full(length, model), full(length, 128)],
        out_shape=[jax.ShapeDtypeStruct((length, model), BF16), jax.ShapeDtypeStruct((length, 128), F32)],
        scratch_shapes=[pltpu.VMEM((length, model), F32)],
        compiler_params=params(),
        cost_estimate=cost(2 * sum(row_bounds) * model * hidden, 2 * levels * model * hidden + 6 * length * model),
        name="own_forward",
    )(act, cot, unsort, w_down, *deps)


AUX = 16


def gates_and_buckets(aux):
    row = lax.broadcasted_iota(jnp.int32, (AUX, 128), 0)
    gates = dot(aux, (row < 3).astype(BF16), TN)
    buckets = dot(aux, (row == 3).astype(BF16), TN)
    return gates, buckets


def weight_kernel(s_ref, c_ref, up_ref, down_ref, *refs, level, rows, group, carried, deps):
    gup_ref, gdown_ref, up_buf, down_buf, s_buf, aux_buf, c_buf, gup, gdown, sems = refs[carried + deps:]
    b = pl.program_id(0)
    steps = pl.num_programs(0)
    slices, piece = s_ref.shape[1], s_ref.shape[3]
    length = c_ref.shape[2]
    span = pl.ds(0, rows)

    def tokens_of(step, slot):
        out = []
        for j in range(group):
            block = step * group + j
            to = pl.ds(j * rows, rows)
            for m in range(slices):
                out.append((s_ref.at[block, m, span], s_buf.at[slot, to, pl.ds(m * piece, piece)]))
            for m in range(length // piece):
                out.append((s_ref.at[block, m, pl.ds(length, AUX)], aux_buf.at[slot, j, pl.ds(0, AUX), pl.ds(m * piece, piece)]))
        return [pltpu.make_async_copy(x, y, sems.at[slot, i]) for i, (x, y) in enumerate(out)]

    def cots_of(step, slot):
        out = []
        for j in range(group):
            block = step * group + j
            to = pl.ds(j * rows, rows)
            for m in range(slices):
                out.append((c_ref.at[block, m, span], c_buf.at[slot, to, pl.ds(m * piece, piece)]))
        return [pltpu.make_async_copy(x, y, sems.at[2 + slot, i]) for i, (x, y) in enumerate(out)]

    up_copy = pltpu.make_async_copy(up_ref.at[level], up_buf, sems.at[4, 0])
    down_copy = pltpu.make_async_copy(down_ref.at[level], down_buf, sems.at[4, 1])
    ends = [pltpu.make_async_copy(gup, gup_ref.at[level], sems.at[4, 2]),
            pltpu.make_async_copy(gdown, gdown_ref.at[level], sems.at[4, 3])]
    slot = lax.rem(b, 2)

    @pl.when(b == 0)
    def _():
        for c in [up_copy] + tokens_of(0, 0) + [down_copy] + cots_of(0, 0):
            c.start()

    @pl.when(b + 1 < steps)
    def _():
        for c in tokens_of(b + 1, 1 - slot) + cots_of(b + 1, 1 - slot):
            c.start()

    @pl.when(b == 0)
    def _():
        up_copy.wait()

    for c in tokens_of(b, slot):
        c.wait()
    columns = [gates_and_buckets(aux_buf[slot, j]) for j in range(group)]
    gate = jnp.concatenate([g[:rows, :1] for g, _ in columns], 0)
    keep = jnp.concatenate([k[:rows, :1] for _, k in columns], 0) >= level
    pre = dot(s_buf[slot], up_buf[...])
    active = jnp.where(keep, jnp.maximum(pre, 0.0), 0.0)
    act = (active * active * gate).astype(BF16)

    @pl.when(b == 0)
    def _():
        down_copy.wait()

    for c in cots_of(b, slot):
        c.wait()
    gact = dot(c_buf[slot], down_buf[...], NT)
    gpre = (gact * (2.0 * gate) * active).astype(BF16)

    @pl.when(b == 0)
    def _():
        gup[...] = dot(s_buf[slot], gpre, TN)
        gdown[...] = dot(act, c_buf[slot], TN)

    @pl.when(jnp.logical_and(b > 0, b < steps - 1))
    def _():
        gup[...] += dot(s_buf[slot], gpre, TN)
        gdown[...] += dot(act, c_buf[slot], TN)

    @pl.when(b == steps - 1)
    def _():
        gup[...] += dot(s_buf[slot], gpre, TN)
        ends[0].start()
        gdown[...] += dot(act, c_buf[slot], TN)
        ends[1].start()
        for c in ends:
            c.wait()


def weight_gradients(level, rows, sents, cots, w_up, w_down, carried, deps=()):
    levels, model, hidden = w_up.shape
    blocks, slices, length, piece = cots.shape
    group = max(1, min(4, 1024 // rows))
    while blocks % group or blocks // group < 2:
        group -= 1
    copies = group * (slices + length // piece)
    anywhere = pl.BlockSpec(memory_space=pl.ANY)
    return pl.pallas_call(
        partial(weight_kernel, level=level, rows=rows, group=group, carried=len(carried), deps=len(deps)),
        grid=(blocks // group,),
        in_specs=[anywhere] * (4 + len(carried) + len(deps)),
        out_specs=[anywhere] * 2,
        out_shape=[jax.ShapeDtypeStruct((levels, model, hidden), F32), jax.ShapeDtypeStruct((levels, hidden, model), F32)],
        input_output_aliases={4: 0, 5: 1} if carried else {},
        scratch_shapes=[
            pltpu.VMEM((model, hidden), BF16), pltpu.VMEM((hidden, model), BF16),
            pltpu.VMEM((2, group * rows, model), BF16), pltpu.VMEM((2, group, AUX, length), BF16),
            pltpu.VMEM((2, group * rows, model), BF16),
            pltpu.VMEM((model, hidden), F32), pltpu.VMEM((hidden, model), F32),
            pltpu.SemaphoreType.DMA((5, max(4, copies))),
        ],
        compiler_params=params(),
        cost_estimate=cost(8 * blocks * rows * model * hidden, 4 * blocks * length * model + 16 * model * hidden),
        name=f"weight_gradients_{level}",
    )(sents, cots, w_up, w_down, *carried, *deps)


def unpack_kernel(order_ref, *refs, count, carried):
    chunk_refs = refs[:count]
    qkv_ref, out_ref = refs[count + carried:]
    size = qkv_ref.shape[1]
    for k in range(count):
        @pl.when(pl.program_id(0) == k)
        def _(k=k):
            for c in range(3):
                qkv_ref[c] = chunk_refs[k][c * size:(c + 1) * size].astype(F32)
            out_ref[...] = chunk_refs[k][3 * size:4 * size].astype(F32).T


def unpack(order, chunks, size, total, carried=()):
    height, local = chunks[0].shape
    anywhere = pl.BlockSpec(memory_space=pl.ANY)
    count = len(chunks)
    return pl.pallas_call(
        partial(unpack_kernel, count=count, carried=len(carried)),
        grid_spec=pltpu.PrefetchScalarGridSpec(
            num_scalar_prefetch=1,
            grid=(count,),
            in_specs=[pl.BlockSpec((height, local), lambda b, o: (0, 0), pipeline_mode=pl.Buffered(1))] * count
            + [anywhere] * len(carried),
            out_specs=[
                pl.BlockSpec((3, size, local), lambda b, o: (0, o[b], 0)),
                pl.BlockSpec((local, size), lambda b, o: (0, o[b])),
            ],
        ),
        out_shape=[
            jax.ShapeDtypeStruct((3, total * size, local), F32),
            jax.ShapeDtypeStruct((local, total * size), F32),
        ],
        input_output_aliases={count + 1: 0, count + 2: 1} if carried else {},
        compiler_params=params(),
        cost_estimate=cost(0, 24 * count * size * local),
        name="unpack_some" if not carried else "unpack_rest",
    )(order, *chunks, *carried)


def add_kernel(*refs, count):
    total = refs[0][...].astype(F32)
    for ref in refs[1:count]:
        total = total + ref[...].astype(F32)
    refs[-1][...] = total.astype(BF16)


def add_rows(parts, deps=()):
    rows, columns = parts[0].shape
    block = pl.BlockSpec((rows // 4, columns), lambda i: (i, 0))
    return pl.pallas_call(
        partial(add_kernel, count=len(parts)),
        grid=(4,),
        in_specs=[block] * len(parts) + [pl.BlockSpec(memory_space=pl.ANY)] * len(deps),
        out_specs=block,
        out_shape=jax.ShapeDtypeStruct((rows, columns), BF16),
        compiler_params=params(),
        cost_estimate=cost(rows * columns, 6 * rows * columns),
        name="add_rows",
    )(*parts, *deps)


def pass_kernel(*refs):
    pass


def after(arrays, deps):
    anywhere = pl.BlockSpec(memory_space=pl.ANY)
    return pl.pallas_call(
        pass_kernel,
        in_specs=[anywhere] * (len(arrays) + len(deps)),
        out_specs=[anywhere] * len(arrays),
        out_shape=[jax.ShapeDtypeStruct(x.shape, x.dtype) for x in arrays],
        input_output_aliases={i: i for i in range(len(arrays))},
        compiler_params=params(),
        cost_estimate=cost(0, 0),
        name="after",
    )(*arrays, *deps)


def join_kernel(index_ref, right_local, left_local, right_ref, left_ref, *rest, cut, deps):
    right_out, left_out = rest[deps:]
    size = right_local.shape[1]
    if right_ref.shape[1] == size:
        right_out[0] = (right_local[0].astype(F32) + right_ref[0].astype(F32)).astype(BF16)
        left_out[0] = (left_local[0].astype(F32) + left_ref[0].astype(F32)).astype(BF16)
    else:
        right_out[0, :cut] = (right_local[0, :cut].astype(F32) + right_ref[0].astype(F32)).astype(BF16)
        right_out[0, cut:] = right_local[0, cut:]
        left_out[0, :cut] = left_local[0, :cut]
        left_out[0, cut:] = (left_local[0, cut:].astype(F32) + left_ref[0].astype(F32)).astype(BF16)


def join(grads, indices, right, left, size, deps=()):
    kinds, _, local = grads.shape
    arrived = right.shape[1]
    out = pl.BlockSpec((1, size, local), lambda i, o: (i, 0, 0))
    return pl.pallas_call(
        partial(join_kernel, cut=size // 2, deps=len(deps)),
        grid_spec=pltpu.PrefetchScalarGridSpec(
            num_scalar_prefetch=1,
            grid=(kinds,),
            in_specs=[
                pl.BlockSpec((1, size, local), lambda i, o: (i, o[0], 0)),
                pl.BlockSpec((1, size, local), lambda i, o: (i, o[1], 0)),
                pl.BlockSpec((1, arrived, local), lambda i, o: (i, 0, 0)),
                pl.BlockSpec((1, arrived, local), lambda i, o: (i, 0, 0)),
            ] + [pl.BlockSpec(memory_space=pl.ANY)] * len(deps),
            out_specs=[out, out],
        ),
        out_shape=[jax.ShapeDtypeStruct((kinds, size, local), BF16)] * 2,
        compiler_params=params(),
        cost_estimate=cost(2 * kinds * size * local, 12 * kinds * size * local),
        name="join",
    )(indices, grads, grads, right, left, *deps)


def join_own_kernel(index_ref, local_ref, right_ref, left_ref, extra_ref, *rest):
    kinds, size, _ = right_ref.shape
    for c in range(kinds):
        total = local_ref[c].astype(F32) + right_ref[c].astype(F32) + left_ref[c].astype(F32)
        rest[-1][c * size:(c + 1) * size] = total.astype(BF16)
    rest[-1][kinds * size:] = extra_ref[...]


def join_own(grads, indices, right, left, extra, deps=()):
    kinds, size, local = right.shape
    block = pl.BlockSpec((kinds, size, local), lambda i, o: (0, 0, 0))
    height = kinds * size + extra.shape[0]
    return pl.pallas_call(
        join_own_kernel,
        grid_spec=pltpu.PrefetchScalarGridSpec(
            num_scalar_prefetch=1,
            grid=(1,),
            in_specs=[pl.BlockSpec((kinds, size, local), lambda i, o: (0, o[0], 0)), block, block,
                      pl.BlockSpec(extra.shape, lambda i, o: (0, 0))]
            + [pl.BlockSpec(memory_space=pl.ANY)] * len(deps),
            out_specs=pl.BlockSpec((height, local), lambda i, o: (0, 0)),
        ),
        out_shape=jax.ShapeDtypeStruct((height, local), BF16),
        compiler_params=params(),
        cost_estimate=cost(2 * kinds * size * local, 8 * kinds * size * local),
        name="join_own",
    )(indices, grads, right, left, extra, *deps)


def ring_order(count):
    nz = 4 if count % 4 == 0 else 1
    ny = count // nz
    if nz == 1 or ny % 2:
        return list(range(count))
    order = [(z, 0) for z in range(nz)]
    for y in range(1, ny):
        line = list(range(1, nz))
        order += [(z, y) for z in (reversed(line) if y % 2 else line)]
    order += [(0, y) for y in range(ny - 1, 0, -1)]
    return [z * ny + y for z, y in order]


class Ring:
    def __init__(self):
        self.log = []
        self.count = lax.axis_size("dp")
        self.order = ring_order(self.count)
        n = self.count
        place = [0] * n
        for p, d in enumerate(self.order):
            place[d] = p
        self.position = jnp.array(place, jnp.int32)[lax.axis_index("dp")]
        self.right = [(self.order[p], self.order[(p + 1) % n]) for p in range(n)]
        self.left = [(self.order[(p + 1) % n], self.order[p]) for p in range(n)]

    def to_right(self, x):
        out = lax.ppermute(x, "dp", self.right)
        self.log.append(out)
        return out

    def to_left(self, x):
        out = lax.ppermute(x, "dp", self.left)
        self.log.append(out)
        return out

    def logged(self, f, *args):
        self.log = []
        out = f(*args)
        pairs = [tuple(self.log[i:i + 2]) for i in range(0, len(self.log), 2)]
        self.log = []
        return out, pairs

    def gather(self, x, axis):
        out = [x]
        r = l = x
        for _ in range(self.count // 2 - 1):
            r, l = self.to_right(r), self.to_left(l)
            out += [r, l]
        size = x.shape[axis]
        cut = size // 32 * 16
        first = self.to_right(lax.slice_in_dim(r, 0, cut, axis=axis))
        second = self.to_left(lax.slice_in_dim(l, cut, size, axis=axis))
        out.append(jnp.concatenate([first, second], axis))
        return out

    def offsets(self):
        out = [0]
        for k in range(1, self.count // 2):
            out += [-k, k]
        return out + [self.count // 2]

    def indices(self):
        return [(self.position + k) % self.count for k in self.offsets()]

    def reduce_start(self, x):
        size = x.shape[1] // self.count
        cut = size // 2
        far = self.count // 2
        at = ((self.position + far) % self.count) * size
        r = lax.dynamic_slice_in_dim(x, at, cut, axis=1)
        l = lax.dynamic_slice_in_dim(x, at + cut, cut, axis=1)
        return (self.to_right(r), self.to_left(l)), (r, l)

    def reduce_step(self, x, arrived, k, deps=()):
        indices = jnp.stack([(self.position + k) % self.count, (self.position - k) % self.count]).astype(jnp.int32)
        r, l = join(x, indices, *arrived, x.shape[1] // self.count, deps)
        return (self.to_right(r), self.to_left(l)), (r, l)

    def reduce_end(self, x, arrived, extra, deps=()):
        return join_own(x, self.position[None].astype(jnp.int32), *arrived, extra, deps)


def core_swap(x):
    n = lax.axis_size("mp")
    return lax.ppermute(x, "mp", [(i, i ^ 1) for i in range(n)])


def sum_over_x(x):
    n = lax.axis_size("mp") // 2
    index = lax.axis_index("mp")
    parts = [x] + [
        lax.ppermute(x, "mp", [(i, (i + 2 * k) % (2 * n)) for i in range(2 * n)]) for k in range(1, n)
    ]
    if n == 1:
        return x.astype(F32)
    if n == 2:
        return parts[0].astype(F32) + parts[1].astype(F32)
    stacked = jnp.stack(parts)
    total = None
    for j in range(n):
        term = lax.dynamic_index_in_dim(stacked, (index // 2 - j) % n, 0, keepdims=False).astype(F32)
        total = term if total is None else total + term
    return total


def on_device(tokens, gain_first, w_qkv, w_out, gain_second, router, w_up, w_down, slot, cotangent):
    length, model = tokens.shape
    buckets = w_up.shape[0]
    devices_dp = lax.axis_size("dp")
    groups = devices_dp // buckets
    capacity = length * 5 // (4 * devices_dp)
    row_bounds = [min(length, (buckets - level) * groups * capacity) for level in range(buckets)]
    ring = Ring()
    core = lax.axis_index("mp") % 2
    half = length // 2

    bucket_ids = slot // capacity // groups
    places = jnp.arange(length, dtype=jnp.int32)
    key = (buckets - 1 - bucket_ids) * length + places
    rank = jnp.sum((key[None, :] < key[:, None]).astype(jnp.int32), 1)
    rank_here = jnp.roll(rank, -core * half)
    sort_rows = places[:, None] == rank[None, :]
    sort_here = places[:, None] == rank_here[None, :]
    sort_low = sort_here.astype(BF16)
    unsort_low = (rank_here[:, None] == places[None, :]).astype(BF16)
    bucket_sorted = jnp.sum(jnp.where(sort_rows, bucket_ids[None, :], 0), 1)

    def part_of(x, c, axis=0):
        size = x.shape[axis] // 2
        return lax.dynamic_slice_in_dim(x, c * size, size, axis=axis)

    def own_rows(x):
        return part_of(x, core)

    def other_rows(x):
        return part_of(x, 1 - core)

    def joined(mine, other):
        return jnp.concatenate([jnp.where(core == 0, mine, other), jnp.where(core == 0, other, mine)], 0)

    cot_sorted = dot(sort_rows.astype(BF16), cotangent).astype(BF16)
    slices = lax.axis_size("mp")
    piece = model // slices
    me = lax.axis_index("mp")
    cot_piece = lax.dynamic_slice_in_dim(cot_sorted, me * piece, piece, axis=1)
    cots = lax.all_gather(cot_piece, ("dp", "mp"), axis=0).reshape(devices_dp, slices, length, piece)

    w3 = jnp.transpose(w_qkv, (1, 0, 2))
    cos, sin = rotary_table(length, HEAD)
    part_mine, part_other, normed_low, qkv, lse, mixed = attend(tokens, gain_first[None, :], w3, cos, sin, w_out)
    attn_rows = add_rows([part_mine, core_swap(part_other)], (cot_piece,))
    attn = sum_over_x(attn_rows)

    resid = own_rows(tokens).astype(F32) + attn
    inv = lax.rsqrt(jnp.mean(resid * resid, -1, keepdims=True) + EPSILON)
    xhat = resid * inv
    normed_second = xhat * gain_second
    logits = jnp.dot(normed_second, router, precision=HIGHEST)
    prob = jax.nn.softmax(logits, axis=-1)
    onehot = (own_rows(bucket_ids)[:, None] == jnp.arange(buckets)[None, :]).astype(F32)
    gate = buckets * jnp.sum(prob * onehot, -1)
    sent_half = normed_second.astype(BF16)
    sent_both = jnp.concatenate([sent_half, core_swap(sent_half)], 0)
    gate_both = jnp.concatenate([gate, core_swap(gate)], 0)
    gate_sorted = jnp.sum(jnp.where(sort_here, gate_both[None, :], 0.0), 1)

    sent_sorted = dot(sort_low, sent_both).astype(BF16)

    gate_1 = low(gate_sorted)
    gate_2 = low(gate_sorted - gate_1.astype(F32))
    gate_3 = low(gate_sorted - gate_1.astype(F32) - gate_2.astype(F32))
    aux = jnp.stack([gate_1, gate_2, gate_3, bucket_sorted.astype(BF16)] + [jnp.zeros_like(gate_1)] * (AUX - 4))
    sent_piece = jnp.concatenate([
        lax.dynamic_slice_in_dim(sent_sorted, me * piece, piece, axis=1),
        lax.dynamic_slice_in_dim(aux, (me % (length // piece)) * piece, piece, axis=1)], 0)
    sents = lax.all_gather(sent_piece, ("dp", "mp"), axis=0).reshape(devices_dp, slices, length + AUX, piece)

    wide = lambda x: jnp.broadcast_to(x[:, None], (length, 128))
    gsent_mine, gsent_other, act = own_grad(
        sent_sorted, cot_sorted, wide(bucket_sorted), wide(gate_sorted), unsort_low, w_up, w_down, row_bounds,
        (sent_piece,))
    gsent_rows = add_rows([gsent_mine, core_swap(gsent_other)])
    grad_sent = sum_over_x(gsent_rows).astype(BF16).astype(F32)
    ffn_part, ggate_part = own_forward(
        act, cot_sorted, sort_rows.astype(BF16).T, w_down, row_bounds, (gsent_rows,))
    ffn_rows = sum_over_x(add_rows([own_rows(ffn_part), core_swap(other_rows(ffn_part))])).astype(BF16).astype(F32)
    ggate_part = jnp.sum(jnp.where(sort_rows, ggate_part[:, :1], 0.0), 0)
    grad_gate = ggate_part + core_swap(ggate_part)
    grad_gate = sum_over_x(own_rows(grad_gate))

    grad_output = own_rows(cotangent).astype(F32)
    output_half = (resid + gate[:, None] * ffn_rows).astype(BF16)
    grad_prob = buckets * grad_gate[:, None] * onehot
    grad_logits = prob * (grad_prob - jnp.sum(grad_prob * prob, -1, keepdims=True))
    grad_router = jnp.dot(normed_second.T, grad_logits, precision=HIGHEST)
    grad_second = grad_sent + jnp.dot(grad_logits, router.T, precision=HIGHEST)
    grad_gain_second = jnp.sum(grad_second * xhat, 0)
    scaled = grad_second * gain_second
    grad_resid = grad_output + inv * (scaled - xhat * jnp.mean(scaled * xhat, -1, keepdims=True))
    ga_half = low(grad_resid)
    grad_attn = joined(ga_half, core_swap(ga_half))

    grads, first_part = attend_back(
        grad_attn, normed_low, qkv, lse, mixed, w_out, w3, cos, sin)

    grad_first = sum_over_x(add_rows([own_rows(first_part), core_swap(other_rows(first_part))])).astype(BF16).astype(F32)
    source = own_rows(tokens).astype(F32)
    inv_first = lax.rsqrt(jnp.mean(source * source, -1, keepdims=True) + EPSILON)
    xhat_first = source * inv_first
    grad_gain_first = jnp.sum(grad_first * xhat_first, 0)
    scaled_first = grad_first * gain_first
    grad_source = inv_first * (scaled_first - xhat_first * jnp.mean(scaled_first * xhat_first, -1, keepdims=True))
    tokens_half = (grad_source + grad_resid).astype(BF16)
    output = joined(output_half, core_swap(output_half))
    grad_tokens = joined(tokens_half, core_swap(tokens_half))
    small = jnp.concatenate([grad_router.T, grad_gain_second[None], grad_gain_first[None]], 0)
    small = jnp.pad(small, ((0, -small.shape[0] % 8), (0, 0)))
    local = w3.shape[2]
    extra = low(small + core_swap(small)).reshape(-1, local)

    carried = ()
    arrived, sending = ring.reduce_start(grads)
    far = devices_dp // 2
    chunks = None
    step = 0

    def advance(step, arrived, deps):
        nonlocal chunks
        if step < far - 1:
            return ring.reduce_step(grads, arrived, far - 1 - step, deps)
        if step == far - 1:
            chunks = [ring.reduce_end(grads, arrived, extra, deps)]
            r = l = chunks[0]
        else:
            r, l = after(arrived, deps) if deps else arrived
            chunks.extend([r, l])
        if step < 2 * far - 2:
            sending = (r, l)
            r, l = ring.to_right(r), ring.to_left(l)
        else:
            cut = r.shape[0] // 32 * 16
            sending = (r[:cut], l[cut:])
            r, l = ring.to_right(sending[0]), ring.to_left(sending[1])
            chunks.append(jnp.concatenate([r, l], 0))
        return (r, l), sending

    steps = 2 * far - 1
    while step < far - 1:
        arrived, sending = advance(step, arrived, ())
        step += 1
    for level in range(buckets):
        carried = weight_gradients(level, row_bounds[level], sents, cots, w_up, w_down, tuple(carried), sending)
        if step < steps:
            arrived, sending = advance(step, arrived, (carried[0],))
            step += 1
        else:
            sending = ()
    while step < steps:
        arrived, sending = advance(step, arrived, ())
        step += 1
    grad_up, grad_down = carried
    order = jnp.stack(ring.indices()).astype(jnp.int32)
    size = model // devices_dp
    unpacked = unpack(order[:-1], chunks[:-1], size, devices_dp)
    grad_wqkv, grad_wout = unpack(order[-1:], chunks[-1:], size, devices_dp, unpacked)
    terms = jnp.stack([x[4 * size:] for x in chunks])
    by_place = jnp.zeros((devices_dp,), jnp.int32).at[order].set(jnp.arange(devices_dp, dtype=jnp.int32))
    small = jnp.sum(terms[by_place].astype(F32), 0).reshape(small.shape)

    return (
        output,
        grad_tokens,
        small[buckets + 1],
        jnp.transpose(grad_wqkv, (1, 0, 2)),
        grad_wout,
        small[buckets],
        small[:buckets].T,
        grad_up,
        grad_down,
    )


def solution(mesh):
    placed = (
        P("dp", None),
        P(),
        P(None, None, "mp"),
        P("mp", None),
        P(),
        P(),
        P(None, None, "mp"),
        P(None, "mp", None),
        P("dp"),
        P("dp", None),
    )
    return jax.shard_map(
        on_device,
        mesh=mesh,
        in_specs=placed,
        out_specs=(
            P("dp", None),
            P("dp", None),
            P(),
            P(None, None, "mp"),
            P("mp", None),
            P(),
            P(),
            P(None, None, "mp"),
            P(None, "mp", None),
        ),
        check_vma=False,
    )
```

time: 622 us -> 530 us (0.85)
  starting transfers between devices: 66 us -> 26.3 us
  Pallas kernels: 287 us -> 251 us
  other arithmetic: 61.2 us -> 25.6 us
  waiting for transfers between devices: 123 us -> 150 us
  local copies, waits for them, and re-layouts: 53.5 us -> 34.5 us
  between operations: 9.64 us -> 21.4 us
    pallas_call x8 -> x17, Pallas kernels: 221 us -> 184 us  [the longest x4 138 us: weight_gradients(): pl.pallas_call(partial(weight_kernel, level=level, rows=rows, group=group...]
    ppermute x5, waiting for transfers between devices: 31.8 us -> 64.1 us  [sum_over_x(): lax.ppermute(x, 'mp', [(i, (i + 2 * k) % (2 * n)) for i in range(2 * n)])]
    ppermute x24 -> x8, starting transfers between devices: 34.7 us -> 12.8 us  [to_right(): out = lax.ppermute(x, 'dp', self.right)]
    dynamic_update_slice x16 -> x0, other arithmetic: 20.2 us -> none  [the longest x8 13.6 us: on_device(): lax.dynamic_update_slice_in_dim(grad_wqkv, b.astype(F32), at * b.shape[1]...]
    convert_element_type x12 -> x3, other arithmetic: 17 us -> 0.73 us  [low(): return lax.reduce_precision(x, 8, 7).astype(BF16)]
    ppermute x24 -> x8, starting transfers between devices: 17.4 us -> 4.15 us  [to_left(): out = lax.ppermute(x, 'dp', self.left)]
    ppermute x24 -> x8, waiting for transfers between devices: 39 us -> 27.5 us  [to_left(): out = lax.ppermute(x, 'dp', self.left)]
    slice x11 -> x4, local copies, waits for them, and re-layouts: 10.3 us -> 2.81 us  [the longest x2 2.16 us: advance(): sending = (r[:cut], l[cut:])]
  transfers between devices with their start and end apart: 81 -> 34, of which waited for: 20 -> 14; matrix products, arithmetic and copies ran while one was open for 19% -> 11% of each run, Pallas kernels for 44% -> 48%
where the time goes in v2:
time: 530 us; the launch traced here: 520 us
  Pallas kernels  251 us (47%)
  waiting for transfers between devices  150 us (28%)
  local copies, waits for them, and re-layouts  34.5 us (7%)
  starting transfers between devices  26.3 us (5%)
  other arithmetic  25.6 us (5%)
  between operations  21.4 us (4%)
  matrix products  11 us (2%)
    pallas_call x4, Pallas kernels, weight_gradients(): pl.pallas_call(partial(weight_kernel, level=level, rows=rows, group=group...  138 us
    ppermute x5, waiting for transfers between devices, sum_over_x(): lax.ppermute(x, 'mp', [(i, (i + 2 * k) % (2 * n)) for i in range(2 * n)])  64.1 us
    ppermute x8, waiting for transfers between devices, to_right(): out = lax.ppermute(x, 'dp', self.right)  48.6 us
    ppermute x8, waiting for transfers between devices, to_left(): out = lax.ppermute(x, 'dp', self.left)  27.5 us
    pallas_call x1, Pallas kernels, attend_back(): pl.pallas_call(partial(attend_back_kernel, heads=heads, steps=steps, deps...  23.6 us
    pallas_call x1, Pallas kernels, own_grad(): pl.pallas_call(partial(own_grad_kernel, row_bounds=tuple(row_bounds), dep...  17.5 us
    pallas_call x1, Pallas kernels, attend(): pl.pallas_call(partial(attend_kernel, heads=heads, steps=steps), grid=(st...  15.8 us
    unnamed x60, local copies, waits for them, and re-layouts  15.4 us
  transfers between devices with their start and end apart: 34, of which 14 were waited for; matrix products, arithmetic and copies ran while one was open for 11% of the time, Pallas kernels for 48%

profile of v2, /device:TPU:0, one launch (start us, length us, event | category | flops | bytes accessed | tf_op | source)
XLA Modules:
  0.0 519.8 jit_solution(1155050788998472446)
XLA Ops:
  14.0 15.8 %attend.1 = (bf16[256,2048]{1,0:T(8,128)(2,1)}, bf16[256,2048]{1,0:T(8,128)(2,1)}, bf16[512,2048]{1,0:T(8,128)(2,1)}, bf16[3,512,512]{2,1,0:T(8,128)(2,1)}, f32[...) custom-call(bf16[512,2048]{1,0:T(8,128)(2,1)} %x_ref.1, f32[1,2048]{1,0:T(1,128)} %bitcast.69, ...), custom_call_target="tpu_custom_call" | custom-call | flops 1207959552 | bytes 3145728 | tf_op jit(solution)/shard_map/attend/pallas_call | solution.py:102
  40.5 38.3 %collective-permute-done.1 = bf16[256,2048]{1,0:T(8,128)(2,1)S(1)} collective-permute-done((bf16[256,2048]{1,0:T(8,128)(2,1)}, bf16[256,2048]{1,0:T(8,128)(2,1)S(1)}, u32[]{:S(2)}, u32[]{:S(2)}) %collective-permute-start.1) | collective-permute-done | bytes 1048608 | tf_op jit(solution)/shard_map/ppermute | solution.py:666
  94.1 17.5 %own_grad.1 = (bf16[256,2048]{1,0:T(8,128)(2,1)}, bf16[256,2048]{1,0:T(8,128)(2,1)}, bf16[4,512,512]{2,1,0:T(8,128)(2,1)}) custom-call(bf16[512,2048]{1,0:T(8,128)(2,1)} %copy-done.15, bf16[512,2048]{1,0:T(8,128)(2,1)} %copy-done.5, s32[512,128]{1,0:T(8,128)} %broadcast_in_dim.61.bucket_ref, f32[512,128]{1,0:T(8,128)} %broadcast_in_dim.64.gate_ref, ...), custom_call_target="tpu_custom_call" | custom-call | flops 2315255808 | bytes 5767168 | tf_op jit(solution)/shard_map/own_grad/pallas_call | solution.py:248
  115.4 3.6 add_rows.5.rest_0_
  121.8 10.5 %own_forward.1 = (bf16[512,2048]{1,0:T(8,128)(2,1)}, f32[512,128]{1,0:T(8,128)}) custom-call(bf16[4,512,512]{2,1,0:T(8,128)(2,1)} %get-tuple-element.48.act_ref, bf16[512,2048]{1,0:T(8,128)(2,1)} %copy-done.5, bf16[512,512]{1,0:T(8,128)(2,1)} %fusion.24.unsort_ref, bf16[4,512,2048]{2,1,0:T(8,128)(2,1)} %down_ref.11, bf16[256,2048]{1,0:T(8,128)(2,1)} %add_rows.5.rest_0_), custom_call_target="tpu_custom_call" | custom-call | flops 771751936 | bytes 3670016 | tf_op jit(solution)/shard_map/own_forward/pallas_call | solution.py:288
  135.2 11.0 %collective-permute-done.10 = f32[256]{0:T(256)S(1)} collective-permute-done((f32[256]{0:T(256)S(1)}, f32[256]{0:T(256)S(1)}, u32[]{:S(2)}, u32[]{:S(2)}) %collective-permute-start.10) | collective-permute-done | bytes 1056 | tf_op jit(solution)/shard_map/ppermute | solution.py:666
  156.0 23.6 %attend_back.1 = (bf16[4,2048,512]{2,1,0:T(8,128)(2,1)}, bf16[512,2048]{1,0:T(8,128)(2,1)}) custom-call(bf16[512,2048]{1,0:T(8,128)(2,1)} %pad_maximum_fusion.1.ga_ref, bf16[512,2048]{1,0:T(8,128)(2,1)} %get-tuple-element.53.normed_ref, bf16[3,512,512]{2,1,0:T(8,128)(2,1)} %get-tuple-element.54.qkv_ref, f32[4,512,128]{2,1,0:T(8,128)} %get-tuple-element.55.lse_ref, ...), custom_call_target="tpu_custom_call" | custom-call | flops 2483027968 | bytes 6291456 | tf_op jit(solution)/shard_map/attend_back/pallas_call | solution.py:195
  197.4 15.6 %collective-permute-done.16.left_ref = bf16[4,128,512]{2,1,0:T(8,128)(2,1)} collective-permute-done((bf16[4,128,512]{2,1,0:T(8,128)(2,1)}, bf16[4,128,512]{2,1,0:T(8,128)(2,1)}, u32[]{:S(2)}, u32[]{:S(2)}) %collective-permute-start.16) | collective-permute-done | bytes 524320 | tf_op jit(solution)/shard_map/ppermute | solution.py:606
  213.0 4.6 join.3
  219.7 3.8 add_rows.7
  226.1 3.7 add_rows.6
  231.6 34.0 %collective-permute-done.17.right_ref = bf16[4,256,512]{2,1,0:T(8,128)(2,1)} collective-permute-done((bf16[4,256,512]{2,1,0:T(8,128)(2,1)}, bf16[4,256,512]{2,1,0:T(8,128)(2,1)}, u32[]{:S(2)}, u32[]{:S(2)}) %collective-permute-start.17) | collective-permute-done | bytes 1048608 | tf_op jit(solution)/shard_map/ppermute | solution.py:601
  265.6 8.4 %collective-permute-done.18.left_ref = bf16[4,256,512]{2,1,0:T(8,128)(2,1)} collective-permute-done((bf16[4,256,512]{2,1,0:T(8,128)(2,1)}, bf16[4,256,512]{2,1,0:T(8,128)(2,1)}, u32[]{:S(2)}, u32[]{:S(2)}) %collective-permute-start.18) | collective-permute-done | bytes 1048608 | tf_op jit(solution)/shard_map/ppermute | solution.py:606
  274.1 4.8 join.4
  282.0 14.8 %collective-permute-done.6 = bf16[256,2048]{1,0:T(8,128)(2,1)} collective-permute-done((bf16[256,2048]{1,0:T(8,128)(2,1)}, bf16[256,2048]{1,0:T(8,128)(2,1)}, u32[]{:S(2)}, u32[]{:S(2)}) %collective-permute-start.6) | collective-permute-done | bytes 1048608 | tf_op jit(solution)/shard_map/ppermute | solution.py:666
  296.8 3.9 fusion.6
  301.3 14.6 %collective-permute-done.19.right_ref = bf16[4,256,512]{2,1,0:T(8,128)(2,1)} collective-permute-done((bf16[4,256,512]{2,1,0:T(8,128)(2,1)}, bf16[4,256,512]{2,1,0:T(8,128)(2,1)}, u32[]{:S(2)}, u32[]{:S(2)}) %collective-permute-start.19) | collective-permute-done | bytes 1048608 | tf_op jit(solution)/shard_map/ppermute | solution.py:601
  317.8 4.8 join.5
  325.9 44.0 %weight_gradients_0.1 = (f32[4,2048,512]{2,1,0:T(8,128)}, f32[4,512,2048]{2,1,0:T(8,128)}) custom-call(bf16[8,4,528,512]{3,2,1,0:T(8,128)(2,1)} %bitcast.58, bf16[8,4,512,512]{3,2,1,0:T(8,128)(2,1)} %bitcast.62, bf16[4,2048,512]{2,1,0:T(8,128)(2,1)} %up_ref.9, bf16[4,512,2048]{2,1,0:T(8,128)(2,1)} %down_ref.11, ...), custom_call_target="tpu_custom_call" | custom-call | flops 8589934592 | bytes 12582912 | tf_op jit(solution)/shard_map/weight_gradients_0/pallas_call | solution.py:409
  371.3 3.9 join_own.1.refs_2_.refs_3_.refs_0_
  378.9 42.9 %weight_gradients_1.1 = (f32[4,2048,512]{2,1,0:T(8,128)}, f32[4,512,2048]{2,1,0:T(8,128)}) custom-call(bf16[8,4,528,512]{3,2,1,0:T(8,128)(2,1)} %bitcast.59, bf16[8,4,512,512]{3,2,1,0:T(8,128)(2,1)} %bitcast.63, bf16[4,2048,512]{2,1,0:T(8,128)(2,1)} %up_ref.9, bf16[4,512,2048]{2,1,0:T(8,128)(2,1)} %down_ref.11, ...), custom_call_target="tpu_custom_call", output_to_operand_aliasing={{0}: (4, {}), {1}: (5, {})} | custom-call | flops 8053063680 | bytes 12582912 | tf_op jit(solution)/shard_map/weight_gradients_1/pallas_call | solution.py:409
  429.7 32.1 %weight_gradients_2.1 = (f32[4,2048,512]{2,1,0:T(8,128)}, f32[4,512,2048]{2,1,0:T(8,128)}) custom-call(bf16[8,4,528,512]{3,2,1,0:T(8,128)(2,1)} %bitcast.60, bf16[8,4,512,512]{3,2,1,0:T(8,128)(2,1)} %bitcast.64, bf16[4,2048,512]{2,1,0:T(8,128)(2,1)} %up_ref.9, bf16[4,512,2048]{2,1,0:T(8,128)(2,1)} %down_ref.11, ...), custom_call_target="tpu_custom_call", output_to_operand_aliasing={{0}: (4, {}), {1}: (5, {})} | custom-call | flops 5368709120 | bytes 12582912 | tf_op jit(solution)/shard_map/weight_gradients_2/pallas_call | solution.py:409
  468.2 19.3 %weight_gradients_3.1 = (f32[4,2048,512]{2,1,0:T(8,128)}, f32[4,512,2048]{2,1,0:T(8,128)}) custom-call(bf16[8,4,528,512]{3,2,1,0:T(8,128)(2,1)} %bitcast.61, bf16[8,4,512,512]{3,2,1,0:T(8,128)(2,1)} %bitcast.65, bf16[4,2048,512]{2,1,0:T(8,128)(2,1)} %up_ref.9, bf16[4,512,2048]{2,1,0:T(8,128)(2,1)} %down_ref.11, ...), custom_call_target="tpu_custom_call", output_to_operand_aliasing={{0}: (4, {}), {1}: (5, {})} | custom-call | flops 2684354560 | bytes 12582912 | tf_op jit(solution)/shard_map/weight_gradients_3/pallas_call | solution.py:409
  495.0 9.8 %unpack_some.1 = (f32[3,2048,512]{2,1,0:T(8,128)}, f32[512,2048]{1,0:T(8,128)}) custom-call(s32[7]{0:T(128)} %stack.129.order_ref, bf16[1056,512]{1,0:T(8,128)(2,1)} %join_own.1.refs_2_.refs_3_.refs_0_, bf16[1056,512]{1,0:T(8,128)(2,1)} %get-tuple-element.68.refs_2_.refs_1_, bf16[1056,512]{1,0:T(8,128)(2,1)} %get-tuple-element.69.refs_3_.refs_2_, ...), custom_call_target="tpu_custom_call" | custom-call | bytes 5505024 | tf_op jit(solution)/shard_map/unpack_some/pallas_call | solution.py:445
  (205 shorter events, 113.1 us)
Async XLA Ops:
  7.2 318.7 %all-gather.7.cloned.1.call-start = ((), (), s32[]{:S(2)}) async-start(), calls=%async_computation.1 | async-start | bytes 17301504 | tf_op jit(solution)/shard_map/all_gather | solution.py:720
  12.0 313.9 %all-gather.5.cloned.1.call-start = ((), (), s32[]{:S(2)}) async-start(), calls=%async_computation | async-start | bytes 17842176 | tf_op jit(solution)/shard_map/all_gather | solution.py:750
  37.4 41.4 %collective-permute-start.1 = (bf16[256,2048]{1,0:T(8,128)(2,1)}, bf16[256,2048]{1,0:T(8,128)(2,1)S(1)}, u32[]{:S(2)}, u32[]{:S(2)}) collective-permute-start(bf16[256,2048]{1,0:T(8,128)(2,1)} %add_rows.4), channel_id=1, source_target_pairs={{0,2},{1,3},{2,0},{3,1},{4,6},{5,7},{6,4},{7,5},{8,10},{9,11},{10,... | collective-permute-start | bytes 3145736 | tf_op jit(solution)/shard_map/ppermute | solution.py:666
  119.1 27.2 %collective-permute-start.8 = (bf16[256,2048]{1,0:T(8,128)(2,1)}, bf16[256,2048]{1,0:T(8,128)(2,1)S(1)}, u32[]{:S(2)}, u32[]{:S(2)}) collective-permute-start(bf16[256,2048]{1,0:T(8,128)(2,1)} %add_rows.5.rest_0_), channel_id=1, source_target_pairs={{0,2},{1,3},{2,0},{3,1},{4,6},{5,7},{6,4},{7,5},{8,10},{9,11},{10,... | collective-permute-start | bytes 3145736 | tf_op jit(solution)/shard_map/ppermute | solution.py:666
  182.3 37.4 %collective-permute-start.12 = (bf16[256,2048]{1,0:T(8,128)(2,1)S(1)}, bf16[256,2048]{1,0:T(8,128)(2,1)}, u32[]{:S(2)}, u32[]{:S(2)}) collective-permute-start(bf16[256,2048]{1,0:T(8,128)(2,1)S(1)} %get-tuple-element.99), channel_id=1, source_target_pairs={{0,1},{1,0},{2,3},{3,2},{4,5},{5,4},{6,7},{7,6},{8,9},{9,8},{10,11... | collective-permute-start | bytes 3145736 | tf_op jit(solution)/shard_map/ppermute | solution.py:659
  186.1 26.9 %collective-permute-start.16 = (bf16[4,128,512]{2,1,0:T(8,128)(2,1)}, bf16[4,128,512]{2,1,0:T(8,128)(2,1)}, u32[]{:S(2)}, u32[]{:S(2)}) collective-permute-start(bf16[4,128,512]{2,1,0:T(8,128)(2,1)} %get-tuple-element.93), channel_id=1, source_target_pairs={{8,0},{16,8},{24,16},{28,24},{20,28},{12,20},{4,12},{0,4},{9,1},{1... | collective-permute-start | bytes 1572872 | tf_op jit(solution)/shard_map/ppermute | solution.py:606
  187.6 25.4 %collective-permute-start.15 = (bf16[4,128,512]{2,1,0:T(8,128)(2,1)}, bf16[4,128,512]{2,1,0:T(8,128)(2,1)}, u32[]{:S(2)}, u32[]{:S(2)}) collective-permute-start(bf16[4,128,512]{2,1,0:T(8,128)(2,1)} %get-tuple-element.94), channel_id=1, source_target_pairs={{0,8},{8,16},{16,24},{24,28},{28,20},{20,12},{12,4},{4,0},{1,9},{9... | collective-permute-start | bytes 1572872 | tf_op jit(solution)/shard_map/ppermute | solution.py:601
  189.6 36.5 %collective-permute-start.5 = (bf16[256,2048]{1,0:T(8,128)(2,1)}, bf16[256,2048]{1,0:T(8,128)(2,1)}, u32[]{:S(2)}, u32[]{:S(2)}) collective-permute-start(bf16[256,2048]{1,0:T(8,128)(2,1)} %get-tuple-element.106), channel_id=1, source_target_pairs={{0,1},{1,0},{2,3},{3,2},{4,5},{5,4},{6,7},{7,6},{8,9},{9,8},{10,11... | collective-permute-start | bytes 3145736 | tf_op jit(solution)/shard_map/ppermute | solution.py:659
  217.6 48.0 %collective-permute-start.17 = (bf16[4,256,512]{2,1,0:T(8,128)(2,1)}, bf16[4,256,512]{2,1,0:T(8,128)(2,1)}, u32[]{:S(2)}, u32[]{:S(2)}) collective-permute-start(bf16[4,256,512]{2,1,0:T(8,128)(2,1)} %get-tuple-element.59), channel_id=1, source_target_pairs={{0,8},{8,16},{16,24},{24,28},{28,20},{20,12},{12,4},{4,0},{1,9},{9... | collective-permute-start | bytes 3145736 | tf_op jit(solution)/shard_map/ppermute | solution.py:601
  219.0 55.0 %collective-permute-start.18 = (bf16[4,256,512]{2,1,0:T(8,128)(2,1)}, bf16[4,256,512]{2,1,0:T(8,128)(2,1)}, u32[]{:S(2)}, u32[]{:S(2)}) collective-permute-start(bf16[4,256,512]{2,1,0:T(8,128)(2,1)} %get-tuple-element.60), channel_id=1, source_target_pairs={{8,0},{16,8},{24,16},{28,24},{20,28},{12,20},{4,12},{0,4},{9,1},{1... | collective-permute-start | bytes 3145736 | tf_op jit(solution)/shard_map/ppermute | solution.py:606
  223.5 57.5 %collective-permute-start.13 = (bf16[256,2048]{1,0:T(8,128)(2,1)}, bf16[256,2048]{1,0:T(8,128)(2,1)S(1)}, u32[]{:S(2)}, u32[]{:S(2)}) collective-permute-start(bf16[256,2048]{1,0:T(8,128)(2,1)} %add_rows.7), channel_id=1, source_target_pairs={{0,2},{1,3},{2,0},{3,1},{4,6},{5,7},{6,4},{7,5},{8,10},{9,11},{10,... | collective-permute-start | bytes 3145736 | tf_op jit(solution)/shard_map/ppermute | solution.py:666
  229.8 67.1 %collective-permute-start.6 = (bf16[256,2048]{1,0:T(8,128)(2,1)}, bf16[256,2048]{1,0:T(8,128)(2,1)}, u32[]{:S(2)}, u32[]{:S(2)}) collective-permute-start(bf16[256,2048]{1,0:T(8,128)(2,1)} %add_rows.6), channel_id=1, source_target_pairs={{0,2},{1,3},{2,0},{3,1},{4,6},{5,7},{6,4},{7,5},{8,10},{9,11},{10,... | collective-permute-start | bytes 3145736 | tf_op jit(solution)/shard_map/ppermute | solution.py:666
  278.9 36.9 %collective-permute-start.19 = (bf16[4,256,512]{2,1,0:T(8,128)(2,1)}, bf16[4,256,512]{2,1,0:T(8,128)(2,1)}, u32[]{:S(2)}, u32[]{:S(2)}) collective-permute-start(bf16[4,256,512]{2,1,0:T(8,128)(2,1)} %get-tuple-element.61), channel_id=1, source_target_pairs={{0,8},{8,16},{16,24},{24,28},{28,20},{20,12},{12,4},{4,0},{1,9},{9... | collective-permute-start | bytes 3145736 | tf_op jit(solution)/shard_map/ppermute | solution.py:601
  280.3 37.5 %collective-permute-start.20 = (bf16[4,256,512]{2,1,0:T(8,128)(2,1)}, bf16[4,256,512]{2,1,0:T(8,128)(2,1)}, u32[]{:S(2)}, u32[]{:S(2)}) collective-permute-start(bf16[4,256,512]{2,1,0:T(8,128)(2,1)} %get-tuple-element.62), channel_id=1, source_target_pairs={{8,0},{16,8},{24,16},{28,24},{20,28},{12,20},{4,12},{0,4},{9,1},{1... | collective-permute-start | bytes 3145736 | tf_op jit(solution)/shard_map/ppermute | solution.py:606
  281.9 43.3 %collective-permute-start.23 = (f32[8,2048]{1,0:T(8,128)S(1)}, f32[8,2048]{1,0:T(8,128)S(1)}, u32[]{:S(2)}, u32[]{:S(2)}) collective-permute-start(f32[8,2048]{1,0:T(8,128)S(1)} %select_maximum_fusion), channel_id=1, source_target_pairs={{0,1},{1,0},{2,3},{3,2},{4,5},{5,4},{6,7},{7,6},{8,9},{9,8},{10,11... | collective-permute-start | bytes 196616 | tf_op jit(solution)/shard_map/ppermute | solution.py:659
  300.8 76.4 %collective-permute-start.14 = (bf16[256,2048]{1,0:T(8,128)(2,1)}, bf16[256,2048]{1,0:T(8,128)(2,1)}, u32[]{:S(2)}, u32[]{:S(2)}) collective-permute-start(bf16[256,2048]{1,0:T(8,128)(2,1)} %get-tuple-element.97), channel_id=1, source_target_pairs={{0,1},{1,0},{2,3},{3,2},{4,5},{5,4},{6,7},{7,6},{8,9},{9,8},{10,11... | collective-permute-start | bytes 3145736 | tf_op jit(solution)/shard_map/ppermute | solution.py:659
  300.8 124.4 %collective-permute-start.7 = (bf16[256,2048]{1,0:T(8,128)(2,1)S(1)}, bf16[256,2048]{1,0:T(8,128)(2,1)}, u32[]{:S(2)}, u32[]{:S(2)}) collective-permute-start(bf16[256,2048]{1,0:T(8,128)(2,1)S(1)} %get-tuple-element.98), channel_id=1, source_target_pairs={{0,1},{1,0},{2,3},{3,2},{4,5},{5,4},{6,7},{7,6},{8,9},{9,8},{10,11... | collective-permute-start | bytes 3145736 | tf_op jit(solution)/shard_map/ppermute | solution.py:659
  322.7 47.3 %collective-permute-start.21 = (bf16[4,256,512]{2,1,0:T(8,128)(2,1)}, bf16[4,256,512]{2,1,0:T(8,128)(2,1)S(1)}, u32[]{:S(2)}, u32[]{:S(2)}) collective-permute-start(bf16[4,256,512]{2,1,0:T(8,128)(2,1)} %get-tuple-element.63.refs_0_), channel_id=1, source_target_pairs={{0,8},{8,16},{16,24},{24,28},{28,20},{20,12},{12,4},{4,0},{1,9},{9... | collective-permute-start | bytes 3145736 | tf_op jit(solution)/shard_map/ppermute | solution.py:601
  325.2 44.8 %collective-permute-start.22 = (bf16[4,256,512]{2,1,0:T(8,128)(2,1)}, bf16[4,256,512]{2,1,0:T(8,128)(2,1)S(1)}, u32[]{:S(2)}, u32[]{:S(2)}) collective-permute-start(bf16[4,256,512]{2,1,0:T(8,128)(2,1)} %get-tuple-element.64.refs_1_), channel_id=1, source_target_pairs={{8,0},{16,8},{24,16},{28,24},{20,28},{12,20},{4,12},{0,4},{9,1},{1... | collective-permute-start | bytes 3145736 | tf_op jit(solution)/shard_map/ppermute | solution.py:606
  375.2 46.6 %collective-permute-start.25 = (bf16[1056,512]{1,0:T(8,128)(2,1)}, bf16[1056,512]{1,0:T(8,128)(2,1)S(1)}, u32[]{:S(2)}, u32[]{:S(2)}) collective-permute-start(bf16[1056,512]{1,0:T(8,128)(2,1)} %join_own.1.refs_2_.refs_3_.refs_0_), channel_id=1, source_target_pairs={{8,0},{16,8},{24,16},{28,24},{20,28},{12,20},{4,12},{0,4},{9,1},{1... | collective-permute-start | bytes 3244040 | tf_op jit(solution)/shard_map/ppermute | solution.py:606
  376.1 45.7 %collective-permute-start.24 = (bf16[1056,512]{1,0:T(8,128)(2,1)}, bf16[1056,512]{1,0:T(8,128)(2,1)S(1)}, u32[]{:S(2)}, u32[]{:S(2)}) collective-permute-start(bf16[1056,512]{1,0:T(8,128)(2,1)} %join_own.1.refs_2_.refs_3_.refs_0_), channel_id=1, source_target_pairs={{0,8},{8,16},{16,24},{24,28},{28,20},{20,12},{12,4},{4,0},{1,9},{9... | collective-permute-start | bytes 3244040 | tf_op jit(solution)/shard_map/ppermute | solution.py:601
  423.2 38.6 %collective-permute-start.26 = (bf16[1056,512]{1,0:T(8,128)(2,1)}, bf16[1056,512]{1,0:T(8,128)(2,1)S(1)}, u32[]{:S(2)}, u32[]{:S(2)}) collective-permute-start(bf16[1056,512]{1,0:T(8,128)(2,1)} %get-tuple-element.68.refs_2_.refs_1_), channel_id=1, source_target_pairs={{0,8},{8,16},{16,24},{24,28},{28,20},{20,12},{12,4},{4,0},{1,9},{9... | collective-permute-start | bytes 3244040 | tf_op jit(solution)/shard_map/ppermute | solution.py:601
  425.2 36.6 %collective-permute-start.27 = (bf16[1056,512]{1,0:T(8,128)(2,1)}, bf16[1056,512]{1,0:T(8,128)(2,1)S(1)}, u32[]{:S(2)}, u32[]{:S(2)}) collective-permute-start(bf16[1056,512]{1,0:T(8,128)(2,1)} %get-tuple-element.69.refs_3_.refs_2_), channel_id=1, source_target_pairs={{8,0},{16,8},{24,16},{28,24},{20,28},{12,20},{4,12},{0,4},{9,1},{1... | collective-permute-start | bytes 3244040 | tf_op jit(solution)/shard_map/ppermute | solution.py:606
  463.1 24.4 %collective-permute-start.28 = (bf16[1056,512]{1,0:T(8,128)(2,1)}, bf16[1056,512]{1,0:T(8,128)(2,1)S(1)}, u32[]{:S(2)}, u32[]{:S(2)}) collective-permute-start(bf16[1056,512]{1,0:T(8,128)(2,1)} %get-tuple-element.72.refs_2_.refs_3_), channel_id=1, source_target_pairs={{0,8},{8,16},{16,24},{24,28},{28,20},{20,12},{12,4},{4,0},{1,9},{9... | collective-permute-start | bytes 3244040 | tf_op jit(solution)/shard_map/ppermute | solution.py:601
  (35 other events, 449.6 us)
Sparse Core Ops, SparseCore 0:
  12.1 133.3 all-gather.6
  148.5 159.3 all-gather.4

commit v3 on v2

--- a/solution.py
+++ b/solution.py
@@ -312,12 +312,13 @@
     return gates, buckets
 
 
-def weight_kernel(s_ref, c_ref, up_ref, down_ref, *refs, level, rows, group, carried, deps):
+def weight_kernel(s_ref, aux_ref, c_ref, up_ref, down_ref, *refs, level, start, rows, group, fresh, carried, deps):
     gup_ref, gdown_ref, up_buf, down_buf, s_buf, aux_buf, c_buf, gup, gdown, sems = refs[carried + deps:]
     b = pl.program_id(0)
     steps = pl.num_programs(0)
     slices, piece = s_ref.shape[1], s_ref.shape[3]
     length = c_ref.shape[2]
+    aux_at = aux_ref.shape[2] - AUX
     span = pl.ds(0, rows)
 
     def tokens_of(step, slot):
@@ -328,7 +329,7 @@
             for m in range(slices):
                 out.append((s_ref.at[block, m, span], s_buf.at[slot, to, pl.ds(m * piece, piece)]))
             for m in range(length // piece):
-                out.append((s_ref.at[block, m, pl.ds(length, AUX)], aux_buf.at[slot, j, pl.ds(0, AUX), pl.ds(m * piece, piece)]))
+                out.append((aux_ref.at[block, m, pl.ds(aux_at, AUX)], aux_buf.at[slot, j, pl.ds(0, AUX), pl.ds(m * piece, piece)]))
         return [pltpu.make_async_copy(x, y, sems.at[slot, i]) for i, (x, y) in enumerate(out)]
 
     def cots_of(step, slot):
@@ -337,18 +338,21 @@
             block = step * group + j
             to = pl.ds(j * rows, rows)
             for m in range(slices):
-                out.append((c_ref.at[block, m, span], c_buf.at[slot, to, pl.ds(m * piece, piece)]))
+                out.append((c_ref.at[block, m, pl.ds(start, rows)], c_buf.at[slot, to, pl.ds(m * piece, piece)]))
         return [pltpu.make_async_copy(x, y, sems.at[2 + slot, i]) for i, (x, y) in enumerate(out)]
 
     up_copy = pltpu.make_async_copy(up_ref.at[level], up_buf, sems.at[4, 0])
     down_copy = pltpu.make_async_copy(down_ref.at[level], down_buf, sems.at[4, 1])
     ends = [pltpu.make_async_copy(gup, gup_ref.at[level], sems.at[4, 2]),
             pltpu.make_async_copy(gdown, gdown_ref.at[level], sems.at[4, 3])]
+    begins = [] if fresh else [
+        pltpu.make_async_copy(refs[0].at[level], gup, sems.at[5, 0]),
+        pltpu.make_async_copy(refs[1].at[level], gdown, sems.at[5, 1])]
     slot = lax.rem(b, 2)
 
     @pl.when(b == 0)
     def _():
-        for c in [up_copy] + tokens_of(0, 0) + [down_copy] + cots_of(0, 0):
+        for c in [up_copy] + tokens_of(0, 0) + [down_copy] + cots_of(0, 0) + begins:
             c.start()
 
     @pl.when(b + 1 < steps)
@@ -363,8 +367,8 @@
     for c in tokens_of(b, slot):
         c.wait()
     columns = [gates_and_buckets(aux_buf[slot, j]) for j in range(group)]
-    gate = jnp.concatenate([g[:rows, :1] for g, _ in columns], 0)
-    keep = jnp.concatenate([k[:rows, :1] for _, k in columns], 0) >= level
+    gate = jnp.concatenate([g[start:start + rows, :1] for g, _ in columns], 0)
+    keep = jnp.concatenate([k[start:start + rows, :1] for _, k in columns], 0) >= level
     pre = dot(s_buf[slot], up_buf[...])
     active = jnp.where(keep, jnp.maximum(pre, 0.0), 0.0)
     act = (active * active * gate).astype(BF16)
@@ -380,8 +384,14 @@
 
     @pl.when(b == 0)
     def _():
-        gup[...] = dot(s_buf[slot], gpre, TN)
-        gdown[...] = dot(act, c_buf[slot], TN)
+        if fresh:
+            gup[...] = dot(s_buf[slot], gpre, TN)
+            gdown[...] = dot(act, c_buf[slot], TN)
+        else:
+            for c in begins:
+                c.wait()
+            gup[...] += dot(s_buf[slot], gpre, TN)
+            gdown[...] += dot(act, c_buf[slot], TN)
 
     @pl.when(jnp.logical_and(b > 0, b < steps - 1))
     def _():
@@ -398,7 +408,7 @@
             c.wait()
 
 
-def weight_gradients(level, rows, sents, cots, w_up, w_down, carried, deps=()):
+def weight_gradients(level, start, rows, sents, aux, cots, w_up, w_down, carried, fresh, deps=()):
     levels, model, hidden = w_up.shape
     blocks, slices, length, piece = cots.shape
     group = max(1, min(4, 1024 // rows))
@@ -407,23 +417,24 @@
     copies = group * (slices + length // piece)
     anywhere = pl.BlockSpec(memory_space=pl.ANY)
     return pl.pallas_call(
-        partial(weight_kernel, level=level, rows=rows, group=group, carried=len(carried), deps=len(deps)),
+        partial(weight_kernel, level=level, start=start, rows=rows, group=group, fresh=fresh, carried=len(carried),
+                deps=len(deps)),
         grid=(blocks // group,),
-        in_specs=[anywhere] * (4 + len(carried) + len(deps)),
+        in_specs=[anywhere] * (5 + len(carried) + len(deps)),
         out_specs=[anywhere] * 2,
         out_shape=[jax.ShapeDtypeStruct((levels, model, hidden), F32), jax.ShapeDtypeStruct((levels, hidden, model), F32)],
-        input_output_aliases={4: 0, 5: 1} if carried else {},
+        input_output_aliases={5: 0, 6: 1} if carried else {},
         scratch_shapes=[
             pltpu.VMEM((model, hidden), BF16), pltpu.VMEM((hidden, model), BF16),
             pltpu.VMEM((2, group * rows, model), BF16), pltpu.VMEM((2, group, AUX, length), BF16),
             pltpu.VMEM((2, group * rows, model), BF16),
             pltpu.VMEM((model, hidden), F32), pltpu.VMEM((hidden, model), F32),
-            pltpu.SemaphoreType.DMA((5, max(4, copies))),
+            pltpu.SemaphoreType.DMA((6, max(4, copies))),
         ],
         compiler_params=params(),
         cost_estimate=cost(8 * blocks * rows * model * hidden, 4 * blocks * length * model + 16 * model * hidden),
-        name=f"weight_gradients_{level}",
-    )(sents, cots, w_up, w_down, *carried, *deps)
+        name=f"weight_gradients_{level}_from_{start}",
+    )(sents, aux, cots, w_up, w_down, *carried, *deps)
 
 
 def unpack_kernel(order_ref, *refs, count, carried):
@@ -744,26 +755,26 @@
     gate_2 = low(gate_sorted - gate_1.astype(F32))
     gate_3 = low(gate_sorted - gate_1.astype(F32) - gate_2.astype(F32))
     aux = jnp.stack([gate_1, gate_2, gate_3, bucket_sorted.astype(BF16)] + [jnp.zeros_like(gate_1)] * (AUX - 4))
+    sent_mine = lax.dynamic_slice_in_dim(sent_sorted, me * piece, piece, axis=1)
     sent_piece = jnp.concatenate([
-        lax.dynamic_slice_in_dim(sent_sorted, me * piece, piece, axis=1),
-        lax.dynamic_slice_in_dim(aux, (me % (length // piece)) * piece, piece, axis=1)], 0)
-    sents = lax.all_gather(sent_piece, ("dp", "mp"), axis=0).reshape(devices_dp, slices, length + AUX, piece)
+        sent_mine[:half], lax.dynamic_slice_in_dim(aux, (me % (length // piece)) * piece, piece, axis=1)], 0)
+    sents = lax.all_gather(sent_piece, ("dp", "mp"), axis=0).reshape(devices_dp, slices, half + AUX, piece)
 
     wide = lambda x: jnp.broadcast_to(x[:, None], (length, 128))
     gsent_mine, gsent_other, act = own_grad(
         sent_sorted, cot_sorted, wide(bucket_sorted), wide(gate_sorted), unsort_low, w_up, w_down, row_bounds,
         (sent_piece,))
     gsent_rows = add_rows([gsent_mine, core_swap(gsent_other)])
+    sent_more, = after([sent_mine[half:]], (gsent_rows,))
+    sents_more = lax.all_gather(sent_more, ("dp", "mp"), axis=0).reshape(devices_dp, slices, half, piece)
     grad_sent = sum_over_x(gsent_rows).astype(BF16).astype(F32)
     ffn_part, ggate_part = own_forward(
-        act, cot_sorted, sort_rows.astype(BF16).T, w_down, row_bounds, (gsent_rows,))
-    ffn_rows = sum_over_x(add_rows([own_rows(ffn_part), core_swap(other_rows(ffn_part))])).astype(BF16).astype(F32)
+        act, cot_sorted, sort_rows.astype(BF16).T, w_down, row_bounds, (gsent_rows, sent_more))
     ggate_part = jnp.sum(jnp.where(sort_rows, ggate_part[:, :1], 0.0), 0)
     grad_gate = ggate_part + core_swap(ggate_part)
     grad_gate = sum_over_x(own_rows(grad_gate))
 
     grad_output = own_rows(cotangent).astype(F32)
-    output_half = (resid + gate[:, None] * ffn_rows).astype(BF16)
     grad_prob = buckets * grad_gate[:, None] * onehot
     grad_logits = prob * (grad_prob - jnp.sum(grad_prob * prob, -1, keepdims=True))
     grad_router = jnp.dot(normed_second.T, grad_logits, precision=HIGHEST)
@@ -776,21 +787,6 @@
 
     grads, first_part = attend_back(
         grad_attn, normed_low, qkv, lse, mixed, w_out, w3, cos, sin)
-
-    grad_first = sum_over_x(add_rows([own_rows(first_part), core_swap(other_rows(first_part))])).astype(BF16).astype(F32)
-    source = own_rows(tokens).astype(F32)
-    inv_first = lax.rsqrt(jnp.mean(source * source, -1, keepdims=True) + EPSILON)
-    xhat_first = source * inv_first
-    grad_gain_first = jnp.sum(grad_first * xhat_first, 0)
-    scaled_first = grad_first * gain_first
-    grad_source = inv_first * (scaled_first - xhat_first * jnp.mean(scaled_first * xhat_first, -1, keepdims=True))
-    tokens_half = (grad_source + grad_resid).astype(BF16)
-    output = joined(output_half, core_swap(output_half))
-    grad_tokens = joined(tokens_half, core_swap(tokens_half))
-    small = jnp.concatenate([grad_router.T, grad_gain_second[None], grad_gain_first[None]], 0)
-    small = jnp.pad(small, ((0, -small.shape[0] % 8), (0, 0)))
-    local = w3.shape[2]
-    extra = low(small + core_swap(small)).reshape(-1, local)
 
     carried = ()
     arrived, sending = ring.reduce_start(grads)
@@ -819,11 +815,34 @@
         return (r, l), sending
 
     steps = 2 * far - 1
-    while step < far - 1:
+    while step < min(far - 1, 1):
         arrived, sending = advance(step, arrived, ())
         step += 1
-    for level in range(buckets):
-        carried = weight_gradients(level, row_bounds[level], sents, cots, w_up, w_down, tuple(carried), sending)
+    ring_busy = tuple(sending)
+
+    ffn_rows = sum_over_x(add_rows([own_rows(ffn_part), core_swap(other_rows(ffn_part))], ring_busy)).astype(BF16).astype(F32)
+    output_half = (resid + gate[:, None] * ffn_rows).astype(BF16)
+
+    grad_first = sum_over_x(add_rows([own_rows(first_part), core_swap(other_rows(first_part))], ring_busy)).astype(BF16).astype(F32)
+    source = own_rows(tokens).astype(F32)
+    inv_first = lax.rsqrt(jnp.mean(source * source, -1, keepdims=True) + EPSILON)
+    xhat_first = source * inv_first
+    grad_gain_first = jnp.sum(grad_first * xhat_first, 0)
+    scaled_first = grad_first * gain_first
+    grad_source = inv_first * (scaled_first - xhat_first * jnp.mean(scaled_first * xhat_first, -1, keepdims=True))
+    tokens_half = (grad_source + grad_resid).astype(BF16)
+    output = joined(output_half, core_swap(output_half))
+    grad_tokens = joined(tokens_half, core_swap(tokens_half))
+    small = jnp.concatenate([grad_router.T, grad_gain_second[None], grad_gain_first[None]], 0)
+    small = jnp.pad(small, ((0, -small.shape[0] % 8), (0, 0)))
+    local = w3.shape[2]
+    extra = low(small + core_swap(small)).reshape(-1, local)
+
+    calls = [(level, 0, min(rows, half), sents, True) for level, rows in enumerate(row_bounds)]
+    calls += [(level, half, rows - half, sents_more, False) for level, rows in enumerate(row_bounds) if rows > half]
+    for level, start, rows, tokens_all, fresh in calls:
+        carried = weight_gradients(
+            level, start, rows, tokens_all, sents, cots, w_up, w_down, tuple(carried), fresh, sending)
         if step < steps:
             arrived, sending = advance(step, arrived, (carried[0],))
             step += 1

time: 530 us -> 577 us (1.089)
  Pallas kernels: 251 us -> 274 us
  waiting for transfers between devices: 150 us -> 172 us
    all_gather x1, waiting for transfers between devices: 0.01 us -> 71.6 us  [on_device(): lax.all_gather(cot_piece, ('dp', 'mp'), axis=0)]
    ppermute x8, waiting for transfers between devices: 48.6 us -> 6.35 us  [to_right(): out = lax.ppermute(x, 'dp', self.right)]
    pallas_call x4 -> x7, Pallas kernels: 138 us -> 160 us  [weight_gradients(): pl.pallas_call(partial(weight_kernel, level=level, start=start, rows=rows...]
    ppermute x8, starting transfers between devices: 12.8 us -> 6.61 us  [to_right(): out = lax.ppermute(x, 'dp', self.right)]
    unnamed x60 -> x70, local copies, waits for them, and re-layouts: 15.4 us -> 16 us
  transfers between devices with their start and end apart: 34 -> 35, of which waited for: 14 -> 14; matrix products, arithmetic and copies ran while one was open for 11% -> 9% of each run, Pallas kernels for 48% -> 44%
where the time goes in v3:
time: 577 us; the launch traced here: 567 us
  Pallas kernels  274 us (47%)
  waiting for transfers between devices  172 us (30%)
  local copies, waits for them, and re-layouts  36 us (6%)
  other arithmetic  27.9 us (5%)
  starting transfers between devices  25.8 us (4%)
  between operations  21.1 us (4%)
  matrix products  11 us (2%)
    pallas_call x7, Pallas kernels, weight_gradients(): pl.pallas_call(partial(weight_kernel, level=level, start=start, rows=rows...  160 us
    all_gather x1, waiting for transfers between devices, on_device(): lax.all_gather(cot_piece, ('dp', 'mp'), axis=0)  71.6 us
    ppermute x5, waiting for transfers between devices, sum_over_x(): lax.ppermute(x, 'mp', [(i, (i + 2 * k) % (2 * n)) for i in range(2 * n)])  64.3 us
    pallas_call x1, Pallas kernels, attend_back(): pl.pallas_call(partial(attend_back_kernel, heads=heads, steps=steps, deps...  23.6 us
    ppermute x8, waiting for transfers between devices, to_left(): out = lax.ppermute(x, 'dp', self.left)  22.2 us
    pallas_call x1, Pallas kernels, own_grad(): pl.pallas_call(partial(own_grad_kernel, row_bounds=tuple(row_bounds), dep...  17.3 us
    unnamed x70, local copies, waits for them, and re-layouts  16 us
    pallas_call x1, Pallas kernels, attend(): pl.pallas_call(partial(attend_kernel, heads=heads, steps=steps), grid=(st...  15.7 us
  transfers between devices with their start and end apart: 35, of which 14 were waited for; matrix products, arithmetic and copies ran while one was open for 9% of the time, Pallas kernels for 44%

profile of v3, /device:TPU:0, one launch (start us, length us, event | category | flops | bytes accessed | tf_op | source)
XLA Modules:
  0.0 567.5 jit_solution(4759231440000959788)
XLA Ops:
  9.2 15.7 %attend.1 = (bf16[256,2048]{1,0:T(8,128)(2,1)}, bf16[256,2048]{1,0:T(8,128)(2,1)}, bf16[512,2048]{1,0:T(8,128)(2,1)}, bf16[3,512,512]{2,1,0:T(8,128)(2,1)}, f32[...) custom-call(bf16[512,2048]{1,0:T(8,128)(2,1)} %x_ref.1, f32[1,2048]{1,0:T(1,128)} %bitcast.83, ...), custom_call_target="tpu_custom_call" | custom-call | flops 1207959552 | bytes 3145728 | tf_op jit(solution)/shard_map/attend/pallas_call | solution.py:102
  36.9 23.7 %collective-permute-done.1 = bf16[256,2048]{1,0:T(8,128)(2,1)S(1)} collective-permute-done((bf16[256,2048]{1,0:T(8,128)(2,1)}, bf16[256,2048]{1,0:T(8,128)(2,1)S(1)}, u32[]{:S(2)}, u32[]{:S(2)}) %collective-permute-start.1) | collective-permute-done | bytes 1048608 | tf_op jit(solution)/shard_map/ppermute | solution.py:677
  76.6 17.3 %own_grad.1 = (bf16[256,2048]{1,0:T(8,128)(2,1)}, bf16[256,2048]{1,0:T(8,128)(2,1)}, bf16[4,512,512]{2,1,0:T(8,128)(2,1)}) custom-call(bf16[512,2048]{1,0:T(8,128)(2,1)} %copy-done.17, bf16[512,2048]{1,0:T(8,128)(2,1)} %copy-done.7, s32[512,128]{1,0:T(8,128)} %broadcast_in_dim.61.bucket_ref, f32[512,128]{1,0:T(8,128)} %broadcast_in_dim.64.gate_ref, ...), custom_call_target="tpu_custom_call" | custom-call | flops 2315255808 | bytes 5767168 | tf_op jit(solution)/shard_map/own_grad/pallas_call | solution.py:248
  104.2 10.3 %own_forward.1 = (bf16[512,2048]{1,0:T(8,128)(2,1)}, f32[512,128]{1,0:T(8,128)}) custom-call(bf16[4,512,512]{2,1,0:T(8,128)(2,1)} %get-tuple-element.54.act_ref, bf16[512,2048]{1,0:T(8,128)(2,1)} %copy-done.7, bf16[512,512]{1,0:T(8,128)(2,1)} %fusion.24.unsort_ref, bf16[4,512,2048]{2,1,0:T(8,128)(2,1)} %down_ref.17, ...), custom_call_target="tpu_custom_call" | custom-call | flops 771751936 | bytes 3670016 | tf_op jit(solution)/shard_map/own_forward/pallas_call | solution.py:288
  117.5 19.3 %collective-permute-done.8 = f32[256]{0:T(256)S(1)} collective-permute-done((f32[256]{0:T(256)S(1)}, f32[256]{0:T(256)S(1)}, u32[]{:S(2)}, u32[]{:S(2)}) %collective-permute-start.8) | collective-permute-done | bytes 1056 | tf_op jit(solution)/shard_map/ppermute | solution.py:677
  146.5 23.6 %attend_back.1 = (bf16[4,2048,512]{2,1,0:T(8,128)(2,1)}, bf16[512,2048]{1,0:T(8,128)(2,1)}) custom-call(bf16[512,2048]{1,0:T(8,128)(2,1)} %pad_maximum_fusion.ga_ref, bf16[512,2048]{1,0:T(8,128)(2,1)} %get-tuple-element.59.normed_ref, bf16[3,512,512]{2,1,0:T(8,128)(2,1)} %get-tuple-element.60.qkv_ref, f32[4,512,128]{2,1,0:T(8,128)} %get-tuple-element.61.lse_ref, ...), custom_call_target="tpu_custom_call" | custom-call | flops 2483027968 | bytes 6291456 | tf_op jit(solution)/shard_map/attend_back/pallas_call | solution.py:195
  187.3 12.0 %collective-permute-done.11.left_ref = bf16[4,128,512]{2,1,0:T(8,128)(2,1)} collective-permute-done((bf16[4,128,512]{2,1,0:T(8,128)(2,1)}, bf16[4,128,512]{2,1,0:T(8,128)(2,1)}, u32[]{:S(2)}, u32[]{:S(2)}) %collective-permute-start.11) | collective-permute-done | bytes 524320 | tf_op jit(solution)/shard_map/ppermute | solution.py:617
  199.3 4.6 join.3
  220.0 21.2 %collective-permute-done.15 = bf16[256,2048]{1,0:T(8,128)(2,1)} collective-permute-done((bf16[256,2048]{1,0:T(8,128)(2,1)}, bf16[256,2048]{1,0:T(8,128)(2,1)}, u32[]{:S(2)}, u32[]{:S(2)}) %collective-permute-start.15) | collective-permute-done | bytes 1048608 | tf_op jit(solution)/shard_map/ppermute | solution.py:677
  243.4 71.6 %all-gather.9.cloned.1.call-done = bf16[16384,512]{1,0:T(8,128)(2,1)} async-done(((bf16[512,512]{1,0:T(8,128)(2,1)}), bf16[16384,512]{1,0:T(8,128)(2,1)}) %all-gather.9.cloned.1.call-update) | async-done | bytes 16777232 | tf_op jit(solution)/shard_map/all_gather | solution.py:731
  314.9 25.8 %weight_gradients_0_from_0.1 = (f32[4,2048,512]{2,1,0:T(8,128)}, f32[4,512,2048]{2,1,0:T(8,128)}) custom-call(bf16[8,4,272,512]{3,2,1,0:T(8,128)(2,1)} %bitcast.59, bf16[8,4,272,512]{3,2,1,0:T(8,128)(2,1)} %bitcast.60, bf16[8,4,512,512]{3,2,1,0:T(8,128)(2,1)} %bitcast.70, bf16[4,2048,512]{2,1,0:T(8,128)(2,1)} %up_ref.15, bf16[4,512,2048]{2,1,0:T(8,128)(2,1)} %down_ref.17, ...), custom_call_target="tpu_custom_call" | custom-call | flops 4294967296 | bytes 12582912 | tf_op jit(solution)/shard_map/weight_gradients_0_from_0/pallas_call | solution.py:419
  340.8 5.6 join.4
  348.4 4.3 fusion.6
  352.7 25.5 %weight_gradients_1_from_0.1 = (f32[4,2048,512]{2,1,0:T(8,128)}, f32[4,512,2048]{2,1,0:T(8,128)}) custom-call(bf16[8,4,272,512]{3,2,1,0:T(8,128)(2,1)} %bitcast.61, bf16[8,4,272,512]{3,2,1,0:T(8,128)(2,1)} %bitcast.62, bf16[8,4,512,512]{3,2,1,0:T(8,128)(2,1)} %bitcast.71, ...), custom_call_target="tpu_custom_call", output_to_operand_aliasing={{0}: (5, {}), {1}: (6, {})} | custom-call | flops 4294967296 | bytes 12582912 | tf_op jit(solution)/shard_map/weight_gradients_1_from_0/pallas_call | solution.py:419
  378.3 5.0 collective-permute-done.19.right_ref
  383.3 9.1 %collective-permute-done.20.left_ref = bf16[4,256,512]{2,1,0:T(8,128)(2,1)} collective-permute-done((bf16[4,256,512]{2,1,0:T(8,128)(2,1)}, bf16[4,256,512]{2,1,0:T(8,128)(2,1)}, u32[]{:S(2)}, u32[]{:S(2)}) %collective-permute-start.20) | collective-permute-done | bytes 1048608 | tf_op jit(solution)/shard_map/ppermute | solution.py:617
  392.4 5.0 join.5
  401.5 26.0 %weight_gradients_2_from_0.1 = (f32[4,2048,512]{2,1,0:T(8,128)}, f32[4,512,2048]{2,1,0:T(8,128)}) custom-call(bf16[8,4,272,512]{3,2,1,0:T(8,128)(2,1)} %bitcast.63, bf16[8,4,272,512]{3,2,1,0:T(8,128)(2,1)} %bitcast.64, bf16[8,4,512,512]{3,2,1,0:T(8,128)(2,1)} %bitcast.72, ...), custom_call_target="tpu_custom_call", output_to_operand_aliasing={{0}: (5, {}), {1}: (6, {})} | custom-call | flops 4294967296 | bytes 12582912 | tf_op jit(solution)/shard_map/weight_gradients_2_from_0/pallas_call | solution.py:419
  428.5 3.9 join_own.1.refs_2_.refs_3_.refs_0_
  438.1 19.3 %weight_gradients_3_from_0.1 = (f32[4,2048,512]{2,1,0:T(8,128)}, f32[4,512,2048]{2,1,0:T(8,128)}) custom-call(bf16[8,4,272,512]{3,2,1,0:T(8,128)(2,1)} %bitcast.65, bf16[8,4,272,512]{3,2,1,0:T(8,128)(2,1)} %bitcast.66, bf16[8,4,512,512]{3,2,1,0:T(8,128)(2,1)} %bitcast.73, ...), custom_call_target="tpu_custom_call", output_to_operand_aliasing={{0}: (5, {}), {1}: (6, {})} | custom-call | flops 2684354560 | bytes 12582912 | tf_op jit(solution)/shard_map/weight_gradients_3_from_0/pallas_call | solution.py:419
  466.7 25.9 %weight_gradients_0_from_256.1 = (f32[4,2048,512]{2,1,0:T(8,128)}, f32[4,512,2048]{2,1,0:T(8,128)}) custom-call(bf16[8,4,256,512]{3,2,1,0:T(8,128)(2,1)} %bitcast.77, bf16[8,4,272,512]{3,2,1,0:T(8,128)(2,1)} %bitcast.67, bf16[8,4,512,512]{3,2,1,0:T(8,128)(2,1)} %bitcast.74, ...), custom_call_target="tpu_custom_call", output_to_operand_aliasing={{0}: (5, {}), {1}: (6, {})} | custom-call | flops 4294967296 | bytes 12582912 | tf_op jit(solution)/shard_map/weight_gradients_0_from_256/pallas_call | solution.py:419
  499.0 24.2 %weight_gradients_1_from_256.1 = (f32[4,2048,512]{2,1,0:T(8,128)}, f32[4,512,2048]{2,1,0:T(8,128)}) custom-call(bf16[8,4,256,512]{3,2,1,0:T(8,128)(2,1)} %bitcast.78, bf16[8,4,272,512]{3,2,1,0:T(8,128)(2,1)} %bitcast.68, bf16[8,4,512,512]{3,2,1,0:T(8,128)(2,1)} %bitcast.75, ...), custom_call_target="tpu_custom_call", output_to_operand_aliasing={{0}: (5, {}), {1}: (6, {})} | custom-call | flops 3758096384 | bytes 12582912 | tf_op jit(solution)/shard_map/weight_gradients_1_from_256/pallas_call | solution.py:419
  529.2 9.8 %unpack_some.1 = (f32[3,2048,512]{2,1,0:T(8,128)}, f32[512,2048]{1,0:T(8,128)}) custom-call(s32[7]{0:T(128)} %stack.129.order_ref, bf16[1056,512]{1,0:T(8,128)(2,1)} %join_own.1.refs_2_.refs_3_.refs_0_, bf16[1056,512]{1,0:T(8,128)(2,1)} %get-tuple-element.78.refs_2_.refs_1_, bf16[1056,512]{1,0:T(8,128)(2,1)} %get-tuple-element.79.refs_3_.refs_2_, ...), custom_call_target="tpu_custom_call" | custom-call | bytes 5505024 | tf_op jit(solution)/shard_map/unpack_some/pallas_call | solution.py:456
  539.0 13.7 %weight_gradients_2_from_256.1 = (f32[4,2048,512]{2,1,0:T(8,128)}, f32[4,512,2048]{2,1,0:T(8,128)}) custom-call(bf16[8,4,256,512]{3,2,1,0:T(8,128)(2,1)} %bitcast.79, bf16[8,4,272,512]{3,2,1,0:T(8,128)(2,1)} %bitcast.69, bf16[8,4,512,512]{3,2,1,0:T(8,128)(2,1)} %bitcast.76, ...), custom_call_target="tpu_custom_call", output_to_operand_aliasing={{0}: (5, {}), {1}: (6, {})} | custom-call | flops 1073741824 | bytes 12582912 | tf_op jit(solution)/shard_map/weight_gradients_2_from_256/pallas_call | solution.py:419
  (222 shorter events, 123.7 us)
Async XLA Ops:
  7.2 236.2 %all-gather.7.cloned.1.call-start = ((), (), s32[]{:S(2)}) async-start(), calls=%async_computation | async-start | bytes 9191424 | tf_op jit(solution)/shard_map/all_gather | solution.py:761
  34.1 26.5 %collective-permute-start.1 = (bf16[256,2048]{1,0:T(8,128)(2,1)}, bf16[256,2048]{1,0:T(8,128)(2,1)S(1)}, u32[]{:S(2)}, u32[]{:S(2)}) collective-permute-start(bf16[256,2048]{1,0:T(8,128)(2,1)} %add_rows.4), channel_id=1, source_target_pairs={{0,2},{1,3},{2,0},{3,1},{4,6},{5,7},{6,4},{7,5},{8,10},{9,11},{10,... | collective-permute-start | bytes 3145736 | tf_op jit(solution)/shard_map/ppermute | solution.py:677
  73.2 241.7 %all-gather.9.cloned.1.call-start = ((), (), s32[]{:S(2)}) async-start(), calls=%async_computation.1 | async-start | bytes 17301504 | tf_op jit(solution)/shard_map/all_gather | solution.py:731
  74.0 392.7 %all-gather.11.cloned.1.call-start = ((), (), s32[]{:S(2)}) async-start(), calls=%async_computation.2 | async-start | bytes 8650752 | tf_op jit(solution)/shard_map/all_gather | solution.py:769
  101.5 35.4 %collective-permute-start.6 = (bf16[256,2048]{1,0:T(8,128)(2,1)}, bf16[256,2048]{1,0:T(8,128)(2,1)S(1)}, u32[]{:S(2)}, u32[]{:S(2)}) collective-permute-start(bf16[256,2048]{1,0:T(8,128)(2,1)} %add_rows.5.refs_1_.rest_0_), channel_id=1, source_target_pairs={{0,2},{1,3},{2,0},{3,1},{4,6},{5,7},{6,4},{7,5},{8,10},{9,11},{10,... | collective-permute-start | bytes 3145736 | tf_op jit(solution)/shard_map/ppermute | solution.py:677
  173.2 30.7 %collective-permute-start.14 = (bf16[256,2048]{1,0:T(8,128)(2,1)}, bf16[256,2048]{1,0:T(8,128)(2,1)S(1)}, u32[]{:S(2)}, u32[]{:S(2)}) collective-permute-start(bf16[256,2048]{1,0:T(8,128)(2,1)} %get-tuple-element.111), channel_id=1, source_target_pairs={{0,1},{1,0},{2,3},{3,2},{4,5},{5,4},{6,7},{7,6},{8,9},{9,8},{10,11... | collective-permute-start | bytes 3145736 | tf_op jit(solution)/shard_map/ppermute | solution.py:670
  180.6 33.7 %collective-permute-start.5 = (bf16[256,2048]{1,0:T(8,128)(2,1)}, bf16[256,2048]{1,0:T(8,128)(2,1)}, u32[]{:S(2)}, u32[]{:S(2)}) collective-permute-start(bf16[256,2048]{1,0:T(8,128)(2,1)} %get-tuple-element.118), channel_id=1, source_target_pairs={{0,1},{1,0},{2,3},{3,2},{4,5},{5,4},{6,7},{7,6},{8,9},{9,8},{10,11... | collective-permute-start | bytes 3145736 | tf_op jit(solution)/shard_map/ppermute | solution.py:670
  208.5 32.7 %collective-permute-start.15 = (bf16[256,2048]{1,0:T(8,128)(2,1)}, bf16[256,2048]{1,0:T(8,128)(2,1)}, u32[]{:S(2)}, u32[]{:S(2)}) collective-permute-start(bf16[256,2048]{1,0:T(8,128)(2,1)} %add_rows.7), channel_id=1, source_target_pairs={{0,2},{1,3},{2,0},{3,1},{4,6},{5,7},{6,4},{7,5},{8,10},{9,11},{10,... | collective-permute-start | bytes 3145736 | tf_op jit(solution)/shard_map/ppermute | solution.py:677
  212.3 128.5 %collective-permute-start.17 = (bf16[4,256,512]{2,1,0:T(8,128)(2,1)}, bf16[4,256,512]{2,1,0:T(8,128)(2,1)}, u32[]{:S(2)}, u32[]{:S(2)}) collective-permute-start(bf16[4,256,512]{2,1,0:T(8,128)(2,1)} %get-tuple-element.64.refs_2_.refs_0_), channel_id=1, source_target_pairs={{0,8},{8,16},{16,24},{24,28},{28,20},{20,12},{12,4},{4,0},{1,9},{9... | collective-permute-start | bytes 3145736 | tf_op jit(solution)/shard_map/ppermute | solution.py:612
  213.8 126.9 %collective-permute-start.18 = (bf16[4,256,512]{2,1,0:T(8,128)(2,1)}, bf16[4,256,512]{2,1,0:T(8,128)(2,1)}, u32[]{:S(2)}, u32[]{:S(2)}) collective-permute-start(bf16[4,256,512]{2,1,0:T(8,128)(2,1)} %get-tuple-element.65.refs_3_.refs_1_), channel_id=1, source_target_pairs={{8,0},{16,8},{24,16},{28,24},{20,28},{12,20},{4,12},{0,4},{9,1},{1... | collective-permute-start | bytes 3145736 | tf_op jit(solution)/shard_map/ppermute | solution.py:617
  218.0 130.4 %collective-permute-start.12 = (bf16[256,2048]{1,0:T(8,128)(2,1)}, bf16[256,2048]{1,0:T(8,128)(2,1)}, u32[]{:S(2)}, u32[]{:S(2)}) collective-permute-start(bf16[256,2048]{1,0:T(8,128)(2,1)} %add_rows.6), channel_id=1, source_target_pairs={{0,2},{1,3},{2,0},{3,1},{4,6},{5,7},{6,4},{7,5},{8,10},{9,11},{10,... | collective-permute-start | bytes 3145736 | tf_op jit(solution)/shard_map/ppermute | solution.py:677
  346.4 37.0 %collective-permute-start.19 = (bf16[4,256,512]{2,1,0:T(8,128)(2,1)}, bf16[4,256,512]{2,1,0:T(8,128)(2,1)}, u32[]{:S(2)}, u32[]{:S(2)}) collective-permute-start(bf16[4,256,512]{2,1,0:T(8,128)(2,1)} %get-tuple-element.68.refs_2_), channel_id=1, source_target_pairs={{0,8},{8,16},{16,24},{24,28},{28,20},{20,12},{12,4},{4,0},{1,9},{9... | collective-permute-start | bytes 3145736 | tf_op jit(solution)/shard_map/ppermute | solution.py:612
  346.4 46.0 %collective-permute-start.20 = (bf16[4,256,512]{2,1,0:T(8,128)(2,1)}, bf16[4,256,512]{2,1,0:T(8,128)(2,1)}, u32[]{:S(2)}, u32[]{:S(2)}) collective-permute-start(bf16[4,256,512]{2,1,0:T(8,128)(2,1)} %get-tuple-element.69.refs_3_), channel_id=1, source_target_pairs={{8,0},{16,8},{24,16},{28,24},{20,28},{12,20},{4,12},{0,4},{9,1},{1... | collective-permute-start | bytes 3145736 | tf_op jit(solution)/shard_map/ppermute | solution.py:617
  352.7 81.7 %collective-permute-start.16 = (bf16[256,2048]{1,0:T(8,128)(2,1)}, bf16[256,2048]{1,0:T(8,128)(2,1)S(1)}, u32[]{:S(2)}, u32[]{:S(2)}) collective-permute-start(bf16[256,2048]{1,0:T(8,128)(2,1)} %get-tuple-element.109), channel_id=1, source_target_pairs={{0,1},{1,0},{2,3},{3,2},{4,5},{5,4},{6,7},{7,6},{8,9},{9,8},{10,11... | collective-permute-start | bytes 3145736 | tf_op jit(solution)/shard_map/ppermute | solution.py:670
  397.4 30.1 %collective-permute-start.21 = (bf16[4,256,512]{2,1,0:T(8,128)(2,1)}, bf16[4,256,512]{2,1,0:T(8,128)(2,1)S(1)}, u32[]{:S(2)}, u32[]{:S(2)}) collective-permute-start(bf16[4,256,512]{2,1,0:T(8,128)(2,1)} %get-tuple-element.72.refs_2_), channel_id=1, source_target_pairs={{0,8},{8,16},{16,24},{24,28},{28,20},{20,12},{12,4},{4,0},{1,9},{9... | collective-permute-start | bytes 3145736 | tf_op jit(solution)/shard_map/ppermute | solution.py:612
  398.9 28.6 %collective-permute-start.22 = (bf16[4,256,512]{2,1,0:T(8,128)(2,1)}, bf16[4,256,512]{2,1,0:T(8,128)(2,1)}, u32[]{:S(2)}, u32[]{:S(2)}) collective-permute-start(bf16[4,256,512]{2,1,0:T(8,128)(2,1)} %get-tuple-element.73.refs_3_), channel_id=1, source_target_pairs={{8,0},{16,8},{24,16},{28,24},{20,28},{12,20},{4,12},{0,4},{9,1},{1... | collective-permute-start | bytes 3145736 | tf_op jit(solution)/shard_map/ppermute | solution.py:617
  400.2 35.6 %collective-permute-start.13 = (bf16[256,2048]{1,0:T(8,128)(2,1)S(1)}, bf16[256,2048]{1,0:T(8,128)(2,1)}, u32[]{:S(2)}, u32[]{:S(2)}) collective-permute-start(bf16[256,2048]{1,0:T(8,128)(2,1)S(1)} %copy-done.15), channel_id=1, source_target_pairs={{0,1},{1,0},{2,3},{3,2},{4,5},{5,4},{6,7},{7,6},{8,9},{9,8},{10,11... | collective-permute-start | bytes 3145736 | tf_op jit(solution)/shard_map/ppermute | solution.py:670
  432.3 26.1 %collective-permute-start.25 = (bf16[1056,512]{1,0:T(8,128)(2,1)}, bf16[1056,512]{1,0:T(8,128)(2,1)S(1)}, u32[]{:S(2)}, u32[]{:S(2)}) collective-permute-start(bf16[1056,512]{1,0:T(8,128)(2,1)} %join_own.1.refs_2_.refs_3_.refs_0_), channel_id=1, source_target_pairs={{8,0},{16,8},{24,16},{28,24},{20,28},{12,20},{4,12},{0,4},{9,1},{1... | collective-permute-start | bytes 3244040 | tf_op jit(solution)/shard_map/ppermute | solution.py:617
  460.8 31.9 %collective-permute-start.26 = (bf16[1056,512]{1,0:T(8,128)(2,1)}, bf16[1056,512]{1,0:T(8,128)(2,1)S(1)}, u32[]{:S(2)}, u32[]{:S(2)}) collective-permute-start(bf16[1056,512]{1,0:T(8,128)(2,1)} %get-tuple-element.78.refs_2_.refs_1_), channel_id=1, source_target_pairs={{0,8},{8,16},{16,24},{24,28},{28,20},{20,12},{12,4},{4,0},{1,9},{9... | collective-permute-start | bytes 3244040 | tf_op jit(solution)/shard_map/ppermute | solution.py:612
  461.4 31.3 %collective-permute-start.27 = (bf16[1056,512]{1,0:T(8,128)(2,1)}, bf16[1056,512]{1,0:T(8,128)(2,1)S(1)}, u32[]{:S(2)}, u32[]{:S(2)}) collective-permute-start(bf16[1056,512]{1,0:T(8,128)(2,1)} %get-tuple-element.79.refs_3_.refs_2_), channel_id=1, source_target_pairs={{8,0},{16,8},{24,16},{28,24},{20,28},{12,20},{4,12},{0,4},{9,1},{1... | collective-permute-start | bytes 3244040 | tf_op jit(solution)/shard_map/ppermute | solution.py:617
  494.0 29.3 %collective-permute-start.28 = (bf16[1056,512]{1,0:T(8,128)(2,1)}, bf16[1056,512]{1,0:T(8,128)(2,1)S(1)}, u32[]{:S(2)}, u32[]{:S(2)}) collective-permute-start(bf16[1056,512]{1,0:T(8,128)(2,1)} %get-tuple-element.82.refs_2_.refs_3_), channel_id=1, source_target_pairs={{0,8},{8,16},{16,24},{24,28},{28,20},{20,12},{12,4},{4,0},{1,9},{9... | collective-permute-start | bytes 3244040 | tf_op jit(solution)/shard_map/ppermute | solution.py:612
  494.6 28.7 %collective-permute-start.29 = (bf16[1056,512]{1,0:T(8,128)(2,1)}, bf16[1056,512]{1,0:T(8,128)(2,1)S(1)}, u32[]{:S(2)}, u32[]{:S(2)}) collective-permute-start(bf16[1056,512]{1,0:T(8,128)(2,1)} %get-tuple-element.83.refs_3_.refs_4_), channel_id=1, source_target_pairs={{8,0},{16,8},{24,16},{28,24},{20,28},{12,20},{4,12},{0,4},{9,1},{1... | collective-permute-start | bytes 3244040 | tf_op jit(solution)/shard_map/ppermute | solution.py:617
  527.1 27.1 %collective-permute-start.30 = (bf16[528,512]{1,0:T(8,128)(2,1)S(1)}, bf16[528,512]{1,0:T(8,128)(2,1)S(1)}, u32[]{:S(2)}, u32[]{:S(2)}) collective-permute-start(bf16[528,512]{1,0:T(8,128)(2,1)S(1)} %slice.65.refs_3_), channel_id=1, source_target_pairs={{8,0},{16,8},{24,16},{28,24},{20,28},{12,20},{4,12},{0,4},{9,1},{1... | collective-permute-start | bytes 1622024 | tf_op jit(solution)/shard_map/ppermute | solution.py:617
  527.8 29.0 %collective-permute-start.31 = (bf16[528,512]{1,0:T(8,128)(2,1)S(1)}, bf16[528,512]{1,0:T(8,128)(2,1)S(1)}, u32[]{:S(2)}, u32[]{:S(2)}) collective-permute-start(bf16[528,512]{1,0:T(8,128)(2,1)S(1)} %slice.68.refs_2_), channel_id=1, source_target_pairs={{0,8},{8,16},{16,24},{24,28},{28,20},{20,12},{12,4},{4,0},{1,9},{9... | collective-permute-start | bytes 1622024 | tf_op jit(solution)/shard_map/ppermute | solution.py:612
  (41 other events, 392.2 us)
Sparse Core Ops, SparseCore 0:
  73.4 90.2 all-gather.6
  166.5 148.4 all-gather.8
  317.8 86.9 all-gather.10

commit v4 on v3

--- a/solution.py
+++ b/solution.py
@@ -312,63 +312,77 @@
     return gates, buckets
 
 
-def weight_kernel(s_ref, aux_ref, c_ref, up_ref, down_ref, *refs, level, start, rows, group, fresh, carried, deps):
-    gup_ref, gdown_ref, up_buf, down_buf, s_buf, aux_buf, c_buf, gup, gdown, sems = refs[carried + deps:]
+def weight_kernel(*refs, level, rows, group, offsets, fresh, carried, deps):
+    count = len(offsets)
+    pieces, refs = refs[:4 * count], refs[4 * count:]
+    up_ref, down_ref = refs[:2]
+    sums = refs[2:2 + carried]
+    gup_ref, gdown_ref, up_buf, down_buf, s_buf, aux_buf, c_buf, gup, gdown, sems = refs[2 + carried + deps:]
     b = pl.program_id(0)
-    steps = pl.num_programs(0)
-    slices, piece = s_ref.shape[1], s_ref.shape[3]
-    length = c_ref.shape[2]
-    aux_at = aux_ref.shape[2] - AUX
-    span = pl.ds(0, rows)
-
-    def tokens_of(step, slot):
+    steps = count // group
+    core = lax.rem(lax.axis_index("mp"), 2)
+    length, part = aux_buf.shape[3], s_buf.shape[2] // 2
+    columns = lambda c: pl.ds(pl.multiple_of(c * part, part), part)
+    slot = lax.rem(b, 2)
+
+    def tokens_of(step):
         out = []
         for j in range(group):
-            block = step * group + j
+            k = step * group + j
             to = pl.ds(j * rows, rows)
-            for m in range(slices):
-                out.append((s_ref.at[block, m, span], s_buf.at[slot, to, pl.ds(m * piece, piece)]))
-            for m in range(length // piece):
-                out.append((aux_ref.at[block, m, pl.ds(aux_at, AUX)], aux_buf.at[slot, j, pl.ds(0, AUX), pl.ds(m * piece, piece)]))
-        return [pltpu.make_async_copy(x, y, sems.at[slot, i]) for i, (x, y) in enumerate(out)]
-
-    def cots_of(step, slot):
+            mine, other = pieces[4 * k + 2], pieces[4 * k + 3]
+            at = offsets[k]
+            out += [
+                (mine.at[pl.ds(at[2], rows)], s_buf.at[step % 2, to, columns(core)]),
+                (other.at[pl.ds(at[3], rows)], s_buf.at[step % 2, to, columns(1 - core)]),
+                (mine.at[pl.ds(at[2] + length, AUX), pl.ds(0, length)], aux_buf.at[step % 2, j]),
+            ]
+        return [pltpu.make_async_copy(x, y, sems.at[step % 2, i]) for i, (x, y) in enumerate(out)]
+
+    def cots_of(step):
         out = []
         for j in range(group):
-            block = step * group + j
+            k = step * group + j
             to = pl.ds(j * rows, rows)
-            for m in range(slices):
-                out.append((c_ref.at[block, m, pl.ds(start, rows)], c_buf.at[slot, to, pl.ds(m * piece, piece)]))
-        return [pltpu.make_async_copy(x, y, sems.at[2 + slot, i]) for i, (x, y) in enumerate(out)]
+            at = offsets[k]
+            out += [
+                (pieces[4 * k].at[pl.ds(at[0], rows)], c_buf.at[step % 2, to, columns(core)]),
+                (pieces[4 * k + 1].at[pl.ds(at[1], rows)], c_buf.at[step % 2, to, columns(1 - core)]),
+            ]
+        return [pltpu.make_async_copy(x, y, sems.at[2 + step % 2, i]) for i, (x, y) in enumerate(out)]
 
     up_copy = pltpu.make_async_copy(up_ref.at[level], up_buf, sems.at[4, 0])
     down_copy = pltpu.make_async_copy(down_ref.at[level], down_buf, sems.at[4, 1])
     ends = [pltpu.make_async_copy(gup, gup_ref.at[level], sems.at[4, 2]),
             pltpu.make_async_copy(gdown, gdown_ref.at[level], sems.at[4, 3])]
     begins = [] if fresh else [
-        pltpu.make_async_copy(refs[0].at[level], gup, sems.at[5, 0]),
-        pltpu.make_async_copy(refs[1].at[level], gdown, sems.at[5, 1])]
-    slot = lax.rem(b, 2)
+        pltpu.make_async_copy(sums[0].at[level], gup, sems.at[5, 0]),
+        pltpu.make_async_copy(sums[1].at[level], gdown, sems.at[5, 1])]
 
     @pl.when(b == 0)
     def _():
-        for c in [up_copy] + tokens_of(0, 0) + [down_copy] + cots_of(0, 0) + begins:
+        for c in [up_copy] + tokens_of(0) + [down_copy] + cots_of(0) + begins:
             c.start()
 
-    @pl.when(b + 1 < steps)
-    def _():
-        for c in tokens_of(b + 1, 1 - slot) + cots_of(b + 1, 1 - slot):
-            c.start()
+    for step in range(1, steps):
+        @pl.when(b == step - 1)
+        def _(step=step):
+            for c in tokens_of(step) + cots_of(step):
+                c.start()
 
     @pl.when(b == 0)
     def _():
         up_copy.wait()
 
-    for c in tokens_of(b, slot):
-        c.wait()
-    columns = [gates_and_buckets(aux_buf[slot, j]) for j in range(group)]
-    gate = jnp.concatenate([g[start:start + rows, :1] for g, _ in columns], 0)
-    keep = jnp.concatenate([k[start:start + rows, :1] for _, k in columns], 0) >= level
+    for step in range(steps):
+        @pl.when(b == step)
+        def _(step=step):
+            for c in tokens_of(step):
+                c.wait()
+
+    columns_of = [gates_and_buckets(aux_buf[slot, j]) for j in range(group)]
+    gate = jnp.concatenate([g[:rows, :1] for g, _ in columns_of], 0)
+    keep = jnp.concatenate([k[:rows, :1] for _, k in columns_of], 0) >= level
     pre = dot(s_buf[slot], up_buf[...])
     active = jnp.where(keep, jnp.maximum(pre, 0.0), 0.0)
     act = (active * active * gate).astype(BF16)
@@ -377,8 +391,12 @@
     def _():
         down_copy.wait()
 
-    for c in cots_of(b, slot):
-        c.wait()
+    for step in range(steps):
+        @pl.when(b == step)
+        def _(step=step):
+            for c in cots_of(step):
+                c.wait()
+
     gact = dot(c_buf[slot], down_buf[...], NT)
     gpre = (gact * (2.0 * gate) * active).astype(BF16)
 
@@ -393,10 +411,11 @@
             gup[...] += dot(s_buf[slot], gpre, TN)
             gdown[...] += dot(act, c_buf[slot], TN)
 
-    @pl.when(jnp.logical_and(b > 0, b < steps - 1))
-    def _():
-        gup[...] += dot(s_buf[slot], gpre, TN)
-        gdown[...] += dot(act, c_buf[slot], TN)
+    if steps > 2:
+        @pl.when(jnp.logical_and(b > 0, b < steps - 1))
+        def _():
+            gup[...] += dot(s_buf[slot], gpre, TN)
+            gdown[...] += dot(act, c_buf[slot], TN)
 
     @pl.when(b == steps - 1)
     def _():
@@ -408,33 +427,33 @@
             c.wait()
 
 
-def weight_gradients(level, start, rows, sents, aux, cots, w_up, w_down, carried, fresh, deps=()):
+def weight_gradients(level, rows, length, blocks, w_up, w_down, carried, fresh, deps=()):
     levels, model, hidden = w_up.shape
-    blocks, slices, length, piece = cots.shape
-    group = max(1, min(4, 1024 // rows))
-    while blocks % group or blocks // group < 2:
-        group -= 1
-    copies = group * (slices + length // piece)
+    count = len(blocks)
+    group = 2
     anywhere = pl.BlockSpec(memory_space=pl.ANY)
+    arrays = [x for block in blocks for x, _ in block]
+    offsets = tuple(tuple(at for _, at in block) for block in blocks)
+    first = len(arrays) + 2
     return pl.pallas_call(
-        partial(weight_kernel, level=level, start=start, rows=rows, group=group, fresh=fresh, carried=len(carried),
+        partial(weight_kernel, level=level, rows=rows, group=group, offsets=offsets, fresh=fresh, carried=len(carried),
                 deps=len(deps)),
-        grid=(blocks // group,),
-        in_specs=[anywhere] * (5 + len(carried) + len(deps)),
+        grid=(count // group,),
+        in_specs=[anywhere] * (first + len(carried) + len(deps)),
         out_specs=[anywhere] * 2,
         out_shape=[jax.ShapeDtypeStruct((levels, model, hidden), F32), jax.ShapeDtypeStruct((levels, hidden, model), F32)],
-        input_output_aliases={5: 0, 6: 1} if carried else {},
+        input_output_aliases={first: 0, first + 1: 1} if carried else {},
         scratch_shapes=[
             pltpu.VMEM((model, hidden), BF16), pltpu.VMEM((hidden, model), BF16),
             pltpu.VMEM((2, group * rows, model), BF16), pltpu.VMEM((2, group, AUX, length), BF16),
             pltpu.VMEM((2, group * rows, model), BF16),
             pltpu.VMEM((model, hidden), F32), pltpu.VMEM((hidden, model), F32),
-            pltpu.SemaphoreType.DMA((6, max(4, copies))),
+            pltpu.SemaphoreType.DMA((6, 3 * group)),
         ],
         compiler_params=params(),
-        cost_estimate=cost(8 * blocks * rows * model * hidden, 4 * blocks * length * model + 16 * model * hidden),
-        name=f"weight_gradients_{level}_from_{start}",
-    )(sents, aux, cots, w_up, w_down, *carried, *deps)
+        cost_estimate=cost(8 * count * rows * model * hidden, 4 * count * rows * model + 16 * model * hidden),
+        name=f"weight_gradients_{level}" + ("" if fresh else "_more"),
+    )(*arrays, w_up, w_down, *carried, *deps)
 
 
 def unpack_kernel(order_ref, *refs, count, carried):
@@ -670,7 +689,7 @@
     return lax.ppermute(x, "mp", [(i, i ^ 1) for i in range(n)])
 
 
-def sum_over_x(x):
+def sum_over_x(x, deps=()):
     n = lax.axis_size("mp") // 2
     index = lax.axis_index("mp")
     parts = [x] + [
@@ -678,6 +697,8 @@
     ]
     if n == 1:
         return x.astype(F32)
+    if deps:
+        parts[1:] = after(parts[1:], deps)
     if n == 2:
         return parts[0].astype(F32) + parts[1].astype(F32)
     stacked = jnp.stack(parts)
@@ -724,16 +745,11 @@
         return jnp.concatenate([jnp.where(core == 0, mine, other), jnp.where(core == 0, other, mine)], 0)
 
     cot_sorted = dot(sort_rows.astype(BF16), cotangent).astype(BF16)
-    slices = lax.axis_size("mp")
-    piece = model // slices
-    me = lax.axis_index("mp")
-    cot_piece = lax.dynamic_slice_in_dim(cot_sorted, me * piece, piece, axis=1)
-    cots = lax.all_gather(cot_piece, ("dp", "mp"), axis=0).reshape(devices_dp, slices, length, piece)
 
     w3 = jnp.transpose(w_qkv, (1, 0, 2))
     cos, sin = rotary_table(length, HEAD)
     part_mine, part_other, normed_low, qkv, lse, mixed = attend(tokens, gain_first[None, :], w3, cos, sin, w_out)
-    attn_rows = add_rows([part_mine, core_swap(part_other)], (cot_piece,))
+    attn_rows = add_rows([part_mine, core_swap(part_other)])
     attn = sum_over_x(attn_rows)
 
     resid = own_rows(tokens).astype(F32) + attn
@@ -755,21 +771,38 @@
     gate_2 = low(gate_sorted - gate_1.astype(F32))
     gate_3 = low(gate_sorted - gate_1.astype(F32) - gate_2.astype(F32))
     aux = jnp.stack([gate_1, gate_2, gate_3, bucket_sorted.astype(BF16)] + [jnp.zeros_like(gate_1)] * (AUX - 4))
-    sent_mine = lax.dynamic_slice_in_dim(sent_sorted, me * piece, piece, axis=1)
-    sent_piece = jnp.concatenate([
-        sent_mine[:half], lax.dynamic_slice_in_dim(aux, (me % (length // piece)) * piece, piece, axis=1)], 0)
-    sents = lax.all_gather(sent_piece, ("dp", "mp"), axis=0).reshape(devices_dp, slices, half + AUX, piece)
+    aux = jnp.pad(aux, ((0, 0), (0, model // 2 - length)))
+    both = jnp.concatenate([part_of(cot_sorted, core, 1), part_of(sent_sorted, core, 1), aux], 0)
+    height = length
+    blocks = [((both, 0), (part_of(cot_sorted, 1 - core, 1), 0), (both, height), (part_of(sent_sorted, 1 - core, 1), 0))]
+
+    def block(mine, other):
+        return (mine, 0), (other, 0), (mine, height), (other, height)
+
+    r, l = ring.to_right(both), ring.to_left(both)
 
     wide = lambda x: jnp.broadcast_to(x[:, None], (length, 128))
     gsent_mine, gsent_other, act = own_grad(
         sent_sorted, cot_sorted, wide(bucket_sorted), wide(gate_sorted), unsort_low, w_up, w_down, row_bounds,
-        (sent_piece,))
+        (both,))
     gsent_rows = add_rows([gsent_mine, core_swap(gsent_other)])
-    sent_more, = after([sent_mine[half:]], (gsent_rows,))
-    sents_more = lax.all_gather(sent_more, ("dp", "mp"), axis=0).reshape(devices_dp, slices, half, piece)
     grad_sent = sum_over_x(gsent_rows).astype(BF16).astype(F32)
     ffn_part, ggate_part = own_forward(
-        act, cot_sorted, sort_rows.astype(BF16).T, w_down, row_bounds, (gsent_rows, sent_more))
+        act, cot_sorted, sort_rows.astype(BF16).T, w_down, row_bounds, (gsent_rows,))
+    far = devices_dp // 2
+    met = []
+
+    def forward(arrived, deps):
+        r, l = after(arrived, deps)
+        if len(met) < far:
+            met.extend([(r, core_swap(r)), (l, core_swap(l))])
+        else:
+            met.extend([(r, None), (l, None)])
+        if len(met) < 2 * far - 2:
+            return ring.to_right(r), ring.to_left(l)
+        return ring.to_right(r[:height]), ring.to_left(l[height:])
+
+    r, l = forward((r, l), (ffn_part,))
     ggate_part = jnp.sum(jnp.where(sort_rows, ggate_part[:, :1], 0.0), 0)
     grad_gate = ggate_part + core_swap(ggate_part)
     grad_gate = sum_over_x(own_rows(grad_gate))
@@ -786,11 +819,10 @@
     grad_attn = joined(ga_half, core_swap(ga_half))
 
     grads, first_part = attend_back(
-        grad_attn, normed_low, qkv, lse, mixed, w_out, w3, cos, sin)
+        grad_attn, normed_low, qkv, lse, mixed, w_out, w3, cos, sin, met[0] + met[1])
 
     carried = ()
     arrived, sending = ring.reduce_start(grads)
-    far = devices_dp // 2
     chunks = None
     step = 0
 
@@ -815,46 +847,86 @@
         return (r, l), sending
 
     steps = 2 * far - 1
-    while step < min(far - 1, 1):
-        arrived, sending = advance(step, arrived, ())
+    while len(met) < far:
+        r, l = forward((r, l), (grads,))
+    near = len(met)
+    sending = sending + met[-2] + met[-1][:1]
+    blocks += [block(*x) for x in met[:far - 1]]
+    carried = ()
+    calls = [(level, rows, True) for level, rows in enumerate(row_bounds)]
+    later = [block(*x) for x in met[far - 1:]]
+    grad_first = ffn_rows = extra = None
+    slots = [0] + list(range(2, buckets)) + [1]
+    for slot_at, level in enumerate(slots):
+        rows = row_bounds[level]
+        carried = weight_gradients(level, rows, length, blocks, w_up, w_down, tuple(carried), True, sending)
+        if slot_at == 0:
+            first_other, = after([other_rows(first_part)], (carried[0],))
+            first_other = core_swap(first_other)
+        if slot_at == 1:
+            first_rows = add_rows([own_rows(first_part), first_other], (carried[0],))
+        if slot_at == 2:
+            grad_first = sum_over_x(first_rows, (carried[0],)).astype(BF16).astype(F32)
+            source = own_rows(tokens).astype(F32)
+            inv_first = lax.rsqrt(jnp.mean(source * source, -1, keepdims=True) + EPSILON)
+            xhat_first = source * inv_first
+            grad_gain_first = jnp.sum(grad_first * xhat_first, 0)
+            scaled_first = grad_first * gain_first
+            grad_source = inv_first * (
+                scaled_first - xhat_first * jnp.mean(scaled_first * xhat_first, -1, keepdims=True))
+            tokens_half = (grad_source + grad_resid).astype(BF16)
+            small = jnp.concatenate([grad_router.T, grad_gain_second[None], grad_gain_first[None]], 0)
+            small = jnp.pad(small, ((0, -small.shape[0] % 8), (0, 0)))
+            small_other = core_swap(small)
+        if slot_at == 3:
+            small_other, = after([small_other], (carried[0],))
+            extra = low(small + small_other).reshape(-1, w3.shape[2])
+            tokens_half, = after([tokens_half], (carried[0],))
+            tokens_other = core_swap(tokens_half)
+            r, l, *held = after([r, l] + [x for x, _ in met[far:]], (carried[0],))
+        arrived, sending = advance(step, arrived, (carried[0],))
         step += 1
-    ring_busy = tuple(sending)
-
-    ffn_rows = sum_over_x(add_rows([own_rows(ffn_part), core_swap(other_rows(ffn_part))], ring_busy)).astype(BF16).astype(F32)
-    output_half = (resid + gate[:, None] * ffn_rows).astype(BF16)
-
-    grad_first = sum_over_x(add_rows([own_rows(first_part), core_swap(other_rows(first_part))], ring_busy)).astype(BF16).astype(F32)
-    source = own_rows(tokens).astype(F32)
-    inv_first = lax.rsqrt(jnp.mean(source * source, -1, keepdims=True) + EPSILON)
-    xhat_first = source * inv_first
-    grad_gain_first = jnp.sum(grad_first * xhat_first, 0)
-    scaled_first = grad_first * gain_first
-    grad_source = inv_first * (scaled_first - xhat_first * jnp.mean(scaled_first * xhat_first, -1, keepdims=True))
-    tokens_half = (grad_source + grad_resid).astype(BF16)
-    output = joined(output_half, core_swap(output_half))
-    grad_tokens = joined(tokens_half, core_swap(tokens_half))
-    small = jnp.concatenate([grad_router.T, grad_gain_second[None], grad_gain_first[None]], 0)
-    small = jnp.pad(small, ((0, -small.shape[0] % 8), (0, 0)))
-    local = w3.shape[2]
-    extra = low(small + core_swap(small)).reshape(-1, local)
-
-    calls = [(level, 0, min(rows, half), sents, True) for level, rows in enumerate(row_bounds)]
-    calls += [(level, half, rows - half, sents_more, False) for level, rows in enumerate(row_bounds) if rows > half]
-    for level, start, rows, tokens_all, fresh in calls:
-        carried = weight_gradients(
-            level, start, rows, tokens_all, sents, cots, w_up, w_down, tuple(carried), fresh, sending)
+        if slot_at == 0:
+            sending = sending + tuple(x for _, x in met[far - 1:])
+        if slot_at == 2:
+            while len(met) < 2 * far - 2:
+                r, l = forward((r, l), (carried[0],))
+            sending = sending + tuple(pair[0] for pair in met[far:])
+    later += [block(x, core_swap(x)) for x in held]
+    later.append(((r, 0), (core_swap(r), 0), (l, 0), (core_swap(l), 0)))
+    steps = 2 * far - 1
+    for level, rows in enumerate(row_bounds):
+        if level == buckets - 1 and step == steps:
+            order = jnp.stack(ring.indices()).astype(jnp.int32)
+            size = model // devices_dp
+            unpacked = unpack(order[:-1], chunks[:-1], size, devices_dp)
+            sending = sending + (unpacked[0],)
+        carried = weight_gradients(level, rows, length, later, w_up, w_down, tuple(carried), False, sending)
+        if level == 0:
+            ffn_other, tokens_other = after([other_rows(ffn_part), tokens_other], (carried[0],))
+            ffn_other = core_swap(ffn_other)
+        if level == 1:
+            ffn_sum = add_rows([own_rows(ffn_part), ffn_other], (carried[0],))
+        if level == 2:
+            ffn_rows = sum_over_x(ffn_sum, (carried[0],)).astype(BF16).astype(F32)
+            output_half = (resid + gate[:, None] * ffn_rows).astype(BF16)
+            output_other = core_swap(output_half)
+        if level == 3:
+            output_other, = after([output_other], (carried[0],))
+        sending = ()
         if step < steps:
             arrived, sending = advance(step, arrived, (carried[0],))
             step += 1
-        else:
-            sending = ()
     while step < steps:
         arrived, sending = advance(step, arrived, ())
         step += 1
     grad_up, grad_down = carried
+    output = joined(output_half, output_other)
+    grad_tokens = joined(tokens_half, tokens_other)
     order = jnp.stack(ring.indices()).astype(jnp.int32)
     size = model // devices_dp
-    unpacked = unpack(order[:-1], chunks[:-1], size, devices_dp)
+    if devices_dp != 8:
+        unpacked = unpack(order[:-1], chunks[:-1], size, devices_dp)
     grad_wqkv, grad_wout = unpack(order[-1:], chunks[-1:], size, devices_dp, unpacked)
     terms = jnp.stack([x[4 * size:] for x in chunks])
     by_place = jnp.zeros((devices_dp,), jnp.int32).at[order].set(jnp.arange(devices_dp, dtype=jnp.int32))

time: 577 us -> 521 us (0.903)
  waiting for transfers between devices: 172 us -> 93.3 us
  local copies, waits for them, and re-layouts: 36 us -> 55.9 us
  between operations: 21.1 us -> 8.57 us
  starting transfers between devices: 25.8 us -> 35.2 us
    all_gather x3 -> x0, waiting for transfers between devices: 71.6 us -> none  [the longest x1 71.6 us: on_device(): lax.all_gather(cot_piece, ('dp', 'mp'), axis=0)]
    ppermute x8 -> x12, waiting for transfers between devices: 6.35 us -> 44.9 us  [to_right(): out = lax.ppermute(x, 'dp', self.right)]
    ppermute x5, waiting for transfers between devices: 64.3 us -> 29.3 us  [sum_over_x(): lax.ppermute(x, 'mp', [(i, (i + 2 * k) % (2 * n)) for i in range(2 * n)])]
    ppermute x8 -> x12, waiting for transfers between devices: 22.2 us -> 4.43 us  [to_left(): out = lax.ppermute(x, 'dp', self.left)]
    unnamed x70 -> x114, local copies, waits for them, and re-layouts: 16 us -> 31.9 us
    ppermute x8 -> x12, starting transfers between devices: 6.61 us -> 17.8 us  [to_right(): out = lax.ppermute(x, 'dp', self.right)]
    ppermute x11 -> x19, waiting for transfers between devices: 7.32 us -> 14.8 us  [core_swap(): return lax.ppermute(x, 'mp', [(i, i ^ 1) for i in range(n)])]
    pallas_call x7 -> x8, Pallas kernels: 160 us -> 162 us  [weight_gradients(): pl.pallas_call(partial(weight_kernel, level=level, rows=rows, group=group...]
  transfers between devices with their start and end apart: 35 -> 48, of which waited for: 14 -> 14; matrix products, arithmetic and copies ran while one was open for 9% -> 13% of each run, Pallas kernels for 44% -> 46%
where the time goes in v4:
time: 521 us; the launch traced here: 515 us
  Pallas kernels  276 us (53%)
  waiting for transfers between devices  93.3 us (18%)
  local copies, waits for them, and re-layouts  55.9 us (11%)
  starting transfers between devices  35.2 us (7%)
  other arithmetic  33.5 us (6%)
  matrix products  11.9 us (2%)
  between operations  8.57 us (2%)
    pallas_call x8, Pallas kernels, weight_gradients(): pl.pallas_call(partial(weight_kernel, level=level, rows=rows, group=group...  162 us
    ppermute x12, waiting for transfers between devices, to_right(): out = lax.ppermute(x, 'dp', self.right)  44.9 us
    unnamed x114, local copies, waits for them, and re-layouts  31.9 us
    ppermute x5, waiting for transfers between devices, sum_over_x(): lax.ppermute(x, 'mp', [(i, (i + 2 * k) % (2 * n)) for i in range(2 * n)])  29.3 us
    pallas_call x1, Pallas kernels, attend_back(): pl.pallas_call(partial(attend_back_kernel, heads=heads, steps=steps, deps...  23.9 us
    ppermute x12, starting transfers between devices, to_right(): out = lax.ppermute(x, 'dp', self.right)  17.8 us
    pallas_call x1, Pallas kernels, own_grad(): pl.pallas_call(partial(own_grad_kernel, row_bounds=tuple(row_bounds), dep...  17.7 us
    pallas_call x1, Pallas kernels, attend(): pl.pallas_call(partial(attend_kernel, heads=heads, steps=steps), grid=(st...  15.7 us
  transfers between devices with their start and end apart: 48, of which 14 were waited for; matrix products, arithmetic and copies ran while one was open for 13% of the time, Pallas kernels for 46%

profile of v4, /device:TPU:0, one launch (start us, length us, event | category | flops | bytes accessed | tf_op | source)
XLA Modules:
  0.0 514.7 jit_solution(11375553160156360915)
XLA Ops:
  2.7 15.7 %attend.1 = (bf16[256,2048]{1,0:T(8,128)(2,1)}, bf16[256,2048]{1,0:T(8,128)(2,1)}, bf16[512,2048]{1,0:T(8,128)(2,1)}, bf16[3,512,512]{2,1,0:T(8,128)(2,1)}, f32[...) custom-call(bf16[512,2048]{1,0:T(8,128)(2,1)} %x_ref.1, f32[1,2048]{1,0:T(1,128)} %bitcast.62, ...), custom_call_target="tpu_custom_call" | custom-call | flops 1207959552 | bytes 3145728 | tf_op jit(solution)/shard_map/attend/pallas_call | solution.py:102
  33.4 19.3 %collective-permute-done.1 = bf16[256,2048]{1,0:T(8,128)(2,1)S(1)} collective-permute-done((bf16[256,2048]{1,0:T(8,128)(2,1)}, bf16[256,2048]{1,0:T(8,128)(2,1)S(1)}, u32[]{:S(2)}, u32[]{:S(2)}) %collective-permute-start.1) | collective-permute-done | bytes 1048608 | tf_op jit(solution)/shard_map/ppermute | solution.py:696
  63.5 17.7 %own_grad.1 = (bf16[256,2048]{1,0:T(8,128)(2,1)}, bf16[256,2048]{1,0:T(8,128)(2,1)}, bf16[4,512,512]{2,1,0:T(8,128)(2,1)}) custom-call(bf16[512,2048]{1,0:T(8,128)(2,1)} %copy-done.22, bf16[512,2048]{1,0:T(8,128)(2,1)} %copy-done.14, s32[512,128]{1,0:T(8,128)} %broadcast_in_dim.61.bucket_ref, f32[512,128]{1,0:T(8,128)} %broadcast_in_dim.64.gate_ref, ...), custom_call_target="tpu_custom_call" | custom-call | flops 2315255808 | bytes 5767168 | tf_op jit(solution)/shard_map/own_grad/pallas_call | solution.py:248
  91.6 10.2 %own_forward.1 = (bf16[512,2048]{1,0:T(8,128)(2,1)}, f32[512,128]{1,0:T(8,128)}) custom-call(bf16[4,512,512]{2,1,0:T(8,128)(2,1)} %get-tuple-element.68.act_ref, bf16[512,2048]{1,0:T(8,128)(2,1)} %copy-done.14, bf16[512,512]{1,0:T(8,128)(2,1)} %fusion.26.unsort_ref, bf16[4,512,2048]{2,1,0:T(8,128)(2,1)} %refs_17_.15, bf16[256,2048]{1,0:T(8,128)(2,1)} %add_rows.5.rest_0_), custom_call_target="tpu_custom_call" | custom-call | flops 771751936 | bytes 3670016 | tf_op jit(solution)/shard_map/own_forward/pallas_call | solution.py:288
  104.7 9.9 %collective-permute-done.7 = f32[256]{0:T(256)S(1)} collective-permute-done((f32[256]{0:T(256)S(1)}, f32[256]{0:T(256)S(1)}, u32[]{:S(2)}, u32[]{:S(2)}) %collective-permute-start.7) | collective-permute-done | bytes 1056 | tf_op jit(solution)/shard_map/ppermute | solution.py:696
  114.7 6.2 %multiply_reduce_fusion = (f32[2048]{0:T(1024)}, f32[256]{0:T(256)S(1)}, f32[256,2048]{1,0:T(8,128)}) fusion(f32[256,2048]{1,0:T(8,128)} %copy-done.8, f32[256]{0:T(256)S(1)} %add_rsqrt_fusion.1, f32[2048]{0:T(1024)S(1)} %copy-done.42, f32[2048,4]{0,1:T(4,128)S(1)} %copy-done, f32[256,4]{0,1:T(4,128)S(1)} %get-tuple-element.128, f32[256]{0:T(256)S(1)} %fusion.32, ...), kind=kOutput, calls=%fused_computation.29 | convolution fusion | flops 31459072 | bytes 6349824 | tf_op jit(solution)/shard_map/dot_general | solution.py:814
  121.0 9.0 %collective-permute-done.9.refs_0_ = bf16[1040,1024]{1,0:T(8,128)(2,1)S(1)} collective-permute-done((bf16[1040,1024]{1,0:T(8,128)(2,1)S(1)}, bf16[1040,1024]{1,0:T(8,128)(2,1)S(1)}, u32[]{:S(2)}, u32[]{:S(2)}) %collective-permute-start.9) | collective-permute-done | bytes 2129952 | tf_op jit(solution)/shard_map/ppermute | solution.py:631
  144.7 23.9 %attend_back.1 = (bf16[4,2048,512]{2,1,0:T(8,128)(2,1)}, bf16[512,2048]{1,0:T(8,128)(2,1)}) custom-call(bf16[512,2048]{1,0:T(8,128)(2,1)} %pad_maximum_fusion.ga_ref, bf16[512,2048]{1,0:T(8,128)(2,1)} %get-tuple-element.73.normed_ref, bf16[3,512,512]{2,1,0:T(8,128)(2,1)} %get-tuple-element.74.qkv_ref, f32[4,512,128]{2,1,0:T(8,128)} %get-tuple-element.75.lse_ref, ...), custom_call_target="tpu_custom_call" | custom-call | flops 2483027968 | bytes 6291456 | tf_op jit(solution)/shard_map/attend_back/pallas_call | solution.py:195
  168.6 13.3 %collective-permute-done.13.refs_0_ = bf16[1040,1024]{1,0:T(8,128)(2,1)} collective-permute-done((bf16[1040,1024]{1,0:T(8,128)(2,1)}, bf16[1040,1024]{1,0:T(8,128)(2,1)}, u32[]{:S(2)}, u32[]{:S(2)}) %collective-permute-start.13) | collective-permute-done | bytes 2129952 | tf_op jit(solution)/shard_map/ppermute | solution.py:631
  194.2 24.4 %weight_gradients_0.1 = (f32[4,2048,512]{2,1,0:T(8,128)}, f32[4,512,2048]{2,1,0:T(8,128)}) custom-call(bf16[1040,1024]{1,0:T(8,128)(2,1)} %fusion.5.rest_0_.refs_0_.refs_2_, bf16[512,1024]{1,0:T(8,128)(2,1)} %get-tuple-element.141.refs_1_, bf16[1040,1024]{1,0:T(8,128)(2,1)} %fusion.5.rest_0_.refs_0_.refs_2_, bf16[512,1024]{1,0:T(8,128)(2,1)} %get-tuple-element.139.refs_3_, ...), custom_call_target="tpu_custom_call" | custom-call | flops 4294967296 | bytes 8388608 | tf_op jit(solution)/shard_map/weight_gradients_0/pallas_call | solution.py:438
  218.6 4.8 join.3
  229.0 18.4 %weight_gradients_2.1 = (f32[4,2048,512]{2,1,0:T(8,128)}, f32[4,512,2048]{2,1,0:T(8,128)}) custom-call(bf16[1040,1024]{1,0:T(8,128)(2,1)} %fusion.5.rest_0_.refs_0_.refs_2_, bf16[512,1024]{1,0:T(8,128)(2,1)} %get-tuple-element.141.refs_1_, bf16[1040,1024]{1,0:T(8,128)(2,1)} %fusion.5.rest_0_.refs_0_.refs_2_, ...), custom_call_target="tpu_custom_call", output_to_operand_aliasing={{0}: (18, {}), {1}: (19, {})} | custom-call | flops 2684354560 | bytes 6815744 | tf_op jit(solution)/shard_map/weight_gradients_2/pallas_call | solution.py:438
  247.4 22.5 %collective-permute-done.21.right_ref = bf16[4,256,512]{2,1,0:T(8,128)(2,1)S(1)} collective-permute-done((bf16[4,256,512]{2,1,0:T(8,128)(2,1)}, bf16[4,256,512]{2,1,0:T(8,128)(2,1)S(1)}, u32[]{:S(2)}, u32[]{:S(2)}) %collective-permute-start.21) | collective-permute-done | bytes 1048608 | tf_op jit(solution)/shard_map/ppermute | solution.py:631
  271.3 4.9 join.4
  287.9 13.3 %weight_gradients_3.1 = (f32[4,2048,512]{2,1,0:T(8,128)}, f32[4,512,2048]{2,1,0:T(8,128)}) custom-call(bf16[1040,1024]{1,0:T(8,128)(2,1)} %fusion.5.rest_0_.refs_0_.refs_2_, bf16[512,1024]{1,0:T(8,128)(2,1)} %get-tuple-element.141.refs_1_, bf16[1040,1024]{1,0:T(8,128)(2,1)} %fusion.5.rest_0_.refs_0_.refs_2_, ...), custom_call_target="tpu_custom_call", output_to_operand_aliasing={{0}: (18, {}), {1}: (19, {})} | custom-call | flops 1342177280 | bytes 5505024 | tf_op jit(solution)/shard_map/weight_gradients_3/pallas_call | solution.py:438
  311.6 4.8 join.5
  321.9 23.8 %weight_gradients_1.1 = (f32[4,2048,512]{2,1,0:T(8,128)}, f32[4,512,2048]{2,1,0:T(8,128)}) custom-call(bf16[1040,1024]{1,0:T(8,128)(2,1)} %fusion.5.rest_0_.refs_0_.refs_2_, bf16[512,1024]{1,0:T(8,128)(2,1)} %get-tuple-element.141.refs_1_, bf16[1040,1024]{1,0:T(8,128)(2,1)} %fusion.5.rest_0_.refs_0_.refs_2_, ...), custom_call_target="tpu_custom_call", output_to_operand_aliasing={{0}: (18, {}), {1}: (19, {})} | custom-call | flops 4026531840 | bytes 8126464 | tf_op jit(solution)/shard_map/weight_gradients_1/pallas_call | solution.py:438
  347.8 5.9 %collective-permute-done.36.refs_0_ = f32[8,2048]{1,0:T(8,128)S(1)} collective-permute-done((f32[8,2048]{1,0:T(8,128)S(1)}, f32[8,2048]{1,0:T(8,128)S(1)}, u32[]{:S(2)}, u32[]{:S(2)}) %collective-permute-start.36) | collective-permute-done | bytes 65568 | tf_op jit(solution)/shard_map/ppermute | solution.py:689
  354.3 5.1 fusion.8.refs_0_
  372.8 24.7 %weight_gradients_0_more.1 = (f32[4,2048,512]{2,1,0:T(8,128)}, f32[4,512,2048]{2,1,0:T(8,128)}) custom-call(bf16[1040,1024]{1,0:T(8,128)(2,1)} %get-tuple-element.82.refs_22_.refs_0_.refs_2_, bf16[1040,1024]{1,0:T(8,128)(2,1)} %collective-permute-done.19.refs_22_.refs_1_.refs_3_, ...), custom_call_target="tpu_custom_call", output_to_operand_aliasing={{0}: (18, {}), {1}: (19, {})} | custom-call | flops 4294967296 | bytes 8388608 | tf_op jit(solution)/shard_map/weight_gradients_0_more/pallas_call | solution.py:438
  401.1 23.8 %weight_gradients_1_more.1 = (f32[4,2048,512]{2,1,0:T(8,128)}, f32[4,512,2048]{2,1,0:T(8,128)}) custom-call(bf16[1040,1024]{1,0:T(8,128)(2,1)} %get-tuple-element.82.refs_22_.refs_0_.refs_2_, bf16[1040,1024]{1,0:T(8,128)(2,1)} %collective-permute-done.19.refs_22_.refs_1_.refs_3_, ...), custom_call_target="tpu_custom_call", output_to_operand_aliasing={{0}: (18, {}), {1}: (19, {})} | custom-call | flops 4026531840 | bytes 8126464 | tf_op jit(solution)/shard_map/weight_gradients_1_more/pallas_call | solution.py:438
  442.6 19.0 %weight_gradients_2_more.1 = (f32[4,2048,512]{2,1,0:T(8,128)}, f32[4,512,2048]{2,1,0:T(8,128)}) custom-call(bf16[1040,1024]{1,0:T(8,128)(2,1)} %get-tuple-element.82.refs_22_.refs_0_.refs_2_, bf16[1040,1024]{1,0:T(8,128)(2,1)} %collective-permute-done.19.refs_22_.refs_1_.refs_3_, ...), custom_call_target="tpu_custom_call", output_to_operand_aliasing={{0}: (18, {}), {1}: (19, {})} | custom-call | flops 2684354560 | bytes 6815744 | tf_op jit(solution)/shard_map/weight_gradients_2_more/pallas_call | solution.py:438
  470.7 9.8 %unpack_some.1 = (f32[3,2048,512]{2,1,0:T(8,128)}, f32[512,2048]{1,0:T(8,128)}) custom-call(s32[7]{0:T(128)} %stack.121.order_ref, bf16[1056,512]{1,0:T(8,128)(2,1)} %join_own.1.refs_20_.refs_21_.refs_0_, bf16[1056,512]{1,0:T(8,128)(2,1)} %get-tuple-element.106.refs_20_.refs_1_, bf16[1056,512]{1,0:T(8,128)(2,1)} %get-tuple-element.107.refs_21_.refs_2_, ...), custom_call_target="tpu_custom_call" | custom-call | bytes 5505024 | tf_op jit(solution)/shard_map/unpack_some/pallas_call | solution.py:475
  482.5 15.1 %weight_gradients_3_more.1 = (f32[4,2048,512]{2,1,0:T(8,128)}, f32[4,512,2048]{2,1,0:T(8,128)}) custom-call(bf16[1040,1024]{1,0:T(8,128)(2,1)} %get-tuple-element.82.refs_22_.refs_0_.refs_2_, bf16[1040,1024]{1,0:T(8,128)(2,1)} %collective-permute-done.19.refs_22_.refs_1_.refs_3_, ...), custom_call_target="tpu_custom_call", output_to_operand_aliasing={{0}: (18, {}), {1}: (19, {})} | custom-call | flops 1342177280 | bytes 5505024 | tf_op jit(solution)/shard_map/weight_gradients_3_more/pallas_call | solution.py:438
  (303 shorter events, 160.6 us)
Async XLA Ops:
  81.5 48.5 %collective-permute-start.9 = (bf16[1040,1024]{1,0:T(8,128)(2,1)S(1)}, bf16[1040,1024]{1,0:T(8,128)(2,1)S(1)}, u32[]{:S(2)}, u32[]{:S(2)}) collective-permute-start(bf16[1040,1024]{1,0:T(8,128)(2,1)S(1)} %copy-done.4), channel_id=1, source_target_pairs={{0,8},{8,16},{16,24},{24,28},{28,20},{20,12},{12,4},{4,0},{1,9},{9... | collective-permute-start | bytes 6389768 | tf_op jit(solution)/shard_map/ppermute | solution.py:631
  83.3 48.2 %collective-permute-start.10 = (bf16[1040,1024]{1,0:T(8,128)(2,1)S(1)}, bf16[1040,1024]{1,0:T(8,128)(2,1)S(1)}, u32[]{:S(2)}, u32[]{:S(2)}) collective-permute-start(bf16[1040,1024]{1,0:T(8,128)(2,1)S(1)} %copy-done.4), channel_id=1, source_target_pairs={{8,0},{16,8},{24,16},{28,24},{20,28},{12,20},{4,12},{0,4},{9,1},{1... | collective-permute-start | bytes 6389768 | tf_op jit(solution)/shard_map/ppermute | solution.py:636
  132.8 49.1 %collective-permute-start.13 = (bf16[1040,1024]{1,0:T(8,128)(2,1)}, bf16[1040,1024]{1,0:T(8,128)(2,1)}, u32[]{:S(2)}, u32[]{:S(2)}) collective-permute-start(bf16[1040,1024]{1,0:T(8,128)(2,1)} %get-tuple-element.77.rest_0_.refs_4_.refs_6_), channel_id=1, source_target_pairs={{0,8},{8,16},{16,24},{24,28},{28,20},{20,12},{12,4},{4,0},{1,9},{9... | collective-permute-start | bytes 6389768 | tf_op jit(solution)/shard_map/ppermute | solution.py:631
  134.7 48.7 %collective-permute-start.14 = (bf16[1040,1024]{1,0:T(8,128)(2,1)}, bf16[1040,1024]{1,0:T(8,128)(2,1)S(1)}, u32[]{:S(2)}, u32[]{:S(2)}) collective-permute-start(bf16[1040,1024]{1,0:T(8,128)(2,1)} %get-tuple-element.78.rest_2_.refs_8_.refs_10_), channel_id=1, source_target_pairs={{8,0},{16,8},{24,16},{28,24},{20,28},{12,20},{4,12},{0,4},{9,1},{1... | collective-permute-start | bytes 6389768 | tf_op jit(solution)/shard_map/ppermute | solution.py:636
  184.7 42.3 %collective-permute-start.19 = (bf16[1040,1024]{1,0:T(8,128)(2,1)}, bf16[1040,1024]{1,0:T(8,128)(2,1)}, u32[]{:S(2)}, u32[]{:S(2)}) collective-permute-start(bf16[1040,1024]{1,0:T(8,128)(2,1)} %get-tuple-element.82.refs_22_.refs_0_.refs_2_), channel_id=1, source_target_pairs={{0,1},{1,0},{2,3},{3,2},{4,5},{5,4},{6,7},{7,6},{8,9},{9,8},{10,11... | collective-permute-start | bytes 6389768 | tf_op jit(solution)/shard_map/ppermute | solution.py:689
  188.1 30.5 %collective-permute-start.17 = (bf16[4,128,512]{2,1,0:T(8,128)(2,1)S(1)}, bf16[4,128,512]{2,1,0:T(8,128)(2,1)}, u32[]{:S(2)}, u32[]{:S(2)}) collective-permute-start(bf16[4,128,512]{2,1,0:T(8,128)(2,1)S(1)} %get-tuple-element.134.refs_18_), channel_id=1, source_target_pairs={{0,8},{8,16},{16,24},{24,28},{28,20},{20,12},{12,4},{4,0},{1,9},{9... | collective-permute-start | bytes 1572872 | tf_op jit(solution)/shard_map/ppermute | solution.py:631
  192.1 109.0 %collective-permute-start.25 = (bf16[1040,1024]{1,0:T(8,128)(2,1)}, bf16[1040,1024]{1,0:T(8,128)(2,1)}, u32[]{:S(2)}, u32[]{:S(2)}) collective-permute-start(bf16[1040,1024]{1,0:T(8,128)(2,1)} %get-tuple-element.81.refs_12_.refs_14_.refs_20_), channel_id=1, source_target_pairs={{0,8},{8,16},{16,24},{24,28},{28,20},{20,12},{12,4},{4,0},{1,9},{9... | collective-permute-start | bytes 6389768 | tf_op jit(solution)/shard_map/ppermute | solution.py:631
  193.7 107.5 %collective-permute-start.26 = (bf16[1040,1024]{1,0:T(8,128)(2,1)}, bf16[1040,1024]{1,0:T(8,128)(2,1)S(1)}, u32[]{:S(2)}, u32[]{:S(2)}) collective-permute-start(bf16[1040,1024]{1,0:T(8,128)(2,1)} %get-tuple-element.82.refs_22_.refs_0_.refs_2_), channel_id=1, source_target_pairs={{8,0},{16,8},{24,16},{28,24},{20,28},{12,20},{4,12},{0,4},{9,1},{1... | collective-permute-start | bytes 6389768 | tf_op jit(solution)/shard_map/ppermute | solution.py:636
  223.4 46.5 %collective-permute-start.21 = (bf16[4,256,512]{2,1,0:T(8,128)(2,1)}, bf16[4,256,512]{2,1,0:T(8,128)(2,1)S(1)}, u32[]{:S(2)}, u32[]{:S(2)}) collective-permute-start(bf16[4,256,512]{2,1,0:T(8,128)(2,1)} %get-tuple-element.85.refs_20_), channel_id=1, source_target_pairs={{0,8},{8,16},{16,24},{24,28},{28,20},{20,12},{12,4},{4,0},{1,9},{9... | collective-permute-start | bytes 3145736 | tf_op jit(solution)/shard_map/ppermute | solution.py:631
  225.0 46.4 %collective-permute-start.22 = (bf16[4,256,512]{2,1,0:T(8,128)(2,1)}, bf16[4,256,512]{2,1,0:T(8,128)(2,1)}, u32[]{:S(2)}, u32[]{:S(2)}) collective-permute-start(bf16[4,256,512]{2,1,0:T(8,128)(2,1)} %get-tuple-element.86.refs_21_), channel_id=1, source_target_pairs={{8,0},{16,8},{24,16},{28,24},{20,28},{12,20},{4,12},{0,4},{9,1},{1... | collective-permute-start | bytes 3145736 | tf_op jit(solution)/shard_map/ppermute | solution.py:636
  227.0 51.2 %collective-permute-start.16 = (bf16[256,2048]{1,0:T(8,128)(2,1)}, bf16[256,2048]{1,0:T(8,128)(2,1)}, u32[]{:S(2)}, u32[]{:S(2)}) collective-permute-start(bf16[256,2048]{1,0:T(8,128)(2,1)} %after.16), channel_id=1, source_target_pairs={{0,1},{1,0},{2,3},{3,2},{4,5},{5,4},{6,7},{7,6},{8,9},{9,8},{10,11... | collective-permute-start | bytes 3145736 | tf_op jit(solution)/shard_map/ppermute | solution.py:689
  276.2 34.4 %collective-permute-start.23 = (bf16[4,256,512]{2,1,0:T(8,128)(2,1)}, bf16[4,256,512]{2,1,0:T(8,128)(2,1)S(1)}, u32[]{:S(2)}, u32[]{:S(2)}) collective-permute-start(bf16[4,256,512]{2,1,0:T(8,128)(2,1)} %get-tuple-element.89.refs_20_), channel_id=1, source_target_pairs={{0,8},{8,16},{16,24},{24,28},{28,20},{20,12},{12,4},{4,0},{1,9},{9... | collective-permute-start | bytes 3145736 | tf_op jit(solution)/shard_map/ppermute | solution.py:631
  277.7 32.8 %collective-permute-start.24 = (bf16[4,256,512]{2,1,0:T(8,128)(2,1)}, bf16[4,256,512]{2,1,0:T(8,128)(2,1)}, u32[]{:S(2)}, u32[]{:S(2)}) collective-permute-start(bf16[4,256,512]{2,1,0:T(8,128)(2,1)} %get-tuple-element.90.refs_21_), channel_id=1, source_target_pairs={{8,0},{16,8},{24,16},{28,24},{20,28},{12,20},{4,12},{0,4},{9,1},{1... | collective-permute-start | bytes 3145736 | tf_op jit(solution)/shard_map/ppermute | solution.py:636
  282.3 36.2 %collective-permute-start.20 = (bf16[256,2048]{1,0:T(8,128)(2,1)}, bf16[256,2048]{1,0:T(8,128)(2,1)}, u32[]{:S(2)}, u32[]{:S(2)}) collective-permute-start(bf16[256,2048]{1,0:T(8,128)(2,1)} %add_rows.6), channel_id=1, source_target_pairs={{0,2},{1,3},{2,0},{3,1},{4,6},{5,7},{6,4},{7,5},{8,10},{9,11},{10,... | collective-permute-start | bytes 3145736 | tf_op jit(solution)/shard_map/ppermute | solution.py:696
  304.9 40.7 %collective-permute-start.28 = (bf16[512,1024]{1,0:T(8,128)(2,1)}, bf16[512,1024]{1,0:T(8,128)(2,1)S(1)}, u32[]{:S(2)}, u32[]{:S(2)}) collective-permute-start(bf16[512,1024]{1,0:T(8,128)(2,1)} %slice.54), channel_id=1, source_target_pairs={{0,8},{8,16},{16,24},{24,28},{28,20},{20,12},{12,4},{4,0},{1,9},{9... | collective-permute-start | bytes 3145736 | tf_op jit(solution)/shard_map/ppermute | solution.py:631
  308.7 37.0 %collective-permute-start.29 = (bf16[528,1024]{1,0:T(8,128)(2,1)}, bf16[528,1024]{1,0:T(8,128)(2,1)S(1)}, u32[]{:S(2)}, u32[]{:S(2)}) collective-permute-start(bf16[528,1024]{1,0:T(8,128)(2,1)} %slice.55), channel_id=1, source_target_pairs={{8,0},{16,8},{24,16},{28,24},{20,28},{12,20},{4,12},{0,4},{9,1},{1... | collective-permute-start | bytes 3244040 | tf_op jit(solution)/shard_map/ppermute | solution.py:636
  316.4 37.5 %collective-permute-start.34 = (bf16[4,256,512]{2,1,0:T(8,128)(2,1)}, bf16[4,256,512]{2,1,0:T(8,128)(2,1)}, u32[]{:S(2)}, u32[]{:S(2)}) collective-permute-start(bf16[4,256,512]{2,1,0:T(8,128)(2,1)} %get-tuple-element.93.refs_20_), channel_id=1, source_target_pairs={{0,8},{8,16},{16,24},{24,28},{28,20},{20,12},{12,4},{4,0},{1,9},{9... | collective-permute-start | bytes 3145736 | tf_op jit(solution)/shard_map/ppermute | solution.py:631
  317.9 41.5 %collective-permute-start.35 = (bf16[4,256,512]{2,1,0:T(8,128)(2,1)}, bf16[4,256,512]{2,1,0:T(8,128)(2,1)}, u32[]{:S(2)}, u32[]{:S(2)}) collective-permute-start(bf16[4,256,512]{2,1,0:T(8,128)(2,1)} %get-tuple-element.94.refs_21_), channel_id=1, source_target_pairs={{8,0},{16,8},{24,16},{28,24},{20,28},{12,20},{4,12},{0,4},{9,1},{1... | collective-permute-start | bytes 3145736 | tf_op jit(solution)/shard_map/ppermute | solution.py:636
  359.4 38.1 %collective-permute-start.27 = (bf16[256,2048]{1,0:T(8,128)(2,1)}, bf16[256,2048]{1,0:T(8,128)(2,1)}, u32[]{:S(2)}, u32[]{:S(2)}) collective-permute-start(bf16[256,2048]{1,0:T(8,128)(2,1)} %after.19), channel_id=1, source_target_pairs={{0,1},{1,0},{2,3},{3,2},{4,5},{5,4},{6,7},{7,6},{8,9},{9,8},{10,11... | collective-permute-start | bytes 3145736 | tf_op jit(solution)/shard_map/ppermute | solution.py:689
  365.7 33.3 %collective-permute-start.38 = (bf16[1056,512]{1,0:T(8,128)(2,1)}, bf16[1056,512]{1,0:T(8,128)(2,1)}, u32[]{:S(2)}, u32[]{:S(2)}) collective-permute-start(bf16[1056,512]{1,0:T(8,128)(2,1)} %join_own.1.refs_20_.refs_21_.refs_0_), channel_id=1, source_target_pairs={{0,8},{8,16},{16,24},{24,28},{28,20},{20,12},{12,4},{4,0},{1,9},{9... | collective-permute-start | bytes 3244040 | tf_op jit(solution)/shard_map/ppermute | solution.py:631
  366.9 32.1 %collective-permute-start.39 = (bf16[1056,512]{1,0:T(8,128)(2,1)}, bf16[1056,512]{1,0:T(8,128)(2,1)}, u32[]{:S(2)}, u32[]{:S(2)}) collective-permute-start(bf16[1056,512]{1,0:T(8,128)(2,1)} %join_own.1.refs_20_.refs_21_.refs_0_), channel_id=1, source_target_pairs={{8,0},{16,8},{24,16},{28,24},{20,28},{12,20},{4,12},{0,4},{9,1},{1... | collective-permute-start | bytes 3244040 | tf_op jit(solution)/shard_map/ppermute | solution.py:636
  399.0 36.8 %collective-permute-start.41 = (bf16[1056,512]{1,0:T(8,128)(2,1)}, bf16[1056,512]{1,0:T(8,128)(2,1)S(1)}, u32[]{:S(2)}, u32[]{:S(2)}) collective-permute-start(bf16[1056,512]{1,0:T(8,128)(2,1)} %get-tuple-element.106.refs_20_.refs_1_), channel_id=1, source_target_pairs={{0,8},{8,16},{16,24},{24,28},{28,20},{20,12},{12,4},{4,0},{1,9},{9... | collective-permute-start | bytes 3244040 | tf_op jit(solution)/shard_map/ppermute | solution.py:631
  400.2 35.6 %collective-permute-start.42 = (bf16[1056,512]{1,0:T(8,128)(2,1)}, bf16[1056,512]{1,0:T(8,128)(2,1)S(1)}, u32[]{:S(2)}, u32[]{:S(2)}) collective-permute-start(bf16[1056,512]{1,0:T(8,128)(2,1)} %get-tuple-element.107.refs_21_.refs_2_), channel_id=1, source_target_pairs={{8,0},{16,8},{24,16},{28,24},{20,28},{12,20},{4,12},{0,4},{9,1},{1... | collective-permute-start | bytes 3244040 | tf_op jit(solution)/shard_map/ppermute | solution.py:636
  466.2 43.1 %collective-permute-start.43 = (bf16[256,2048]{1,0:T(8,128)(2,1)S(1)}, bf16[256,2048]{1,0:T(8,128)(2,1)S(1)}, u32[]{:S(2)}, u32[]{:S(2)}) collective-permute-start(bf16[256,2048]{1,0:T(8,128)(2,1)S(1)} %add_convert_fusion), channel_id=1, source_target_pairs={{0,1},{1,0},{2,3},{3,2},{4,5},{5,4},{6,7},{7,6},{8,9},{9,8},{10,11... | collective-permute-start | bytes 3145736 | tf_op jit(solution)/shard_map/ppermute | solution.py:689
  (76 other events, 683.5 us)

commit v5 on v4

--- a/solution.py
+++ b/solution.py
@@ -746,6 +746,9 @@
 
     cot_sorted = dot(sort_rows.astype(BF16), cotangent).astype(BF16)
 
+    cot_own = part_of(cot_sorted, core, 1)
+    cot_first = ring.to_right(cot_own), ring.to_left(cot_own)
+
     w3 = jnp.transpose(w_qkv, (1, 0, 2))
     cos, sin = rotary_table(length, HEAD)
     part_mine, part_other, normed_low, qkv, lse, mixed = attend(tokens, gain_first[None, :], w3, cos, sin, w_out)
@@ -772,19 +775,19 @@
     gate_3 = low(gate_sorted - gate_1.astype(F32) - gate_2.astype(F32))
     aux = jnp.stack([gate_1, gate_2, gate_3, bucket_sorted.astype(BF16)] + [jnp.zeros_like(gate_1)] * (AUX - 4))
     aux = jnp.pad(aux, ((0, 0), (0, model // 2 - length)))
-    both = jnp.concatenate([part_of(cot_sorted, core, 1), part_of(sent_sorted, core, 1), aux], 0)
+    sent_own = jnp.concatenate([part_of(sent_sorted, core, 1), aux], 0)
     height = length
-    blocks = [((both, 0), (part_of(cot_sorted, 1 - core, 1), 0), (both, height), (part_of(sent_sorted, 1 - core, 1), 0))]
+    blocks = [((cot_own, 0), (part_of(cot_sorted, 1 - core, 1), 0), (sent_own, 0), (part_of(sent_sorted, 1 - core, 1), 0))]
 
     def block(mine, other):
         return (mine, 0), (other, 0), (mine, height), (other, height)
 
-    r, l = ring.to_right(both), ring.to_left(both)
+    sent_first = ring.to_right(sent_own), ring.to_left(sent_own)
 
     wide = lambda x: jnp.broadcast_to(x[:, None], (length, 128))
     gsent_mine, gsent_other, act = own_grad(
         sent_sorted, cot_sorted, wide(bucket_sorted), wide(gate_sorted), unsort_low, w_up, w_down, row_bounds,
-        (both,))
+        cot_first + (sent_own,))
     gsent_rows = add_rows([gsent_mine, core_swap(gsent_other)])
     grad_sent = sum_over_x(gsent_rows).astype(BF16).astype(F32)
     ffn_part, ggate_part = own_forward(
@@ -793,7 +796,11 @@
     met = []
 
     def forward(arrived, deps):
-        r, l = after(arrived, deps)
+        if len(arrived) == 4:
+            cot_r, cot_l, sent_r, sent_l = after(arrived, deps)
+            r, l = jnp.concatenate([cot_r, sent_r], 0), jnp.concatenate([cot_l, sent_l], 0)
+        else:
+            r, l = after(arrived, deps)
         if len(met) < far:
             met.extend([(r, core_swap(r)), (l, core_swap(l))])
         else:
@@ -802,7 +809,7 @@
             return ring.to_right(r), ring.to_left(l)
         return ring.to_right(r[:height]), ring.to_left(l[height:])
 
-    r, l = forward((r, l), (ffn_part,))
+    r, l = forward(cot_first + sent_first, (ffn_part,))
     ggate_part = jnp.sum(jnp.where(sort_rows, ggate_part[:, :1], 0.0), 0)
     grad_gate = ggate_part + core_swap(ggate_part)
     grad_gate = sum_over_x(own_rows(grad_gate))
@@ -855,7 +862,7 @@
     carried = ()
     calls = [(level, rows, True) for level, rows in enumerate(row_bounds)]
     later = [block(*x) for x in met[far - 1:]]
-    grad_first = ffn_rows = extra = None
+    extra = None
     slots = [0] + list(range(2, buckets)) + [1]
     for slot_at, level in enumerate(slots):
         rows = row_bounds[level]
@@ -881,11 +888,10 @@
         if slot_at == 3:
             small_other, = after([small_other], (carried[0],))
             extra = low(small + small_other).reshape(-1, w3.shape[2])
-            tokens_half, = after([tokens_half], (carried[0],))
-            tokens_other = core_swap(tokens_half)
-            r, l, *held = after([r, l] + [x for x, _ in met[far:]], (carried[0],))
         arrived, sending = advance(step, arrived, (carried[0],))
         step += 1
+        if slot_at == 3:
+            r, l, *held = after([r, l] + [x for x, _ in met[far:]], (carried[0], sending[0]))
         if slot_at == 0:
             sending = sending + tuple(x for _, x in met[far - 1:])
         if slot_at == 2:
@@ -902,27 +908,31 @@
             unpacked = unpack(order[:-1], chunks[:-1], size, devices_dp)
             sending = sending + (unpacked[0],)
         carried = weight_gradients(level, rows, length, later, w_up, w_down, tuple(carried), False, sending)
+        ready = ()
         if level == 0:
-            ffn_other, tokens_other = after([other_rows(ffn_part), tokens_other], (carried[0],))
-            ffn_other = core_swap(ffn_other)
+            others = [core_swap(x) for x in after([tokens_half, other_rows(ffn_part)], (carried[0],))]
         if level == 1:
-            ffn_sum = add_rows([own_rows(ffn_part), ffn_other], (carried[0],))
+            others = after(others, (carried[0],))
+            grad_tokens = joined(tokens_half, others[0])
+            ffn_sum = add_rows([own_rows(ffn_part), others[1]])
+            ready = (grad_tokens, ffn_sum)
         if level == 2:
             ffn_rows = sum_over_x(ffn_sum, (carried[0],)).astype(BF16).astype(F32)
             output_half = (resid + gate[:, None] * ffn_rows).astype(BF16)
             output_other = core_swap(output_half)
+            ready = (output_half,)
         if level == 3:
             output_other, = after([output_other], (carried[0],))
+            output = joined(output_half, output_other)
         sending = ()
         if step < steps:
             arrived, sending = advance(step, arrived, (carried[0],))
             step += 1
+        sending = sending + ready
     while step < steps:
         arrived, sending = advance(step, arrived, ())
         step += 1
     grad_up, grad_down = carried
-    output = joined(output_half, output_other)
-    grad_tokens = joined(tokens_half, tokens_other)
     order = jnp.stack(ring.indices()).astype(jnp.int32)
     size = model // devices_dp
     if devices_dp != 8:

time: 521 us -> 516 us (level)
  waiting for transfers between devices: 93.3 us -> 82.1 us
    ppermute x19, waiting for transfers between devices: 14.8 us -> 7.89 us  [core_swap(): return lax.ppermute(x, 'mp', [(i, i ^ 1) for i in range(n)])]
    ppermute x12 -> x13, waiting for transfers between devices: 44.9 us -> 38.5 us  [to_right(): out = lax.ppermute(x, 'dp', self.right)]
    ppermute x12 -> x13, starting transfers between devices: 17.8 us -> 21.1 us  [to_right(): out = lax.ppermute(x, 'dp', self.right)]
    unnamed x114 -> x133, local copies, waits for them, and re-layouts: 31.9 us -> 34.7 us
  transfers between devices with their start and end apart: 48 -> 50, of which waited for: 14 -> 13; matrix products, arithmetic and copies ran while one was open for 13% -> 14% of each run, Pallas kernels for 46% -> 47%
where the time goes in v5:
time: 516 us; the launch traced here: 508 us
  Pallas kernels  276 us (53%)
  waiting for transfers between devices  82.1 us (16%)
  local copies, waits for them, and re-layouts  59.8 us (12%)
  starting transfers between devices  38.3 us (7%)
  other arithmetic  30.6 us (6%)
  matrix products  13 us (3%)
  between operations  8.96 us (2%)
    pallas_call x8, Pallas kernels, weight_gradients(): pl.pallas_call(partial(weight_kernel, level=level, rows=rows, group=group...  162 us
    ppermute x13, waiting for transfers between devices, to_right(): out = lax.ppermute(x, 'dp', self.right)  38.5 us
    unnamed x133, local copies, waits for them, and re-layouts  34.7 us
    ppermute x5, waiting for transfers between devices, sum_over_x(): lax.ppermute(x, 'mp', [(i, (i + 2 * k) % (2 * n)) for i in range(2 * n)])  26.1 us
    pallas_call x1, Pallas kernels, attend_back(): pl.pallas_call(partial(attend_back_kernel, heads=heads, steps=steps, deps...  23.6 us
    ppermute x13, starting transfers between devices, to_right(): out = lax.ppermute(x, 'dp', self.right)  21.1 us
    pallas_call x1, Pallas kernels, own_grad(): pl.pallas_call(partial(own_grad_kernel, row_bounds=tuple(row_bounds), dep...  17.6 us
    pallas_call x1, Pallas kernels, attend(): pl.pallas_call(partial(attend_kernel, heads=heads, steps=steps), grid=(st...  15.7 us
  transfers between devices with their start and end apart: 50, of which 13 were waited for; matrix products, arithmetic and copies ran while one was open for 14% of the time, Pallas kernels for 47%

profile of v5, /device:TPU:0, one launch (start us, length us, event | category | flops | bytes accessed | tf_op | source)
XLA Modules:
  0.0 508.4 jit_solution(17514829689395585196)
XLA Ops:
  2.6 15.7 %attend.1 = (bf16[256,2048]{1,0:T(8,128)(2,1)}, bf16[256,2048]{1,0:T(8,128)(2,1)}, bf16[512,2048]{1,0:T(8,128)(2,1)}, bf16[3,512,512]{2,1,0:T(8,128)(2,1)}, f32[...) custom-call(bf16[512,2048]{1,0:T(8,128)(2,1)} %x_ref.1, f32[1,2048]{1,0:T(1,128)} %bitcast.62, ...), custom_call_target="tpu_custom_call" | custom-call | flops 1207959552 | bytes 3145728 | tf_op jit(solution)/shard_map/attend/pallas_call | solution.py:102
  37.0 15.6 %collective-permute-done.1 = bf16[256,2048]{1,0:T(8,128)(2,1)} collective-permute-done((bf16[256,2048]{1,0:T(8,128)(2,1)}, bf16[256,2048]{1,0:T(8,128)(2,1)}, u32[]{:S(2)}, u32[]{:S(2)}) %collective-permute-start.1) | collective-permute-done | bytes 1048608 | tf_op jit(solution)/shard_map/ppermute | solution.py:696
  67.7 17.6 %own_grad.1 = (bf16[256,2048]{1,0:T(8,128)(2,1)}, bf16[256,2048]{1,0:T(8,128)(2,1)}, bf16[4,512,512]{2,1,0:T(8,128)(2,1)}) custom-call(bf16[512,2048]{1,0:T(8,128)(2,1)} %copy-done.29, bf16[512,2048]{1,0:T(8,128)(2,1)} %copy-done.12, s32[512,128]{1,0:T(8,128)} %broadcast_in_dim.61.bucket_ref, f32[512,128]{1,0:T(8,128)} %broadcast_in_dim.64.gate_ref, ...), custom_call_target="tpu_custom_call" | custom-call | flops 2315255808 | bytes 5767168 | tf_op jit(solution)/shard_map/own_grad/pallas_call | solution.py:248
  89.6 4.1 add_rows.5.rest_0_
  95.4 10.1 %own_forward.1 = (bf16[512,2048]{1,0:T(8,128)(2,1)}, f32[512,128]{1,0:T(8,128)}) custom-call(bf16[4,512,512]{2,1,0:T(8,128)(2,1)} %get-tuple-element.72.act_ref, bf16[512,2048]{1,0:T(8,128)(2,1)} %copy-done.12, bf16[512,512]{1,0:T(8,128)(2,1)} %fusion.26.unsort_ref, bf16[4,512,2048]{2,1,0:T(8,128)(2,1)} %refs_17_.15, bf16[256,2048]{1,0:T(8,128)(2,1)} %add_rows.5.rest_0_), custom_call_target="tpu_custom_call" | custom-call | flops 771751936 | bytes 3670016 | tf_op jit(solution)/shard_map/own_forward/pallas_call | solution.py:288
  108.4 10.5 %collective-permute-done.9 = f32[256]{0:T(256)S(1)} collective-permute-done((f32[256]{0:T(256)S(1)}, f32[256]{0:T(256)S(1)}, u32[]{:S(2)}, u32[]{:S(2)}) %collective-permute-start.9) | collective-permute-done | bytes 1056 | tf_op jit(solution)/shard_map/ppermute | solution.py:696
  137.9 23.6 %attend_back.1 = (bf16[4,2048,512]{2,1,0:T(8,128)(2,1)}, bf16[512,2048]{1,0:T(8,128)(2,1)}) custom-call(bf16[512,2048]{1,0:T(8,128)(2,1)} %pad_maximum_fusion.ga_ref, bf16[512,2048]{1,0:T(8,128)(2,1)} %get-tuple-element.77.normed_ref, bf16[3,512,512]{2,1,0:T(8,128)(2,1)} %get-tuple-element.78.qkv_ref, f32[4,512,128]{2,1,0:T(8,128)} %get-tuple-element.79.lse_ref, ...), custom_call_target="tpu_custom_call" | custom-call | flops 2483027968 | bytes 6291456 | tf_op jit(solution)/shard_map/attend_back/pallas_call | solution.py:195
  161.5 11.4 %collective-permute-done.15.refs_0_ = bf16[1040,1024]{1,0:T(8,128)(2,1)} collective-permute-done((bf16[1040,1024]{1,0:T(8,128)(2,1)}, bf16[1040,1024]{1,0:T(8,128)(2,1)}, u32[]{:S(2)}, u32[]{:S(2)}) %collective-permute-start.15) | collective-permute-done | bytes 2129952 | tf_op jit(solution)/shard_map/ppermute | solution.py:631
  187.5 24.4 %weight_gradients_0.1 = (f32[4,2048,512]{2,1,0:T(8,128)}, f32[4,512,2048]{2,1,0:T(8,128)}) custom-call(bf16[512,1024]{1,0:T(8,128)(2,1)} %copy-done.10, bf16[512,1024]{1,0:T(8,128)(2,1)} %get-tuple-element.151.refs_1_, bf16[528,1024]{1,0:T(8,128)(2,1)} %fusion.20.rest_2_.refs_2_, bf16[512,1024]{1,0:T(8,128)(2,1)} %get-tuple-element.149.refs_3_, ...), custom_call_target="tpu_custom_call" | custom-call | flops 4294967296 | bytes 8388608 | tf_op jit(solution)/shard_map/weight_gradients_0/pallas_call | solution.py:438
  212.0 4.7 join.3
  222.3 18.6 %weight_gradients_2.1 = (f32[4,2048,512]{2,1,0:T(8,128)}, f32[4,512,2048]{2,1,0:T(8,128)}) custom-call(bf16[512,1024]{1,0:T(8,128)(2,1)} %copy-done.10, bf16[512,1024]{1,0:T(8,128)(2,1)} %get-tuple-element.151.refs_1_, bf16[528,1024]{1,0:T(8,128)(2,1)} %fusion.20.rest_2_.refs_2_, ...), custom_call_target="tpu_custom_call", output_to_operand_aliasing={{0}: (18, {}), {1}: (19, {})} | custom-call | flops 2684354560 | bytes 6815744 | tf_op jit(solution)/shard_map/weight_gradients_2/pallas_call | solution.py:438
  241.0 22.3 %collective-permute-done.23.right_ref = bf16[4,256,512]{2,1,0:T(8,128)(2,1)S(1)} collective-permute-done((bf16[4,256,512]{2,1,0:T(8,128)(2,1)}, bf16[4,256,512]{2,1,0:T(8,128)(2,1)S(1)}, u32[]{:S(2)}, u32[]{:S(2)}) %collective-permute-start.23) | collective-permute-done | bytes 1048608 | tf_op jit(solution)/shard_map/ppermute | solution.py:631
  264.6 4.9 join.4
  281.7 13.3 %weight_gradients_3.1 = (f32[4,2048,512]{2,1,0:T(8,128)}, f32[4,512,2048]{2,1,0:T(8,128)}) custom-call(bf16[512,1024]{1,0:T(8,128)(2,1)} %copy-done.10, bf16[512,1024]{1,0:T(8,128)(2,1)} %get-tuple-element.151.refs_1_, bf16[528,1024]{1,0:T(8,128)(2,1)} %fusion.20.rest_2_.refs_2_, ...), custom_call_target="tpu_custom_call", output_to_operand_aliasing={{0}: (18, {}), {1}: (19, {})} | custom-call | flops 1342177280 | bytes 5505024 | tf_op jit(solution)/shard_map/weight_gradients_3/pallas_call | solution.py:438
  303.0 4.9 join.5
  313.5 23.8 %weight_gradients_1.1 = (f32[4,2048,512]{2,1,0:T(8,128)}, f32[4,512,2048]{2,1,0:T(8,128)}) custom-call(bf16[512,1024]{1,0:T(8,128)(2,1)} %copy-done.10, bf16[512,1024]{1,0:T(8,128)(2,1)} %get-tuple-element.151.refs_1_, bf16[528,1024]{1,0:T(8,128)(2,1)} %fusion.20.rest_2_.refs_2_, ...), custom_call_target="tpu_custom_call", output_to_operand_aliasing={{0}: (18, {}), {1}: (19, {})} | custom-call | flops 4026531840 | bytes 8126464 | tf_op jit(solution)/shard_map/weight_gradients_1/pallas_call | solution.py:438
  339.5 4.9 collective-permute-done.31.right_ref
  344.4 4.3 collective-permute-done.32.left_ref
  348.7 4.0 join_own.1.refs_5_.refs_20_.refs_21_.refs_0_
  372.4 24.3 %weight_gradients_0_more.1 = (f32[4,2048,512]{2,1,0:T(8,128)}, f32[4,512,2048]{2,1,0:T(8,128)}) custom-call(bf16[1040,1024]{1,0:T(8,128)(2,1)} %get-tuple-element.88.refs_22_.refs_0_.refs_2_, bf16[1040,1024]{1,0:T(8,128)(2,1)} %collective-permute-done.21.refs_22_.refs_1_.refs_3_, ...), custom_call_target="tpu_custom_call", output_to_operand_aliasing={{0}: (18, {}), {1}: (19, {})} | custom-call | flops 4294967296 | bytes 8388608 | tf_op jit(solution)/shard_map/weight_gradients_0_more/pallas_call | solution.py:438
  400.2 23.8 %weight_gradients_1_more.1 = (f32[4,2048,512]{2,1,0:T(8,128)}, f32[4,512,2048]{2,1,0:T(8,128)}) custom-call(bf16[1040,1024]{1,0:T(8,128)(2,1)} %get-tuple-element.88.refs_22_.refs_0_.refs_2_, bf16[1040,1024]{1,0:T(8,128)(2,1)} %collective-permute-done.21.refs_22_.refs_1_.refs_3_, ...), custom_call_target="tpu_custom_call", output_to_operand_aliasing={{0}: (18, {}), {1}: (19, {})} | custom-call | flops 4026531840 | bytes 8126464 | tf_op jit(solution)/shard_map/weight_gradients_1_more/pallas_call | solution.py:438
  438.4 19.0 %weight_gradients_2_more.1 = (f32[4,2048,512]{2,1,0:T(8,128)}, f32[4,512,2048]{2,1,0:T(8,128)}) custom-call(bf16[1040,1024]{1,0:T(8,128)(2,1)} %get-tuple-element.88.refs_22_.refs_0_.refs_2_, bf16[1040,1024]{1,0:T(8,128)(2,1)} %collective-permute-done.21.refs_22_.refs_1_.refs_3_, ...), custom_call_target="tpu_custom_call", output_to_operand_aliasing={{0}: (18, {}), {1}: (19, {})} | custom-call | flops 2684354560 | bytes 6815744 | tf_op jit(solution)/shard_map/weight_gradients_2_more/pallas_call | solution.py:438
  466.0 9.8 %unpack_some.1 = (f32[3,2048,512]{2,1,0:T(8,128)}, f32[512,2048]{1,0:T(8,128)}) custom-call(s32[7]{0:T(128)} %stack.121.order_ref, bf16[1056,512]{1,0:T(8,128)(2,1)} %join_own.1.refs_5_.refs_20_.refs_21_.refs_0_, bf16[1056,512]{1,0:T(8,128)(2,1)} %get-tuple-element.113.refs_20_.refs_1_, bf16[1056,512]{1,0:T(8,128)(2,1)} %get-tuple-element.114.refs_21_.refs_2_, ...), custom_call_target="tpu_custom_call" | custom-call | bytes 5505024 | tf_op jit(solution)/shard_map/unpack_some/pallas_call | solution.py:475
  477.9 15.1 %weight_gradients_3_more.1 = (f32[4,2048,512]{2,1,0:T(8,128)}, f32[4,512,2048]{2,1,0:T(8,128)}) custom-call(bf16[1040,1024]{1,0:T(8,128)(2,1)} %get-tuple-element.88.refs_22_.refs_0_.refs_2_, bf16[1040,1024]{1,0:T(8,128)(2,1)} %collective-permute-done.21.refs_22_.refs_1_.refs_3_, ...), custom_call_target="tpu_custom_call", output_to_operand_aliasing={{0}: (18, {}), {1}: (19, {})} | custom-call | flops 1342177280 | bytes 5505024 | tf_op jit(solution)/shard_map/weight_gradients_3_more/pallas_call | solution.py:438
  (329 shorter events, 168.8 us)
Async XLA Ops:
  33.6 32.2 %collective-permute-start.4 = (bf16[512,1024]{1,0:T(8,128)(2,1)S(1)}, bf16[512,1024]{1,0:T(8,128)(2,1)S(1)}, u32[]{:S(2)}, u32[]{:S(2)}) collective-permute-start(bf16[512,1024]{1,0:T(8,128)(2,1)S(1)} %get-tuple-element.152.refs_0_), channel_id=1, source_target_pairs={{0,8},{8,16},{16,24},{24,28},{28,20},{20,12},{12,4},{4,0},{1,9},{9... | collective-permute-start | bytes 3145736 | tf_op jit(solution)/shard_map/ppermute | solution.py:631
  85.6 33.3 %collective-permute-start.11 = (bf16[528,1024]{1,0:T(8,128)(2,1)S(1)}, bf16[528,1024]{1,0:T(8,128)(2,1)S(1)}, u32[]{:S(2)}, u32[]{:S(2)}) collective-permute-start(bf16[528,1024]{1,0:T(8,128)(2,1)S(1)} %copy-done.8), channel_id=1, source_target_pairs={{0,8},{8,16},{16,24},{24,28},{28,20},{20,12},{12,4},{4,0},{1,9},{9... | collective-permute-start | bytes 3244040 | tf_op jit(solution)/shard_map/ppermute | solution.py:631
  87.4 31.5 %collective-permute-start.12 = (bf16[528,1024]{1,0:T(8,128)(2,1)S(1)}, bf16[528,1024]{1,0:T(8,128)(2,1)S(1)}, u32[]{:S(2)}, u32[]{:S(2)}) collective-permute-start(bf16[528,1024]{1,0:T(8,128)(2,1)S(1)} %copy-done.8), channel_id=1, source_target_pairs={{8,0},{16,8},{24,16},{28,24},{20,28},{12,20},{4,12},{0,4},{9,1},{1... | collective-permute-start | bytes 3244040 | tf_op jit(solution)/shard_map/ppermute | solution.py:636
  93.6 34.5 %collective-permute-start.7 = (bf16[256,2048]{1,0:T(8,128)(2,1)}, bf16[256,2048]{1,0:T(8,128)(2,1)S(1)}, u32[]{:S(2)}, u32[]{:S(2)}) collective-permute-start(bf16[256,2048]{1,0:T(8,128)(2,1)} %add_rows.5.rest_0_), channel_id=1, source_target_pairs={{0,2},{1,3},{2,0},{3,1},{4,6},{5,7},{6,4},{7,5},{8,10},{9,11},{10,... | collective-permute-start | bytes 3145736 | tf_op jit(solution)/shard_map/ppermute | solution.py:696
  123.8 49.1 %collective-permute-start.15 = (bf16[1040,1024]{1,0:T(8,128)(2,1)}, bf16[1040,1024]{1,0:T(8,128)(2,1)}, u32[]{:S(2)}, u32[]{:S(2)}) collective-permute-start(bf16[1040,1024]{1,0:T(8,128)(2,1)} %constant_dynamic-update-slice_fusion.rest_0_.refs_4_.refs_6_), channel_id=1, source_target_pairs={{0,8},{8,16},{16,24},{24,28},{28,20},{20,12},{12,4},{4,0},{1,9},{9... | collective-permute-start | bytes 6389768 | tf_op jit(solution)/shard_map/ppermute | solution.py:631
  127.9 48.7 %collective-permute-start.16 = (bf16[1040,1024]{1,0:T(8,128)(2,1)}, bf16[1040,1024]{1,0:T(8,128)(2,1)S(1)}, u32[]{:S(2)}, u32[]{:S(2)}) collective-permute-start(bf16[1040,1024]{1,0:T(8,128)(2,1)} %constant_dynamic-update-slice_fusion.2.rest_2_.refs_8_.refs_10_), channel_id=1, source_target_pairs={{8,0},{16,8},{24,16},{28,24},{20,28},{12,20},{4,12},{0,4},{9,1},{1... | collective-permute-start | bytes 6389768 | tf_op jit(solution)/shard_map/ppermute | solution.py:636
  178.0 42.3 %collective-permute-start.21 = (bf16[1040,1024]{1,0:T(8,128)(2,1)}, bf16[1040,1024]{1,0:T(8,128)(2,1)}, u32[]{:S(2)}, u32[]{:S(2)}) collective-permute-start(bf16[1040,1024]{1,0:T(8,128)(2,1)} %get-tuple-element.88.refs_22_.refs_0_.refs_2_), channel_id=1, source_target_pairs={{0,1},{1,0},{2,3},{3,2},{4,5},{5,4},{6,7},{7,6},{8,9},{9,8},{10,11... | collective-permute-start | bytes 6389768 | tf_op jit(solution)/shard_map/ppermute | solution.py:689
  185.4 109.6 %collective-permute-start.25 = (bf16[1040,1024]{1,0:T(8,128)(2,1)}, bf16[1040,1024]{1,0:T(8,128)(2,1)}, u32[]{:S(2)}, u32[]{:S(2)}) collective-permute-start(bf16[1040,1024]{1,0:T(8,128)(2,1)} %get-tuple-element.87.refs_12_.refs_14_.refs_20_), channel_id=1, source_target_pairs={{0,8},{8,16},{16,24},{24,28},{28,20},{20,12},{12,4},{4,0},{1,9},{9... | collective-permute-start | bytes 6389768 | tf_op jit(solution)/shard_map/ppermute | solution.py:631
  187.0 108.0 %collective-permute-start.26 = (bf16[1040,1024]{1,0:T(8,128)(2,1)}, bf16[1040,1024]{1,0:T(8,128)(2,1)S(1)}, u32[]{:S(2)}, u32[]{:S(2)}) collective-permute-start(bf16[1040,1024]{1,0:T(8,128)(2,1)} %get-tuple-element.88.refs_22_.refs_0_.refs_2_), channel_id=1, source_target_pairs={{8,0},{16,8},{24,16},{28,24},{20,28},{12,20},{4,12},{0,4},{9,1},{1... | collective-permute-start | bytes 6389768 | tf_op jit(solution)/shard_map/ppermute | solution.py:636
  216.7 46.5 %collective-permute-start.23 = (bf16[4,256,512]{2,1,0:T(8,128)(2,1)}, bf16[4,256,512]{2,1,0:T(8,128)(2,1)S(1)}, u32[]{:S(2)}, u32[]{:S(2)}) collective-permute-start(bf16[4,256,512]{2,1,0:T(8,128)(2,1)} %get-tuple-element.91.refs_20_), channel_id=1, source_target_pairs={{0,8},{8,16},{16,24},{24,28},{28,20},{20,12},{12,4},{4,0},{1,9},{9... | collective-permute-start | bytes 3145736 | tf_op jit(solution)/shard_map/ppermute | solution.py:631
  218.3 46.3 %collective-permute-start.24 = (bf16[4,256,512]{2,1,0:T(8,128)(2,1)}, bf16[4,256,512]{2,1,0:T(8,128)(2,1)}, u32[]{:S(2)}, u32[]{:S(2)}) collective-permute-start(bf16[4,256,512]{2,1,0:T(8,128)(2,1)} %get-tuple-element.92.refs_21_), channel_id=1, source_target_pairs={{8,0},{16,8},{24,16},{28,24},{20,28},{12,20},{4,12},{0,4},{9,1},{1... | collective-permute-start | bytes 3145736 | tf_op jit(solution)/shard_map/ppermute | solution.py:636
  220.3 51.2 %collective-permute-start.18 = (bf16[256,2048]{1,0:T(8,128)(2,1)}, bf16[256,2048]{1,0:T(8,128)(2,1)}, u32[]{:S(2)}, u32[]{:S(2)}) collective-permute-start(bf16[256,2048]{1,0:T(8,128)(2,1)} %after.16), channel_id=1, source_target_pairs={{0,1},{1,0},{2,3},{3,2},{4,5},{5,4},{6,7},{7,6},{8,9},{9,8},{10,11... | collective-permute-start | bytes 3145736 | tf_op jit(solution)/shard_map/ppermute | solution.py:689
  269.5 33.5 %collective-permute-start.29 = (bf16[4,256,512]{2,1,0:T(8,128)(2,1)}, bf16[4,256,512]{2,1,0:T(8,128)(2,1)}, u32[]{:S(2)}, u32[]{:S(2)}) collective-permute-start(bf16[4,256,512]{2,1,0:T(8,128)(2,1)} %get-tuple-element.95.refs_20_), channel_id=1, source_target_pairs={{0,8},{8,16},{16,24},{24,28},{28,20},{20,12},{12,4},{4,0},{1,9},{9... | collective-permute-start | bytes 3145736 | tf_op jit(solution)/shard_map/ppermute | solution.py:631
  271.1 31.9 %collective-permute-start.30 = (bf16[4,256,512]{2,1,0:T(8,128)(2,1)}, bf16[4,256,512]{2,1,0:T(8,128)(2,1)}, u32[]{:S(2)}, u32[]{:S(2)}) collective-permute-start(bf16[4,256,512]{2,1,0:T(8,128)(2,1)} %get-tuple-element.96.refs_21_), channel_id=1, source_target_pairs={{8,0},{16,8},{24,16},{28,24},{20,28},{12,20},{4,12},{0,4},{9,1},{1... | collective-permute-start | bytes 3145736 | tf_op jit(solution)/shard_map/ppermute | solution.py:636
  275.3 34.6 %collective-permute-start.22 = (bf16[256,2048]{1,0:T(8,128)(2,1)}, bf16[256,2048]{1,0:T(8,128)(2,1)}, u32[]{:S(2)}, u32[]{:S(2)}) collective-permute-start(bf16[256,2048]{1,0:T(8,128)(2,1)} %add_rows.6), channel_id=1, source_target_pairs={{0,2},{1,3},{2,0},{3,1},{4,6},{5,7},{6,4},{7,5},{8,10},{9,11},{10,... | collective-permute-start | bytes 3145736 | tf_op jit(solution)/shard_map/ppermute | solution.py:696
  298.7 54.0 %collective-permute-start.27 = (bf16[512,1024]{1,0:T(8,128)(2,1)}, bf16[512,1024]{1,0:T(8,128)(2,1)S(1)}, u32[]{:S(2)}, u32[]{:S(2)}) collective-permute-start(bf16[512,1024]{1,0:T(8,128)(2,1)} %slice.54), channel_id=1, source_target_pairs={{0,8},{8,16},{16,24},{24,28},{28,20},{20,12},{12,4},{4,0},{1,9},{9... | collective-permute-start | bytes 3145736 | tf_op jit(solution)/shard_map/ppermute | solution.py:631
  302.5 50.1 %collective-permute-start.28 = (bf16[528,1024]{1,0:T(8,128)(2,1)}, bf16[528,1024]{1,0:T(8,128)(2,1)S(1)}, u32[]{:S(2)}, u32[]{:S(2)}) collective-permute-start(bf16[528,1024]{1,0:T(8,128)(2,1)} %slice.55), channel_id=1, source_target_pairs={{8,0},{16,8},{24,16},{28,24},{20,28},{12,20},{4,12},{0,4},{9,1},{1... | collective-permute-start | bytes 3244040 | tf_op jit(solution)/shard_map/ppermute | solution.py:636
  307.9 36.5 %collective-permute-start.31 = (bf16[4,256,512]{2,1,0:T(8,128)(2,1)}, bf16[4,256,512]{2,1,0:T(8,128)(2,1)}, u32[]{:S(2)}, u32[]{:S(2)}) collective-permute-start(bf16[4,256,512]{2,1,0:T(8,128)(2,1)} %get-tuple-element.101.refs_20_), channel_id=1, source_target_pairs={{0,8},{8,16},{16,24},{24,28},{28,20},{20,12},{12,4},{4,0},{1,9},{9... | collective-permute-start | bytes 3145736 | tf_op jit(solution)/shard_map/ppermute | solution.py:631
  309.4 39.2 %collective-permute-start.32 = (bf16[4,256,512]{2,1,0:T(8,128)(2,1)}, bf16[4,256,512]{2,1,0:T(8,128)(2,1)}, u32[]{:S(2)}, u32[]{:S(2)}) collective-permute-start(bf16[4,256,512]{2,1,0:T(8,128)(2,1)} %get-tuple-element.102.refs_21_), channel_id=1, source_target_pairs={{8,0},{16,8},{24,16},{28,24},{20,28},{12,20},{4,12},{0,4},{9,1},{1... | collective-permute-start | bytes 3145736 | tf_op jit(solution)/shard_map/ppermute | solution.py:636
  362.7 35.4 %collective-permute-start.40 = (bf16[1056,512]{1,0:T(8,128)(2,1)}, bf16[1056,512]{1,0:T(8,128)(2,1)}, u32[]{:S(2)}, u32[]{:S(2)}) collective-permute-start(bf16[1056,512]{1,0:T(8,128)(2,1)} %join_own.1.refs_5_.refs_20_.refs_21_.refs_0_), channel_id=1, source_target_pairs={{0,8},{8,16},{16,24},{24,28},{28,20},{20,12},{12,4},{4,0},{1,9},{9... | collective-permute-start | bytes 3244040 | tf_op jit(solution)/shard_map/ppermute | solution.py:631
  365.2 32.9 %collective-permute-start.41 = (bf16[1056,512]{1,0:T(8,128)(2,1)}, bf16[1056,512]{1,0:T(8,128)(2,1)}, u32[]{:S(2)}, u32[]{:S(2)}) collective-permute-start(bf16[1056,512]{1,0:T(8,128)(2,1)} %join_own.1.refs_5_.refs_20_.refs_21_.refs_0_), channel_id=1, source_target_pairs={{8,0},{16,8},{24,16},{28,24},{20,28},{12,20},{4,12},{0,4},{9,1},{1... | collective-permute-start | bytes 3244040 | tf_op jit(solution)/shard_map/ppermute | solution.py:636
  398.1 34.7 %collective-permute-start.43 = (bf16[1056,512]{1,0:T(8,128)(2,1)}, bf16[1056,512]{1,0:T(8,128)(2,1)S(1)}, u32[]{:S(2)}, u32[]{:S(2)}) collective-permute-start(bf16[1056,512]{1,0:T(8,128)(2,1)} %get-tuple-element.113.refs_20_.refs_1_), channel_id=1, source_target_pairs={{0,8},{8,16},{16,24},{24,28},{28,20},{20,12},{12,4},{4,0},{1,9},{9... | collective-permute-start | bytes 3244040 | tf_op jit(solution)/shard_map/ppermute | solution.py:631
  399.7 33.1 %collective-permute-start.44 = (bf16[1056,512]{1,0:T(8,128)(2,1)}, bf16[1056,512]{1,0:T(8,128)(2,1)S(1)}, u32[]{:S(2)}, u32[]{:S(2)}) collective-permute-start(bf16[1056,512]{1,0:T(8,128)(2,1)} %get-tuple-element.114.refs_21_.refs_2_), channel_id=1, source_target_pairs={{8,0},{16,8},{24,16},{28,24},{20,28},{12,20},{4,12},{0,4},{9,1},{1... | collective-permute-start | bytes 3244040 | tf_op jit(solution)/shard_map/ppermute | solution.py:636
  461.4 41.4 %collective-permute-start.45 = (bf16[256,2048]{1,0:T(8,128)(2,1)S(1)}, bf16[256,2048]{1,0:T(8,128)(2,1)S(1)}, u32[]{:S(2)}, u32[]{:S(2)}) collective-permute-start(bf16[256,2048]{1,0:T(8,128)(2,1)S(1)} %add_convert_fusion.refs_22_), channel_id=1, source_target_pairs={{0,1},{1,0},{2,3},{3,2},{4,5},{5,4},{6,7},{7,6},{8,9},{9,8},{10,11... | collective-permute-start | bytes 3145736 | tf_op jit(solution)/shard_map/ppermute | solution.py:689
  (86 other events, 695.4 us)

commit v6 on v5

--- a/solution.py
+++ b/solution.py
@@ -826,7 +826,10 @@
     grad_attn = joined(ga_half, core_swap(ga_half))
 
     grads, first_part = attend_back(
-        grad_attn, normed_low, qkv, lse, mixed, w_out, w3, cos, sin, met[0] + met[1])
+        grad_attn, normed_low, qkv, lse, mixed, w_out, w3, cos, sin, (met[0][0], met[1][0]))
+
+    ffn_other, = after([other_rows(ffn_part)], (grads,))
+    ffn_sum = add_rows([own_rows(ffn_part), core_swap(ffn_other)])
 
     carried = ()
     arrived, sending = ring.reduce_start(grads)
@@ -855,20 +858,22 @@
 
     steps = 2 * far - 1
     while len(met) < far:
-        r, l = forward((r, l), (grads,))
+        r, l = forward((r, l), (grads, ffn_sum, met[0][1], met[1][1]))
     near = len(met)
-    sending = sending + met[-2] + met[-1][:1]
+    sending = sending + met[-2] + met[-1]
     blocks += [block(*x) for x in met[:far - 1]]
     carried = ()
     calls = [(level, rows, True) for level, rows in enumerate(row_bounds)]
     later = [block(*x) for x in met[far - 1:]]
     extra = None
-    slots = [0] + list(range(2, buckets)) + [1]
+    slots = list(range(buckets))
     for slot_at, level in enumerate(slots):
         rows = row_bounds[level]
         carried = weight_gradients(level, rows, length, blocks, w_up, w_down, tuple(carried), True, sending)
         if slot_at == 0:
-            first_other, = after([other_rows(first_part)], (carried[0],))
+            ffn_rows = sum_over_x(ffn_sum, (carried[0],)).astype(BF16).astype(F32)
+            output_half = (resid + gate[:, None] * ffn_rows).astype(BF16)
+            first_other, = after([other_rows(first_part)], (carried[0], output_half))
             first_other = core_swap(first_other)
         if slot_at == 1:
             first_rows = add_rows([own_rows(first_part), first_other], (carried[0],))
@@ -892,9 +897,10 @@
         step += 1
         if slot_at == 3:
             r, l, *held = after([r, l] + [x for x, _ in met[far:]], (carried[0], sending[0]))
-        if slot_at == 0:
-            sending = sending + tuple(x for _, x in met[far - 1:])
+        if slot_at == 1:
+            sending = sending + (output_half,)
         if slot_at == 2:
+            sending = sending + (tokens_half, small)
             while len(met) < 2 * far - 2:
                 r, l = forward((r, l), (carried[0],))
             sending = sending + tuple(pair[0] for pair in met[far:])
@@ -910,20 +916,12 @@
         carried = weight_gradients(level, rows, length, later, w_up, w_down, tuple(carried), False, sending)
         ready = ()
         if level == 0:
-            others = [core_swap(x) for x in after([tokens_half, other_rows(ffn_part)], (carried[0],))]
+            others = [core_swap(x) for x in after([tokens_half, output_half], (carried[0],))]
         if level == 1:
             others = after(others, (carried[0],))
             grad_tokens = joined(tokens_half, others[0])
-            ffn_sum = add_rows([own_rows(ffn_part), others[1]])
-            ready = (grad_tokens, ffn_sum)
-        if level == 2:
-            ffn_rows = sum_over_x(ffn_sum, (carried[0],)).astype(BF16).astype(F32)
-            output_half = (resid + gate[:, None] * ffn_rows).astype(BF16)
-            output_other = core_swap(output_half)
-            ready = (output_half,)
-        if level == 3:
-            output_other, = after([output_other], (carried[0],))
-            output = joined(output_half, output_other)
+            output = joined(output_half, others[1])
+            ready = (grad_tokens, output)
         sending = ()
         if step < steps:
             arrived, sending = advance(step, arrived, (carried[0],))

time: 516 us -> 517 us (level)
  waiting for transfers between devices: 82.1 us -> 90 us
  local copies, waits for them, and re-layouts: 59.8 us -> 54.4 us
    ppermute x19, waiting for transfers between devices: 7.89 us -> 14.9 us  [core_swap(): return lax.ppermute(x, 'mp', [(i, i ^ 1) for i in range(n)])]
    unnamed x133 -> x112, local copies, waits for them, and re-layouts: 34.7 us -> 30.1 us
  transfers between devices with their start and end apart: 50 -> 50, of which waited for: 13 -> 18; matrix products, arithmetic and copies ran while one was open for 14% -> 15% of each run, Pallas kernels for 47% -> 45%
where the time goes in v6:
time: 517 us; the launch traced here: 509 us
  Pallas kernels  274 us (53%)
  waiting for transfers between devices  90 us (17%)
  local copies, waits for them, and re-layouts  54.4 us (11%)
  starting transfers between devices  39.2 us (8%)
  other arithmetic  33.6 us (6%)
  matrix products  9.75 us (2%)
  between operations  8.28 us (2%)
    pallas_call x8, Pallas kernels, weight_gradients(): pl.pallas_call(partial(weight_kernel, level=level, rows=rows, group=group...  161 us
    ppermute x13, waiting for transfers between devices, to_right(): out = lax.ppermute(x, 'dp', self.right)  37.9 us
    unnamed x112, local copies, waits for them, and re-layouts  30.1 us
    ppermute x5, waiting for transfers between devices, sum_over_x(): lax.ppermute(x, 'mp', [(i, (i + 2 * k) % (2 * n)) for i in range(2 * n)])  24.3 us
    pallas_call x1, Pallas kernels, attend_back(): pl.pallas_call(partial(attend_back_kernel, heads=heads, steps=steps, deps...  23.8 us
    ppermute x13, starting transfers between devices, to_right(): out = lax.ppermute(x, 'dp', self.right)  20.5 us
    pallas_call x1, Pallas kernels, own_grad(): pl.pallas_call(partial(own_grad_kernel, row_bounds=tuple(row_bounds), dep...  17.5 us
    pallas_call x1, Pallas kernels, attend(): pl.pallas_call(partial(attend_kernel, heads=heads, steps=steps), grid=(st...  15.7 us
  transfers between devices with their start and end apart: 50, of which 18 were waited for; matrix products, arithmetic and copies ran while one was open for 15% of the time, Pallas kernels for 45%

profile of v6, /device:TPU:0, one launch (start us, length us, event | category | flops | bytes accessed | tf_op | source)
XLA Modules:
  0.0 509.5 jit_solution(9269126796009069496)
XLA Ops:
  2.6 15.7 %attend.1 = (bf16[256,2048]{1,0:T(8,128)(2,1)}, bf16[256,2048]{1,0:T(8,128)(2,1)}, bf16[512,2048]{1,0:T(8,128)(2,1)}, bf16[3,512,512]{2,1,0:T(8,128)(2,1)}, f32[...) custom-call(bf16[512,2048]{1,0:T(8,128)(2,1)} %x_ref.1, f32[1,2048]{1,0:T(1,128)} %bitcast.62, ...), custom_call_target="tpu_custom_call" | custom-call | flops 1207959552 | bytes 3145728 | tf_op jit(solution)/shard_map/attend/pallas_call | solution.py:102
  35.7 16.9 %collective-permute-done.1 = bf16[256,2048]{1,0:T(8,128)(2,1)} collective-permute-done((bf16[256,2048]{1,0:T(8,128)(2,1)}, bf16[256,2048]{1,0:T(8,128)(2,1)}, u32[]{:S(2)}, u32[]{:S(2)}) %collective-permute-start.1) | collective-permute-done | bytes 1048608 | tf_op jit(solution)/shard_map/ppermute | solution.py:696
  68.7 17.5 %own_grad.1 = (bf16[256,2048]{1,0:T(8,128)(2,1)}, bf16[256,2048]{1,0:T(8,128)(2,1)}, bf16[4,512,512]{2,1,0:T(8,128)(2,1)}) custom-call(bf16[512,2048]{1,0:T(8,128)(2,1)} %copy-done.28, bf16[512,2048]{1,0:T(8,128)(2,1)} %copy-done.17, s32[512,128]{1,0:T(8,128)} %broadcast_in_dim.61.bucket_ref, f32[512,128]{1,0:T(8,128)} %broadcast_in_dim.64.gate_ref, ...), custom_call_target="tpu_custom_call" | custom-call | flops 2315255808 | bytes 5767168 | tf_op jit(solution)/shard_map/own_grad/pallas_call | solution.py:248
  96.3 10.4 %own_forward.1 = (bf16[512,2048]{1,0:T(8,128)(2,1)}, f32[512,128]{1,0:T(8,128)}) custom-call(bf16[4,512,512]{2,1,0:T(8,128)(2,1)} %get-tuple-element.72.act_ref, bf16[512,2048]{1,0:T(8,128)(2,1)} %copy-done.17, bf16[512,512]{1,0:T(8,128)(2,1)} %fusion.26.unsort_ref, bf16[4,512,2048]{2,1,0:T(8,128)(2,1)} %refs_17_.15, bf16[256,2048]{1,0:T(8,128)(2,1)} %add_rows.5.rest_0_), custom_call_target="tpu_custom_call" | custom-call | flops 771751936 | bytes 3670016 | tf_op jit(solution)/shard_map/own_forward/pallas_call | solution.py:288
  111.7 7.4 %collective-permute-done.9 = f32[256]{0:T(256)S(1)} collective-permute-done((f32[256]{0:T(256)S(1)}, f32[256]{0:T(256)S(1)}, u32[]{:S(2)}, u32[]{:S(2)}) %collective-permute-start.9) | collective-permute-done | bytes 1056 | tf_op jit(solution)/shard_map/ppermute | solution.py:696
  123.5 12.0 %collective-permute-done.11.refs_2_ = bf16[528,1024]{1,0:T(8,128)(2,1)} collective-permute-done((bf16[528,1024]{1,0:T(8,128)(2,1)S(1)}, bf16[528,1024]{1,0:T(8,128)(2,1)}, u32[]{:S(2)}, u32[]{:S(2)}) %collective-permute-start.11) | collective-permute-done | bytes 1081376 | tf_op jit(solution)/shard_map/ppermute | solution.py:631
  149.5 23.8 %attend_back.1 = (bf16[4,2048,512]{2,1,0:T(8,128)(2,1)}, bf16[512,2048]{1,0:T(8,128)(2,1)}) custom-call(bf16[512,2048]{1,0:T(8,128)(2,1)} %pad_maximum_fusion.ga_ref, bf16[512,2048]{1,0:T(8,128)(2,1)} %get-tuple-element.77.normed_ref, bf16[3,512,512]{2,1,0:T(8,128)(2,1)} %get-tuple-element.78.qkv_ref, f32[4,512,128]{2,1,0:T(8,128)} %get-tuple-element.79.lse_ref, ...), custom_call_target="tpu_custom_call" | custom-call | flops 2483027968 | bytes 6291456 | tf_op jit(solution)/shard_map/attend_back/pallas_call | solution.py:195
  180.9 7.6 %collective-permute-done.17.refs_0_ = bf16[1040,1024]{1,0:T(8,128)(2,1)} collective-permute-done((bf16[1040,1024]{1,0:T(8,128)(2,1)S(1)}, bf16[1040,1024]{1,0:T(8,128)(2,1)}, u32[]{:S(2)}, u32[]{:S(2)}) %collective-permute-start.17) | collective-permute-done | bytes 2129952 | tf_op jit(solution)/shard_map/ppermute | solution.py:631
  188.5 4.5 collective-permute-done.18.refs_1_
  204.2 24.4 %weight_gradients_0.1 = (f32[4,2048,512]{2,1,0:T(8,128)}, f32[4,512,2048]{2,1,0:T(8,128)}) custom-call(bf16[512,1024]{1,0:T(8,128)(2,1)} %copy-done.15, bf16[512,1024]{1,0:T(8,128)(2,1)} %get-tuple-element.151.refs_1_, bf16[528,1024]{1,0:T(8,128)(2,1)} %fusion.20.rest_2_.refs_2_, bf16[512,1024]{1,0:T(8,128)(2,1)} %get-tuple-element.149.refs_3_, ...), custom_call_target="tpu_custom_call" | custom-call | flops 4294967296 | bytes 8388608 | tf_op jit(solution)/shard_map/weight_gradients_0/pallas_call | solution.py:438
  234.8 4.6 join.3
  241.5 23.8 %weight_gradients_1.1 = (f32[4,2048,512]{2,1,0:T(8,128)}, f32[4,512,2048]{2,1,0:T(8,128)}) custom-call(bf16[512,1024]{1,0:T(8,128)(2,1)} %copy-done.15, bf16[512,1024]{1,0:T(8,128)(2,1)} %get-tuple-element.151.refs_1_, bf16[528,1024]{1,0:T(8,128)(2,1)} %fusion.20.rest_2_.refs_2_, ...), custom_call_target="tpu_custom_call", output_to_operand_aliasing={{0}: (18, {}), {1}: (19, {})} | custom-call | flops 4026531840 | bytes 8126464 | tf_op jit(solution)/shard_map/weight_gradients_1/pallas_call | solution.py:438
  273.4 7.2 %collective-permute-done.25.right_ref = bf16[4,256,512]{2,1,0:T(8,128)(2,1)S(1)} collective-permute-done((bf16[4,256,512]{2,1,0:T(8,128)(2,1)}, bf16[4,256,512]{2,1,0:T(8,128)(2,1)S(1)}, u32[]{:S(2)}, u32[]{:S(2)}) %collective-permute-start.25) | collective-permute-done | bytes 1048608 | tf_op jit(solution)/shard_map/ppermute | solution.py:631
  282.0 4.9 join.4
  290.5 18.2 %weight_gradients_2.1 = (f32[4,2048,512]{2,1,0:T(8,128)}, f32[4,512,2048]{2,1,0:T(8,128)}) custom-call(bf16[512,1024]{1,0:T(8,128)(2,1)} %copy-done.15, bf16[512,1024]{1,0:T(8,128)(2,1)} %get-tuple-element.151.refs_1_, bf16[528,1024]{1,0:T(8,128)(2,1)} %fusion.20.rest_2_.refs_2_, ...), custom_call_target="tpu_custom_call", output_to_operand_aliasing={{0}: (18, {}), {1}: (19, {})} | custom-call | flops 2684354560 | bytes 6815744 | tf_op jit(solution)/shard_map/weight_gradients_2/pallas_call | solution.py:438
  320.2 5.0 join.5
  331.7 13.2 %weight_gradients_3.1 = (f32[4,2048,512]{2,1,0:T(8,128)}, f32[4,512,2048]{2,1,0:T(8,128)}) custom-call(bf16[512,1024]{1,0:T(8,128)(2,1)} %copy-done.15, bf16[512,1024]{1,0:T(8,128)(2,1)} %get-tuple-element.151.refs_1_, bf16[528,1024]{1,0:T(8,128)(2,1)} %fusion.20.rest_2_.refs_2_, ...), custom_call_target="tpu_custom_call", output_to_operand_aliasing={{0}: (18, {}), {1}: (19, {})} | custom-call | flops 1342177280 | bytes 5505024 | tf_op jit(solution)/shard_map/weight_gradients_3/pallas_call | solution.py:438
  347.1 11.1 %collective-permute-done.33.right_ref = bf16[4,256,512]{2,1,0:T(8,128)(2,1)} collective-permute-done((bf16[4,256,512]{2,1,0:T(8,128)(2,1)}, bf16[4,256,512]{2,1,0:T(8,128)(2,1)}, u32[]{:S(2)}, u32[]{:S(2)}) %collective-permute-start.33) | collective-permute-done | bytes 1048608 | tf_op jit(solution)/shard_map/ppermute | solution.py:631
  358.2 4.3 collective-permute-done.34.left_ref
  383.5 24.3 %weight_gradients_0_more.1 = (f32[4,2048,512]{2,1,0:T(8,128)}, f32[4,512,2048]{2,1,0:T(8,128)}) custom-call(bf16[1040,1024]{1,0:T(8,128)(2,1)} %get-tuple-element.87.refs_22_.refs_0_.refs_2_, bf16[1040,1024]{1,0:T(8,128)(2,1)} %collective-permute-done.20.refs_23_.refs_1_.refs_3_, ...), custom_call_target="tpu_custom_call", output_to_operand_aliasing={{0}: (18, {}), {1}: (19, {})} | custom-call | flops 4294967296 | bytes 8388608 | tf_op jit(solution)/shard_map/weight_gradients_0_more/pallas_call | solution.py:438
  413.2 23.6 %weight_gradients_1_more.1 = (f32[4,2048,512]{2,1,0:T(8,128)}, f32[4,512,2048]{2,1,0:T(8,128)}) custom-call(bf16[1040,1024]{1,0:T(8,128)(2,1)} %get-tuple-element.87.refs_22_.refs_0_.refs_2_, bf16[1040,1024]{1,0:T(8,128)(2,1)} %collective-permute-done.20.refs_23_.refs_1_.refs_3_, ...), custom_call_target="tpu_custom_call", output_to_operand_aliasing={{0}: (18, {}), {1}: (19, {})} | custom-call | flops 4026531840 | bytes 8126464 | tf_op jit(solution)/shard_map/weight_gradients_1_more/pallas_call | solution.py:438
  451.0 18.9 %weight_gradients_2_more.1 = (f32[4,2048,512]{2,1,0:T(8,128)}, f32[4,512,2048]{2,1,0:T(8,128)}) custom-call(bf16[1040,1024]{1,0:T(8,128)(2,1)} %get-tuple-element.87.refs_22_.refs_0_.refs_2_, bf16[1040,1024]{1,0:T(8,128)(2,1)} %collective-permute-done.20.refs_23_.refs_1_.refs_3_, ...), custom_call_target="tpu_custom_call", output_to_operand_aliasing={{0}: (18, {}), {1}: (19, {})} | custom-call | flops 2684354560 | bytes 6815744 | tf_op jit(solution)/shard_map/weight_gradients_2_more/pallas_call | solution.py:438
  474.9 9.8 %unpack_some.1 = (f32[3,2048,512]{2,1,0:T(8,128)}, f32[512,2048]{1,0:T(8,128)}) custom-call(s32[7]{0:T(128)} %stack.140.order_ref, bf16[1056,512]{1,0:T(8,128)(2,1)} %join_own.1.refs_5_.refs_20_.refs_21_.refs_0_, bf16[1056,512]{1,0:T(8,128)(2,1)} %get-tuple-element.113.refs_20_.refs_1_, bf16[1056,512]{1,0:T(8,128)(2,1)} %get-tuple-element.114.refs_21_.refs_2_, ...), custom_call_target="tpu_custom_call" | custom-call | bytes 5505024 | tf_op jit(solution)/shard_map/unpack_some/pallas_call | solution.py:475
  486.5 14.9 %weight_gradients_3_more.1 = (f32[4,2048,512]{2,1,0:T(8,128)}, f32[4,512,2048]{2,1,0:T(8,128)}) custom-call(bf16[1040,1024]{1,0:T(8,128)(2,1)} %get-tuple-element.87.refs_22_.refs_0_.refs_2_, bf16[1040,1024]{1,0:T(8,128)(2,1)} %collective-permute-done.20.refs_23_.refs_1_.refs_3_, ...), custom_call_target="tpu_custom_call", output_to_operand_aliasing={{0}: (18, {}), {1}: (19, {})} | custom-call | flops 1342177280 | bytes 5505024 | tf_op jit(solution)/shard_map/weight_gradients_3_more/pallas_call | solution.py:438
  (307 shorter events, 177.3 us)
Async XLA Ops:
  32.0 35.0 %collective-permute-start.4 = (bf16[512,1024]{1,0:T(8,128)(2,1)S(1)}, bf16[512,1024]{1,0:T(8,128)(2,1)}, u32[]{:S(2)}, u32[]{:S(2)}) collective-permute-start(bf16[512,1024]{1,0:T(8,128)(2,1)S(1)} %get-tuple-element.152.refs_0_), channel_id=1, source_target_pairs={{0,8},{8,16},{16,24},{24,28},{28,20},{20,12},{12,4},{4,0},{1,9},{9... | collective-permute-start | bytes 3145736 | tf_op jit(solution)/shard_map/ppermute | solution.py:631
  33.6 33.4 %collective-permute-start.5 = (bf16[512,1024]{1,0:T(8,128)(2,1)S(1)}, bf16[512,1024]{1,0:T(8,128)(2,1)}, u32[]{:S(2)}, u32[]{:S(2)}) collective-permute-start(bf16[512,1024]{1,0:T(8,128)(2,1)S(1)} %get-tuple-element.152.refs_0_), channel_id=1, source_target_pairs={{8,0},{16,8},{24,16},{28,24},{20,28},{12,20},{4,12},{0,4},{9,1},{1... | collective-permute-start | bytes 3145736 | tf_op jit(solution)/shard_map/ppermute | solution.py:636
  139.6 41.3 %collective-permute-start.15 = (bf16[1040,1024]{1,0:T(8,128)(2,1)S(1)}, bf16[1040,1024]{1,0:T(8,128)(2,1)S(1)}, u32[]{:S(2)}, u32[]{:S(2)}) collective-permute-start(bf16[1040,1024]{1,0:T(8,128)(2,1)S(1)} %constant_dynamic-update-slice_fusion.rest_0_.refs_4_.refs_6_), channel_id=1, source_target_pairs={{0,1},{1,0},{2,3},{3,2},{4,5},{5,4},{6,7},{7,6},{8,9},{9,8},{10,11... | collective-permute-start | bytes 6389768 | tf_op jit(solution)/shard_map/ppermute | solution.py:689
  139.7 48.8 %collective-permute-start.17 = (bf16[1040,1024]{1,0:T(8,128)(2,1)S(1)}, bf16[1040,1024]{1,0:T(8,128)(2,1)}, u32[]{:S(2)}, u32[]{:S(2)}) collective-permute-start(bf16[1040,1024]{1,0:T(8,128)(2,1)S(1)} %constant_dynamic-update-slice_fusion.rest_0_.refs_4_.refs_6_), channel_id=1, source_target_pairs={{0,8},{8,16},{16,24},{24,28},{28,20},{20,12},{12,4},{4,0},{1,9},{9... | collective-permute-start | bytes 6389768 | tf_op jit(solution)/shard_map/ppermute | solution.py:631
  144.1 36.8 %collective-permute-start.16 = (bf16[1040,1024]{1,0:T(8,128)(2,1)S(1)}, bf16[1040,1024]{1,0:T(8,128)(2,1)}, u32[]{:S(2)}, u32[]{:S(2)}) collective-permute-start(bf16[1040,1024]{1,0:T(8,128)(2,1)S(1)} %constant_dynamic-update-slice_fusion.2.rest_1_.refs_8_.refs_10_), channel_id=1, source_target_pairs={{0,1},{1,0},{2,3},{3,2},{4,5},{5,4},{6,7},{7,6},{8,9},{9,8},{10,11... | collective-permute-start | bytes 6389768 | tf_op jit(solution)/shard_map/ppermute | solution.py:689
  144.3 48.7 %collective-permute-start.18 = (bf16[1040,1024]{1,0:T(8,128)(2,1)S(1)}, bf16[1040,1024]{1,0:T(8,128)(2,1)}, u32[]{:S(2)}, u32[]{:S(2)}) collective-permute-start(bf16[1040,1024]{1,0:T(8,128)(2,1)S(1)} %constant_dynamic-update-slice_fusion.2.rest_1_.refs_8_.refs_10_), channel_id=1, source_target_pairs={{8,0},{16,8},{24,16},{28,24},{20,28},{12,20},{4,12},{0,4},{9,1},{1... | collective-permute-start | bytes 6389768 | tf_op jit(solution)/shard_map/ppermute | solution.py:636
  193.5 35.1 %collective-permute-start.14 = (bf16[256,2048]{1,0:T(8,128)(2,1)S(1)}, bf16[256,2048]{1,0:T(8,128)(2,1)}, u32[]{:S(2)}, u32[]{:S(2)}) collective-permute-start(bf16[256,2048]{1,0:T(8,128)(2,1)S(1)} %copy-done.25), channel_id=1, source_target_pairs={{0,2},{1,3},{2,0},{3,1},{4,6},{5,7},{6,4},{7,5},{8,10},{9,11},{10,... | collective-permute-start | bytes 3145736 | tf_op jit(solution)/shard_map/ppermute | solution.py:696
  198.7 36.2 %collective-permute-start.22 = (bf16[4,128,512]{2,1,0:T(8,128)(2,1)}, bf16[4,128,512]{2,1,0:T(8,128)(2,1)}, u32[]{:S(2)}, u32[]{:S(2)}) collective-permute-start(bf16[4,128,512]{2,1,0:T(8,128)(2,1)} %get-tuple-element.142.refs_18_), channel_id=1, source_target_pairs={{0,8},{8,16},{16,24},{24,28},{28,20},{20,12},{12,4},{4,0},{1,9},{9... | collective-permute-start | bytes 1572872 | tf_op jit(solution)/shard_map/ppermute | solution.py:631
  200.2 34.6 %collective-permute-start.23 = (bf16[4,128,512]{2,1,0:T(8,128)(2,1)}, bf16[4,128,512]{2,1,0:T(8,128)(2,1)}, u32[]{:S(2)}, u32[]{:S(2)}) collective-permute-start(bf16[4,128,512]{2,1,0:T(8,128)(2,1)} %get-tuple-element.141.refs_19_), channel_id=1, source_target_pairs={{8,0},{16,8},{24,16},{28,24},{20,28},{12,20},{4,12},{0,4},{9,1},{1... | collective-permute-start | bytes 1572872 | tf_op jit(solution)/shard_map/ppermute | solution.py:636
  202.2 106.6 %collective-permute-start.27 = (bf16[1040,1024]{1,0:T(8,128)(2,1)}, bf16[1040,1024]{1,0:T(8,128)(2,1)}, u32[]{:S(2)}, u32[]{:S(2)}) collective-permute-start(bf16[1040,1024]{1,0:T(8,128)(2,1)} %get-tuple-element.86.refs_12_.refs_14_.refs_20_), channel_id=1, source_target_pairs={{0,8},{8,16},{16,24},{24,28},{28,20},{20,12},{12,4},{4,0},{1,9},{9... | collective-permute-start | bytes 6389768 | tf_op jit(solution)/shard_map/ppermute | solution.py:631
  203.7 105.0 %collective-permute-start.28 = (bf16[1040,1024]{1,0:T(8,128)(2,1)}, bf16[1040,1024]{1,0:T(8,128)(2,1)S(1)}, u32[]{:S(2)}, u32[]{:S(2)}) collective-permute-start(bf16[1040,1024]{1,0:T(8,128)(2,1)} %get-tuple-element.87.refs_22_.refs_0_.refs_2_), channel_id=1, source_target_pairs={{8,0},{16,8},{24,16},{28,24},{20,28},{12,20},{4,12},{0,4},{9,1},{1... | collective-permute-start | bytes 6389768 | tf_op jit(solution)/shard_map/ppermute | solution.py:636
  232.9 32.4 %collective-permute-start.21 = (bf16[256,2048]{1,0:T(8,128)(2,1)}, bf16[256,2048]{1,0:T(8,128)(2,1)}, u32[]{:S(2)}, u32[]{:S(2)}) collective-permute-start(bf16[256,2048]{1,0:T(8,128)(2,1)} %after.18), channel_id=1, source_target_pairs={{0,1},{1,0},{2,3},{3,2},{4,5},{5,4},{6,7},{7,6},{8,9},{9,8},{10,11... | collective-permute-start | bytes 3145736 | tf_op jit(solution)/shard_map/ppermute | solution.py:689
  239.4 41.1 %collective-permute-start.25 = (bf16[4,256,512]{2,1,0:T(8,128)(2,1)}, bf16[4,256,512]{2,1,0:T(8,128)(2,1)S(1)}, u32[]{:S(2)}, u32[]{:S(2)}) collective-permute-start(bf16[4,256,512]{2,1,0:T(8,128)(2,1)} %get-tuple-element.91.refs_20_), channel_id=1, source_target_pairs={{0,8},{8,16},{16,24},{24,28},{28,20},{20,12},{12,4},{4,0},{1,9},{9... | collective-permute-start | bytes 3145736 | tf_op jit(solution)/shard_map/ppermute | solution.py:631
  241.0 40.9 %collective-permute-start.26 = (bf16[4,256,512]{2,1,0:T(8,128)(2,1)}, bf16[4,256,512]{2,1,0:T(8,128)(2,1)}, u32[]{:S(2)}, u32[]{:S(2)}) collective-permute-start(bf16[4,256,512]{2,1,0:T(8,128)(2,1)} %get-tuple-element.92.refs_21_), channel_id=1, source_target_pairs={{8,0},{16,8},{24,16},{28,24},{20,28},{12,20},{4,12},{0,4},{9,1},{1... | collective-permute-start | bytes 3145736 | tf_op jit(solution)/shard_map/ppermute | solution.py:636
  268.9 47.8 %collective-permute-start.24 = (bf16[256,2048]{1,0:T(8,128)(2,1)}, bf16[256,2048]{1,0:T(8,128)(2,1)}, u32[]{:S(2)}, u32[]{:S(2)}) collective-permute-start(bf16[256,2048]{1,0:T(8,128)(2,1)} %add_rows.7), channel_id=1, source_target_pairs={{0,2},{1,3},{2,0},{3,1},{4,6},{5,7},{6,4},{7,5},{8,10},{9,11},{10,... | collective-permute-start | bytes 3145736 | tf_op jit(solution)/shard_map/ppermute | solution.py:696
  286.8 33.4 %collective-permute-start.31 = (bf16[4,256,512]{2,1,0:T(8,128)(2,1)}, bf16[4,256,512]{2,1,0:T(8,128)(2,1)}, u32[]{:S(2)}, u32[]{:S(2)}) collective-permute-start(bf16[4,256,512]{2,1,0:T(8,128)(2,1)} %get-tuple-element.95.refs_20_), channel_id=1, source_target_pairs={{0,8},{8,16},{16,24},{24,28},{28,20},{20,12},{12,4},{4,0},{1,9},{9... | collective-permute-start | bytes 3145736 | tf_op jit(solution)/shard_map/ppermute | solution.py:631
  288.3 31.9 %collective-permute-start.32 = (bf16[4,256,512]{2,1,0:T(8,128)(2,1)}, bf16[4,256,512]{2,1,0:T(8,128)(2,1)}, u32[]{:S(2)}, u32[]{:S(2)}) collective-permute-start(bf16[4,256,512]{2,1,0:T(8,128)(2,1)} %get-tuple-element.96.refs_21_), channel_id=1, source_target_pairs={{8,0},{16,8},{24,16},{28,24},{20,28},{12,20},{4,12},{0,4},{9,1},{1... | collective-permute-start | bytes 3145736 | tf_op jit(solution)/shard_map/ppermute | solution.py:636
  312.4 54.0 %collective-permute-start.29 = (bf16[512,1024]{1,0:T(8,128)(2,1)}, bf16[512,1024]{1,0:T(8,128)(2,1)S(1)}, u32[]{:S(2)}, u32[]{:S(2)}) collective-permute-start(bf16[512,1024]{1,0:T(8,128)(2,1)} %slice.54), channel_id=1, source_target_pairs={{0,8},{8,16},{16,24},{24,28},{28,20},{20,12},{12,4},{4,0},{1,9},{9... | collective-permute-start | bytes 3145736 | tf_op jit(solution)/shard_map/ppermute | solution.py:631
  316.2 50.2 %collective-permute-start.30 = (bf16[528,1024]{1,0:T(8,128)(2,1)}, bf16[528,1024]{1,0:T(8,128)(2,1)S(1)}, u32[]{:S(2)}, u32[]{:S(2)}) collective-permute-start(bf16[528,1024]{1,0:T(8,128)(2,1)} %slice.55), channel_id=1, source_target_pairs={{8,0},{16,8},{24,16},{28,24},{20,28},{12,20},{4,12},{0,4},{9,1},{1... | collective-permute-start | bytes 3244040 | tf_op jit(solution)/shard_map/ppermute | solution.py:636
  325.2 33.0 %collective-permute-start.33 = (bf16[4,256,512]{2,1,0:T(8,128)(2,1)}, bf16[4,256,512]{2,1,0:T(8,128)(2,1)}, u32[]{:S(2)}, u32[]{:S(2)}) collective-permute-start(bf16[4,256,512]{2,1,0:T(8,128)(2,1)} %get-tuple-element.101.refs_20_), channel_id=1, source_target_pairs={{0,8},{8,16},{16,24},{24,28},{28,20},{20,12},{12,4},{4,0},{1,9},{9... | collective-permute-start | bytes 3145736 | tf_op jit(solution)/shard_map/ppermute | solution.py:631
  326.3 36.2 %collective-permute-start.34 = (bf16[4,256,512]{2,1,0:T(8,128)(2,1)}, bf16[4,256,512]{2,1,0:T(8,128)(2,1)}, u32[]{:S(2)}, u32[]{:S(2)}) collective-permute-start(bf16[4,256,512]{2,1,0:T(8,128)(2,1)} %get-tuple-element.102.refs_21_), channel_id=1, source_target_pairs={{8,0},{16,8},{24,16},{28,24},{20,28},{12,20},{4,12},{0,4},{9,1},{1... | collective-permute-start | bytes 3145736 | tf_op jit(solution)/shard_map/ppermute | solution.py:636
  372.1 37.1 %collective-permute-start.42 = (bf16[1056,512]{1,0:T(8,128)(2,1)S(1)}, bf16[1056,512]{1,0:T(8,128)(2,1)}, u32[]{:S(2)}, u32[]{:S(2)}) collective-permute-start(bf16[1056,512]{1,0:T(8,128)(2,1)S(1)} %copy-done.12), channel_id=1, source_target_pairs={{0,8},{8,16},{16,24},{24,28},{28,20},{20,12},{12,4},{4,0},{1,9},{9... | collective-permute-start | bytes 3244040 | tf_op jit(solution)/shard_map/ppermute | solution.py:631
  377.5 31.7 %collective-permute-start.43 = (bf16[1056,512]{1,0:T(8,128)(2,1)S(1)}, bf16[1056,512]{1,0:T(8,128)(2,1)}, u32[]{:S(2)}, u32[]{:S(2)}) collective-permute-start(bf16[1056,512]{1,0:T(8,128)(2,1)S(1)} %copy-done.12), channel_id=1, source_target_pairs={{8,0},{16,8},{24,16},{28,24},{20,28},{12,20},{4,12},{0,4},{9,1},{1... | collective-permute-start | bytes 3244040 | tf_op jit(solution)/shard_map/ppermute | solution.py:636
  409.2 32.9 %collective-permute-start.44 = (bf16[1056,512]{1,0:T(8,128)(2,1)}, bf16[1056,512]{1,0:T(8,128)(2,1)S(1)}, u32[]{:S(2)}, u32[]{:S(2)}) collective-permute-start(bf16[1056,512]{1,0:T(8,128)(2,1)} %get-tuple-element.113.refs_20_.refs_1_), channel_id=1, source_target_pairs={{0,8},{8,16},{16,24},{24,28},{28,20},{20,12},{12,4},{4,0},{1,9},{9... | collective-permute-start | bytes 3244040 | tf_op jit(solution)/shard_map/ppermute | solution.py:631
  (75 other events, 802.8 us)

commit v7 on v6

--- a/solution.py
+++ b/solution.py
@@ -790,8 +790,6 @@
         cot_first + (sent_own,))
     gsent_rows = add_rows([gsent_mine, core_swap(gsent_other)])
     grad_sent = sum_over_x(gsent_rows).astype(BF16).astype(F32)
-    ffn_part, ggate_part = own_forward(
-        act, cot_sorted, sort_rows.astype(BF16).T, w_down, row_bounds, (gsent_rows,))
     far = devices_dp // 2
     met = []
 
@@ -809,7 +807,9 @@
             return ring.to_right(r), ring.to_left(l)
         return ring.to_right(r[:height]), ring.to_left(l[height:])
 
-    r, l = forward(cot_first + sent_first, (ffn_part,))
+    r, l = forward(cot_first + sent_first, (gsent_rows,))
+    ffn_part, ggate_part = own_forward(
+        act, cot_sorted, sort_rows.astype(BF16).T, w_down, row_bounds, (gsent_rows, met[0][0], met[1][0]))
     ggate_part = jnp.sum(jnp.where(sort_rows, ggate_part[:, :1], 0.0), 0)
     grad_gate = ggate_part + core_swap(ggate_part)
     grad_gate = sum_over_x(own_rows(grad_gate))
@@ -826,7 +826,7 @@
     grad_attn = joined(ga_half, core_swap(ga_half))
 
     grads, first_part = attend_back(
-        grad_attn, normed_low, qkv, lse, mixed, w_out, w3, cos, sin, (met[0][0], met[1][0]))
+        grad_attn, normed_low, qkv, lse, mixed, w_out, w3, cos, sin, met[0] + met[1])
 
     ffn_other, = after([other_rows(ffn_part)], (grads,))
     ffn_sum = add_rows([own_rows(ffn_part), core_swap(ffn_other)])
@@ -858,7 +858,7 @@
 
     steps = 2 * far - 1
     while len(met) < far:
-        r, l = forward((r, l), (grads, ffn_sum, met[0][1], met[1][1]))
+        r, l = forward((r, l), (grads, ffn_sum))
     near = len(met)
     sending = sending + met[-2] + met[-1]
     blocks += [block(*x) for x in met[:far - 1]]

time: 517 us -> 503 us (0.973)
  waiting for transfers between devices: 90 us -> 68.6 us
    ppermute x13, waiting for transfers between devices: 37.9 us -> 27.8 us  [to_right(): out = lax.ppermute(x, 'dp', self.right)]
    ppermute x13, waiting for transfers between devices: 12.9 us -> 7.03 us  [to_left(): out = lax.ppermute(x, 'dp', self.left)]
    unnamed x112 -> x116, local copies, waits for them, and re-layouts: 30.1 us -> 34.3 us
  transfers between devices with their start and end apart: 50 -> 50, of which waited for: 18 -> 15; matrix products, arithmetic and copies ran while one was open for 15% -> 16% of each run, Pallas kernels for 45% -> 51%
where the time goes in v7:
time: 503 us; the launch traced here: 495 us
  Pallas kernels  274 us (54%)
  waiting for transfers between devices  68.6 us (14%)
  local copies, waits for them, and re-layouts  58.3 us (12%)
  starting transfers between devices  39.5 us (8%)
  other arithmetic  34.9 us (7%)
  matrix products  11.1 us (2%)
  between operations  8.34 us (2%)
    pallas_call x8, Pallas kernels, weight_gradients(): pl.pallas_call(partial(weight_kernel, level=level, rows=rows, group=group...  161 us
    unnamed x116, local copies, waits for them, and re-layouts  34.3 us
    ppermute x13, waiting for transfers between devices, to_right(): out = lax.ppermute(x, 'dp', self.right)  27.8 us
    pallas_call x1, Pallas kernels, attend_back(): pl.pallas_call(partial(attend_back_kernel, heads=heads, steps=steps, deps...  23.8 us
    ppermute x13, starting transfers between devices, to_right(): out = lax.ppermute(x, 'dp', self.right)  21.3 us
    ppermute x5, waiting for transfers between devices, sum_over_x(): lax.ppermute(x, 'mp', [(i, (i + 2 * k) % (2 * n)) for i in range(2 * n)])  19.6 us
    pallas_call x1, Pallas kernels, own_grad(): pl.pallas_call(partial(own_grad_kernel, row_bounds=tuple(row_bounds), dep...  17.3 us
    pallas_call x1, Pallas kernels, attend(): pl.pallas_call(partial(attend_kernel, heads=heads, steps=steps), grid=(st...  15.7 us
  transfers between devices with their start and end apart: 50, of which 15 were waited for; matrix products, arithmetic and copies ran while one was open for 16% of the time, Pallas kernels for 51%

profile of v7, /device:TPU:0, one launch (start us, length us, event | category | flops | bytes accessed | tf_op | source)
XLA Modules:
  0.0 494.9 jit_solution(12227195721148518327)
XLA Ops:
  2.6 15.7 %attend.1 = (bf16[256,2048]{1,0:T(8,128)(2,1)}, bf16[256,2048]{1,0:T(8,128)(2,1)}, bf16[512,2048]{1,0:T(8,128)(2,1)}, bf16[3,512,512]{2,1,0:T(8,128)(2,1)}, f32[...) custom-call(bf16[512,2048]{1,0:T(8,128)(2,1)} %x_ref.1, f32[1,2048]{1,0:T(1,128)} %bitcast.62, ...), custom_call_target="tpu_custom_call" | custom-call | flops 1207959552 | bytes 3145728 | tf_op jit(solution)/shard_map/attend/pallas_call | solution.py:102
  36.1 16.5 %collective-permute-done.1 = bf16[256,2048]{1,0:T(8,128)(2,1)} collective-permute-done((bf16[256,2048]{1,0:T(8,128)(2,1)}, bf16[256,2048]{1,0:T(8,128)(2,1)}, u32[]{:S(2)}, u32[]{:S(2)}) %collective-permute-start.1) | collective-permute-done | bytes 1048608 | tf_op jit(solution)/shard_map/ppermute | solution.py:696
  70.1 17.3 %own_grad.1 = (bf16[256,2048]{1,0:T(8,128)(2,1)}, bf16[256,2048]{1,0:T(8,128)(2,1)}, bf16[4,512,512]{2,1,0:T(8,128)(2,1)}) custom-call(bf16[512,2048]{1,0:T(8,128)(2,1)} %copy-done.27, bf16[512,2048]{1,0:T(8,128)(2,1)} %copy-done.16, s32[512,128]{1,0:T(8,128)} %broadcast_in_dim.61.bucket_ref, f32[512,128]{1,0:T(8,128)} %broadcast_in_dim.64.gate_ref, ...), custom_call_target="tpu_custom_call" | custom-call | flops 2315255808 | bytes 5767168 | tf_op jit(solution)/shard_map/own_grad/pallas_call | solution.py:248
  103.5 10.4 %own_forward.1 = (bf16[512,2048]{1,0:T(8,128)(2,1)}, f32[512,128]{1,0:T(8,128)}) custom-call(bf16[4,512,512]{2,1,0:T(8,128)(2,1)} %get-tuple-element.72.act_ref, bf16[512,2048]{1,0:T(8,128)(2,1)} %copy-done.16, bf16[512,512]{1,0:T(8,128)(2,1)} %fusion.26.unsort_ref, bf16[4,512,2048]{2,1,0:T(8,128)(2,1)} %refs_17_.15, ...), custom_call_target="tpu_custom_call" | custom-call | flops 771751936 | bytes 3670016 | tf_op jit(solution)/shard_map/own_forward/pallas_call | solution.py:288
  120.5 3.9 multiply_reduce_fusion
  135.8 23.8 %attend_back.1 = (bf16[4,2048,512]{2,1,0:T(8,128)(2,1)}, bf16[512,2048]{1,0:T(8,128)(2,1)}) custom-call(bf16[512,2048]{1,0:T(8,128)(2,1)} %pad_maximum_fusion.ga_ref, bf16[512,2048]{1,0:T(8,128)(2,1)} %get-tuple-element.81.normed_ref, bf16[3,512,512]{2,1,0:T(8,128)(2,1)} %get-tuple-element.82.qkv_ref, f32[4,512,128]{2,1,0:T(8,128)} %get-tuple-element.83.lse_ref, ...), custom_call_target="tpu_custom_call" | custom-call | flops 2483027968 | bytes 6291456 | tf_op jit(solution)/shard_map/attend_back/pallas_call | solution.py:195
  167.1 9.6 %collective-permute-done.17.refs_0_ = bf16[1040,1024]{1,0:T(8,128)(2,1)} collective-permute-done((bf16[1040,1024]{1,0:T(8,128)(2,1)}, bf16[1040,1024]{1,0:T(8,128)(2,1)}, u32[]{:S(2)}, u32[]{:S(2)}) %collective-permute-start.17) | collective-permute-done | bytes 2129952 | tf_op jit(solution)/shard_map/ppermute | solution.py:631
  189.2 24.4 %weight_gradients_0.1 = (f32[4,2048,512]{2,1,0:T(8,128)}, f32[4,512,2048]{2,1,0:T(8,128)}) custom-call(bf16[512,1024]{1,0:T(8,128)(2,1)} %get-tuple-element.152.refs_0_, bf16[512,1024]{1,0:T(8,128)(2,1)} %get-tuple-element.151.refs_1_, bf16[528,1024]{1,0:T(8,128)(2,1)} %copy-done.11, bf16[512,1024]{1,0:T(8,128)(2,1)} %get-tuple-element.149.refs_3_, ...), custom_call_target="tpu_custom_call" | custom-call | flops 4294967296 | bytes 8388608 | tf_op jit(solution)/shard_map/weight_gradients_0/pallas_call | solution.py:438
  219.9 4.6 join.3
  226.5 23.8 %weight_gradients_1.1 = (f32[4,2048,512]{2,1,0:T(8,128)}, f32[4,512,2048]{2,1,0:T(8,128)}) custom-call(bf16[512,1024]{1,0:T(8,128)(2,1)} %get-tuple-element.152.refs_0_, bf16[512,1024]{1,0:T(8,128)(2,1)} %get-tuple-element.151.refs_1_, bf16[528,1024]{1,0:T(8,128)(2,1)} %copy-done.11, ...), custom_call_target="tpu_custom_call", output_to_operand_aliasing={{0}: (18, {}), {1}: (19, {})} | custom-call | flops 4026531840 | bytes 8126464 | tf_op jit(solution)/shard_map/weight_gradients_1/pallas_call | solution.py:438
  258.4 7.2 %collective-permute-done.25.right_ref = bf16[4,256,512]{2,1,0:T(8,128)(2,1)S(1)} collective-permute-done((bf16[4,256,512]{2,1,0:T(8,128)(2,1)}, bf16[4,256,512]{2,1,0:T(8,128)(2,1)S(1)}, u32[]{:S(2)}, u32[]{:S(2)}) %collective-permute-start.25) | collective-permute-done | bytes 1048608 | tf_op jit(solution)/shard_map/ppermute | solution.py:631
  267.0 4.9 join.4
  275.6 18.2 %weight_gradients_2.1 = (f32[4,2048,512]{2,1,0:T(8,128)}, f32[4,512,2048]{2,1,0:T(8,128)}) custom-call(bf16[512,1024]{1,0:T(8,128)(2,1)} %get-tuple-element.152.refs_0_, bf16[512,1024]{1,0:T(8,128)(2,1)} %get-tuple-element.151.refs_1_, bf16[528,1024]{1,0:T(8,128)(2,1)} %copy-done.11, ...), custom_call_target="tpu_custom_call", output_to_operand_aliasing={{0}: (18, {}), {1}: (19, {})} | custom-call | flops 2684354560 | bytes 6815744 | tf_op jit(solution)/shard_map/weight_gradients_2/pallas_call | solution.py:438
  305.3 5.0 %join.5 = (bf16[4,256,512]{2,1,0:T(8,128)(2,1)}, bf16[4,256,512]{2,1,0:T(8,128)(2,1)}) custom-call(s32[2]{0:T(128)} %pad_add_fusion.3.index_ref, bf16[4,2048,512]{2,1,0:T(8,128)(2,1)} %get-tuple-element.85.refs_1_.refs_2_.right_local.left_local.local_ref, bf16[4,2048,512]{2,1,0:T(8,128)(2,1)} %get-tuple-element.85.refs_1_.refs_2_.right_local.left_local.local_ref, ...), custom_call_target="tpu_custom_call" | custom-call | flops 262144 | bytes 1572864 | tf_op jit(solution)/shard_map/join/pallas_call | solution.py:555
  312.6 4.2 fusion.7.refs_22_
  316.8 13.2 %weight_gradients_3.1 = (f32[4,2048,512]{2,1,0:T(8,128)}, f32[4,512,2048]{2,1,0:T(8,128)}) custom-call(bf16[512,1024]{1,0:T(8,128)(2,1)} %get-tuple-element.152.refs_0_, bf16[512,1024]{1,0:T(8,128)(2,1)} %get-tuple-element.151.refs_1_, bf16[528,1024]{1,0:T(8,128)(2,1)} %copy-done.11, ...), custom_call_target="tpu_custom_call", output_to_operand_aliasing={{0}: (18, {}), {1}: (19, {})} | custom-call | flops 1342177280 | bytes 5505024 | tf_op jit(solution)/shard_map/weight_gradients_3/pallas_call | solution.py:438
  332.2 11.0 %collective-permute-done.33.right_ref = bf16[4,256,512]{2,1,0:T(8,128)(2,1)} collective-permute-done((bf16[4,256,512]{2,1,0:T(8,128)(2,1)}, bf16[4,256,512]{2,1,0:T(8,128)(2,1)}, u32[]{:S(2)}, u32[]{:S(2)}) %collective-permute-start.33) | collective-permute-done | bytes 1048608 | tf_op jit(solution)/shard_map/ppermute | solution.py:631
  343.3 4.3 collective-permute-done.34.left_ref
  347.5 3.9 join_own.1.refs_5_.refs_20_.refs_21_.refs_0_
  368.5 24.3 %weight_gradients_0_more.1 = (f32[4,2048,512]{2,1,0:T(8,128)}, f32[4,512,2048]{2,1,0:T(8,128)}) custom-call(bf16[1040,1024]{1,0:T(8,128)(2,1)} %get-tuple-element.87.refs_22_.refs_0_.refs_2_, bf16[1040,1024]{1,0:T(8,128)(2,1)} %collective-permute-done.20.refs_23_.refs_1_.refs_3_, ...), custom_call_target="tpu_custom_call", output_to_operand_aliasing={{0}: (18, {}), {1}: (19, {})} | custom-call | flops 4294967296 | bytes 8388608 | tf_op jit(solution)/shard_map/weight_gradients_0_more/pallas_call | solution.py:438
  398.2 23.6 %weight_gradients_1_more.1 = (f32[4,2048,512]{2,1,0:T(8,128)}, f32[4,512,2048]{2,1,0:T(8,128)}) custom-call(bf16[1040,1024]{1,0:T(8,128)(2,1)} %get-tuple-element.87.refs_22_.refs_0_.refs_2_, bf16[1040,1024]{1,0:T(8,128)(2,1)} %collective-permute-done.20.refs_23_.refs_1_.refs_3_, ...), custom_call_target="tpu_custom_call", output_to_operand_aliasing={{0}: (18, {}), {1}: (19, {})} | custom-call | flops 4026531840 | bytes 8126464 | tf_op jit(solution)/shard_map/weight_gradients_1_more/pallas_call | solution.py:438
  437.3 18.9 %weight_gradients_2_more.1 = (f32[4,2048,512]{2,1,0:T(8,128)}, f32[4,512,2048]{2,1,0:T(8,128)}) custom-call(bf16[1040,1024]{1,0:T(8,128)(2,1)} %get-tuple-element.87.refs_22_.refs_0_.refs_2_, bf16[1040,1024]{1,0:T(8,128)(2,1)} %collective-permute-done.20.refs_23_.refs_1_.refs_3_, ...), custom_call_target="tpu_custom_call", output_to_operand_aliasing={{0}: (18, {}), {1}: (19, {})} | custom-call | flops 2684354560 | bytes 6815744 | tf_op jit(solution)/shard_map/weight_gradients_2_more/pallas_call | solution.py:438
  460.3 9.8 %unpack_some.1 = (f32[3,2048,512]{2,1,0:T(8,128)}, f32[512,2048]{1,0:T(8,128)}) custom-call(s32[7]{0:T(128)} %stack.140.order_ref, bf16[1056,512]{1,0:T(8,128)(2,1)} %join_own.1.refs_5_.refs_20_.refs_21_.refs_0_, bf16[1056,512]{1,0:T(8,128)(2,1)} %get-tuple-element.113.refs_20_.refs_1_, bf16[1056,512]{1,0:T(8,128)(2,1)} %get-tuple-element.114.refs_21_.refs_2_, ...), custom_call_target="tpu_custom_call" | custom-call | bytes 5505024 | tf_op jit(solution)/shard_map/unpack_some/pallas_call | solution.py:475
  472.0 14.9 %weight_gradients_3_more.1 = (f32[4,2048,512]{2,1,0:T(8,128)}, f32[4,512,2048]{2,1,0:T(8,128)}) custom-call(bf16[1040,1024]{1,0:T(8,128)(2,1)} %get-tuple-element.87.refs_22_.refs_0_.refs_2_, bf16[1040,1024]{1,0:T(8,128)(2,1)} %collective-permute-done.20.refs_23_.refs_1_.refs_3_, ...), custom_call_target="tpu_custom_call", output_to_operand_aliasing={{0}: (18, {}), {1}: (19, {})} | custom-call | flops 1342177280 | bytes 5505024 | tf_op jit(solution)/shard_map/weight_gradients_3_more/pallas_call | solution.py:438
  (311 shorter events, 173.0 us)
Async XLA Ops:
  32.4 35.9 %collective-permute-start.4 = (bf16[512,1024]{1,0:T(8,128)(2,1)}, bf16[512,1024]{1,0:T(8,128)(2,1)S(1)}, u32[]{:S(2)}, u32[]{:S(2)}) collective-permute-start(bf16[512,1024]{1,0:T(8,128)(2,1)} %get-tuple-element.152.refs_0_), channel_id=1, source_target_pairs={{0,8},{8,16},{16,24},{24,28},{28,20},{20,12},{12,4},{4,0},{1,9},{9... | collective-permute-start | bytes 3145736 | tf_op jit(solution)/shard_map/ppermute | solution.py:631
  34.0 34.3 %collective-permute-start.5 = (bf16[512,1024]{1,0:T(8,128)(2,1)}, bf16[512,1024]{1,0:T(8,128)(2,1)}, u32[]{:S(2)}, u32[]{:S(2)}) collective-permute-start(bf16[512,1024]{1,0:T(8,128)(2,1)} %get-tuple-element.152.refs_0_), channel_id=1, source_target_pairs={{8,0},{16,8},{24,16},{28,24},{20,28},{12,20},{4,12},{0,4},{9,1},{1... | collective-permute-start | bytes 3145736 | tf_op jit(solution)/shard_map/ppermute | solution.py:636
  66.0 30.6 %collective-permute-start.7 = (bf16[528,1024]{1,0:T(8,128)(2,1)S(1)}, bf16[528,1024]{1,0:T(8,128)(2,1)S(1)}, u32[]{:S(2)}, u32[]{:S(2)}) collective-permute-start(bf16[528,1024]{1,0:T(8,128)(2,1)S(1)} %fusion.20.rest_2_.refs_2_), channel_id=1, source_target_pairs={{0,8},{8,16},{16,24},{24,28},{28,20},{20,12},{12,4},{4,0},{1,9},{9... | collective-permute-start | bytes 3244040 | tf_op jit(solution)/shard_map/ppermute | solution.py:631
  127.6 49.1 %collective-permute-start.17 = (bf16[1040,1024]{1,0:T(8,128)(2,1)}, bf16[1040,1024]{1,0:T(8,128)(2,1)}, u32[]{:S(2)}, u32[]{:S(2)}) collective-permute-start(bf16[1040,1024]{1,0:T(8,128)(2,1)} %copy-done.5), channel_id=1, source_target_pairs={{0,8},{8,16},{16,24},{24,28},{28,20},{20,12},{12,4},{4,0},{1,9},{9... | collective-permute-start | bytes 6389768 | tf_op jit(solution)/shard_map/ppermute | solution.py:631
  129.5 48.5 %collective-permute-start.18 = (bf16[1040,1024]{1,0:T(8,128)(2,1)S(1)}, bf16[1040,1024]{1,0:T(8,128)(2,1)}, u32[]{:S(2)}, u32[]{:S(2)}) collective-permute-start(bf16[1040,1024]{1,0:T(8,128)(2,1)S(1)} %copy-done.4), channel_id=1, source_target_pairs={{8,0},{16,8},{24,16},{28,24},{20,28},{12,20},{4,12},{0,4},{9,1},{1... | collective-permute-start | bytes 6389768 | tf_op jit(solution)/shard_map/ppermute | solution.py:636
  178.5 35.1 %collective-permute-start.16 = (bf16[256,2048]{1,0:T(8,128)(2,1)S(1)}, bf16[256,2048]{1,0:T(8,128)(2,1)}, u32[]{:S(2)}, u32[]{:S(2)}) collective-permute-start(bf16[256,2048]{1,0:T(8,128)(2,1)S(1)} %copy-done.26), channel_id=1, source_target_pairs={{0,2},{1,3},{2,0},{3,1},{4,6},{5,7},{6,4},{7,5},{8,10},{9,11},{10,... | collective-permute-start | bytes 3145736 | tf_op jit(solution)/shard_map/ppermute | solution.py:696
  183.7 36.2 %collective-permute-start.22 = (bf16[4,128,512]{2,1,0:T(8,128)(2,1)}, bf16[4,128,512]{2,1,0:T(8,128)(2,1)}, u32[]{:S(2)}, u32[]{:S(2)}) collective-permute-start(bf16[4,128,512]{2,1,0:T(8,128)(2,1)} %get-tuple-element.142.refs_18_), channel_id=1, source_target_pairs={{0,8},{8,16},{16,24},{24,28},{28,20},{20,12},{12,4},{4,0},{1,9},{9... | collective-permute-start | bytes 1572872 | tf_op jit(solution)/shard_map/ppermute | solution.py:631
  185.3 34.6 %collective-permute-start.23 = (bf16[4,128,512]{2,1,0:T(8,128)(2,1)}, bf16[4,128,512]{2,1,0:T(8,128)(2,1)}, u32[]{:S(2)}, u32[]{:S(2)}) collective-permute-start(bf16[4,128,512]{2,1,0:T(8,128)(2,1)} %get-tuple-element.141.refs_19_), channel_id=1, source_target_pairs={{8,0},{16,8},{24,16},{28,24},{20,28},{12,20},{4,12},{0,4},{9,1},{1... | collective-permute-start | bytes 1572872 | tf_op jit(solution)/shard_map/ppermute | solution.py:636
  187.2 106.6 %collective-permute-start.27 = (bf16[1040,1024]{1,0:T(8,128)(2,1)}, bf16[1040,1024]{1,0:T(8,128)(2,1)}, u32[]{:S(2)}, u32[]{:S(2)}) collective-permute-start(bf16[1040,1024]{1,0:T(8,128)(2,1)} %get-tuple-element.86.refs_12_.refs_14_.refs_20_), channel_id=1, source_target_pairs={{0,8},{8,16},{16,24},{24,28},{28,20},{20,12},{12,4},{4,0},{1,9},{9... | collective-permute-start | bytes 6389768 | tf_op jit(solution)/shard_map/ppermute | solution.py:631
  188.8 105.0 %collective-permute-start.28 = (bf16[1040,1024]{1,0:T(8,128)(2,1)}, bf16[1040,1024]{1,0:T(8,128)(2,1)S(1)}, u32[]{:S(2)}, u32[]{:S(2)}) collective-permute-start(bf16[1040,1024]{1,0:T(8,128)(2,1)} %get-tuple-element.87.refs_22_.refs_0_.refs_2_), channel_id=1, source_target_pairs={{8,0},{16,8},{24,16},{28,24},{20,28},{12,20},{4,12},{0,4},{9,1},{1... | collective-permute-start | bytes 6389768 | tf_op jit(solution)/shard_map/ppermute | solution.py:636
  217.9 32.4 %collective-permute-start.21 = (bf16[256,2048]{1,0:T(8,128)(2,1)}, bf16[256,2048]{1,0:T(8,128)(2,1)}, u32[]{:S(2)}, u32[]{:S(2)}) collective-permute-start(bf16[256,2048]{1,0:T(8,128)(2,1)} %after.18), channel_id=1, source_target_pairs={{0,1},{1,0},{2,3},{3,2},{4,5},{5,4},{6,7},{7,6},{8,9},{9,8},{10,11... | collective-permute-start | bytes 3145736 | tf_op jit(solution)/shard_map/ppermute | solution.py:689
  224.5 41.1 %collective-permute-start.25 = (bf16[4,256,512]{2,1,0:T(8,128)(2,1)}, bf16[4,256,512]{2,1,0:T(8,128)(2,1)S(1)}, u32[]{:S(2)}, u32[]{:S(2)}) collective-permute-start(bf16[4,256,512]{2,1,0:T(8,128)(2,1)} %get-tuple-element.91.refs_20_), channel_id=1, source_target_pairs={{0,8},{8,16},{16,24},{24,28},{28,20},{20,12},{12,4},{4,0},{1,9},{9... | collective-permute-start | bytes 3145736 | tf_op jit(solution)/shard_map/ppermute | solution.py:631
  226.1 40.9 %collective-permute-start.26 = (bf16[4,256,512]{2,1,0:T(8,128)(2,1)}, bf16[4,256,512]{2,1,0:T(8,128)(2,1)}, u32[]{:S(2)}, u32[]{:S(2)}) collective-permute-start(bf16[4,256,512]{2,1,0:T(8,128)(2,1)} %get-tuple-element.92.refs_21_), channel_id=1, source_target_pairs={{8,0},{16,8},{24,16},{28,24},{20,28},{12,20},{4,12},{0,4},{9,1},{1... | collective-permute-start | bytes 3145736 | tf_op jit(solution)/shard_map/ppermute | solution.py:636
  254.0 47.8 %collective-permute-start.24 = (bf16[256,2048]{1,0:T(8,128)(2,1)}, bf16[256,2048]{1,0:T(8,128)(2,1)}, u32[]{:S(2)}, u32[]{:S(2)}) collective-permute-start(bf16[256,2048]{1,0:T(8,128)(2,1)} %add_rows.7), channel_id=1, source_target_pairs={{0,2},{1,3},{2,0},{3,1},{4,6},{5,7},{6,4},{7,5},{8,10},{9,11},{10,... | collective-permute-start | bytes 3145736 | tf_op jit(solution)/shard_map/ppermute | solution.py:696
  271.9 33.4 %collective-permute-start.31 = (bf16[4,256,512]{2,1,0:T(8,128)(2,1)}, bf16[4,256,512]{2,1,0:T(8,128)(2,1)}, u32[]{:S(2)}, u32[]{:S(2)}) collective-permute-start(bf16[4,256,512]{2,1,0:T(8,128)(2,1)} %get-tuple-element.95.refs_20_), channel_id=1, source_target_pairs={{0,8},{8,16},{16,24},{24,28},{28,20},{20,12},{12,4},{4,0},{1,9},{9... | collective-permute-start | bytes 3145736 | tf_op jit(solution)/shard_map/ppermute | solution.py:631
  273.4 31.9 %collective-permute-start.32 = (bf16[4,256,512]{2,1,0:T(8,128)(2,1)}, bf16[4,256,512]{2,1,0:T(8,128)(2,1)}, u32[]{:S(2)}, u32[]{:S(2)}) collective-permute-start(bf16[4,256,512]{2,1,0:T(8,128)(2,1)} %get-tuple-element.96.refs_21_), channel_id=1, source_target_pairs={{8,0},{16,8},{24,16},{28,24},{20,28},{12,20},{4,12},{0,4},{9,1},{1... | collective-permute-start | bytes 3145736 | tf_op jit(solution)/shard_map/ppermute | solution.py:636
  297.4 54.0 %collective-permute-start.29 = (bf16[512,1024]{1,0:T(8,128)(2,1)}, bf16[512,1024]{1,0:T(8,128)(2,1)S(1)}, u32[]{:S(2)}, u32[]{:S(2)}) collective-permute-start(bf16[512,1024]{1,0:T(8,128)(2,1)} %slice.54), channel_id=1, source_target_pairs={{0,8},{8,16},{16,24},{24,28},{28,20},{20,12},{12,4},{4,0},{1,9},{9... | collective-permute-start | bytes 3145736 | tf_op jit(solution)/shard_map/ppermute | solution.py:631
  301.3 50.1 %collective-permute-start.30 = (bf16[528,1024]{1,0:T(8,128)(2,1)}, bf16[528,1024]{1,0:T(8,128)(2,1)S(1)}, u32[]{:S(2)}, u32[]{:S(2)}) collective-permute-start(bf16[528,1024]{1,0:T(8,128)(2,1)} %slice.55), channel_id=1, source_target_pairs={{8,0},{16,8},{24,16},{28,24},{20,28},{12,20},{4,12},{0,4},{9,1},{1... | collective-permute-start | bytes 3244040 | tf_op jit(solution)/shard_map/ppermute | solution.py:636
  310.3 32.9 %collective-permute-start.33 = (bf16[4,256,512]{2,1,0:T(8,128)(2,1)}, bf16[4,256,512]{2,1,0:T(8,128)(2,1)}, u32[]{:S(2)}, u32[]{:S(2)}) collective-permute-start(bf16[4,256,512]{2,1,0:T(8,128)(2,1)} %get-tuple-element.101.refs_20_), channel_id=1, source_target_pairs={{0,8},{8,16},{16,24},{24,28},{28,20},{20,12},{12,4},{4,0},{1,9},{9... | collective-permute-start | bytes 3145736 | tf_op jit(solution)/shard_map/ppermute | solution.py:631
  311.8 35.7 %collective-permute-start.34 = (bf16[4,256,512]{2,1,0:T(8,128)(2,1)}, bf16[4,256,512]{2,1,0:T(8,128)(2,1)}, u32[]{:S(2)}, u32[]{:S(2)}) collective-permute-start(bf16[4,256,512]{2,1,0:T(8,128)(2,1)} %get-tuple-element.102.refs_21_), channel_id=1, source_target_pairs={{8,0},{16,8},{24,16},{28,24},{20,28},{12,20},{4,12},{0,4},{9,1},{1... | collective-permute-start | bytes 3145736 | tf_op jit(solution)/shard_map/ppermute | solution.py:636
  357.1 37.1 %collective-permute-start.42 = (bf16[1056,512]{1,0:T(8,128)(2,1)S(1)}, bf16[1056,512]{1,0:T(8,128)(2,1)}, u32[]{:S(2)}, u32[]{:S(2)}) collective-permute-start(bf16[1056,512]{1,0:T(8,128)(2,1)S(1)} %copy-done.12), channel_id=1, source_target_pairs={{0,8},{8,16},{16,24},{24,28},{28,20},{20,12},{12,4},{4,0},{1,9},{9... | collective-permute-start | bytes 3244040 | tf_op jit(solution)/shard_map/ppermute | solution.py:631
  362.5 31.7 %collective-permute-start.43 = (bf16[1056,512]{1,0:T(8,128)(2,1)S(1)}, bf16[1056,512]{1,0:T(8,128)(2,1)}, u32[]{:S(2)}, u32[]{:S(2)}) collective-permute-start(bf16[1056,512]{1,0:T(8,128)(2,1)S(1)} %copy-done.12), channel_id=1, source_target_pairs={{8,0},{16,8},{24,16},{28,24},{20,28},{12,20},{4,12},{0,4},{9,1},{1... | collective-permute-start | bytes 3244040 | tf_op jit(solution)/shard_map/ppermute | solution.py:636
  394.2 32.9 %collective-permute-start.44 = (bf16[1056,512]{1,0:T(8,128)(2,1)}, bf16[1056,512]{1,0:T(8,128)(2,1)S(1)}, u32[]{:S(2)}, u32[]{:S(2)}) collective-permute-start(bf16[1056,512]{1,0:T(8,128)(2,1)} %get-tuple-element.113.refs_20_.refs_1_), channel_id=1, source_target_pairs={{0,8},{8,16},{16,24},{24,28},{28,20},{20,12},{12,4},{4,0},{1,9},{9... | collective-permute-start | bytes 3244040 | tf_op jit(solution)/shard_map/ppermute | solution.py:631
  395.9 31.3 %collective-permute-start.45 = (bf16[1056,512]{1,0:T(8,128)(2,1)}, bf16[1056,512]{1,0:T(8,128)(2,1)S(1)}, u32[]{:S(2)}, u32[]{:S(2)}) collective-permute-start(bf16[1056,512]{1,0:T(8,128)(2,1)} %get-tuple-element.114.refs_21_.refs_2_), channel_id=1, source_target_pairs={{8,0},{16,8},{24,16},{28,24},{20,28},{12,20},{4,12},{0,4},{9,1},{1... | collective-permute-start | bytes 3244040 | tf_op jit(solution)/shard_map/ppermute | solution.py:636
  (77 other events, 715.5 us)

commit v8 on v7

--- a/solution.py
+++ b/solution.py
@@ -908,11 +908,6 @@
     later.append(((r, 0), (core_swap(r), 0), (l, 0), (core_swap(l), 0)))
     steps = 2 * far - 1
     for level, rows in enumerate(row_bounds):
-        if level == buckets - 1 and step == steps:
-            order = jnp.stack(ring.indices()).astype(jnp.int32)
-            size = model // devices_dp
-            unpacked = unpack(order[:-1], chunks[:-1], size, devices_dp)
-            sending = sending + (unpacked[0],)
         carried = weight_gradients(level, rows, length, later, w_up, w_down, tuple(carried), False, sending)
         ready = ()
         if level == 0:
@@ -933,9 +928,7 @@
     grad_up, grad_down = carried
     order = jnp.stack(ring.indices()).astype(jnp.int32)
     size = model // devices_dp
-    if devices_dp != 8:
-        unpacked = unpack(order[:-1], chunks[:-1], size, devices_dp)
-    grad_wqkv, grad_wout = unpack(order[-1:], chunks[-1:], size, devices_dp, unpacked)
+    grad_wqkv, grad_wout = unpack(order, chunks, size, devices_dp)
     terms = jnp.stack([x[4 * size:] for x in chunks])
     by_place = jnp.zeros((devices_dp,), jnp.int32).at[order].set(jnp.arange(devices_dp, dtype=jnp.int32))
     small = jnp.sum(terms[by_place].astype(F32), 0).reshape(small.shape)

time: 503 us -> 500 us (level)
    ppermute x13, starting transfers between devices: 7.28 us -> 19.3 us  [to_left(): out = lax.ppermute(x, 'dp', self.left)]
    ppermute x13, starting transfers between devices: 21.3 us -> 9.32 us  [to_right(): out = lax.ppermute(x, 'dp', self.right)]
    ppermute x13, waiting for transfers between devices: 27.8 us -> 22.6 us  [to_right(): out = lax.ppermute(x, 'dp', self.right)]
    pallas_call x2 -> x1, Pallas kernels: 12.6 us -> 11 us  [unpack(): pl.pallas_call(partial(unpack_kernel, count=count, carried=len(carried)),...]
    unnamed x116 -> x120, local copies, waits for them, and re-layouts: 34.3 us -> 34.9 us
  transfers between devices with their start and end apart: 50 -> 50, of which waited for: 15 -> 14; matrix products, arithmetic and copies ran while one was open for 16% -> 15% of each run, Pallas kernels for 51% -> 49%
where the time goes in v8:
time: 500 us; the launch traced here: 492 us
  Pallas kernels  273 us (55%)
  waiting for transfers between devices  68.2 us (14%)
  local copies, waits for them, and re-layouts  59.2 us (12%)
  starting transfers between devices  39.6 us (8%)
  other arithmetic  33.6 us (7%)
  matrix products  11.1 us (2%)
  between operations  8.32 us (2%)
    pallas_call x8, Pallas kernels, weight_gradients(): pl.pallas_call(partial(weight_kernel, level=level, rows=rows, group=group...  161 us
    unnamed x120, local copies, waits for them, and re-layouts  34.9 us
    pallas_call x1, Pallas kernels, attend_back(): pl.pallas_call(partial(attend_back_kernel, heads=heads, steps=steps, deps...  23.8 us
    ppermute x13, waiting for transfers between devices, to_right(): out = lax.ppermute(x, 'dp', self.right)  22.6 us
    ppermute x5, waiting for transfers between devices, sum_over_x(): lax.ppermute(x, 'mp', [(i, (i + 2 * k) % (2 * n)) for i in range(2 * n)])  20.3 us
    ppermute x13, starting transfers between devices, to_left(): out = lax.ppermute(x, 'dp', self.left)  19.3 us
    pallas_call x1, Pallas kernels, own_grad(): pl.pallas_call(partial(own_grad_kernel, row_bounds=tuple(row_bounds), dep...  17.3 us
    pallas_call x1, Pallas kernels, attend(): pl.pallas_call(partial(attend_kernel, heads=heads, steps=steps), grid=(st...  15.7 us
  transfers between devices with their start and end apart: 50, of which 14 were waited for; matrix products, arithmetic and copies ran while one was open for 15% of the time, Pallas kernels for 49%

profile of v8, /device:TPU:0, one launch (start us, length us, event | category | flops | bytes accessed | tf_op | source)
XLA Modules:
  0.0 492.5 jit_solution(14120170491941802176)
XLA Ops:
  2.6 15.7 %attend.1 = (bf16[256,2048]{1,0:T(8,128)(2,1)}, bf16[256,2048]{1,0:T(8,128)(2,1)}, bf16[512,2048]{1,0:T(8,128)(2,1)}, bf16[3,512,512]{2,1,0:T(8,128)(2,1)}, f32[...) custom-call(bf16[512,2048]{1,0:T(8,128)(2,1)} %x_ref.1, f32[1,2048]{1,0:T(1,128)} %bitcast.61, ...), custom_call_target="tpu_custom_call" | custom-call | flops 1207959552 | bytes 3145728 | tf_op jit(solution)/shard_map/attend/pallas_call | solution.py:102
  36.1 16.5 %collective-permute-done.1 = bf16[256,2048]{1,0:T(8,128)(2,1)} collective-permute-done((bf16[256,2048]{1,0:T(8,128)(2,1)}, bf16[256,2048]{1,0:T(8,128)(2,1)}, u32[]{:S(2)}, u32[]{:S(2)}) %collective-permute-start.1) | collective-permute-done | bytes 1048608 | tf_op jit(solution)/shard_map/ppermute | solution.py:696
  70.1 17.3 %own_grad.1 = (bf16[256,2048]{1,0:T(8,128)(2,1)}, bf16[256,2048]{1,0:T(8,128)(2,1)}, bf16[4,512,512]{2,1,0:T(8,128)(2,1)}) custom-call(bf16[512,2048]{1,0:T(8,128)(2,1)} %copy-done.28, bf16[512,2048]{1,0:T(8,128)(2,1)} %copy-done.16, s32[512,128]{1,0:T(8,128)} %broadcast_in_dim.61.bucket_ref, f32[512,128]{1,0:T(8,128)} %broadcast_in_dim.64.gate_ref, ...), custom_call_target="tpu_custom_call" | custom-call | flops 2315255808 | bytes 5767168 | tf_op jit(solution)/shard_map/own_grad/pallas_call | solution.py:248
  102.9 10.4 %own_forward.1 = (bf16[512,2048]{1,0:T(8,128)(2,1)}, f32[512,128]{1,0:T(8,128)}) custom-call(bf16[4,512,512]{2,1,0:T(8,128)(2,1)} %get-tuple-element.70.act_ref, bf16[512,2048]{1,0:T(8,128)(2,1)} %copy-done.16, bf16[512,512]{1,0:T(8,128)(2,1)} %fusion.26.unsort_ref, bf16[4,512,2048]{2,1,0:T(8,128)(2,1)} %refs_17_.15, ...), custom_call_target="tpu_custom_call" | custom-call | flops 771751936 | bytes 3670016 | tf_op jit(solution)/shard_map/own_forward/pallas_call | solution.py:288
  120.5 3.9 multiply_reduce_fusion
  135.8 23.8 %attend_back.1 = (bf16[4,2048,512]{2,1,0:T(8,128)(2,1)}, bf16[512,2048]{1,0:T(8,128)(2,1)}) custom-call(bf16[512,2048]{1,0:T(8,128)(2,1)} %pad_maximum_fusion.ga_ref, bf16[512,2048]{1,0:T(8,128)(2,1)} %get-tuple-element.79.normed_ref, bf16[3,512,512]{2,1,0:T(8,128)(2,1)} %get-tuple-element.80.qkv_ref, f32[4,512,128]{2,1,0:T(8,128)} %get-tuple-element.81.lse_ref, ...), custom_call_target="tpu_custom_call" | custom-call | flops 2483027968 | bytes 6291456 | tf_op jit(solution)/shard_map/attend_back/pallas_call | solution.py:195
  167.2 9.6 %collective-permute-done.18.refs_1_ = bf16[1040,1024]{1,0:T(8,128)(2,1)} collective-permute-done((bf16[1040,1024]{1,0:T(8,128)(2,1)}, bf16[1040,1024]{1,0:T(8,128)(2,1)}, u32[]{:S(2)}, u32[]{:S(2)}) %collective-permute-start.18) | collective-permute-done | bytes 2129952 | tf_op jit(solution)/shard_map/ppermute | solution.py:636
  190.1 24.4 %weight_gradients_0.1 = (f32[4,2048,512]{2,1,0:T(8,128)}, f32[4,512,2048]{2,1,0:T(8,128)}) custom-call(bf16[512,1024]{1,0:T(8,128)(2,1)} %get-tuple-element.148.refs_0_, bf16[512,1024]{1,0:T(8,128)(2,1)} %get-tuple-element.147.refs_1_, bf16[528,1024]{1,0:T(8,128)(2,1)} %copy-done.11, bf16[512,1024]{1,0:T(8,128)(2,1)} %get-tuple-element.145.refs_3_, ...), custom_call_target="tpu_custom_call" | custom-call | flops 4294967296 | bytes 8388608 | tf_op jit(solution)/shard_map/weight_gradients_0/pallas_call | solution.py:438
  220.7 4.6 join.3
  227.4 23.8 %weight_gradients_1.1 = (f32[4,2048,512]{2,1,0:T(8,128)}, f32[4,512,2048]{2,1,0:T(8,128)}) custom-call(bf16[512,1024]{1,0:T(8,128)(2,1)} %get-tuple-element.148.refs_0_, bf16[512,1024]{1,0:T(8,128)(2,1)} %get-tuple-element.147.refs_1_, bf16[528,1024]{1,0:T(8,128)(2,1)} %copy-done.11, ...), custom_call_target="tpu_custom_call", output_to_operand_aliasing={{0}: (18, {}), {1}: (19, {})} | custom-call | flops 4026531840 | bytes 8126464 | tf_op jit(solution)/shard_map/weight_gradients_1/pallas_call | solution.py:438
  259.2 6.4 %collective-permute-done.25.right_ref = bf16[4,256,512]{2,1,0:T(8,128)(2,1)S(1)} collective-permute-done((bf16[4,256,512]{2,1,0:T(8,128)(2,1)}, bf16[4,256,512]{2,1,0:T(8,128)(2,1)S(1)}, u32[]{:S(2)}, u32[]{:S(2)}) %collective-permute-start.25) | collective-permute-done | bytes 1048608 | tf_op jit(solution)/shard_map/ppermute | solution.py:631
  266.5 4.8 join.4
  275.1 18.2 %weight_gradients_2.1 = (f32[4,2048,512]{2,1,0:T(8,128)}, f32[4,512,2048]{2,1,0:T(8,128)}) custom-call(bf16[512,1024]{1,0:T(8,128)(2,1)} %get-tuple-element.148.refs_0_, bf16[512,1024]{1,0:T(8,128)(2,1)} %get-tuple-element.147.refs_1_, bf16[528,1024]{1,0:T(8,128)(2,1)} %copy-done.11, ...), custom_call_target="tpu_custom_call", output_to_operand_aliasing={{0}: (18, {}), {1}: (19, {})} | custom-call | flops 2684354560 | bytes 6815744 | tf_op jit(solution)/shard_map/weight_gradients_2/pallas_call | solution.py:438
  304.9 5.0 %join.5 = (bf16[4,256,512]{2,1,0:T(8,128)(2,1)}, bf16[4,256,512]{2,1,0:T(8,128)(2,1)}) custom-call(s32[2]{0:T(128)} %pad_add_fusion.3.index_ref, bf16[4,2048,512]{2,1,0:T(8,128)(2,1)} %get-tuple-element.83.refs_1_.refs_2_.right_local.left_local.local_ref, bf16[4,2048,512]{2,1,0:T(8,128)(2,1)} %get-tuple-element.83.refs_1_.refs_2_.right_local.left_local.local_ref, ...), custom_call_target="tpu_custom_call" | custom-call | flops 262144 | bytes 1572864 | tf_op jit(solution)/shard_map/join/pallas_call | solution.py:555
  312.2 4.2 fusion.7.refs_22_
  316.4 13.2 %weight_gradients_3.1 = (f32[4,2048,512]{2,1,0:T(8,128)}, f32[4,512,2048]{2,1,0:T(8,128)}) custom-call(bf16[512,1024]{1,0:T(8,128)(2,1)} %get-tuple-element.148.refs_0_, bf16[512,1024]{1,0:T(8,128)(2,1)} %get-tuple-element.147.refs_1_, bf16[528,1024]{1,0:T(8,128)(2,1)} %copy-done.11, ...), custom_call_target="tpu_custom_call", output_to_operand_aliasing={{0}: (18, {}), {1}: (19, {})} | custom-call | flops 1342177280 | bytes 5505024 | tf_op jit(solution)/shard_map/weight_gradients_3/pallas_call | solution.py:438
  331.7 15.0 %collective-permute-done.33.right_ref = bf16[4,256,512]{2,1,0:T(8,128)(2,1)} collective-permute-done((bf16[4,256,512]{2,1,0:T(8,128)(2,1)}, bf16[4,256,512]{2,1,0:T(8,128)(2,1)}, u32[]{:S(2)}, u32[]{:S(2)}) %collective-permute-start.33) | collective-permute-done | bytes 1048608 | tf_op jit(solution)/shard_map/ppermute | solution.py:631
  346.8 3.9 join_own.1.refs_5_.refs_20_.refs_21_.refs_0_
  356.8 4.9 collective-permute-done.38.refs_13_
  368.8 24.3 %weight_gradients_0_more.1 = (f32[4,2048,512]{2,1,0:T(8,128)}, f32[4,512,2048]{2,1,0:T(8,128)}) custom-call(bf16[1040,1024]{1,0:T(8,128)(2,1)} %get-tuple-element.85.refs_22_.refs_0_.refs_2_, bf16[1040,1024]{1,0:T(8,128)(2,1)} %collective-permute-done.20.refs_23_.refs_1_.refs_3_, ...), custom_call_target="tpu_custom_call", output_to_operand_aliasing={{0}: (18, {}), {1}: (19, {})} | custom-call | flops 4294967296 | bytes 8388608 | tf_op jit(solution)/shard_map/weight_gradients_0_more/pallas_call | solution.py:438
  398.5 23.6 %weight_gradients_1_more.1 = (f32[4,2048,512]{2,1,0:T(8,128)}, f32[4,512,2048]{2,1,0:T(8,128)}) custom-call(bf16[1040,1024]{1,0:T(8,128)(2,1)} %get-tuple-element.85.refs_22_.refs_0_.refs_2_, bf16[1040,1024]{1,0:T(8,128)(2,1)} %collective-permute-done.20.refs_23_.refs_1_.refs_3_, ...), custom_call_target="tpu_custom_call", output_to_operand_aliasing={{0}: (18, {}), {1}: (19, {})} | custom-call | flops 4026531840 | bytes 8126464 | tf_op jit(solution)/shard_map/weight_gradients_1_more/pallas_call | solution.py:438
  436.3 19.0 %weight_gradients_2_more.1 = (f32[4,2048,512]{2,1,0:T(8,128)}, f32[4,512,2048]{2,1,0:T(8,128)}) custom-call(bf16[1040,1024]{1,0:T(8,128)(2,1)} %get-tuple-element.85.refs_22_.refs_0_.refs_2_, bf16[1040,1024]{1,0:T(8,128)(2,1)} %collective-permute-done.20.refs_23_.refs_1_.refs_3_, ...), custom_call_target="tpu_custom_call", output_to_operand_aliasing={{0}: (18, {}), {1}: (19, {})} | custom-call | flops 2684354560 | bytes 6815744 | tf_op jit(solution)/shard_map/weight_gradients_2_more/pallas_call | solution.py:438
  461.3 14.9 %weight_gradients_3_more.1 = (f32[4,2048,512]{2,1,0:T(8,128)}, f32[4,512,2048]{2,1,0:T(8,128)}) custom-call(bf16[1040,1024]{1,0:T(8,128)(2,1)} %get-tuple-element.85.refs_22_.refs_0_.refs_2_, bf16[1040,1024]{1,0:T(8,128)(2,1)} %collective-permute-done.20.refs_23_.refs_1_.refs_3_, ...), custom_call_target="tpu_custom_call", output_to_operand_aliasing={{0}: (18, {}), {1}: (19, {})} | custom-call | flops 1342177280 | bytes 5505024 | tf_op jit(solution)/shard_map/weight_gradients_3_more/pallas_call | solution.py:438
  481.3 11.0 %unpack_some.1 = (f32[3,2048,512]{2,1,0:T(8,128)}, f32[512,2048]{1,0:T(8,128)}) custom-call(s32[8]{0:T(128)} %stack.132.order_ref, bf16[1056,512]{1,0:T(8,128)(2,1)} %join_own.1.refs_5_.refs_20_.refs_21_.refs_0_, bf16[1056,512]{1,0:T(8,128)(2,1)} %get-tuple-element.111.refs_20_.refs_1_, bf16[1056,512]{1,0:T(8,128)(2,1)} %get-tuple-element.112.refs_21_.refs_2_, ...), custom_call_target="tpu_custom_call" | custom-call | bytes 6291456 | tf_op jit(solution)/shard_map/unpack_some/pallas_call | solution.py:475
  (314 shorter events, 165.6 us)
Async XLA Ops:
  32.4 35.9 %collective-permute-start.4 = (bf16[512,1024]{1,0:T(8,128)(2,1)}, bf16[512,1024]{1,0:T(8,128)(2,1)S(1)}, u32[]{:S(2)}, u32[]{:S(2)}) collective-permute-start(bf16[512,1024]{1,0:T(8,128)(2,1)} %get-tuple-element.148.refs_0_), channel_id=1, source_target_pairs={{0,8},{8,16},{16,24},{24,28},{28,20},{20,12},{12,4},{4,0},{1,9},{9... | collective-permute-start | bytes 3145736 | tf_op jit(solution)/shard_map/ppermute | solution.py:631
  34.0 34.3 %collective-permute-start.5 = (bf16[512,1024]{1,0:T(8,128)(2,1)}, bf16[512,1024]{1,0:T(8,128)(2,1)}, u32[]{:S(2)}, u32[]{:S(2)}) collective-permute-start(bf16[512,1024]{1,0:T(8,128)(2,1)} %get-tuple-element.148.refs_0_), channel_id=1, source_target_pairs={{8,0},{16,8},{24,16},{28,24},{20,28},{12,20},{4,12},{0,4},{9,1},{1... | collective-permute-start | bytes 3145736 | tf_op jit(solution)/shard_map/ppermute | solution.py:636
  66.0 30.6 %collective-permute-start.7 = (bf16[528,1024]{1,0:T(8,128)(2,1)S(1)}, bf16[528,1024]{1,0:T(8,128)(2,1)S(1)}, u32[]{:S(2)}, u32[]{:S(2)}) collective-permute-start(bf16[528,1024]{1,0:T(8,128)(2,1)S(1)} %fusion.20.rest_2_.refs_2_), channel_id=1, source_target_pairs={{0,8},{8,16},{16,24},{24,28},{28,20},{20,12},{12,4},{4,0},{1,9},{9... | collective-permute-start | bytes 3244040 | tf_op jit(solution)/shard_map/ppermute | solution.py:631
  127.7 49.1 %collective-permute-start.18 = (bf16[1040,1024]{1,0:T(8,128)(2,1)}, bf16[1040,1024]{1,0:T(8,128)(2,1)}, u32[]{:S(2)}, u32[]{:S(2)}) collective-permute-start(bf16[1040,1024]{1,0:T(8,128)(2,1)} %copy-done.5), channel_id=1, source_target_pairs={{8,0},{16,8},{24,16},{28,24},{20,28},{12,20},{4,12},{0,4},{9,1},{1... | collective-permute-start | bytes 6389768 | tf_op jit(solution)/shard_map/ppermute | solution.py:636
  129.5 48.5 %collective-permute-start.17 = (bf16[1040,1024]{1,0:T(8,128)(2,1)S(1)}, bf16[1040,1024]{1,0:T(8,128)(2,1)}, u32[]{:S(2)}, u32[]{:S(2)}) collective-permute-start(bf16[1040,1024]{1,0:T(8,128)(2,1)S(1)} %copy-done.4), channel_id=1, source_target_pairs={{0,8},{8,16},{16,24},{24,28},{28,20},{20,12},{12,4},{4,0},{1,9},{9... | collective-permute-start | bytes 6389768 | tf_op jit(solution)/shard_map/ppermute | solution.py:631
  178.5 36.0 %collective-permute-start.16 = (bf16[256,2048]{1,0:T(8,128)(2,1)S(1)}, bf16[256,2048]{1,0:T(8,128)(2,1)}, u32[]{:S(2)}, u32[]{:S(2)}) collective-permute-start(bf16[256,2048]{1,0:T(8,128)(2,1)S(1)} %copy-done.27), channel_id=1, source_target_pairs={{0,2},{1,3},{2,0},{3,1},{4,6},{5,7},{6,4},{7,5},{8,10},{9,11},{10,... | collective-permute-start | bytes 3145736 | tf_op jit(solution)/shard_map/ppermute | solution.py:696
  183.7 37.0 %collective-permute-start.22 = (bf16[4,128,512]{2,1,0:T(8,128)(2,1)}, bf16[4,128,512]{2,1,0:T(8,128)(2,1)}, u32[]{:S(2)}, u32[]{:S(2)}) collective-permute-start(bf16[4,128,512]{2,1,0:T(8,128)(2,1)} %get-tuple-element.138.refs_18_), channel_id=1, source_target_pairs={{0,8},{8,16},{16,24},{24,28},{28,20},{20,12},{12,4},{4,0},{1,9},{9... | collective-permute-start | bytes 1572872 | tf_op jit(solution)/shard_map/ppermute | solution.py:631
  184.2 36.5 %collective-permute-start.23 = (bf16[4,128,512]{2,1,0:T(8,128)(2,1)}, bf16[4,128,512]{2,1,0:T(8,128)(2,1)}, u32[]{:S(2)}, u32[]{:S(2)}) collective-permute-start(bf16[4,128,512]{2,1,0:T(8,128)(2,1)} %get-tuple-element.137.refs_19_), channel_id=1, source_target_pairs={{8,0},{16,8},{24,16},{28,24},{20,28},{12,20},{4,12},{0,4},{9,1},{1... | collective-permute-start | bytes 1572872 | tf_op jit(solution)/shard_map/ppermute | solution.py:636
  187.2 106.2 %collective-permute-start.27 = (bf16[1040,1024]{1,0:T(8,128)(2,1)}, bf16[1040,1024]{1,0:T(8,128)(2,1)}, u32[]{:S(2)}, u32[]{:S(2)}) collective-permute-start(bf16[1040,1024]{1,0:T(8,128)(2,1)} %get-tuple-element.84.refs_12_.refs_14_.refs_20_), channel_id=1, source_target_pairs={{0,8},{8,16},{16,24},{24,28},{28,20},{20,12},{12,4},{4,0},{1,9},{9... | collective-permute-start | bytes 6389768 | tf_op jit(solution)/shard_map/ppermute | solution.py:631
  188.5 104.8 %collective-permute-start.28 = (bf16[1040,1024]{1,0:T(8,128)(2,1)}, bf16[1040,1024]{1,0:T(8,128)(2,1)S(1)}, u32[]{:S(2)}, u32[]{:S(2)}) collective-permute-start(bf16[1040,1024]{1,0:T(8,128)(2,1)} %get-tuple-element.85.refs_22_.refs_0_.refs_2_), channel_id=1, source_target_pairs={{8,0},{16,8},{24,16},{28,24},{20,28},{12,20},{4,12},{0,4},{9,1},{1... | collective-permute-start | bytes 6389768 | tf_op jit(solution)/shard_map/ppermute | solution.py:636
  218.8 32.4 %collective-permute-start.21 = (bf16[256,2048]{1,0:T(8,128)(2,1)}, bf16[256,2048]{1,0:T(8,128)(2,1)}, u32[]{:S(2)}, u32[]{:S(2)}) collective-permute-start(bf16[256,2048]{1,0:T(8,128)(2,1)} %after.18), channel_id=1, source_target_pairs={{0,1},{1,0},{2,3},{3,2},{4,5},{5,4},{6,7},{7,6},{8,9},{9,8},{10,11... | collective-permute-start | bytes 3145736 | tf_op jit(solution)/shard_map/ppermute | solution.py:689
  225.4 40.2 %collective-permute-start.25 = (bf16[4,256,512]{2,1,0:T(8,128)(2,1)}, bf16[4,256,512]{2,1,0:T(8,128)(2,1)S(1)}, u32[]{:S(2)}, u32[]{:S(2)}) collective-permute-start(bf16[4,256,512]{2,1,0:T(8,128)(2,1)} %get-tuple-element.89.refs_20_), channel_id=1, source_target_pairs={{0,8},{8,16},{16,24},{24,28},{28,20},{20,12},{12,4},{4,0},{1,9},{9... | collective-permute-start | bytes 3145736 | tf_op jit(solution)/shard_map/ppermute | solution.py:631
  225.8 40.2 %collective-permute-start.26 = (bf16[4,256,512]{2,1,0:T(8,128)(2,1)}, bf16[4,256,512]{2,1,0:T(8,128)(2,1)}, u32[]{:S(2)}, u32[]{:S(2)}) collective-permute-start(bf16[4,256,512]{2,1,0:T(8,128)(2,1)} %get-tuple-element.90.refs_21_), channel_id=1, source_target_pairs={{8,0},{16,8},{24,16},{28,24},{20,28},{12,20},{4,12},{0,4},{9,1},{1... | collective-permute-start | bytes 3145736 | tf_op jit(solution)/shard_map/ppermute | solution.py:636
  254.8 46.4 %collective-permute-start.24 = (bf16[256,2048]{1,0:T(8,128)(2,1)}, bf16[256,2048]{1,0:T(8,128)(2,1)}, u32[]{:S(2)}, u32[]{:S(2)}) collective-permute-start(bf16[256,2048]{1,0:T(8,128)(2,1)} %add_rows.7), channel_id=1, source_target_pairs={{0,2},{1,3},{2,0},{3,1},{4,6},{5,7},{6,4},{7,5},{8,10},{9,11},{10,... | collective-permute-start | bytes 3145736 | tf_op jit(solution)/shard_map/ppermute | solution.py:696
  271.4 33.6 %collective-permute-start.31 = (bf16[4,256,512]{2,1,0:T(8,128)(2,1)}, bf16[4,256,512]{2,1,0:T(8,128)(2,1)}, u32[]{:S(2)}, u32[]{:S(2)}) collective-permute-start(bf16[4,256,512]{2,1,0:T(8,128)(2,1)} %get-tuple-element.93.refs_20_), channel_id=1, source_target_pairs={{0,8},{8,16},{16,24},{24,28},{28,20},{20,12},{12,4},{4,0},{1,9},{9... | collective-permute-start | bytes 3145736 | tf_op jit(solution)/shard_map/ppermute | solution.py:631
  272.4 32.5 %collective-permute-start.32 = (bf16[4,256,512]{2,1,0:T(8,128)(2,1)}, bf16[4,256,512]{2,1,0:T(8,128)(2,1)}, u32[]{:S(2)}, u32[]{:S(2)}) collective-permute-start(bf16[4,256,512]{2,1,0:T(8,128)(2,1)} %get-tuple-element.94.refs_21_), channel_id=1, source_target_pairs={{8,0},{16,8},{24,16},{28,24},{20,28},{12,20},{4,12},{0,4},{9,1},{1... | collective-permute-start | bytes 3145736 | tf_op jit(solution)/shard_map/ppermute | solution.py:636
  297.0 53.7 %collective-permute-start.30 = (bf16[528,1024]{1,0:T(8,128)(2,1)}, bf16[528,1024]{1,0:T(8,128)(2,1)S(1)}, u32[]{:S(2)}, u32[]{:S(2)}) collective-permute-start(bf16[528,1024]{1,0:T(8,128)(2,1)} %slice.55), channel_id=1, source_target_pairs={{8,0},{16,8},{24,16},{28,24},{20,28},{12,20},{4,12},{0,4},{9,1},{1... | collective-permute-start | bytes 3244040 | tf_op jit(solution)/shard_map/ppermute | solution.py:636
  300.8 49.8 %collective-permute-start.29 = (bf16[512,1024]{1,0:T(8,128)(2,1)}, bf16[512,1024]{1,0:T(8,128)(2,1)S(1)}, u32[]{:S(2)}, u32[]{:S(2)}) collective-permute-start(bf16[512,1024]{1,0:T(8,128)(2,1)} %slice.54), channel_id=1, source_target_pairs={{0,8},{8,16},{16,24},{24,28},{28,20},{20,12},{12,4},{4,0},{1,9},{9... | collective-permute-start | bytes 3145736 | tf_op jit(solution)/shard_map/ppermute | solution.py:631
  310.0 36.8 %collective-permute-start.33 = (bf16[4,256,512]{2,1,0:T(8,128)(2,1)}, bf16[4,256,512]{2,1,0:T(8,128)(2,1)}, u32[]{:S(2)}, u32[]{:S(2)}) collective-permute-start(bf16[4,256,512]{2,1,0:T(8,128)(2,1)} %get-tuple-element.99.refs_20_), channel_id=1, source_target_pairs={{0,8},{8,16},{16,24},{24,28},{28,20},{20,12},{12,4},{4,0},{1,9},{9... | collective-permute-start | bytes 3145736 | tf_op jit(solution)/shard_map/ppermute | solution.py:631
  310.4 36.3 %collective-permute-start.34 = (bf16[4,256,512]{2,1,0:T(8,128)(2,1)}, bf16[4,256,512]{2,1,0:T(8,128)(2,1)}, u32[]{:S(2)}, u32[]{:S(2)}) collective-permute-start(bf16[4,256,512]{2,1,0:T(8,128)(2,1)} %get-tuple-element.100.refs_21_), channel_id=1, source_target_pairs={{8,0},{16,8},{24,16},{28,24},{20,28},{12,20},{4,12},{0,4},{9,1},{1... | collective-permute-start | bytes 3145736 | tf_op jit(solution)/shard_map/ppermute | solution.py:636
  356.3 38.2 %collective-permute-start.42 = (bf16[1056,512]{1,0:T(8,128)(2,1)S(1)}, bf16[1056,512]{1,0:T(8,128)(2,1)}, u32[]{:S(2)}, u32[]{:S(2)}) collective-permute-start(bf16[1056,512]{1,0:T(8,128)(2,1)S(1)} %copy-done.12), channel_id=1, source_target_pairs={{0,8},{8,16},{16,24},{24,28},{28,20},{20,12},{12,4},{4,0},{1,9},{9... | collective-permute-start | bytes 3244040 | tf_op jit(solution)/shard_map/ppermute | solution.py:631
  361.7 32.8 %collective-permute-start.43 = (bf16[1056,512]{1,0:T(8,128)(2,1)S(1)}, bf16[1056,512]{1,0:T(8,128)(2,1)}, u32[]{:S(2)}, u32[]{:S(2)}) collective-permute-start(bf16[1056,512]{1,0:T(8,128)(2,1)S(1)} %copy-done.12), channel_id=1, source_target_pairs={{8,0},{16,8},{24,16},{28,24},{20,28},{12,20},{4,12},{0,4},{9,1},{1... | collective-permute-start | bytes 3244040 | tf_op jit(solution)/shard_map/ppermute | solution.py:636
  394.5 32.9 %collective-permute-start.44 = (bf16[1056,512]{1,0:T(8,128)(2,1)}, bf16[1056,512]{1,0:T(8,128)(2,1)S(1)}, u32[]{:S(2)}, u32[]{:S(2)}) collective-permute-start(bf16[1056,512]{1,0:T(8,128)(2,1)} %get-tuple-element.111.refs_20_.refs_1_), channel_id=1, source_target_pairs={{0,8},{8,16},{16,24},{24,28},{28,20},{20,12},{12,4},{4,0},{1,9},{9... | collective-permute-start | bytes 3244040 | tf_op jit(solution)/shard_map/ppermute | solution.py:631
  395.1 32.5 %collective-permute-start.45 = (bf16[1056,512]{1,0:T(8,128)(2,1)}, bf16[1056,512]{1,0:T(8,128)(2,1)S(1)}, u32[]{:S(2)}, u32[]{:S(2)}) collective-permute-start(bf16[1056,512]{1,0:T(8,128)(2,1)} %get-tuple-element.112.refs_21_.refs_2_), channel_id=1, source_target_pairs={{8,0},{16,8},{24,16},{28,24},{20,28},{12,20},{4,12},{0,4},{9,1},{1... | collective-permute-start | bytes 3244040 | tf_op jit(solution)/shard_map/ppermute | solution.py:636
  (79 other events, 710.5 us)

commit v9 on v8

--- a/solution.py
+++ b/solution.py
@@ -896,7 +896,9 @@
         arrived, sending = advance(step, arrived, (carried[0],))
         step += 1
         if slot_at == 3:
-            r, l, *held = after([r, l] + [x for x, _ in met[far:]], (carried[0], sending[0]))
+            held = after([x for x, _ in met[far:]], (carried[0],))
+            held = [(x, core_swap(x)) for x in held]
+            r, l = after((r, l), (carried[0], sending[0]))
         if slot_at == 1:
             sending = sending + (output_half,)
         if slot_at == 2:
@@ -904,7 +906,7 @@
             while len(met) < 2 * far - 2:
                 r, l = forward((r, l), (carried[0],))
             sending = sending + tuple(pair[0] for pair in met[far:])
-    later += [block(x, core_swap(x)) for x in held]
+    later += [block(*x) for x in held]
     later.append(((r, 0), (core_swap(r), 0), (l, 0), (core_swap(l), 0)))
     steps = 2 * far - 1
     for level, rows in enumerate(row_bounds):

time: 500 us -> 503 us (level)
  waiting for transfers between devices: 68.2 us -> 73.5 us
    ppermute x13, waiting for transfers between devices: 22.6 us -> 32.6 us  [to_right(): out = lax.ppermute(x, 'dp', self.right)]
    unnamed x120 -> x130, local copies, waits for them, and re-layouts: 34.9 us -> 32.5 us
where the time goes in v9:
time: 503 us; the launch traced here: 496 us
  Pallas kernels  272 us (54%)
  waiting for transfers between devices  73.5 us (15%)
  local copies, waits for them, and re-layouts  55.7 us (11%)
  starting transfers between devices  39.8 us (8%)
  other arithmetic  33.1 us (7%)
  matrix products  12.7 us (3%)
  between operations  8.35 us (2%)
    pallas_call x8, Pallas kernels, weight_gradients(): pl.pallas_call(partial(weight_kernel, level=level, rows=rows, group=group...  161 us
    ppermute x13, waiting for transfers between devices, to_right(): out = lax.ppermute(x, 'dp', self.right)  32.6 us
    unnamed x130, local copies, waits for them, and re-layouts  32.5 us
    pallas_call x1, Pallas kernels, attend_back(): pl.pallas_call(partial(attend_back_kernel, heads=heads, steps=steps, deps...  23.8 us
    ppermute x5, waiting for transfers between devices, sum_over_x(): lax.ppermute(x, 'mp', [(i, (i + 2 * k) % (2 * n)) for i in range(2 * n)])  20.3 us
    ppermute x13, starting transfers between devices, to_left(): out = lax.ppermute(x, 'dp', self.left)  17.4 us
    pallas_call x1, Pallas kernels, own_grad(): pl.pallas_call(partial(own_grad_kernel, row_bounds=tuple(row_bounds), dep...  17.3 us
    pallas_call x1, Pallas kernels, attend(): pl.pallas_call(partial(attend_kernel, heads=heads, steps=steps), grid=(st...  15.7 us
  transfers between devices with their start and end apart: 50, of which 14 were waited for; matrix products, arithmetic and copies ran while one was open for 15% of the time, Pallas kernels for 49%

profile of v9, /device:TPU:0, one launch (start us, length us, event | category | flops | bytes accessed | tf_op | source)
XLA Modules:
  0.0 495.7 jit_solution(10214355338818226065)
XLA Ops:
  2.6 15.7 %attend.1 = (bf16[256,2048]{1,0:T(8,128)(2,1)}, bf16[256,2048]{1,0:T(8,128)(2,1)}, bf16[512,2048]{1,0:T(8,128)(2,1)}, bf16[3,512,512]{2,1,0:T(8,128)(2,1)}, f32[...) custom-call(bf16[512,2048]{1,0:T(8,128)(2,1)} %x_ref.1, f32[1,2048]{1,0:T(1,128)} %bitcast.61, ...), custom_call_target="tpu_custom_call" | custom-call | flops 1207959552 | bytes 3145728 | tf_op jit(solution)/shard_map/attend/pallas_call | solution.py:102
  36.0 16.6 %collective-permute-done.1 = bf16[256,2048]{1,0:T(8,128)(2,1)} collective-permute-done((bf16[256,2048]{1,0:T(8,128)(2,1)}, bf16[256,2048]{1,0:T(8,128)(2,1)}, u32[]{:S(2)}, u32[]{:S(2)}) %collective-permute-start.1) | collective-permute-done | bytes 1048608 | tf_op jit(solution)/shard_map/ppermute | solution.py:696
  70.1 17.3 %own_grad.1 = (bf16[256,2048]{1,0:T(8,128)(2,1)}, bf16[256,2048]{1,0:T(8,128)(2,1)}, bf16[4,512,512]{2,1,0:T(8,128)(2,1)}) custom-call(bf16[512,2048]{1,0:T(8,128)(2,1)} %copy-done.28, bf16[512,2048]{1,0:T(8,128)(2,1)} %copy-done.14, s32[512,128]{1,0:T(8,128)} %broadcast_in_dim.61.bucket_ref, f32[512,128]{1,0:T(8,128)} %broadcast_in_dim.64.gate_ref, ...), custom_call_target="tpu_custom_call" | custom-call | flops 2315255808 | bytes 5767168 | tf_op jit(solution)/shard_map/own_grad/pallas_call | solution.py:248
  102.9 10.4 %own_forward.1 = (bf16[512,2048]{1,0:T(8,128)(2,1)}, f32[512,128]{1,0:T(8,128)}) custom-call(bf16[4,512,512]{2,1,0:T(8,128)(2,1)} %get-tuple-element.70.act_ref, bf16[512,2048]{1,0:T(8,128)(2,1)} %copy-done.14, bf16[512,512]{1,0:T(8,128)(2,1)} %fusion.26.unsort_ref, bf16[4,512,2048]{2,1,0:T(8,128)(2,1)} %refs_17_.15, ...), custom_call_target="tpu_custom_call" | custom-call | flops 771751936 | bytes 3670016 | tf_op jit(solution)/shard_map/own_forward/pallas_call | solution.py:288
  116.7 3.8 collective-permute-done.11
  120.5 3.9 multiply_reduce_fusion
  135.8 23.8 %attend_back.1 = (bf16[4,2048,512]{2,1,0:T(8,128)(2,1)}, bf16[512,2048]{1,0:T(8,128)(2,1)}) custom-call(bf16[512,2048]{1,0:T(8,128)(2,1)} %pad_maximum_fusion.ga_ref, bf16[512,2048]{1,0:T(8,128)(2,1)} %get-tuple-element.79.normed_ref, bf16[3,512,512]{2,1,0:T(8,128)(2,1)} %get-tuple-element.80.qkv_ref, f32[4,512,128]{2,1,0:T(8,128)} %get-tuple-element.81.lse_ref, ...), custom_call_target="tpu_custom_call" | custom-call | flops 2483027968 | bytes 6291456 | tf_op jit(solution)/shard_map/attend_back/pallas_call | solution.py:195
  167.1 9.7 %collective-permute-done.18.refs_1_ = bf16[1040,1024]{1,0:T(8,128)(2,1)} collective-permute-done((bf16[1040,1024]{1,0:T(8,128)(2,1)}, bf16[1040,1024]{1,0:T(8,128)(2,1)}, u32[]{:S(2)}, u32[]{:S(2)}) %collective-permute-start.18) | collective-permute-done | bytes 2129952 | tf_op jit(solution)/shard_map/ppermute | solution.py:636
  191.1 24.4 %weight_gradients_0.1 = (f32[4,2048,512]{2,1,0:T(8,128)}, f32[4,512,2048]{2,1,0:T(8,128)}) custom-call(bf16[512,1024]{1,0:T(8,128)(2,1)} %get-tuple-element.148.refs_0_, bf16[512,1024]{1,0:T(8,128)(2,1)} %get-tuple-element.147.refs_1_, bf16[528,1024]{1,0:T(8,128)(2,1)} %copy-done.11, bf16[512,1024]{1,0:T(8,128)(2,1)} %get-tuple-element.145.refs_3_, ...), custom_call_target="tpu_custom_call" | custom-call | flops 4294967296 | bytes 8388608 | tf_op jit(solution)/shard_map/weight_gradients_0/pallas_call | solution.py:438
  216.5 4.6 join.3
  227.8 23.8 %weight_gradients_1.1 = (f32[4,2048,512]{2,1,0:T(8,128)}, f32[4,512,2048]{2,1,0:T(8,128)}) custom-call(bf16[512,1024]{1,0:T(8,128)(2,1)} %get-tuple-element.148.refs_0_, bf16[512,1024]{1,0:T(8,128)(2,1)} %get-tuple-element.147.refs_1_, bf16[528,1024]{1,0:T(8,128)(2,1)} %copy-done.11, ...), custom_call_target="tpu_custom_call", output_to_operand_aliasing={{0}: (18, {}), {1}: (19, {})} | custom-call | flops 4026531840 | bytes 8126464 | tf_op jit(solution)/shard_map/weight_gradients_1/pallas_call | solution.py:438
  251.6 14.8 %collective-permute-done.25.right_ref = bf16[4,256,512]{2,1,0:T(8,128)(2,1)} collective-permute-done((bf16[4,256,512]{2,1,0:T(8,128)(2,1)}, bf16[4,256,512]{2,1,0:T(8,128)(2,1)}, u32[]{:S(2)}, u32[]{:S(2)}) %collective-permute-start.25) | collective-permute-done | bytes 1048608 | tf_op jit(solution)/shard_map/ppermute | solution.py:631
  266.7 4.9 join.4
  274.5 4.0 add_rows.7
  283.9 18.2 %weight_gradients_2.1 = (f32[4,2048,512]{2,1,0:T(8,128)}, f32[4,512,2048]{2,1,0:T(8,128)}) custom-call(bf16[512,1024]{1,0:T(8,128)(2,1)} %get-tuple-element.148.refs_0_, bf16[512,1024]{1,0:T(8,128)(2,1)} %get-tuple-element.147.refs_1_, bf16[528,1024]{1,0:T(8,128)(2,1)} %copy-done.11, ...), custom_call_target="tpu_custom_call", output_to_operand_aliasing={{0}: (18, {}), {1}: (19, {})} | custom-call | flops 2684354560 | bytes 6815744 | tf_op jit(solution)/shard_map/weight_gradients_2/pallas_call | solution.py:438
  310.1 4.9 join.5
  324.9 13.2 %weight_gradients_3.1 = (f32[4,2048,512]{2,1,0:T(8,128)}, f32[4,512,2048]{2,1,0:T(8,128)}) custom-call(bf16[512,1024]{1,0:T(8,128)(2,1)} %get-tuple-element.148.refs_0_, bf16[512,1024]{1,0:T(8,128)(2,1)} %get-tuple-element.147.refs_1_, bf16[528,1024]{1,0:T(8,128)(2,1)} %copy-done.11, ...), custom_call_target="tpu_custom_call", output_to_operand_aliasing={{0}: (18, {}), {1}: (19, {})} | custom-call | flops 1342177280 | bytes 5505024 | tf_op jit(solution)/shard_map/weight_gradients_3/pallas_call | solution.py:438
  338.3 16.6 %collective-permute-done.35.right_ref = bf16[4,256,512]{2,1,0:T(8,128)(2,1)} collective-permute-done((bf16[4,256,512]{2,1,0:T(8,128)(2,1)}, bf16[4,256,512]{2,1,0:T(8,128)(2,1)}, u32[]{:S(2)}, u32[]{:S(2)}) %collective-permute-start.35) | collective-permute-done | bytes 1048608 | tf_op jit(solution)/shard_map/ppermute | solution.py:631
  357.4 3.9 join_own.1.refs_3_.refs_20_.refs_21_.refs_0_
  372.3 24.3 %weight_gradients_0_more.1 = (f32[4,2048,512]{2,1,0:T(8,128)}, f32[4,512,2048]{2,1,0:T(8,128)}) custom-call(bf16[1040,1024]{1,0:T(8,128)(2,1)} %get-tuple-element.85.refs_22_.refs_0_.refs_2_, bf16[1040,1024]{1,0:T(8,128)(2,1)} %collective-permute-done.20.refs_23_.refs_1_.refs_3_, ...), custom_call_target="tpu_custom_call", output_to_operand_aliasing={{0}: (18, {}), {1}: (19, {})} | custom-call | flops 4294967296 | bytes 8388608 | tf_op jit(solution)/shard_map/weight_gradients_0_more/pallas_call | solution.py:438
  402.0 23.6 %weight_gradients_1_more.1 = (f32[4,2048,512]{2,1,0:T(8,128)}, f32[4,512,2048]{2,1,0:T(8,128)}) custom-call(bf16[1040,1024]{1,0:T(8,128)(2,1)} %get-tuple-element.85.refs_22_.refs_0_.refs_2_, bf16[1040,1024]{1,0:T(8,128)(2,1)} %collective-permute-done.20.refs_23_.refs_1_.refs_3_, ...), custom_call_target="tpu_custom_call", output_to_operand_aliasing={{0}: (18, {}), {1}: (19, {})} | custom-call | flops 4026531840 | bytes 8126464 | tf_op jit(solution)/shard_map/weight_gradients_1_more/pallas_call | solution.py:438
  439.7 18.8 %weight_gradients_2_more.1 = (f32[4,2048,512]{2,1,0:T(8,128)}, f32[4,512,2048]{2,1,0:T(8,128)}) custom-call(bf16[1040,1024]{1,0:T(8,128)(2,1)} %get-tuple-element.85.refs_22_.refs_0_.refs_2_, bf16[1040,1024]{1,0:T(8,128)(2,1)} %collective-permute-done.20.refs_23_.refs_1_.refs_3_, ...), custom_call_target="tpu_custom_call", output_to_operand_aliasing={{0}: (18, {}), {1}: (19, {})} | custom-call | flops 2684354560 | bytes 6815744 | tf_op jit(solution)/shard_map/weight_gradients_2_more/pallas_call | solution.py:438
  464.6 14.8 %weight_gradients_3_more.1 = (f32[4,2048,512]{2,1,0:T(8,128)}, f32[4,512,2048]{2,1,0:T(8,128)}) custom-call(bf16[1040,1024]{1,0:T(8,128)(2,1)} %get-tuple-element.85.refs_22_.refs_0_.refs_2_, bf16[1040,1024]{1,0:T(8,128)(2,1)} %collective-permute-done.20.refs_23_.refs_1_.refs_3_, ...), custom_call_target="tpu_custom_call", output_to_operand_aliasing={{0}: (18, {}), {1}: (19, {})} | custom-call | flops 1342177280 | bytes 5505024 | tf_op jit(solution)/shard_map/weight_gradients_3_more/pallas_call | solution.py:438
  484.5 11.0 %unpack_some.1 = (f32[3,2048,512]{2,1,0:T(8,128)}, f32[512,2048]{1,0:T(8,128)}) custom-call(s32[8]{0:T(128)} %stack.132.order_ref, bf16[1056,512]{1,0:T(8,128)(2,1)} %join_own.1.refs_3_.refs_20_.refs_21_.refs_0_, bf16[1056,512]{1,0:T(8,128)(2,1)} %get-tuple-element.111.refs_20_.refs_1_, bf16[1056,512]{1,0:T(8,128)(2,1)} %get-tuple-element.112.refs_21_.refs_2_, ...), custom_call_target="tpu_custom_call" | custom-call | bytes 6291456 | tf_op jit(solution)/shard_map/unpack_some/pallas_call | solution.py:475
  (325 shorter events, 160.5 us)
Async XLA Ops:
  32.4 35.9 %collective-permute-start.4 = (bf16[512,1024]{1,0:T(8,128)(2,1)}, bf16[512,1024]{1,0:T(8,128)(2,1)S(1)}, u32[]{:S(2)}, u32[]{:S(2)}) collective-permute-start(bf16[512,1024]{1,0:T(8,128)(2,1)} %get-tuple-element.148.refs_0_), channel_id=1, source_target_pairs={{0,8},{8,16},{16,24},{24,28},{28,20},{20,12},{12,4},{4,0},{1,9},{9... | collective-permute-start | bytes 3145736 | tf_op jit(solution)/shard_map/ppermute | solution.py:631
  34.0 34.3 %collective-permute-start.5 = (bf16[512,1024]{1,0:T(8,128)(2,1)}, bf16[512,1024]{1,0:T(8,128)(2,1)}, u32[]{:S(2)}, u32[]{:S(2)}) collective-permute-start(bf16[512,1024]{1,0:T(8,128)(2,1)} %get-tuple-element.148.refs_0_), channel_id=1, source_target_pairs={{8,0},{16,8},{24,16},{28,24},{20,28},{12,20},{4,12},{0,4},{9,1},{1... | collective-permute-start | bytes 3145736 | tf_op jit(solution)/shard_map/ppermute | solution.py:636
  66.1 30.6 %collective-permute-start.7 = (bf16[528,1024]{1,0:T(8,128)(2,1)S(1)}, bf16[528,1024]{1,0:T(8,128)(2,1)S(1)}, u32[]{:S(2)}, u32[]{:S(2)}) collective-permute-start(bf16[528,1024]{1,0:T(8,128)(2,1)S(1)} %fusion.20.rest_2_.refs_2_), channel_id=1, source_target_pairs={{0,8},{8,16},{16,24},{24,28},{28,20},{20,12},{12,4},{4,0},{1,9},{9... | collective-permute-start | bytes 3244040 | tf_op jit(solution)/shard_map/ppermute | solution.py:631
  127.7 49.1 %collective-permute-start.18 = (bf16[1040,1024]{1,0:T(8,128)(2,1)}, bf16[1040,1024]{1,0:T(8,128)(2,1)}, u32[]{:S(2)}, u32[]{:S(2)}) collective-permute-start(bf16[1040,1024]{1,0:T(8,128)(2,1)} %copy-done.5), channel_id=1, source_target_pairs={{8,0},{16,8},{24,16},{28,24},{20,28},{12,20},{4,12},{0,4},{9,1},{1... | collective-permute-start | bytes 6389768 | tf_op jit(solution)/shard_map/ppermute | solution.py:636
  129.5 48.5 %collective-permute-start.17 = (bf16[1040,1024]{1,0:T(8,128)(2,1)S(1)}, bf16[1040,1024]{1,0:T(8,128)(2,1)}, u32[]{:S(2)}, u32[]{:S(2)}) collective-permute-start(bf16[1040,1024]{1,0:T(8,128)(2,1)S(1)} %copy-done.4), channel_id=1, source_target_pairs={{0,8},{8,16},{16,24},{24,28},{28,20},{20,12},{12,4},{4,0},{1,9},{9... | collective-permute-start | bytes 6389768 | tf_op jit(solution)/shard_map/ppermute | solution.py:631
  178.5 44.6 %collective-permute-start.16 = (bf16[256,2048]{1,0:T(8,128)(2,1)S(1)}, bf16[256,2048]{1,0:T(8,128)(2,1)}, u32[]{:S(2)}, u32[]{:S(2)}) collective-permute-start(bf16[256,2048]{1,0:T(8,128)(2,1)S(1)} %copy-done.27), channel_id=1, source_target_pairs={{0,2},{1,3},{2,0},{3,1},{4,6},{5,7},{6,4},{7,5},{8,10},{9,11},{10,... | collective-permute-start | bytes 3145736 | tf_op jit(solution)/shard_map/ppermute | solution.py:696
  184.5 31.0 %collective-permute-start.22 = (bf16[4,128,512]{2,1,0:T(8,128)(2,1)S(1)}, bf16[4,128,512]{2,1,0:T(8,128)(2,1)S(1)}, u32[]{:S(2)}, u32[]{:S(2)}) collective-permute-start(bf16[4,128,512]{2,1,0:T(8,128)(2,1)S(1)} %get-tuple-element.138.refs_18_), channel_id=1, source_target_pairs={{0,8},{8,16},{16,24},{24,28},{28,20},{20,12},{12,4},{4,0},{1,9},{9... | collective-permute-start | bytes 1572872 | tf_op jit(solution)/shard_map/ppermute | solution.py:631
  188.2 113.9 %collective-permute-start.27 = (bf16[1040,1024]{1,0:T(8,128)(2,1)}, bf16[1040,1024]{1,0:T(8,128)(2,1)}, u32[]{:S(2)}, u32[]{:S(2)}) collective-permute-start(bf16[1040,1024]{1,0:T(8,128)(2,1)} %get-tuple-element.84.refs_12_.refs_14_.refs_20_), channel_id=1, source_target_pairs={{0,8},{8,16},{16,24},{24,28},{28,20},{20,12},{12,4},{4,0},{1,9},{9... | collective-permute-start | bytes 6389768 | tf_op jit(solution)/shard_map/ppermute | solution.py:631
  189.5 112.6 %collective-permute-start.28 = (bf16[1040,1024]{1,0:T(8,128)(2,1)}, bf16[1040,1024]{1,0:T(8,128)(2,1)S(1)}, u32[]{:S(2)}, u32[]{:S(2)}) collective-permute-start(bf16[1040,1024]{1,0:T(8,128)(2,1)} %get-tuple-element.85.refs_22_.refs_0_.refs_2_), channel_id=1, source_target_pairs={{8,0},{16,8},{24,16},{28,24},{20,28},{12,20},{4,12},{0,4},{9,1},{1... | collective-permute-start | bytes 6389768 | tf_op jit(solution)/shard_map/ppermute | solution.py:636
  221.1 45.2 %collective-permute-start.25 = (bf16[4,256,512]{2,1,0:T(8,128)(2,1)}, bf16[4,256,512]{2,1,0:T(8,128)(2,1)}, u32[]{:S(2)}, u32[]{:S(2)}) collective-permute-start(bf16[4,256,512]{2,1,0:T(8,128)(2,1)} %get-tuple-element.89.refs_20_), channel_id=1, source_target_pairs={{0,8},{8,16},{16,24},{24,28},{28,20},{20,12},{12,4},{4,0},{1,9},{9... | collective-permute-start | bytes 3145736 | tf_op jit(solution)/shard_map/ppermute | solution.py:631
  221.6 45.1 %collective-permute-start.26 = (bf16[4,256,512]{2,1,0:T(8,128)(2,1)}, bf16[4,256,512]{2,1,0:T(8,128)(2,1)}, u32[]{:S(2)}, u32[]{:S(2)}) collective-permute-start(bf16[4,256,512]{2,1,0:T(8,128)(2,1)} %get-tuple-element.90.refs_21_), channel_id=1, source_target_pairs={{8,0},{16,8},{24,16},{28,24},{20,28},{12,20},{4,12},{0,4},{9,1},{1... | collective-permute-start | bytes 3145736 | tf_op jit(solution)/shard_map/ppermute | solution.py:636
  225.9 47.7 %collective-permute-start.21 = (bf16[256,2048]{1,0:T(8,128)(2,1)}, bf16[256,2048]{1,0:T(8,128)(2,1)S(1)}, u32[]{:S(2)}, u32[]{:S(2)}) collective-permute-start(bf16[256,2048]{1,0:T(8,128)(2,1)} %after.19), channel_id=1, source_target_pairs={{0,1},{1,0},{2,3},{3,2},{4,5},{5,4},{6,7},{7,6},{8,9},{9,8},{10,11... | collective-permute-start | bytes 3145736 | tf_op jit(solution)/shard_map/ppermute | solution.py:689
  271.5 38.6 %collective-permute-start.29 = (bf16[4,256,512]{2,1,0:T(8,128)(2,1)}, bf16[4,256,512]{2,1,0:T(8,128)(2,1)}, u32[]{:S(2)}, u32[]{:S(2)}) collective-permute-start(bf16[4,256,512]{2,1,0:T(8,128)(2,1)} %get-tuple-element.93.refs_20_), channel_id=1, source_target_pairs={{0,8},{8,16},{16,24},{24,28},{28,20},{20,12},{12,4},{4,0},{1,9},{9... | collective-permute-start | bytes 3145736 | tf_op jit(solution)/shard_map/ppermute | solution.py:631
  273.1 37.0 %collective-permute-start.30 = (bf16[4,256,512]{2,1,0:T(8,128)(2,1)}, bf16[4,256,512]{2,1,0:T(8,128)(2,1)}, u32[]{:S(2)}, u32[]{:S(2)}) collective-permute-start(bf16[4,256,512]{2,1,0:T(8,128)(2,1)} %get-tuple-element.94.refs_21_), channel_id=1, source_target_pairs={{8,0},{16,8},{24,16},{28,24},{20,28},{12,20},{4,12},{0,4},{9,1},{1... | collective-permute-start | bytes 3145736 | tf_op jit(solution)/shard_map/ppermute | solution.py:636
  278.5 38.1 %collective-permute-start.24 = (bf16[256,2048]{1,0:T(8,128)(2,1)}, bf16[256,2048]{1,0:T(8,128)(2,1)S(1)}, u32[]{:S(2)}, u32[]{:S(2)}) collective-permute-start(bf16[256,2048]{1,0:T(8,128)(2,1)} %add_rows.7), channel_id=1, source_target_pairs={{0,2},{1,3},{2,0},{3,1},{4,6},{5,7},{6,4},{7,5},{8,10},{9,11},{10,... | collective-permute-start | bytes 3145736 | tf_op jit(solution)/shard_map/ppermute | solution.py:696
  305.8 55.5 %collective-permute-start.34 = (bf16[528,1024]{1,0:T(8,128)(2,1)}, bf16[528,1024]{1,0:T(8,128)(2,1)}, u32[]{:S(2)}, u32[]{:S(2)}) collective-permute-start(bf16[528,1024]{1,0:T(8,128)(2,1)} %slice.55), channel_id=1, source_target_pairs={{8,0},{16,8},{24,16},{28,24},{20,28},{12,20},{4,12},{0,4},{9,1},{1... | collective-permute-start | bytes 3244040 | tf_op jit(solution)/shard_map/ppermute | solution.py:636
  309.5 51.8 %collective-permute-start.33 = (bf16[512,1024]{1,0:T(8,128)(2,1)}, bf16[512,1024]{1,0:T(8,128)(2,1)}, u32[]{:S(2)}, u32[]{:S(2)}) collective-permute-start(bf16[512,1024]{1,0:T(8,128)(2,1)} %slice.54), channel_id=1, source_target_pairs={{0,8},{8,16},{16,24},{24,28},{28,20},{20,12},{12,4},{4,0},{1,9},{9... | collective-permute-start | bytes 3145736 | tf_op jit(solution)/shard_map/ppermute | solution.py:631
  315.0 39.9 %collective-permute-start.35 = (bf16[4,256,512]{2,1,0:T(8,128)(2,1)}, bf16[4,256,512]{2,1,0:T(8,128)(2,1)}, u32[]{:S(2)}, u32[]{:S(2)}) collective-permute-start(bf16[4,256,512]{2,1,0:T(8,128)(2,1)} %get-tuple-element.99.refs_20_), channel_id=1, source_target_pairs={{0,8},{8,16},{16,24},{24,28},{28,20},{20,12},{12,4},{4,0},{1,9},{9... | collective-permute-start | bytes 3145736 | tf_op jit(solution)/shard_map/ppermute | solution.py:631
  320.0 36.4 %collective-permute-start.36 = (bf16[4,256,512]{2,1,0:T(8,128)(2,1)}, bf16[4,256,512]{2,1,0:T(8,128)(2,1)S(1)}, u32[]{:S(2)}, u32[]{:S(2)}) collective-permute-start(bf16[4,256,512]{2,1,0:T(8,128)(2,1)} %get-tuple-element.100.refs_21_), channel_id=1, source_target_pairs={{8,0},{16,8},{24,16},{28,24},{20,28},{12,20},{4,12},{0,4},{9,1},{1... | collective-permute-start | bytes 3145736 | tf_op jit(solution)/shard_map/ppermute | solution.py:636
  338.1 32.8 %collective-permute-start.31 = (bf16[1040,1024]{1,0:T(8,128)(2,1)}, bf16[1040,1024]{1,0:T(8,128)(2,1)S(1)}, u32[]{:S(2)}, u32[]{:S(2)}) collective-permute-start(bf16[1040,1024]{1,0:T(8,128)(2,1)} %get-tuple-element.102.refs_4_.refs_6_), channel_id=1, source_target_pairs={{0,1},{1,0},{2,3},{3,2},{4,5},{5,4},{6,7},{7,6},{8,9},{9,8},{10,11... | collective-permute-start | bytes 6389768 | tf_op jit(solution)/shard_map/ppermute | solution.py:689
  364.6 33.3 %collective-permute-start.42 = (bf16[1056,512]{1,0:T(8,128)(2,1)S(1)}, bf16[1056,512]{1,0:T(8,128)(2,1)}, u32[]{:S(2)}, u32[]{:S(2)}) collective-permute-start(bf16[1056,512]{1,0:T(8,128)(2,1)S(1)} %copy-done.12), channel_id=1, source_target_pairs={{0,8},{8,16},{16,24},{24,28},{28,20},{20,12},{12,4},{4,0},{1,9},{9... | collective-permute-start | bytes 3244040 | tf_op jit(solution)/shard_map/ppermute | solution.py:631
  365.2 32.7 %collective-permute-start.43 = (bf16[1056,512]{1,0:T(8,128)(2,1)S(1)}, bf16[1056,512]{1,0:T(8,128)(2,1)}, u32[]{:S(2)}, u32[]{:S(2)}) collective-permute-start(bf16[1056,512]{1,0:T(8,128)(2,1)S(1)} %copy-done.12), channel_id=1, source_target_pairs={{8,0},{16,8},{24,16},{28,24},{20,28},{12,20},{4,12},{0,4},{9,1},{1... | collective-permute-start | bytes 3244040 | tf_op jit(solution)/shard_map/ppermute | solution.py:636
  398.0 32.9 %collective-permute-start.44 = (bf16[1056,512]{1,0:T(8,128)(2,1)}, bf16[1056,512]{1,0:T(8,128)(2,1)S(1)}, u32[]{:S(2)}, u32[]{:S(2)}) collective-permute-start(bf16[1056,512]{1,0:T(8,128)(2,1)} %get-tuple-element.111.refs_20_.refs_1_), channel_id=1, source_target_pairs={{0,8},{8,16},{16,24},{24,28},{28,20},{20,12},{12,4},{4,0},{1,9},{9... | collective-permute-start | bytes 3244040 | tf_op jit(solution)/shard_map/ppermute | solution.py:631
  398.6 32.4 %collective-permute-start.45 = (bf16[1056,512]{1,0:T(8,128)(2,1)}, bf16[1056,512]{1,0:T(8,128)(2,1)S(1)}, u32[]{:S(2)}, u32[]{:S(2)}) collective-permute-start(bf16[1056,512]{1,0:T(8,128)(2,1)} %get-tuple-element.112.refs_21_.refs_2_), channel_id=1, source_target_pairs={{8,0},{16,8},{24,16},{28,24},{20,28},{12,20},{4,12},{0,4},{9,1},{1... | collective-permute-start | bytes 3244040 | tf_op jit(solution)/shard_map/ppermute | solution.py:636
  (84 other events, 726.0 us)

commit v10 on v8

--- a/solution.py
+++ b/solution.py
@@ -504,10 +504,10 @@
 
 def add_rows(parts, deps=()):
     rows, columns = parts[0].shape
-    block = pl.BlockSpec((rows // 4, columns), lambda i: (i, 0))
+    block = pl.BlockSpec((rows // 2, columns), lambda i: (i, 0))
     return pl.pallas_call(
         partial(add_kernel, count=len(parts)),
-        grid=(4,),
+        grid=(2,),
         in_specs=[block] * len(parts) + [pl.BlockSpec(memory_space=pl.ANY)] * len(deps),
         out_specs=block,
         out_shape=jax.ShapeDtypeStruct((rows, columns), BF16),

time: 500 us -> 498 us (level)
  Pallas kernels: 273 us -> 268 us
where the time goes in v10:
time: 498 us; the launch traced here: 490 us
  Pallas kernels  268 us (54%)
  waiting for transfers between devices  70.5 us (14%)
  local copies, waits for them, and re-layouts  59.2 us (12%)
  starting transfers between devices  39.6 us (8%)
  other arithmetic  33.6 us (7%)
  matrix products  11.1 us (2%)
  between operations  8.32 us (2%)
    pallas_call x8, Pallas kernels, weight_gradients(): pl.pallas_call(partial(weight_kernel, level=level, rows=rows, group=group...  161 us
    unnamed x120, local copies, waits for them, and re-layouts  34.9 us
    pallas_call x1, Pallas kernels, attend_back(): pl.pallas_call(partial(attend_back_kernel, heads=heads, steps=steps, deps...  23.8 us
    ppermute x13, waiting for transfers between devices, to_right(): out = lax.ppermute(x, 'dp', self.right)  23.8 us
    ppermute x5, waiting for transfers between devices, sum_over_x(): lax.ppermute(x, 'mp', [(i, (i + 2 * k) % (2 * n)) for i in range(2 * n)])  20.3 us
    ppermute x13, starting transfers between devices, to_left(): out = lax.ppermute(x, 'dp', self.left)  19.3 us
    pallas_call x1, Pallas kernels, own_grad(): pl.pallas_call(partial(own_grad_kernel, row_bounds=tuple(row_bounds), dep...  17.3 us
    pallas_call x1, Pallas kernels, attend(): pl.pallas_call(partial(attend_kernel, heads=heads, steps=steps), grid=(st...  15.7 us
  transfers between devices with their start and end apart: 50, of which 14 were waited for; matrix products, arithmetic and copies ran while one was open for 15% of the time, Pallas kernels for 49%

profile of v10, /device:TPU:0, one launch (start us, length us, event | category | flops | bytes accessed | tf_op | source)
XLA Modules:
  0.0 490.1 jit_solution(4260815056275310870)
XLA Ops:
  2.6 15.7 %attend.1 = (bf16[256,2048]{1,0:T(8,128)(2,1)}, bf16[256,2048]{1,0:T(8,128)(2,1)}, bf16[512,2048]{1,0:T(8,128)(2,1)}, bf16[3,512,512]{2,1,0:T(8,128)(2,1)}, f32[...) custom-call(bf16[512,2048]{1,0:T(8,128)(2,1)} %x_ref.1, f32[1,2048]{1,0:T(1,128)} %bitcast.61, ...), custom_call_target="tpu_custom_call" | custom-call | flops 1207959552 | bytes 3145728 | tf_op jit(solution)/shard_map/attend/pallas_call | solution.py:102
  34.9 16.5 %collective-permute-done.1 = bf16[256,2048]{1,0:T(8,128)(2,1)} collective-permute-done((bf16[256,2048]{1,0:T(8,128)(2,1)}, bf16[256,2048]{1,0:T(8,128)(2,1)}, u32[]{:S(2)}, u32[]{:S(2)}) %collective-permute-start.1) | collective-permute-done | bytes 1048608 | tf_op jit(solution)/shard_map/ppermute | solution.py:696
  68.9 17.3 %own_grad.1 = (bf16[256,2048]{1,0:T(8,128)(2,1)}, bf16[256,2048]{1,0:T(8,128)(2,1)}, bf16[4,512,512]{2,1,0:T(8,128)(2,1)}) custom-call(bf16[512,2048]{1,0:T(8,128)(2,1)} %copy-done.28, bf16[512,2048]{1,0:T(8,128)(2,1)} %copy-done.16, s32[512,128]{1,0:T(8,128)} %broadcast_in_dim.61.bucket_ref, f32[512,128]{1,0:T(8,128)} %broadcast_in_dim.64.gate_ref, ...), custom_call_target="tpu_custom_call" | custom-call | flops 2315255808 | bytes 5767168 | tf_op jit(solution)/shard_map/own_grad/pallas_call | solution.py:248
  100.5 10.4 %own_forward.1 = (bf16[512,2048]{1,0:T(8,128)(2,1)}, f32[512,128]{1,0:T(8,128)}) custom-call(bf16[4,512,512]{2,1,0:T(8,128)(2,1)} %get-tuple-element.70.act_ref, bf16[512,2048]{1,0:T(8,128)(2,1)} %copy-done.16, bf16[512,512]{1,0:T(8,128)(2,1)} %fusion.26.unsort_ref, bf16[4,512,2048]{2,1,0:T(8,128)(2,1)} %refs_17_.15, ...), custom_call_target="tpu_custom_call" | custom-call | flops 771751936 | bytes 3670016 | tf_op jit(solution)/shard_map/own_forward/pallas_call | solution.py:288
  118.2 3.9 multiply_reduce_fusion
  133.4 23.8 %attend_back.1 = (bf16[4,2048,512]{2,1,0:T(8,128)(2,1)}, bf16[512,2048]{1,0:T(8,128)(2,1)}) custom-call(bf16[512,2048]{1,0:T(8,128)(2,1)} %pad_maximum_fusion.ga_ref, bf16[512,2048]{1,0:T(8,128)(2,1)} %get-tuple-element.79.normed_ref, bf16[3,512,512]{2,1,0:T(8,128)(2,1)} %get-tuple-element.80.qkv_ref, f32[4,512,128]{2,1,0:T(8,128)} %get-tuple-element.81.lse_ref, ...), custom_call_target="tpu_custom_call" | custom-call | flops 2483027968 | bytes 6291456 | tf_op jit(solution)/shard_map/attend_back/pallas_call | solution.py:195
  163.6 10.8 %collective-permute-done.18.refs_1_ = bf16[1040,1024]{1,0:T(8,128)(2,1)} collective-permute-done((bf16[1040,1024]{1,0:T(8,128)(2,1)}, bf16[1040,1024]{1,0:T(8,128)(2,1)}, u32[]{:S(2)}, u32[]{:S(2)}) %collective-permute-start.18) | collective-permute-done | bytes 2129952 | tf_op jit(solution)/shard_map/ppermute | solution.py:636
  187.7 24.4 %weight_gradients_0.1 = (f32[4,2048,512]{2,1,0:T(8,128)}, f32[4,512,2048]{2,1,0:T(8,128)}) custom-call(bf16[512,1024]{1,0:T(8,128)(2,1)} %get-tuple-element.148.refs_0_, bf16[512,1024]{1,0:T(8,128)(2,1)} %get-tuple-element.147.refs_1_, bf16[528,1024]{1,0:T(8,128)(2,1)} %copy-done.11, bf16[512,1024]{1,0:T(8,128)(2,1)} %get-tuple-element.145.refs_3_, ...), custom_call_target="tpu_custom_call" | custom-call | flops 4294967296 | bytes 8388608 | tf_op jit(solution)/shard_map/weight_gradients_0/pallas_call | solution.py:438
  218.3 4.6 join.3
  225.0 23.8 %weight_gradients_1.1 = (f32[4,2048,512]{2,1,0:T(8,128)}, f32[4,512,2048]{2,1,0:T(8,128)}) custom-call(bf16[512,1024]{1,0:T(8,128)(2,1)} %get-tuple-element.148.refs_0_, bf16[512,1024]{1,0:T(8,128)(2,1)} %get-tuple-element.147.refs_1_, bf16[528,1024]{1,0:T(8,128)(2,1)} %copy-done.11, ...), custom_call_target="tpu_custom_call", output_to_operand_aliasing={{0}: (18, {}), {1}: (19, {})} | custom-call | flops 4026531840 | bytes 8126464 | tf_op jit(solution)/shard_map/weight_gradients_1/pallas_call | solution.py:438
  255.7 7.5 %collective-permute-done.25.right_ref = bf16[4,256,512]{2,1,0:T(8,128)(2,1)S(1)} collective-permute-done((bf16[4,256,512]{2,1,0:T(8,128)(2,1)}, bf16[4,256,512]{2,1,0:T(8,128)(2,1)S(1)}, u32[]{:S(2)}, u32[]{:S(2)}) %collective-permute-start.25) | collective-permute-done | bytes 1048608 | tf_op jit(solution)/shard_map/ppermute | solution.py:631
  264.1 4.8 join.4
  272.7 18.2 %weight_gradients_2.1 = (f32[4,2048,512]{2,1,0:T(8,128)}, f32[4,512,2048]{2,1,0:T(8,128)}) custom-call(bf16[512,1024]{1,0:T(8,128)(2,1)} %get-tuple-element.148.refs_0_, bf16[512,1024]{1,0:T(8,128)(2,1)} %get-tuple-element.147.refs_1_, bf16[528,1024]{1,0:T(8,128)(2,1)} %copy-done.11, ...), custom_call_target="tpu_custom_call", output_to_operand_aliasing={{0}: (18, {}), {1}: (19, {})} | custom-call | flops 2684354560 | bytes 6815744 | tf_op jit(solution)/shard_map/weight_gradients_2/pallas_call | solution.py:438
  302.6 5.0 %join.5 = (bf16[4,256,512]{2,1,0:T(8,128)(2,1)}, bf16[4,256,512]{2,1,0:T(8,128)(2,1)}) custom-call(s32[2]{0:T(128)} %pad_add_fusion.3.index_ref, bf16[4,2048,512]{2,1,0:T(8,128)(2,1)} %get-tuple-element.83.refs_1_.refs_2_.right_local.left_local.local_ref, bf16[4,2048,512]{2,1,0:T(8,128)(2,1)} %get-tuple-element.83.refs_1_.refs_2_.right_local.left_local.local_ref, ...), custom_call_target="tpu_custom_call" | custom-call | flops 262144 | bytes 1572864 | tf_op jit(solution)/shard_map/join/pallas_call | solution.py:555
  309.8 4.2 fusion.7.refs_22_
  314.0 13.2 %weight_gradients_3.1 = (f32[4,2048,512]{2,1,0:T(8,128)}, f32[4,512,2048]{2,1,0:T(8,128)}) custom-call(bf16[512,1024]{1,0:T(8,128)(2,1)} %get-tuple-element.148.refs_0_, bf16[512,1024]{1,0:T(8,128)(2,1)} %get-tuple-element.147.refs_1_, bf16[528,1024]{1,0:T(8,128)(2,1)} %copy-done.11, ...), custom_call_target="tpu_custom_call", output_to_operand_aliasing={{0}: (18, {}), {1}: (19, {})} | custom-call | flops 1342177280 | bytes 5505024 | tf_op jit(solution)/shard_map/weight_gradients_3/pallas_call | solution.py:438
  329.4 15.0 %collective-permute-done.33.right_ref = bf16[4,256,512]{2,1,0:T(8,128)(2,1)} collective-permute-done((bf16[4,256,512]{2,1,0:T(8,128)(2,1)}, bf16[4,256,512]{2,1,0:T(8,128)(2,1)}, u32[]{:S(2)}, u32[]{:S(2)}) %collective-permute-start.33) | collective-permute-done | bytes 1048608 | tf_op jit(solution)/shard_map/ppermute | solution.py:631
  344.4 3.9 join_own.1.refs_5_.refs_20_.refs_21_.refs_0_
  354.5 4.9 collective-permute-done.38.refs_13_
  366.5 24.3 %weight_gradients_0_more.1 = (f32[4,2048,512]{2,1,0:T(8,128)}, f32[4,512,2048]{2,1,0:T(8,128)}) custom-call(bf16[1040,1024]{1,0:T(8,128)(2,1)} %get-tuple-element.85.refs_22_.refs_0_.refs_2_, bf16[1040,1024]{1,0:T(8,128)(2,1)} %collective-permute-done.20.refs_23_.refs_1_.refs_3_, ...), custom_call_target="tpu_custom_call", output_to_operand_aliasing={{0}: (18, {}), {1}: (19, {})} | custom-call | flops 4294967296 | bytes 8388608 | tf_op jit(solution)/shard_map/weight_gradients_0_more/pallas_call | solution.py:438
  396.2 23.6 %weight_gradients_1_more.1 = (f32[4,2048,512]{2,1,0:T(8,128)}, f32[4,512,2048]{2,1,0:T(8,128)}) custom-call(bf16[1040,1024]{1,0:T(8,128)(2,1)} %get-tuple-element.85.refs_22_.refs_0_.refs_2_, bf16[1040,1024]{1,0:T(8,128)(2,1)} %collective-permute-done.20.refs_23_.refs_1_.refs_3_, ...), custom_call_target="tpu_custom_call", output_to_operand_aliasing={{0}: (18, {}), {1}: (19, {})} | custom-call | flops 4026531840 | bytes 8126464 | tf_op jit(solution)/shard_map/weight_gradients_1_more/pallas_call | solution.py:438
  433.9 19.0 %weight_gradients_2_more.1 = (f32[4,2048,512]{2,1,0:T(8,128)}, f32[4,512,2048]{2,1,0:T(8,128)}) custom-call(bf16[1040,1024]{1,0:T(8,128)(2,1)} %get-tuple-element.85.refs_22_.refs_0_.refs_2_, bf16[1040,1024]{1,0:T(8,128)(2,1)} %collective-permute-done.20.refs_23_.refs_1_.refs_3_, ...), custom_call_target="tpu_custom_call", output_to_operand_aliasing={{0}: (18, {}), {1}: (19, {})} | custom-call | flops 2684354560 | bytes 6815744 | tf_op jit(solution)/shard_map/weight_gradients_2_more/pallas_call | solution.py:438
  459.0 14.9 %weight_gradients_3_more.1 = (f32[4,2048,512]{2,1,0:T(8,128)}, f32[4,512,2048]{2,1,0:T(8,128)}) custom-call(bf16[1040,1024]{1,0:T(8,128)(2,1)} %get-tuple-element.85.refs_22_.refs_0_.refs_2_, bf16[1040,1024]{1,0:T(8,128)(2,1)} %collective-permute-done.20.refs_23_.refs_1_.refs_3_, ...), custom_call_target="tpu_custom_call", output_to_operand_aliasing={{0}: (18, {}), {1}: (19, {})} | custom-call | flops 1342177280 | bytes 5505024 | tf_op jit(solution)/shard_map/weight_gradients_3_more/pallas_call | solution.py:438
  478.9 11.0 %unpack_some.1 = (f32[3,2048,512]{2,1,0:T(8,128)}, f32[512,2048]{1,0:T(8,128)}) custom-call(s32[8]{0:T(128)} %stack.132.order_ref, bf16[1056,512]{1,0:T(8,128)(2,1)} %join_own.1.refs_5_.refs_20_.refs_21_.refs_0_, bf16[1056,512]{1,0:T(8,128)(2,1)} %get-tuple-element.111.refs_20_.refs_1_, bf16[1056,512]{1,0:T(8,128)(2,1)} %get-tuple-element.112.refs_21_.refs_2_, ...), custom_call_target="tpu_custom_call" | custom-call | bytes 6291456 | tf_op jit(solution)/shard_map/unpack_some/pallas_call | solution.py:475
  (314 shorter events, 160.9 us)
Async XLA Ops:
  31.2 35.9 %collective-permute-start.4 = (bf16[512,1024]{1,0:T(8,128)(2,1)}, bf16[512,1024]{1,0:T(8,128)(2,1)S(1)}, u32[]{:S(2)}, u32[]{:S(2)}) collective-permute-start(bf16[512,1024]{1,0:T(8,128)(2,1)} %get-tuple-element.148.refs_0_), channel_id=1, source_target_pairs={{0,8},{8,16},{16,24},{24,28},{28,20},{20,12},{12,4},{4,0},{1,9},{9... | collective-permute-start | bytes 3145736 | tf_op jit(solution)/shard_map/ppermute | solution.py:631
  32.8 34.3 %collective-permute-start.5 = (bf16[512,1024]{1,0:T(8,128)(2,1)}, bf16[512,1024]{1,0:T(8,128)(2,1)}, u32[]{:S(2)}, u32[]{:S(2)}) collective-permute-start(bf16[512,1024]{1,0:T(8,128)(2,1)} %get-tuple-element.148.refs_0_), channel_id=1, source_target_pairs={{8,0},{16,8},{24,16},{28,24},{20,28},{12,20},{4,12},{0,4},{9,1},{1... | collective-permute-start | bytes 3145736 | tf_op jit(solution)/shard_map/ppermute | solution.py:636
  64.9 29.4 %collective-permute-start.7 = (bf16[528,1024]{1,0:T(8,128)(2,1)S(1)}, bf16[528,1024]{1,0:T(8,128)(2,1)S(1)}, u32[]{:S(2)}, u32[]{:S(2)}) collective-permute-start(bf16[528,1024]{1,0:T(8,128)(2,1)S(1)} %fusion.20.rest_2_.refs_2_), channel_id=1, source_target_pairs={{0,8},{8,16},{16,24},{24,28},{28,20},{20,12},{12,4},{4,0},{1,9},{9... | collective-permute-start | bytes 3244040 | tf_op jit(solution)/shard_map/ppermute | solution.py:631
  125.3 49.1 %collective-permute-start.18 = (bf16[1040,1024]{1,0:T(8,128)(2,1)}, bf16[1040,1024]{1,0:T(8,128)(2,1)}, u32[]{:S(2)}, u32[]{:S(2)}) collective-permute-start(bf16[1040,1024]{1,0:T(8,128)(2,1)} %copy-done.5), channel_id=1, source_target_pairs={{8,0},{16,8},{24,16},{28,24},{20,28},{12,20},{4,12},{0,4},{9,1},{1... | collective-permute-start | bytes 6389768 | tf_op jit(solution)/shard_map/ppermute | solution.py:636
  127.1 48.5 %collective-permute-start.17 = (bf16[1040,1024]{1,0:T(8,128)(2,1)S(1)}, bf16[1040,1024]{1,0:T(8,128)(2,1)}, u32[]{:S(2)}, u32[]{:S(2)}) collective-permute-start(bf16[1040,1024]{1,0:T(8,128)(2,1)S(1)} %copy-done.4), channel_id=1, source_target_pairs={{0,8},{8,16},{16,24},{24,28},{28,20},{20,12},{12,4},{4,0},{1,9},{9... | collective-permute-start | bytes 6389768 | tf_op jit(solution)/shard_map/ppermute | solution.py:631
  176.1 36.0 %collective-permute-start.16 = (bf16[256,2048]{1,0:T(8,128)(2,1)S(1)}, bf16[256,2048]{1,0:T(8,128)(2,1)}, u32[]{:S(2)}, u32[]{:S(2)}) collective-permute-start(bf16[256,2048]{1,0:T(8,128)(2,1)S(1)} %copy-done.27), channel_id=1, source_target_pairs={{0,2},{1,3},{2,0},{3,1},{4,6},{5,7},{6,4},{7,5},{8,10},{9,11},{10,... | collective-permute-start | bytes 3145736 | tf_op jit(solution)/shard_map/ppermute | solution.py:696
  181.3 37.0 %collective-permute-start.22 = (bf16[4,128,512]{2,1,0:T(8,128)(2,1)}, bf16[4,128,512]{2,1,0:T(8,128)(2,1)}, u32[]{:S(2)}, u32[]{:S(2)}) collective-permute-start(bf16[4,128,512]{2,1,0:T(8,128)(2,1)} %get-tuple-element.138.refs_18_), channel_id=1, source_target_pairs={{0,8},{8,16},{16,24},{24,28},{28,20},{20,12},{12,4},{4,0},{1,9},{9... | collective-permute-start | bytes 1572872 | tf_op jit(solution)/shard_map/ppermute | solution.py:631
  181.8 36.5 %collective-permute-start.23 = (bf16[4,128,512]{2,1,0:T(8,128)(2,1)}, bf16[4,128,512]{2,1,0:T(8,128)(2,1)}, u32[]{:S(2)}, u32[]{:S(2)}) collective-permute-start(bf16[4,128,512]{2,1,0:T(8,128)(2,1)} %get-tuple-element.137.refs_19_), channel_id=1, source_target_pairs={{8,0},{16,8},{24,16},{28,24},{20,28},{12,20},{4,12},{0,4},{9,1},{1... | collective-permute-start | bytes 1572872 | tf_op jit(solution)/shard_map/ppermute | solution.py:636
  184.8 106.2 %collective-permute-start.27 = (bf16[1040,1024]{1,0:T(8,128)(2,1)}, bf16[1040,1024]{1,0:T(8,128)(2,1)}, u32[]{:S(2)}, u32[]{:S(2)}) collective-permute-start(bf16[1040,1024]{1,0:T(8,128)(2,1)} %get-tuple-element.84.refs_12_.refs_14_.refs_20_), channel_id=1, source_target_pairs={{0,8},{8,16},{16,24},{24,28},{28,20},{20,12},{12,4},{4,0},{1,9},{9... | collective-permute-start | bytes 6389768 | tf_op jit(solution)/shard_map/ppermute | solution.py:631
  186.1 104.8 %collective-permute-start.28 = (bf16[1040,1024]{1,0:T(8,128)(2,1)}, bf16[1040,1024]{1,0:T(8,128)(2,1)S(1)}, u32[]{:S(2)}, u32[]{:S(2)}) collective-permute-start(bf16[1040,1024]{1,0:T(8,128)(2,1)} %get-tuple-element.85.refs_22_.refs_0_.refs_2_), channel_id=1, source_target_pairs={{8,0},{16,8},{24,16},{28,24},{20,28},{12,20},{4,12},{0,4},{9,1},{1... | collective-permute-start | bytes 6389768 | tf_op jit(solution)/shard_map/ppermute | solution.py:636
  216.4 32.4 %collective-permute-start.21 = (bf16[256,2048]{1,0:T(8,128)(2,1)}, bf16[256,2048]{1,0:T(8,128)(2,1)}, u32[]{:S(2)}, u32[]{:S(2)}) collective-permute-start(bf16[256,2048]{1,0:T(8,128)(2,1)} %after.18), channel_id=1, source_target_pairs={{0,1},{1,0},{2,3},{3,2},{4,5},{5,4},{6,7},{7,6},{8,9},{9,8},{10,11... | collective-permute-start | bytes 3145736 | tf_op jit(solution)/shard_map/ppermute | solution.py:689
  223.0 40.2 %collective-permute-start.25 = (bf16[4,256,512]{2,1,0:T(8,128)(2,1)}, bf16[4,256,512]{2,1,0:T(8,128)(2,1)S(1)}, u32[]{:S(2)}, u32[]{:S(2)}) collective-permute-start(bf16[4,256,512]{2,1,0:T(8,128)(2,1)} %get-tuple-element.89.refs_20_), channel_id=1, source_target_pairs={{0,8},{8,16},{16,24},{24,28},{28,20},{20,12},{12,4},{4,0},{1,9},{9... | collective-permute-start | bytes 3145736 | tf_op jit(solution)/shard_map/ppermute | solution.py:631
  223.4 40.2 %collective-permute-start.26 = (bf16[4,256,512]{2,1,0:T(8,128)(2,1)}, bf16[4,256,512]{2,1,0:T(8,128)(2,1)}, u32[]{:S(2)}, u32[]{:S(2)}) collective-permute-start(bf16[4,256,512]{2,1,0:T(8,128)(2,1)} %get-tuple-element.90.refs_21_), channel_id=1, source_target_pairs={{8,0},{16,8},{24,16},{28,24},{20,28},{12,20},{4,12},{0,4},{9,1},{1... | collective-permute-start | bytes 3145736 | tf_op jit(solution)/shard_map/ppermute | solution.py:636
  251.3 47.6 %collective-permute-start.24 = (bf16[256,2048]{1,0:T(8,128)(2,1)}, bf16[256,2048]{1,0:T(8,128)(2,1)}, u32[]{:S(2)}, u32[]{:S(2)}) collective-permute-start(bf16[256,2048]{1,0:T(8,128)(2,1)} %add_rows.7), channel_id=1, source_target_pairs={{0,2},{1,3},{2,0},{3,1},{4,6},{5,7},{6,4},{7,5},{8,10},{9,11},{10,... | collective-permute-start | bytes 3145736 | tf_op jit(solution)/shard_map/ppermute | solution.py:696
  269.0 33.6 %collective-permute-start.31 = (bf16[4,256,512]{2,1,0:T(8,128)(2,1)}, bf16[4,256,512]{2,1,0:T(8,128)(2,1)}, u32[]{:S(2)}, u32[]{:S(2)}) collective-permute-start(bf16[4,256,512]{2,1,0:T(8,128)(2,1)} %get-tuple-element.93.refs_20_), channel_id=1, source_target_pairs={{0,8},{8,16},{16,24},{24,28},{28,20},{20,12},{12,4},{4,0},{1,9},{9... | collective-permute-start | bytes 3145736 | tf_op jit(solution)/shard_map/ppermute | solution.py:631
  270.0 32.5 %collective-permute-start.32 = (bf16[4,256,512]{2,1,0:T(8,128)(2,1)}, bf16[4,256,512]{2,1,0:T(8,128)(2,1)}, u32[]{:S(2)}, u32[]{:S(2)}) collective-permute-start(bf16[4,256,512]{2,1,0:T(8,128)(2,1)} %get-tuple-element.94.refs_21_), channel_id=1, source_target_pairs={{8,0},{16,8},{24,16},{28,24},{20,28},{12,20},{4,12},{0,4},{9,1},{1... | collective-permute-start | bytes 3145736 | tf_op jit(solution)/shard_map/ppermute | solution.py:636
  294.6 53.7 %collective-permute-start.30 = (bf16[528,1024]{1,0:T(8,128)(2,1)}, bf16[528,1024]{1,0:T(8,128)(2,1)S(1)}, u32[]{:S(2)}, u32[]{:S(2)}) collective-permute-start(bf16[528,1024]{1,0:T(8,128)(2,1)} %slice.55), channel_id=1, source_target_pairs={{8,0},{16,8},{24,16},{28,24},{20,28},{12,20},{4,12},{0,4},{9,1},{1... | collective-permute-start | bytes 3244040 | tf_op jit(solution)/shard_map/ppermute | solution.py:636
  298.4 49.8 %collective-permute-start.29 = (bf16[512,1024]{1,0:T(8,128)(2,1)}, bf16[512,1024]{1,0:T(8,128)(2,1)S(1)}, u32[]{:S(2)}, u32[]{:S(2)}) collective-permute-start(bf16[512,1024]{1,0:T(8,128)(2,1)} %slice.54), channel_id=1, source_target_pairs={{0,8},{8,16},{16,24},{24,28},{28,20},{20,12},{12,4},{4,0},{1,9},{9... | collective-permute-start | bytes 3145736 | tf_op jit(solution)/shard_map/ppermute | solution.py:631
  307.6 36.8 %collective-permute-start.33 = (bf16[4,256,512]{2,1,0:T(8,128)(2,1)}, bf16[4,256,512]{2,1,0:T(8,128)(2,1)}, u32[]{:S(2)}, u32[]{:S(2)}) collective-permute-start(bf16[4,256,512]{2,1,0:T(8,128)(2,1)} %get-tuple-element.99.refs_20_), channel_id=1, source_target_pairs={{0,8},{8,16},{16,24},{24,28},{28,20},{20,12},{12,4},{4,0},{1,9},{9... | collective-permute-start | bytes 3145736 | tf_op jit(solution)/shard_map/ppermute | solution.py:631
  308.1 36.3 %collective-permute-start.34 = (bf16[4,256,512]{2,1,0:T(8,128)(2,1)}, bf16[4,256,512]{2,1,0:T(8,128)(2,1)}, u32[]{:S(2)}, u32[]{:S(2)}) collective-permute-start(bf16[4,256,512]{2,1,0:T(8,128)(2,1)} %get-tuple-element.100.refs_21_), channel_id=1, source_target_pairs={{8,0},{16,8},{24,16},{28,24},{20,28},{12,20},{4,12},{0,4},{9,1},{1... | collective-permute-start | bytes 3145736 | tf_op jit(solution)/shard_map/ppermute | solution.py:636
  354.0 38.2 %collective-permute-start.42 = (bf16[1056,512]{1,0:T(8,128)(2,1)S(1)}, bf16[1056,512]{1,0:T(8,128)(2,1)}, u32[]{:S(2)}, u32[]{:S(2)}) collective-permute-start(bf16[1056,512]{1,0:T(8,128)(2,1)S(1)} %copy-done.12), channel_id=1, source_target_pairs={{0,8},{8,16},{16,24},{24,28},{28,20},{20,12},{12,4},{4,0},{1,9},{9... | collective-permute-start | bytes 3244040 | tf_op jit(solution)/shard_map/ppermute | solution.py:631
  359.3 32.9 %collective-permute-start.43 = (bf16[1056,512]{1,0:T(8,128)(2,1)S(1)}, bf16[1056,512]{1,0:T(8,128)(2,1)}, u32[]{:S(2)}, u32[]{:S(2)}) collective-permute-start(bf16[1056,512]{1,0:T(8,128)(2,1)S(1)} %copy-done.12), channel_id=1, source_target_pairs={{8,0},{16,8},{24,16},{28,24},{20,28},{12,20},{4,12},{0,4},{9,1},{1... | collective-permute-start | bytes 3244040 | tf_op jit(solution)/shard_map/ppermute | solution.py:636
  392.2 32.9 %collective-permute-start.44 = (bf16[1056,512]{1,0:T(8,128)(2,1)}, bf16[1056,512]{1,0:T(8,128)(2,1)S(1)}, u32[]{:S(2)}, u32[]{:S(2)}) collective-permute-start(bf16[1056,512]{1,0:T(8,128)(2,1)} %get-tuple-element.111.refs_20_.refs_1_), channel_id=1, source_target_pairs={{0,8},{8,16},{16,24},{24,28},{28,20},{20,12},{12,4},{4,0},{1,9},{9... | collective-permute-start | bytes 3244040 | tf_op jit(solution)/shard_map/ppermute | solution.py:631
  392.7 32.5 %collective-permute-start.45 = (bf16[1056,512]{1,0:T(8,128)(2,1)}, bf16[1056,512]{1,0:T(8,128)(2,1)S(1)}, u32[]{:S(2)}, u32[]{:S(2)}) collective-permute-start(bf16[1056,512]{1,0:T(8,128)(2,1)} %get-tuple-element.112.refs_21_.refs_2_), channel_id=1, source_target_pairs={{8,0},{16,8},{24,16},{28,24},{20,28},{12,20},{4,12},{0,4},{9,1},{1... | collective-permute-start | bytes 3244040 | tf_op jit(solution)/shard_map/ppermute | solution.py:636
  (79 other events, 708.1 us)
